TPU v7x, 768 devices: a whole 4x8x12 slice. The times are simulated.
768 devices in a mesh: row: 24 (over z_lo, y), col: 32 (over x, z_hi, core).
Axes of the slice: x: 4, y: 8, z: 12 (z_hi: 4, z_lo: 3; z = z_hi * 3 + z_lo), core: 2. Of those that a mesh axis runs over, the one named last changes fastest.
Arguments:
- features: bfloat16 [98304, 256], P(('row', 'col')), may hold values from -6 to 6
- weight: bfloat16 [256, 256], replicated, may hold values from -0.375 to 0.375
- tiles: bfloat16 [9216, 128, 128], P(('row', 'col')), may hold values from 0 to 0.0099487305
- tile_pos: int32 [9216], P(('row', 'col')), may hold values from -1 to 767, as said below
- edge_keep: int32 [2, 9216], P(None, ('row', 'col')), may hold values 0 or 1
- feature_keep: int32 [2, 256], replicated, may hold values 0 or 1
- negatives: int32 [98304, 1024], P(('row', 'col')), may hold values from 0 to 3071, as said below
Outputs:
- node_loss: float32 [98304], P(('row', 'col'))
- weight_grad: float32 [256, 256], replicated
Inputs may be any that keep to these rules, and one draw needn't show every extreme that they name: `tile_pos`: on each device the first count slots hold distinct positions and the rest are -1; every device has at least one tile, at least one device has all 12 slots filled. `negatives`: indices into the node's column group, each node's list in ascending order; an index may repeat within a node's list.
All inputs are finite; a program needn't handle non-finite values. No bound on the sum of `edge_keep` on one device may be relied on, other than what follows from the above.
Results may differ from a plain program's by a relative error of at most 0.0035.
Values may be sent and summed in bfloat16 or wider, within the bound.
No kernel may reach another device: no remote copies, remote signals or barrier semaphores. Data moves between devices by JAX's collectives and lax.ppermute only.
A program may use at most 64 MiB of HBM per device.

v0:
```python
import jax
import jax.numpy as jnp
from jax import lax
from jax.sharding import PartitionSpec as P

tau = 0.5
eps = 1e-06


def shards(features, weight, tiles, tile_pos, edge_keep, feature_keep, negatives):
    nodes_here, width = features.shape
    row_count = lax.axis_size("row")
    col_count = lax.axis_size("col")
    tile_rows = row_count * nodes_here // 128
    tile_cols = col_count * nodes_here // 128
    group = row_count * nodes_here
    rowgroup = lax.all_gather(features, "col", axis=0, tiled=True)
    xrows = rowgroup.reshape(tile_cols, 128, width)
    valid = (tile_pos >= 0).astype(jnp.float32)
    clamped = jnp.maximum(tile_pos, 0)
    trow = clamped // tile_cols
    tcol = clamped % tile_cols
    weights_kept = edge_keep.astype(jnp.float32) * valid[None, :]
    product = jnp.einsum("kab,kbf->kaf", tiles, xrows[tcol], preferred_element_type=jnp.float32)
    onehot = (trow[None, :] == jnp.arange(tile_rows)[:, None]).astype(jnp.float32)
    mixing = weights_kept[:, None, :] * onehot[None, :, :]
    summed = jnp.einsum("vtk,kaf->vtaf", mixing, product, precision=lax.Precision.HIGHEST)
    partial_value = summed.reshape(2, group, width).astype(jnp.bfloat16)
    agg = lax.psum_scatter(partial_value, "row", scatter_dimension=1, tiled=True).astype(
        jnp.float32
    )
    agg = agg * feature_keep.astype(jnp.float32)[:, None, :]
    agg_b = agg.astype(jnp.bfloat16)
    z_vals = jnp.einsum("vnf,fg->vng", agg_b, weight, preferred_element_type=jnp.float32)
    rinv = lax.rsqrt(jnp.sum(z_vals * z_vals, -1, keepdims=True) + eps)
    emb = z_vals * rinv
    emb_b = emb.astype(jnp.bfloat16)
    grouped = lax.all_gather(emb_b, "row", axis=1, tiled=True)
    hb1, hb2 = (emb_b[0], emb_b[1])
    h1f, h2f = (hb1.astype(jnp.float32), hb2.astype(jnp.float32))
    counts = (
        jnp.zeros((nodes_here, group), jnp.float32)
        .at[jnp.arange(nodes_here)[:, None], negatives]
        .add(1.0)
    )
    pos = jnp.sum(h1f * h2f, -1) / tau
    s12 = jnp.dot(hb1, grouped[1].T, preferred_element_type=jnp.float32) / tau
    s21 = jnp.dot(hb2, grouped[0].T, preferred_element_type=jnp.float32) / tau
    e12 = counts * jnp.exp(s12)
    e21 = counts * jnp.exp(s21)
    tot1 = jnp.exp(pos) + jnp.sum(e12, 1)
    tot2 = jnp.exp(pos) + jnp.sum(e21, 1)
    node_loss = 0.5 * (jnp.log(tot1) - pos + (jnp.log(tot2) - pos))
    coef = 1.0 / (2.0 * tau * jnp.sqrt(jnp.float32(row_count * col_count * nodes_here)))
    p_one = jnp.exp(pos) / tot1
    p_two = jnp.exp(pos) / tot2
    q_one = (e12 / tot1[:, None]).astype(jnp.bfloat16)
    q_two = (e21 / tot2[:, None]).astype(jnp.bfloat16)
    recv_one, recv_two = (
        lax.all_to_all(q_one, "row", split_axis=1, concat_axis=0, tiled=True),
        lax.all_to_all(q_two, "row", split_axis=1, concat_axis=0, tiled=True),
    )
    back_one = coef * jnp.dot(recv_two.T, grouped[1], preferred_element_type=jnp.float32)
    back_two = coef * jnp.dot(recv_one.T, grouped[0], preferred_element_type=jnp.float32)
    both = (p_one + p_two - 2.0)[:, None]
    d_one = (
        coef * (both * h2f + jnp.dot(q_one, grouped[1], preferred_element_type=jnp.float32))
        + back_one
    )
    d_two = (
        coef * (both * h1f + jnp.dot(q_two, grouped[0], preferred_element_type=jnp.float32))
        + back_two
    )
    d_both = jnp.stack([d_one, d_two])
    dz_vals = (d_both - emb * jnp.sum(emb * d_both, -1, keepdims=True)) * rinv
    local_grad = jnp.einsum(
        "vnf,vng->fg", agg_b.astype(jnp.float32), dz_vals, precision=lax.Precision.HIGHEST
    )
    weight_grad = lax.psum(local_grad, ("row", "col"))
    return (node_loss, weight_grad)


def solution(mesh):
    in_specs = (
        P(("row", "col"), None),
        P(),
        P(("row", "col"), None, None),
        P(("row", "col")),
        P(None, ("row", "col")),
        P(),
        P(("row", "col"), None),
    )
    out_specs = (P(("row", "col")), P())
    return jax.shard_map(shards, mesh=mesh, in_specs=in_specs, out_specs=out_specs, check_vma=False)
```

profile of v0, /device:TPU:1, one launch (start us, length us, event | category | flops | bytes accessed | tf_op | source)
XLA Modules:
  0.0 1674.4 jit_solution(8966332632922561710)
XLA Ops:
  7.2 0.7 all-gather.3.cloned.1.call-update
  8.0 0.7 and_select_fusion.1
  8.6 0.7 compare_convert_fusion
  9.3 0.7 convert_multiply_fusion.3
  10.0 82.3 %all-gather.3.cloned.1.call-done = bf16[4096,256]{1,0:T(8,128)(2,1)} async-done(((bf16[128,256]{1,0:T(8,128)(2,1)}), bf16[4096,256]{1,0:T(8,128)(2,1)}) %all-gather.3.cloned.1.call-update) | async-done | bytes 2097168 | tf_op jit(solution)/shard_map/all_gather | solution.py:17
  92.3 2.2 gather_fusion
  94.5 1.6 fusion.39
  96.1 2.2 copy.14
  98.3 5.5 convolution_convert_fusion
  103.9 2.4 copy.10
  106.3 0.6 copy-done.14
  106.9 100.4 %reduce-scatter.2.cloned.1.call-done = bf16[2,128,256]{2,1,0:T(8,128)(2,1)} async-done(((bf16[2,3072,256]{2,1,0:T(8,128)(2,1)}), bf16[2,128,256]{2,1,0:T(8,128)(2,1)}) %reduce-scatter.2.cloned.1.call-update) | async-done | bytes 131088 | tf_op jit(solution)/shard_map/reduce_scatter | solution.py:29
  207.4 1.2 multiply_reduce_fusion.2
  208.6 0.7 copy-done.6
  209.2 0.7 multiply_convert_fusion.1
  211.1 903.1 %scatter_custom_fusion = f32[393216]{0:T(1024)S(1)} fusion(s32[131072]{0:T(1024)S(1)} %bitcast.99, f32[131072]{0:T(1024)S(1)} %broadcast.92, f32[]{:T(128)} %constant.50.clone.1), kind=kCustom, calls=%fused_computation.33 | custom fusion | flops 131072 | bytes 1572868
  1114.5 1.0 fusion.24
  1115.6 2.3 fusion.38
  1118.0 1.9 fusion.37
  1119.9 0.5 add_add_fusion
  1120.4 1.2 copy_bitcast_fusion.1
  1121.6 4.6 all-to-all-start
  1126.2 2.7 copy_bitcast_fusion
  1128.9 9.7 all-to-all-done
  1138.7 6.0 all-to-all-start.1
  1144.8 2.2 fusion.5
  1147.0 17.9 %all-to-all-done.1 = bf16[128,24,128]{2,0,1:T(8,128)(2,1)} async-done(((bf16[128,24,128]{2,0,1:T(8,128)(2,1)}), bf16[128,24,128]{2,0,1:T(8,128)(2,1)}, u32[]{:S(2)}, u32[]{:S(2)}) %all-to-all-start.1) | async-done | bytes 786464 | tf_op jit(solution)/shard_map/all_to_all | solution.py:60
  1164.9 1.7 fusion.7
  1167.1 1.0 copy-done.4
  1169.2 1.1 convolution_bitcast_fusion
  1170.3 495.8 %all-reduce.2.cloned.1.call-done = f32[256,256]{1,0:T(8,128)} async-done(((f32[256,256]{1,0:T(8,128)}), f32[256,256]{1,0:T(8,128)}) %all-reduce.2.cloned.1.call-update) | async-done | bytes 262160 | tf_op jit(solution)/shard_map/psum | solution.py:79
  1666.1 1.7 copy.23
  (56 shorter events, 3.3 us)
Async XLA Ops:
  7.2 87.4 %copy-start = (bf16[12,128,128]{2,1,0:T(8,128)(2,1)S(1)}, bf16[12,128,128]{2,1,0:T(8,128)(2,1)}, u32[]{:S(2)}) copy-start(bf16[12,128,128]{2,1,0:T(8,128)(2,1)} %param.9) | copy-start | bytes 1179652
  7.2 85.2 %all-gather.3.cloned.1.call-start = ((), (), s32[]{:S(2)}) async-start(), calls=%async_computation.3 | async-start | bytes 2162688 | tf_op jit(solution)/shard_map/all_gather | solution.py:17
  7.9 199.4 %reduce-scatter.2.cloned.1.call-start = ((), (), s32[]{:S(2)}) async-start(), calls=%async_computation.4 | async-start | bytes 3276800 | tf_op jit(solution)/shard_map/reduce_scatter | solution.py:29
  106.2 0.7 copy-start.14
  106.2 101.1 %copy-start.13 = (bf16[256,256]{1,0:T(8,128)(2,1)S(1)}, bf16[256,256]{1,0:T(8,128)(2,1)}, u32[]{:S(2)}) copy-start(bf16[256,256]{1,0:T(8,128)(2,1)} %param.8) | copy-start | bytes 393220
  106.3 103.8 %copy-start.10 = (s32[128,1024]{1,0:T(8,128)S(1)}, s32[128,1024]{1,0:T(8,128)}, u32[]{:S(2)}) copy-start(s32[128,1024]{1,0:T(8,128)} %param.13) | copy-start | bytes 1572868
  106.3 103.9 %copy-start.15 = (s32[2]{0:T(128)S(1)}, s32[2]{0:T(128)}, u32[]{:S(2)}) copy-start(s32[2]{0:T(128)} %constant.63) | copy-start | bytes 28
  106.3 1009.3 %all-gather.5.cloned.1.call-start = ((), (), s32[]{:S(2)}) async-start(), calls=%async_computation.5 | async-start | bytes 3276800 | tf_op jit(solution)/shard_map/all_gather | solution.py:38
  208.5 0.7 copy-start.6
  210.0 0.7 copy-start.16
  1115.5 2.4 copy-start.8
  1115.6 2.4 copy-start.1
  1118.0 2.4 copy-start.3
  1121.6 17.1 %all-to-all-start = ((bf16[128,24,128]{2,0,1:T(8,128)(2,1)}), bf16[128,24,128]{2,0,1:T(8,128)(2,1)}, u32[]{:S(2)}, u32[]{:S(2)}) async-start(bf16[128,24,128]{2,0,1:T(8,128)(2,1)} %copy_bitcast_fusion.1), calls=%async_computation.1 | async-start | bytes 1572864 | tf_op jit(solution)/shard_map/all_to_all | solution.py:61
  1126.2 18.5 %copy-start.2 = (bf16[2,3072,256]{2,1,0:T(8,128)(2,1)S(1)}, bf16[2,3072,256]{2,1,0:T(8,128)(2,1)}, u32[]{:S(2)}) copy-start(bf16[2,3072,256]{2,1,0:T(8,128)(2,1)} %all-gather.5.cloned.1.call-done) | copy-start | bytes 9437188
  1138.7 26.2 %all-to-all-start.1 = ((bf16[128,24,128]{2,0,1:T(8,128)(2,1)}), bf16[128,24,128]{2,0,1:T(8,128)(2,1)}, u32[]{:S(2)}, u32[]{:S(2)}) async-start(bf16[128,24,128]{2,0,1:T(8,128)(2,1)} %copy_bitcast_fusion), calls=%async_computation.2 | async-start | bytes 1572864 | tf_op jit(solution)/shard_map/all_to_all | solution.py:60
  1144.7 521.5 %all-reduce.2.cloned.1.call-start = ((), (), s32[]{:S(2)}) async-start(), calls=%async_computation.6 | async-start | bytes 524288 | tf_op jit(solution)/shard_map/psum | solution.py:79
  1164.9 1.7 copy-start.5
  1164.9 1.7 copy-start.9
  1164.9 1.7 copy-start.12
  1164.9 1.7 copy-start.17
  1166.6 1.4 copy-start.4
  1168.1 0.9 copy-start.7
  1168.1 1.1 copy-start.11
Sparse Core Ops, SparseCore 0:
  11.7 80.5 all-gather.2
  106.4 100.9 reduce-scatter.1
  210.1 129.0 all-gather.4
  1170.5 495.6 all-reduce.1
where the time goes:
time: 1670 us
  other arithmetic  912 us (55%)
  waiting for transfers between devices  707 us (42%)
  matrix products  18.3 us (1%)
    unnamed x4, other arithmetic  904 us
    psum x1, waiting for transfers between devices, shards(): weight_grad = lax.psum(local_grad, ('row', 'col'))  496 us
    reduce_scatter x1, waiting for transfers between devices, shards(): lax.psum_scatter(partial_value, 'row', scatter_dimension=1, tiled=True)  100 us
    all_gather x1, waiting for transfers between devices, shards(): rowgroup = lax.all_gather(features, 'col', axis=0, tiled=True)  82.3 us
  transfers between devices with their start and end apart: 6, of which 5 were waited for; matrix products, arithmetic and copies ran while one was open for 54% of the time, Pallas kernels for 0%

commit v1 on v0

v1 whole, which is shorter than its diff:
```python
import functools

import jax
import jax.numpy as jnp
from jax import lax
from jax.experimental import pallas as pl
from jax.experimental.pallas import tpu as pltpu
from jax.sharding import Mesh
from jax.sharding import PartitionSpec as P

tau = 0.5
eps = 1e-06
T = 128
ZL = 3
FS = 96
f32 = jnp.float32
bf16 = jnp.bfloat16
NT = (((1,), (1,)), ((), ()))
NN = (((1,), (0,)), ((), ()))
ROW = ("zl", "y")
COL = ("x", "zh", "core")
PARAMS = dict(vmem_limit_bytes=48 * 1024 * 1024)


def dot(a, b, dims):
    return lax.dot_general(a, b, dims, preferred_element_type=f32)


def counts_kernel(blocks, neg_ref, out_ref, acc_ref):
    nodes, negs = neg_ref.shape
    rows = 8 * ((blocks + 7) // 8)
    low_iota = lax.broadcasted_iota(jnp.int32, (T, negs), 0)
    high_iota = lax.broadcasted_iota(jnp.int32, (rows, negs), 0)

    def step(i, carry):
        base = pl.multiple_of(i * 8, 8)
        index = neg_ref[pl.ds(base, 8), :]
        low = index & (T - 1)
        high = index >> 7
        for j in range(8):
            low_hot = jnp.where(low[j : j + 1, :] == low_iota, 1.0, 0.0).astype(bf16)
            high_hot = jnp.where(high[j : j + 1, :] == high_iota, 1.0, 0.0).astype(bf16)
            found = dot(high_hot, low_hot, NT)
            acc_ref[pl.ds(base + j, rows, stride=nodes), :] = found
        return carry

    lax.fori_loop(0, nodes // 8, step, 0)

    def turn(h, carry):
        block = acc_ref[pl.ds(pl.multiple_of(h * nodes, nodes), nodes), :]
        out_ref[h] = block.T.astype(jnp.int32).astype(jnp.int16)
        return carry

    lax.fori_loop(0, blocks, turn, 0)


def count_negatives(negatives, blocks):
    nodes = negatives.shape[0]
    rows = 8 * ((blocks + 7) // 8)
    return pl.pallas_call(
        functools.partial(counts_kernel, blocks),
        out_shape=jax.ShapeDtypeStruct((blocks, T, nodes), jnp.int16),
        scratch_shapes=[pltpu.VMEM((rows * nodes, T), f32)],
        compiler_params=pltpu.CompilerParams(**PARAMS),
        cost_estimate=pl.CostEstimate(
            flops=2 * 16 * nodes * T * T * 64, bytes_accessed=2 << 20, transcendentals=0
        ),
        name="counts",
    )(negatives)


def tiles_kernel(cols, ysize, meta_ref, core_ref, own_ref, other_ref, *refs):
    tile_refs, (out_ref, acc_ref) = refs[:ZL], refs[ZL:]
    acc_ref[...] = jnp.zeros_like(acc_ref)
    core = core_ref[0]
    for s in range(ZL):

        def slot(k, carry, s=s):
            place = meta_ref[s, 0, k]

            @pl.when(place >= 0)
            def _():
                tcol = lax.rem(place, cols)
                trow = lax.div(place, cols)
                at = lax.div(tcol, 2)
                mine = lax.rem(tcol, 2) == core
                rows = jnp.where(mine, own_ref[at, s], other_ref[at, s])
                product = dot(rows, tile_refs[s][k], NT)
                yy, zz = lax.rem(trow, ysize), lax.div(trow, ysize)
                for v in range(2):
                    kept = meta_ref[s, 1 + v, k].astype(f32)
                    acc_ref[yy, zz, v] += kept * product

            return carry

        lax.fori_loop(0, tile_refs[s].shape[0], slot, 0)
    out_ref[...] = acc_ref[...].astype(bf16)


def tile_sums(meta, core, own, other, tiles, cols, ysize):
    shape = (ysize, ZL, 2, FS, T)
    return pl.pallas_call(
        functools.partial(tiles_kernel, cols, ysize),
        out_shape=jax.ShapeDtypeStruct(shape, bf16),
        in_specs=[pl.BlockSpec(memory_space=pltpu.SMEM)] * 2
        + [pl.BlockSpec(memory_space=pltpu.VMEM)] * (2 + ZL),
        scratch_shapes=[pltpu.VMEM(shape, f32)],
        compiler_params=pltpu.CompilerParams(**PARAMS),
        name="tile_sums",
    )(meta, core, own, other, *tiles)


def anchors_of(n_ref, v):
    return jnp.concatenate(
        [jnp.concatenate([n_ref[s, z, v] for s in range(ZL)], 0) for z in range(ZL)], 1
    )


def embed(weight_t, agg):
    z = dot(weight_t, agg, NN)
    rinv = lax.rsqrt(jnp.sum(z * z, 0, keepdims=True) + eps)
    return z * rinv, rinv


def scores_kernel(n_ref, a_ref, w_ref, c_ref, tot_ref, e_ref):
    weight_t = w_ref[...]
    width = a_ref.shape[2]
    anchors = [embed(weight_t, anchors_of(n_ref, v))[0].astype(bf16) for v in range(2)]
    tot_ref[...] = jnp.zeros_like(tot_ref)

    def member(y, carry):
        base = pl.multiple_of(y * T, T)
        count = jnp.concatenate(
            [c_ref[z, y].astype(jnp.int32).astype(f32) for z in range(ZL)], 1
        )
        for v in range(2):
            emb = embed(weight_t[:, :width], a_ref[y, 1 - v])[0]
            score = dot(emb.T.astype(bf16), anchors[v], NN)
            term = count * jnp.exp(score * (1.0 / tau))
            e_ref[v, pl.ds(base, T), :] = term
            tot_ref[v : v + 1, :] += jnp.sum(term, 0, keepdims=True)
        return carry

    lax.fori_loop(0, a_ref.shape[0], member, 0)


def split_dot(agg, dz):
    high = dz.astype(bf16)
    low = (dz - high.astype(f32)).astype(bf16)
    return dot(agg, high, NT) + dot(agg, low, NT)


def grads_kernel(coef, n_ref, a_ref, w_ref, e_ref, tot_ref, mask_ref, loss_ref, grad_ref):
    weight_t = w_ref[...]
    ysize, _, width, _ = a_ref.shape
    agg_n = [anchors_of(n_ref, v) for v in range(2)]
    emb_n, rinv_n = zip(*[embed(weight_t, agg) for agg in agg_n])
    low_n = [emb.astype(bf16) for emb in emb_n]
    full_n = [emb.astype(f32) for emb in low_n]
    pos = jnp.sum(full_n[0] * full_n[1], 0, keepdims=True) * (1.0 / tau)
    own = jnp.exp(pos)
    tot = [own + sum(tot_ref[z, v : v + 1, :] for z in range(ZL)) for v in range(2)]
    loss = 0.5 * ((jnp.log(tot[0]) - pos) + (jnp.log(tot[1]) - pos))
    loss_ref[...] = jnp.broadcast_to(loss, loss_ref.shape)
    inverse = [1.0 / t for t in tot]
    both = (own * inverse[0] + own * inverse[1] - 2.0) * mask_ref[0:1, :]

    def back(emb, rinv, d):
        return (d - emb * jnp.sum(emb * d, 0, keepdims=True)) * rinv

    grad_ref[...] = jnp.zeros_like(grad_ref)

    def member(y, carry):
        base = pl.multiple_of(y * T, T)
        parts = [embed(weight_t[:, :width], a_ref[y, v]) for v in range(2)]
        low = [emb.astype(bf16) for emb, _ in parts]
        q = [(e_ref[v, pl.ds(base, T), :] * inverse[v]).astype(bf16) for v in range(2)]
        d_one = coef * dot(low_n[1], q[1], NT)
        d_two = coef * dot(low_n[0], q[0], NT)
        for v, d in ((0, d_one), (1, d_two)):
            dz = back(parts[v][0], parts[v][1], d)
            grad_ref[...] += split_dot(a_ref[y, v], dz)
        return carry[0] + dot(low[1], q[0], NN), carry[1] + dot(low[0], q[1], NN)

    sums = (jnp.zeros_like(pos) + jnp.zeros((weight_t.shape[0], 1), f32),) * 2
    sums = lax.fori_loop(0, ysize, member, sums)
    for v in range(2):
        d = coef * (both * full_n[1 - v] + sums[v])
        dz = back(emb_n[v], rinv_n[v], d)
        grad_ref[...] += split_dot(agg_n[v], dz)[:width]


def vmem_call(kernel, out_shape, name):
    return pl.pallas_call(
        kernel,
        out_shape=out_shape,
        compiler_params=pltpu.CompilerParams(**PARAMS),
        name=name,
    )


def swap(x, axis):
    return lax.all_to_all(x, axis, 0, 0, tiled=True)


def share(x, axis):
    return swap(jnp.broadcast_to(x[None], (lax.axis_size(axis),) + x.shape), axis)


def shift(x, axis, by):
    size = lax.axis_size(axis)
    return lax.ppermute(x, axis, [(i, (i + by) % size) for i in range(size)])


def reduce_all(grad):
    rows, width = grad.shape
    plane = ("y", "x", "core")
    size = lax.axis_size(plane)
    part = jnp.sum(swap(grad.reshape(size, -1, T), plane), 0)
    part = jnp.sum(share(part, ("zl", "zh")), 0)
    return share(part, plane).reshape(rows, width)


def shards(features, weight, tiles, tile_pos, edge_keep, feature_keep, negatives):
    nodes, width = features.shape
    ysize, xsize = lax.axis_size("y"), lax.axis_size("x")
    zsize = lax.axis_size("zh")
    cols = xsize * zsize * lax.axis_size("core")
    zl, core = lax.axis_index("zl"), lax.axis_index("core")
    total = lax.axis_size(ROW) * cols * nodes
    pad = ZL * FS - width

    meta = jnp.concatenate([tile_pos[None], edge_keep], 0)
    metas = jnp.stack([meta] + [shift(meta, "zl", s) for s in range(1, ZL)])
    all_tiles = [tiles] + [shift(tiles, "zl", s) for s in range(1, ZL)]

    turned = jnp.pad(features.T, ((0, pad), (0, 0))).reshape(ZL, FS, nodes)

    def slice_for(s):
        return lax.dynamic_index_in_dim(turned, lax.rem(zl + s, ZL), 0, keepdims=False)

    mine = jnp.stack([slice_for(0)] + [shift(slice_for(s), "zl", s) for s in range(1, ZL)])
    own = share(mine, ("x", "zh"))
    other = shift(own, "core", 1)

    counts = count_negatives(negatives, ZL * ysize)
    counts = swap(counts, "zl").reshape(ZL, ysize, nodes, nodes)

    part = tile_sums(metas, core.reshape(1), own, other, all_tiles, cols, ysize)
    got = swap(part, "y")
    keep = jnp.pad(feature_keep, ((0, 0), (0, pad))).reshape(2, ZL, FS)
    keep = lax.dynamic_index_in_dim(keep, zl, 1, keepdims=False).astype(f32)
    agg = (jnp.sum(got.astype(f32), 0) * keep[None, :, :, None]).astype(bf16)
    anchors = share(agg, "zl")
    one = lax.dynamic_index_in_dim(anchors, zl, 1, keepdims=False)
    one = one.transpose(1, 0, 2, 3).reshape(2, ZL * FS, nodes)[:, :width]
    members = share(one, "y")

    weight_t = jnp.pad(weight.T, ((0, 0), (0, pad)))
    group = ZL * nodes
    tot, terms = vmem_call(
        scores_kernel,
        (
            jax.ShapeDtypeStruct((8, group), f32),
            jax.ShapeDtypeStruct((2, ysize * nodes, group), f32),
        ),
        "scores",
    )(anchors, members, weight_t, counts)
    tots = share(tot, "zl")
    mask = (jnp.arange(group) // nodes == zl).astype(f32)
    coef = 1.0 / (2.0 * tau * float(total) ** 0.5)
    loss, grad = vmem_call(
        functools.partial(grads_kernel, coef),
        (
            jax.ShapeDtypeStruct((8, group), f32),
            jax.ShapeDtypeStruct((width, width), f32),
        ),
        "grads",
    )(anchors, members, weight_t, terms, tots, jnp.broadcast_to(mask, (8, group)))
    node_loss = lax.dynamic_slice_in_dim(loss[0], zl * nodes, nodes)
    return node_loss, reduce_all(grad)


def solution(mesh):
    rows, cols = mesh.devices.shape
    fine = Mesh(mesh.devices.reshape(ZL, rows // ZL, cols // 8, 4, 2), ROW + COL)
    every = ROW + COL
    in_specs = (
        P(every, None),
        P(),
        P(every, None, None),
        P(every),
        P(None, every),
        P(),
        P(every, None),
    )
    out_specs = (P(every), P())
    return jax.shard_map(shards, mesh=fine, in_specs=in_specs, out_specs=out_specs, check_vma=False)
```

time: 1670 us -> 297 us (0.18)
  other arithmetic: 912 us -> 0.37 us
  waiting for transfers between devices: 707 us -> 104 us
  blocking collectives: 0 us -> 97.6 us
  starting transfers between devices: 10.8 us -> 49.5 us
  Pallas kernels: 0 us -> 34.1 us
  matrix products: 18.3 us -> 0 us
    unnamed x4 -> x0, other arithmetic: 904 us -> none
    psum x1 -> x0, waiting for transfers between devices: 496 us -> none  [shards(): weight_grad = lax.psum(local_grad, ('row', 'col'))]
    reduce_scatter x1 -> x0, waiting for transfers between devices: 100 us -> none  [shards(): lax.psum_scatter(partial_value, 'row', scatter_dimension=1, tiled=True)]
    all_to_all x0 -> x3, blocking collectives: none -> 97.6 us  [swap(): return lax.all_to_all(x, axis, 0, 0, tiled=True)]
    all_gather x2 -> x0, waiting for transfers between devices: 82.3 us -> none  [the longest x1 82.3 us: shards(): rowgroup = lax.all_gather(features, 'col', axis=0, tiled=True)]
    all_to_all x2 -> x6, waiting for transfers between devices: 27.6 us -> 90.2 us  [swap(): return lax.all_to_all(x, axis, 0, 0, tiled=True)]
    pallas_call x0 -> x4, Pallas kernels: none -> 34.1 us  [the longest x1 16.7 us: count_negatives(): pl.pallas_call(functools.partial(counts_kernel, blocks), out_shape=jax.Sh...]
    ppermute x0 -> x7, starting transfers between devices: none -> 23.8 us  [shift(): return lax.ppermute(x, axis, [(i, (i + by) % size) for i in range(size)])]
  transfers between devices with their start and end apart: 6 -> 13, of which waited for: 5 -> 8; matrix products, arithmetic and copies ran while one was open for 54% -> 0% of each run, Pallas kernels for 0% -> 6%
where the time goes in v1:
time: 297 us; the launch traced here: 296 us
  waiting for transfers between devices  104 us (35%)
  blocking collectives  97.6 us (33%)
  starting transfers between devices  49.5 us (17%)
  Pallas kernels  34.1 us (11%)
  local copies, waits for them, and re-layouts  9.65 us (3%)
    all_to_all x3, blocking collectives, swap(): return lax.all_to_all(x, axis, 0, 0, tiled=True)  97.6 us
    all_to_all x6, waiting for transfers between devices, swap(): return lax.all_to_all(x, axis, 0, 0, tiled=True)  90.2 us
    all_to_all x6, starting transfers between devices, swap(): return lax.all_to_all(x, axis, 0, 0, tiled=True)  25.7 us
    ppermute x7, starting transfers between devices, shift(): return lax.ppermute(x, axis, [(i, (i + by) % size) for i in range(size)])  23.8 us
    pallas_call x1, Pallas kernels, count_negatives(): pl.pallas_call(functools.partial(counts_kernel, blocks), out_shape=jax.Sh...  16.7 us
    ppermute x7, waiting for transfers between devices, shift(): return lax.ppermute(x, axis, [(i, (i + by) % size) for i in range(size)])  13.5 us
    pallas_call x1, Pallas kernels, shards(): vmem_call(functools.partial(grads_kernel, coef), (jax.ShapeDtypeStruct((8...  7.82 us
  transfers between devices with their start and end apart: 13, of which 8 were waited for; matrix products, arithmetic and copies ran while one was open for 0% of the time, Pallas kernels for 6%

profile of v1, /device:TPU:1, one launch (start us, length us, event | category | flops | bytes accessed | tf_op | source)
XLA Modules:
  0.0 295.9 jit_solution(4173923818968681184)
XLA Ops:
  0.7 0.9 copy.18
  1.7 6.6 %collective-permute-start.3 = (bf16[96,128]{1,0:T(8,128)(2,1)S(1)}, bf16[96,128]{1,0:T(8,128)(2,1)S(1)}, u32[]{:S(2)}, u32[]{:S(2)}) collective-permute-start(bf16[96,128]{1,0:T(8,128)(2,1)S(1)} %get-tuple-element.11), channel_id=1, source_target_pairs={{0,512},{256,0},{512,256},{1,513},{257,1},{513,257},{2,514},{258,2... | collective-permute-start | bytes 73736 | tf_op jit(solution)/shard_map/ppermute | solution.py:212
  8.3 1.9 collective-permute-start.2
  10.3 3.5 %collective-permute-done.2 = bf16[96,128]{1,0:T(8,128)(2,1)S(1)} collective-permute-done((bf16[96,128]{1,0:T(8,128)(2,1)S(1)}, bf16[96,128]{1,0:T(8,128)(2,1)S(1)}, u32[]{:S(2)}, u32[]{:S(2)}) %collective-permute-start.2) | collective-permute-done | bytes 24608 | tf_op jit(solution)/shard_map/ppermute | solution.py:212
  14.0 61.6 %all_to_all.45.own_ref = bf16[16,3,96,128]{3,2,1,0:T(8,128)(2,1)S(1)} all-to-all(bf16[16,3,96,128]{3,2,1,0:T(8,128)(2,1)S(1)} %broadcast_in_dim.17), channel_id=1, replica_groups=mesh['zl'=3,'y'=8,'x'=4,'zh'=4,'core'=2] {'x','zh'}, dimensions={0} | all-to-all | bytes 2359296 | tf_op jit(solution)/shard_map/all_to_all | solution.py:203
  75.6 2.9 collective-permute-start.4
  78.5 1.9 collective-permute-start.5
  80.4 4.3 %collective-permute-start.6 = (bf16[12,128,128]{2,1,0:T(8,128)(2,1)S(1)}, bf16[12,128,128]{2,1,0:T(8,128)(2,1)S(1)}, u32[]{:S(2)}, u32[]{:S(2)}) collective-permute-start(bf16[12,128,128]{2,1,0:T(8,128)(2,1)S(1)} %copy-done.2), channel_id=1, source_target_pairs={{0,512},{256,0},{512,256},{1,513},{257,1},{513,257},{2,514},{258,2... | collective-permute-start | bytes 1179656 | tf_op jit(solution)/shard_map/ppermute | solution.py:212
  84.8 1.9 collective-permute-start
  86.7 4.3 %collective-permute-start.1 = (s32[3,12]{1,0:T(4,128)S(1)}, s32[3,12]{1,0:T(4,128)S(1)}, u32[]{:S(2)}, u32[]{:S(2)}) collective-permute-start(s32[3,12]{1,0:T(4,128)S(1)} %get-tuple-element.14), channel_id=1, source_target_pairs={{0,512},{256,0},{512,256},{1,513},{257,1},{513,257},{2,514},{258,2... | collective-permute-start | bytes 440 | tf_op jit(solution)/shard_map/ppermute | solution.py:212
  90.9 9.3 %collective-permute-done = s32[3,12]{1,0:T(4,128)S(1)} collective-permute-done((s32[3,12]{1,0:T(4,128)S(1)}, s32[3,12]{1,0:T(4,128)S(1)}, u32[]{:S(2)}, u32[]{:S(2)}) %collective-permute-start) | collective-permute-done | bytes 176 | tf_op jit(solution)/shard_map/ppermute | solution.py:212
  100.9 4.7 %tile_sums.1 = bf16[8,3,2,96,128]{4,3,2,1,0:T(8,128)(2,1)} custom-call(s32[3,3,12]{2,1,0:T(4,128)S(1)} %pad_add_fusion.meta_ref, s32[1]{0:T(128)} %bitcast.4.core_ref, bf16[16,3,96,128]{3,2,1,0:T(8,128)(2,1)S(1)} %all_to_all.45.own_ref, bf16[16,3,96,128]{3,2,1,0:T(8,128)(2,1)S(1)} %collective-permute-done.4.other_ref, bf16[12,128,128]{2,1,0:T(8,128)(2,1)S(1)} %copy-done.2, ...), custom_call_target="tpu_custom_call" | custom-call | tf_op jit(solution)/shard_map/tile_sums/pallas_call | solution.py:102
  105.6 5.4 %all-to-all-start.1 = ((bf16[8,3,2,96,128]{4,3,2,1,0:T(8,128)(2,1)}), bf16[8,3,2,96,128]{4,3,2,1,0:T(8,128)(2,1)S(1)}, u32[]{:S(2)}, u32[]{:S(2)}) async-start(bf16[8,3,2,96,128]{4,3,2,1,0:T(8,128)(2,1)} %tile_sums.1), calls=%async_computation.1 | async-start | bytes 2359296 | tf_op jit(solution)/shard_map/all_to_all | solution.py:203
  111.1 31.9 %all-to-all-done.1 = bf16[8,3,2,96,128]{4,3,2,1,0:T(8,128)(2,1)S(1)} async-done(((bf16[8,3,2,96,128]{4,3,2,1,0:T(8,128)(2,1)}), bf16[8,3,2,96,128]{4,3,2,1,0:T(8,128)(2,1)S(1)}, u32[]{:S(2)}, u32[]{:S(2)}) %all-to-all-start.1) | async-done | bytes 1179680 | tf_op jit(solution)/shard_map/all_to_all | solution.py:203
  143.3 0.9 broadcast_in_dim.18
  144.2 3.5 %all-to-all-start.2 = ((bf16[3,3,2,96,128]{4,3,2,1,0:T(8,128)(2,1)}), bf16[3,3,2,96,128]{4,3,2,1,0:T(8,128)(2,1)S(1)}, u32[]{:S(2)}, u32[]{:S(2)}) async-start(bf16[3,3,2,96,128]{4,3,2,1,0:T(8,128)(2,1)} %broadcast_in_dim.18), calls=%async_computation.2 | async-start | bytes 884736 | tf_op jit(solution)/shard_map/all_to_all | solution.py:203
  147.7 16.7 %counts.1 = s16[24,128,128]{2,1,0:T(8,128)(2,1)} custom-call(s32[128,1024]{1,0:T(8,128)S(1)} %copy-done.3), custom_call_target="tpu_custom_call" | custom-call | flops 4294967296 | bytes 2097152 | tf_op jit(solution)/shard_map/counts/pallas_call | solution.py:60
  164.3 3.6 %all-to-all-start.4 = ((s16[24,128,128]{2,1,0:T(8,128)(2,1)}), s16[24,128,128]{2,1,0:T(8,128)(2,1)S(1)}, u32[]{:S(2)}, u32[]{:S(2)}) async-start(s16[24,128,128]{2,1,0:T(8,128)(2,1)} %counts.1), calls=%async_computation.4 | async-start | bytes 1572864 | tf_op jit(solution)/shard_map/all_to_all | solution.py:203
  168.0 13.0 %all-to-all-done.4 = s16[24,128,128]{2,1,0:T(8,128)(2,1)S(1)} async-done(((s16[24,128,128]{2,1,0:T(8,128)(2,1)}), s16[24,128,128]{2,1,0:T(8,128)(2,1)S(1)}, u32[]{:S(2)}, u32[]{:S(2)}) %all-to-all-start.4) | async-done | bytes 786464 | tf_op jit(solution)/shard_map/all_to_all | solution.py:203
  181.0 1.2 broadcast_in_dim.19
  182.2 3.7 %all-to-all-start.3 = ((bf16[8,2,256,128]{3,2,1,0:T(8,128)(2,1)}), bf16[8,2,256,128]{3,2,1,0:T(8,128)(2,1)S(1)}, u32[]{:S(2)}, u32[]{:S(2)}) async-start(bf16[8,2,256,128]{3,2,1,0:T(8,128)(2,1)} %broadcast_in_dim.19), calls=%async_computation.3 | async-start | bytes 2097152 | tf_op jit(solution)/shard_map/all_to_all | solution.py:203
  186.1 29.0 %all-to-all-done.3.a_ref = bf16[8,2,256,128]{3,2,1,0:T(8,128)(2,1)S(1)} async-done(((bf16[8,2,256,128]{3,2,1,0:T(8,128)(2,1)}), bf16[8,2,256,128]{3,2,1,0:T(8,128)(2,1)S(1)}, u32[]{:S(2)}, u32[]{:S(2)}) %all-to-all-start.3) | async-done | bytes 1048608 | tf_op jit(solution)/shard_map/all_to_all | solution.py:203
  215.0 4.9 %scores.1 = (f32[8,384]{1,0:T(8,128)S(1)}, f32[2,1024,384]{2,1,0:T(8,128)S(1)}) custom-call(bf16[3,3,2,96,128]{4,3,2,1,0:T(8,128)(2,1)S(1)} %all-to-all-done.2.n_ref, bf16[8,2,256,128]{3,2,1,0:T(8,128)(2,1)S(1)} %all-to-all-done.3.a_ref, bf16[256,288]{1,0:T(8,128)(2,1)S(1)} %pad.14.w_ref, s16[3,8,128,128]{3,2,1,0:T(8,128)(2,1)S(1)} %bitcast.24), custom_call_target="tpu_custom_call" | custom-call | tf_op jit(solution)/shard_map/scores/pallas_call | solution.py:261
  220.0 1.6 copy-done
  222.2 3.3 %all-to-all-start.5 = ((f32[3,8,384]{2,1,0:T(8,128)}), f32[3,8,384]{2,1,0:T(8,128)S(1)}, u32[]{:S(2)}, u32[]{:S(2)}) async-start(f32[3,8,384]{2,1,0:T(8,128)} %broadcast_in_dim.20), calls=%async_computation.5 | async-start | bytes 73728 | tf_op jit(solution)/shard_map/all_to_all | solution.py:203
  225.5 3.6 %all-to-all-done.5.tot_ref = f32[3,8,384]{2,1,0:T(8,128)S(1)} async-done(((f32[3,8,384]{2,1,0:T(8,128)}), f32[3,8,384]{2,1,0:T(8,128)S(1)}, u32[]{:S(2)}, u32[]{:S(2)}) %all-to-all-start.5) | async-done | bytes 36896 | tf_op jit(solution)/shard_map/all_to_all | solution.py:203
  229.2 1.9 copy-done.1
  231.1 7.8 %grads.1 = (f32[8,384]{1,0:T(8,128)S(1)}, f32[256,256]{1,0:T(8,128)S(1)}) custom-call(bf16[3,3,2,96,128]{4,3,2,1,0:T(8,128)(2,1)S(1)} %all-to-all-done.2.n_ref, bf16[8,2,256,128]{3,2,1,0:T(8,128)(2,1)S(1)} %all-to-all-done.3.a_ref, bf16[256,288]{1,0:T(8,128)(2,1)S(1)} %pad.14.w_ref, f32[2,1024,384]{2,1,0:T(8,128)S(1)} %copy-done.1, ...), custom_call_target="tpu_custom_call" | custom-call | tf_op jit(solution)/shard_map/grads/pallas_call | solution.py:272
  238.9 19.8 %all_to_all.46 = f32[64,8,128]{2,1,0:T(8,128)S(1)} all-to-all(f32[64,8,128]{2,1,0:T(8,128)S(1)} %reshape.46), channel_id=1, replica_groups=mesh['zl'=3,'y'=8,'x'=4,'zh'=4,'core'=2] {'y','x','core'}, dimensions={0} | all-to-all | bytes 524288 | tf_op jit(solution)/shard_map/all_to_all | solution.py:203
  258.8 16.2 %all_to_all.47 = f32[12,8,128]{2,1,0:T(8,128)S(1)} all-to-all(f32[12,8,128]{2,1,0:T(8,128)S(1)} %broadcast_in_dim.22), channel_id=1, replica_groups=mesh['zl'=3,'y'=8,'x'=4,'zh'=4,'core'=2] {'zl','zh'}, dimensions={0} | all-to-all | bytes 98304 | tf_op jit(solution)/shard_map/all_to_all | solution.py:203
  275.7 6.3 %all-to-all-start.8 = ((f32[64,8,128]{2,1,0:T(8,128)}), f32[64,8,128]{2,1,0:T(8,128)S(1)}, u32[]{:S(2)}, u32[]{:S(2)}) async-start(f32[64,8,128]{2,1,0:T(8,128)} %broadcast_in_dim.23), calls=%async_computation.8 | async-start | bytes 524288 | tf_op jit(solution)/shard_map/all_to_all | solution.py:203
  282.5 12.6 %all-to-all-done.8 = f32[64,8,128]{2,1,0:T(8,128)S(1)} async-done(((f32[64,8,128]{2,1,0:T(8,128)}), f32[64,8,128]{2,1,0:T(8,128)S(1)}, u32[]{:S(2)}, u32[]{:S(2)}) %all-to-all-start.8) | async-done | bytes 262176 | tf_op jit(solution)/shard_map/all_to_all | solution.py:203
  (47 shorter events, 4.1 us)
Async XLA Ops:
  1.7 8.6 %collective-permute-start.3 = (bf16[96,128]{1,0:T(8,128)(2,1)S(1)}, bf16[96,128]{1,0:T(8,128)(2,1)S(1)}, u32[]{:S(2)}, u32[]{:S(2)}) collective-permute-start(bf16[96,128]{1,0:T(8,128)(2,1)S(1)} %get-tuple-element.11), channel_id=1, source_target_pairs={{0,512},{256,0},{512,256},{1,513},{257,1},{513,257},{2,514},{258,2... | collective-permute-start | bytes 73736 | tf_op jit(solution)/shard_map/ppermute | solution.py:212
  8.3 5.5 %collective-permute-start.2 = (bf16[96,128]{1,0:T(8,128)(2,1)S(1)}, bf16[96,128]{1,0:T(8,128)(2,1)S(1)}, u32[]{:S(2)}, u32[]{:S(2)}) collective-permute-start(bf16[96,128]{1,0:T(8,128)(2,1)S(1)} %get-tuple-element.12), channel_id=1, source_target_pairs={{0,256},{256,512},{512,0},{1,257},{257,513},{513,1},{2,258},{258,5... | collective-permute-start | bytes 73736 | tf_op jit(solution)/shard_map/ppermute | solution.py:212
  14.0 64.5 %copy-start.2 = (bf16[12,128,128]{2,1,0:T(8,128)(2,1)S(1)}, bf16[12,128,128]{2,1,0:T(8,128)(2,1)}, u32[]{:S(2)}) copy-start(bf16[12,128,128]{2,1,0:T(8,128)(2,1)} %refs_0_.1) | copy-start | bytes 1179652
  14.0 70.7 %copy-start.6 = (s32[2,12]{1,0:T(2,128)S(1)}, s32[2,12]{1,0:T(2,128)}, u32[]{:S(2)}) copy-start(s32[2,12]{1,0:T(2,128)} %param.11) | copy-start | bytes 292
  14.0 70.7 %copy-start.7 = (s32[12]{0:T(128)S(1)}, s32[12]{0:T(128)}, u32[]{:S(2)}) copy-start(s32[12]{0:T(128)} %param.10) | copy-start | bytes 148
  75.6 25.3 %collective-permute-start.4 = (bf16[16,3,96,128]{3,2,1,0:T(8,128)(2,1)S(1)}, bf16[16,3,96,128]{3,2,1,0:T(8,128)(2,1)S(1)}, u32[]{:S(2)}, u32[]{:S(2)}) collective-permute-start(bf16[16,3,96,128]{3,2,1,0:T(8,128)(2,1)S(1)} %all_to_all.45.own_ref), channel_id=1, source_target_pairs={{0,1},{1,0},{2,3},{3,2},{4,5},{5,4},{6,7},{7,6},{8,9},{9,8},{10,11... | collective-permute-start | bytes 3538952 | tf_op jit(solution)/shard_map/ppermute | solution.py:212
  78.5 22.4 %collective-permute-start.5 = (bf16[12,128,128]{2,1,0:T(8,128)(2,1)S(1)}, bf16[12,128,128]{2,1,0:T(8,128)(2,1)S(1)}, u32[]{:S(2)}, u32[]{:S(2)}) collective-permute-start(bf16[12,128,128]{2,1,0:T(8,128)(2,1)S(1)} %copy-done.2), channel_id=1, source_target_pairs={{0,256},{256,512},{512,0},{1,257},{257,513},{513,1},{2,258},{258,5... | collective-permute-start | bytes 1179656 | tf_op jit(solution)/shard_map/ppermute | solution.py:212
  80.4 20.5 %collective-permute-start.6 = (bf16[12,128,128]{2,1,0:T(8,128)(2,1)S(1)}, bf16[12,128,128]{2,1,0:T(8,128)(2,1)S(1)}, u32[]{:S(2)}, u32[]{:S(2)}) collective-permute-start(bf16[12,128,128]{2,1,0:T(8,128)(2,1)S(1)} %copy-done.2), channel_id=1, source_target_pairs={{0,512},{256,0},{512,256},{1,513},{257,1},{513,257},{2,514},{258,2... | collective-permute-start | bytes 1179656 | tf_op jit(solution)/shard_map/ppermute | solution.py:212
  84.8 15.5 %collective-permute-start = (s32[3,12]{1,0:T(4,128)S(1)}, s32[3,12]{1,0:T(4,128)S(1)}, u32[]{:S(2)}, u32[]{:S(2)}) collective-permute-start(s32[3,12]{1,0:T(4,128)S(1)} %get-tuple-element.14), channel_id=1, source_target_pairs={{0,256},{256,512},{512,0},{1,257},{257,513},{513,1},{2,258},{258,5... | collective-permute-start | bytes 440 | tf_op jit(solution)/shard_map/ppermute | solution.py:212
  86.7 14.2 %collective-permute-start.1 = (s32[3,12]{1,0:T(4,128)S(1)}, s32[3,12]{1,0:T(4,128)S(1)}, u32[]{:S(2)}, u32[]{:S(2)}) collective-permute-start(s32[3,12]{1,0:T(4,128)S(1)} %get-tuple-element.14), channel_id=1, source_target_pairs={{0,512},{256,0},{512,256},{1,513},{257,1},{513,257},{2,514},{258,2... | collective-permute-start | bytes 440 | tf_op jit(solution)/shard_map/ppermute | solution.py:212
  105.6 5.4 %copy-start.5 = (s32[2,256]{1,0:T(2,128)S(1)}, s32[2,256]{1,0:T(2,128)}, u32[]{:S(2)}) copy-start(s32[2,256]{1,0:T(2,128)} %param.12) | copy-start | bytes 6148
  105.6 37.4 %all-to-all-start.1 = ((bf16[8,3,2,96,128]{4,3,2,1,0:T(8,128)(2,1)}), bf16[8,3,2,96,128]{4,3,2,1,0:T(8,128)(2,1)S(1)}, u32[]{:S(2)}, u32[]{:S(2)}) async-start(bf16[8,3,2,96,128]{4,3,2,1,0:T(8,128)(2,1)} %tile_sums.1), calls=%async_computation.1 | async-start | bytes 2359296 | tf_op jit(solution)/shard_map/all_to_all | solution.py:203
  143.2 4.5 %copy-start.3 = (s32[128,1024]{1,0:T(8,128)S(1)}, s32[128,1024]{1,0:T(8,128)}, u32[]{:S(2)}) copy-start(s32[128,1024]{1,0:T(8,128)} %neg_ref.1) | copy-start | bytes 1572868
  144.2 20.2 %all-to-all-start.2 = ((bf16[3,3,2,96,128]{4,3,2,1,0:T(8,128)(2,1)}), bf16[3,3,2,96,128]{4,3,2,1,0:T(8,128)(2,1)S(1)}, u32[]{:S(2)}, u32[]{:S(2)}) async-start(bf16[3,3,2,96,128]{4,3,2,1,0:T(8,128)(2,1)} %broadcast_in_dim.18), calls=%async_computation.2 | async-start | bytes 884736 | tf_op jit(solution)/shard_map/all_to_all | solution.py:203
  164.3 16.7 %all-to-all-start.4 = ((s16[24,128,128]{2,1,0:T(8,128)(2,1)}), s16[24,128,128]{2,1,0:T(8,128)(2,1)S(1)}, u32[]{:S(2)}, u32[]{:S(2)}) async-start(s16[24,128,128]{2,1,0:T(8,128)(2,1)} %counts.1), calls=%async_computation.4 | async-start | bytes 1572864 | tf_op jit(solution)/shard_map/all_to_all | solution.py:203
  182.2 3.7 %copy-start.4 = (bf16[256,256]{1,0:T(8,128)(2,1)S(1)}, bf16[256,256]{1,0:T(8,128)(2,1)}, u32[]{:S(2)}) copy-start(bf16[256,256]{1,0:T(8,128)(2,1)} %param.8) | copy-start | bytes 393220
  182.2 32.8 %all-to-all-start.3 = ((bf16[8,2,256,128]{3,2,1,0:T(8,128)(2,1)}), bf16[8,2,256,128]{3,2,1,0:T(8,128)(2,1)S(1)}, u32[]{:S(2)}, u32[]{:S(2)}) async-start(bf16[8,2,256,128]{3,2,1,0:T(8,128)(2,1)} %broadcast_in_dim.19), calls=%async_computation.3 | async-start | bytes 2097152 | tf_op jit(solution)/shard_map/all_to_all | solution.py:203
  220.0 1.6 copy-start
  222.2 6.9 %all-to-all-start.5 = ((f32[3,8,384]{2,1,0:T(8,128)}), f32[3,8,384]{2,1,0:T(8,128)S(1)}, u32[]{:S(2)}, u32[]{:S(2)}) async-start(f32[3,8,384]{2,1,0:T(8,128)} %broadcast_in_dim.20), calls=%async_computation.5 | async-start | bytes 73728 | tf_op jit(solution)/shard_map/all_to_all | solution.py:203
  229.2 1.9 copy-start.1
  275.7 19.5 %all-to-all-start.8 = ((f32[64,8,128]{2,1,0:T(8,128)}), f32[64,8,128]{2,1,0:T(8,128)S(1)}, u32[]{:S(2)}, u32[]{:S(2)}) async-start(f32[64,8,128]{2,1,0:T(8,128)} %broadcast_in_dim.23), calls=%async_computation.8 | async-start | bytes 524288 | tf_op jit(solution)/shard_map/all_to_all | solution.py:203

commit v2 on v1

--- a/solution.py
+++ b/solution.py
@@ -69,35 +69,39 @@
     )(negatives)
 
 
-def tiles_kernel(cols, ysize, meta_ref, core_ref, own_ref, other_ref, *refs):
+def behind(zl, s):
+    return lax.rem(zl + ZL - s, ZL)
+
+
+def tiles_kernel(cols, ysize, meta_ref, place_ref, own_ref, other_ref, *refs):
     tile_refs, (out_ref, acc_ref) = refs[:ZL], refs[ZL:]
+    zsize = own_ref.shape[1] // ZL
     acc_ref[...] = jnp.zeros_like(acc_ref)
-    core = core_ref[0]
+    core, zl = place_ref[0], place_ref[1]
     for s in range(ZL):
 
         def slot(k, carry, s=s):
-            place = meta_ref[s, 0, k]
-
-            @pl.when(place >= 0)
+            trow, tcol = meta_ref[s, 0, k], meta_ref[s, 1, k]
+
+            @pl.when(trow >= 0)
             def _():
-                tcol = lax.rem(place, cols)
-                trow = lax.div(place, cols)
-                at = lax.div(tcol, 2)
+                chip = lax.div(tcol, 2)
+                at = lax.div(chip, zsize), behind(zl, s) * zsize + lax.rem(chip, zsize)
                 mine = lax.rem(tcol, 2) == core
-                rows = jnp.where(mine, own_ref[at, s], other_ref[at, s])
-                product = dot(rows, tile_refs[s][k], NT)
+                rows = jnp.where(mine, own_ref[at], other_ref[at])
+                product = dot(rows, tile_refs[s][pl.ds(pl.multiple_of(k * T, T), T), :], NT)
                 yy, zz = lax.rem(trow, ysize), lax.div(trow, ysize)
                 for v in range(2):
-                    kept = meta_ref[s, 1 + v, k].astype(f32)
+                    kept = meta_ref[s, 2 + v, k].astype(f32)
                     acc_ref[yy, zz, v] += kept * product
 
             return carry
 
-        lax.fori_loop(0, tile_refs[s].shape[0], slot, 0)
+        lax.fori_loop(0, meta_ref.shape[2], slot, 0)
     out_ref[...] = acc_ref[...].astype(bf16)
 
 
-def tile_sums(meta, core, own, other, tiles, cols, ysize):
+def tile_sums(meta, place, own, other, tiles, cols, ysize):
     shape = (ysize, ZL, 2, FS, T)
     return pl.pallas_call(
         functools.partial(tiles_kernel, cols, ysize),
@@ -107,12 +111,13 @@
         scratch_shapes=[pltpu.VMEM(shape, f32)],
         compiler_params=pltpu.CompilerParams(**PARAMS),
         name="tile_sums",
-    )(meta, core, own, other, *tiles)
-
-
-def anchors_of(n_ref, v):
+    )(meta, place, own, other, *tiles)
+
+
+def anchors_of(n_ref, zl, v):
+    shares = [n_ref.at[behind(zl, s)] for s in range(ZL)]
     return jnp.concatenate(
-        [jnp.concatenate([n_ref[s, z, v] for s in range(ZL)], 0) for z in range(ZL)], 1
+        [jnp.concatenate([share[z, v] for share in shares], 0) for z in range(ZL)], 1
     )
 
 
@@ -122,16 +127,17 @@
     return z * rinv, rinv
 
 
-def scores_kernel(n_ref, a_ref, w_ref, c_ref, tot_ref, e_ref):
+def scores_kernel(place_ref, n_ref, a_ref, w_ref, c_ref, tot_ref, e_ref):
     weight_t = w_ref[...]
     width = a_ref.shape[2]
-    anchors = [embed(weight_t, anchors_of(n_ref, v))[0].astype(bf16) for v in range(2)]
+    zl = place_ref[1]
+    anchors = [embed(weight_t, anchors_of(n_ref, zl, v))[0].astype(bf16) for v in range(2)]
     tot_ref[...] = jnp.zeros_like(tot_ref)
 
     def member(y, carry):
         base = pl.multiple_of(y * T, T)
         count = jnp.concatenate(
-            [c_ref[z, y].astype(jnp.int32).astype(f32) for z in range(ZL)], 1
+            [c_ref[behind(zl, z), y].astype(jnp.int32).astype(f32) for z in range(ZL)], 1
         )
         for v in range(2):
             emb = embed(weight_t[:, :width], a_ref[y, 1 - v])[0]
@@ -150,10 +156,10 @@
     return dot(agg, high, NT) + dot(agg, low, NT)
 
 
-def grads_kernel(coef, n_ref, a_ref, w_ref, e_ref, tot_ref, mask_ref, loss_ref, grad_ref):
+def grads_kernel(coef, place_ref, n_ref, a_ref, w_ref, e_ref, tot_ref, mask_ref, loss_ref, grad_ref):
     weight_t = w_ref[...]
     ysize, _, width, _ = a_ref.shape
-    agg_n = [anchors_of(n_ref, v) for v in range(2)]
+    agg_n = [anchors_of(n_ref, place_ref[1], v) for v in range(2)]
     emb_n, rinv_n = zip(*[embed(weight_t, agg) for agg in agg_n])
     low_n = [emb.astype(bf16) for emb in emb_n]
     full_n = [emb.astype(f32) for emb in low_n]
@@ -190,10 +196,12 @@
         grad_ref[...] += split_dot(agg_n[v], dz)[:width]
 
 
-def vmem_call(kernel, out_shape, name):
+def vmem_call(kernel, out_shape, inputs, name):
     return pl.pallas_call(
         kernel,
         out_shape=out_shape,
+        in_specs=[pl.BlockSpec(memory_space=pltpu.SMEM)]
+        + [pl.BlockSpec(memory_space=pltpu.VMEM)] * (inputs - 1),
         compiler_params=pltpu.CompilerParams(**PARAMS),
         name=name,
     )
@@ -212,49 +220,65 @@
     return lax.ppermute(x, axis, [(i, (i + by) % size) for i in range(size)])
 
 
+def around(x, pick):
+    return [pick(x, 0)] + [shift(pick(x, s), "zl", s) for s in range(1, ZL)]
+
+
 def reduce_all(grad):
     rows, width = grad.shape
-    plane = ("y", "x", "core")
+    plane = ("y", "x")
     size = lax.axis_size(plane)
     part = jnp.sum(swap(grad.reshape(size, -1, T), plane), 0)
-    part = jnp.sum(share(part, ("zl", "zh")), 0)
+    part = jnp.sum(share(part, ("zl", "zh", "core")), 0)
     return share(part, plane).reshape(rows, width)
+
+
+def packed(tiles, tile_pos, edge_keep, cols):
+    slots = tile_pos.shape[0]
+    held = tile_pos >= 0
+    trow = jnp.where(held, tile_pos // cols, -1)
+    tcol = jnp.where(held, tile_pos % cols, 0)
+    meta = jnp.concatenate([trow[None], tcol[None], edge_keep], 0).astype(bf16)
+    meta = jnp.pad(meta, ((0, 16 - meta.shape[0]), (0, T - slots)))
+    return jnp.concatenate([tiles.reshape(slots * T, T), meta], 0)
 
 
 def shards(features, weight, tiles, tile_pos, edge_keep, feature_keep, negatives):
     nodes, width = features.shape
+    slots = tiles.shape[0]
     ysize, xsize = lax.axis_size("y"), lax.axis_size("x")
     zsize = lax.axis_size("zh")
     cols = xsize * zsize * lax.axis_size("core")
     zl, core = lax.axis_index("zl"), lax.axis_index("core")
+    place = jnp.stack([core, zl])
     total = lax.axis_size(ROW) * cols * nodes
     pad = ZL * FS - width
 
-    meta = jnp.concatenate([tile_pos[None], edge_keep], 0)
-    metas = jnp.stack([meta] + [shift(meta, "zl", s) for s in range(1, ZL)])
-    all_tiles = [tiles] + [shift(tiles, "zl", s) for s in range(1, ZL)]
-
-    turned = jnp.pad(features.T, ((0, pad), (0, 0))).reshape(ZL, FS, nodes)
-
-    def slice_for(s):
-        return lax.dynamic_index_in_dim(turned, lax.rem(zl + s, ZL), 0, keepdims=False)
-
-    mine = jnp.stack([slice_for(0)] + [shift(slice_for(s), "zl", s) for s in range(1, ZL)])
-    own = share(mine, ("x", "zh"))
+    turned = jnp.pad(features.T, ((0, pad), (0, 0))).reshape(ZL, 1, FS, nodes)
+    sent = jnp.broadcast_to(turned, (ZL, zsize, FS, nodes)).reshape(ZL * zsize, FS, nodes)
+    near = swap(sent, ("zl", "zh"))
+    counts = count_negatives(negatives, ZL * ysize)
+    all_tiles = around(packed(tiles, tile_pos, edge_keep, cols), lambda x, s: x)
+    near, counts, all_tiles = lax.optimization_barrier((near, counts, all_tiles))
+    own = share(near, "x")
     other = shift(own, "core", 1)
-
-    counts = count_negatives(negatives, ZL * ysize)
-    counts = swap(counts, "zl").reshape(ZL, ysize, nodes, nodes)
-
-    part = tile_sums(metas, core.reshape(1), own, other, all_tiles, cols, ysize)
+    metas = jnp.stack([x[slots * T : slots * T + 4, :slots] for x in all_tiles]).astype(jnp.int32)
+
+    part = tile_sums(metas, place, own, other, all_tiles, cols, ysize)
+    part, counts = lax.optimization_barrier((part, counts))
     got = swap(part, "y")
+    counts = counts.reshape(ZL, ysize, nodes, nodes)
+    ahead = lambda x, s: lax.dynamic_index_in_dim(x, lax.rem(zl + s, ZL), 0, keepdims=False)
+    counts = jnp.stack(around(counts, ahead))
+    got, counts = lax.optimization_barrier((got, counts))
     keep = jnp.pad(feature_keep, ((0, 0), (0, pad))).reshape(2, ZL, FS)
     keep = lax.dynamic_index_in_dim(keep, zl, 1, keepdims=False).astype(f32)
     agg = (jnp.sum(got.astype(f32), 0) * keep[None, :, :, None]).astype(bf16)
-    anchors = share(agg, "zl")
-    one = lax.dynamic_index_in_dim(anchors, zl, 1, keepdims=False)
+    one = swap(agg, "zl")
+    one, agg = lax.optimization_barrier((one, agg))
     one = one.transpose(1, 0, 2, 3).reshape(2, ZL * FS, nodes)[:, :width]
     members = share(one, "y")
+    anchors = jnp.stack(around(agg, lambda x, s: x))
 
     weight_t = jnp.pad(weight.T, ((0, 0), (0, pad)))
     group = ZL * nodes
@@ -264,8 +288,9 @@
             jax.ShapeDtypeStruct((8, group), f32),
             jax.ShapeDtypeStruct((2, ysize * nodes, group), f32),
         ),
+        5,
         "scores",
-    )(anchors, members, weight_t, counts)
+    )(place, anchors, members, weight_t, counts)
     tots = share(tot, "zl")
     mask = (jnp.arange(group) // nodes == zl).astype(f32)
     coef = 1.0 / (2.0 * tau * float(total) ** 0.5)
@@ -275,8 +300,9 @@
             jax.ShapeDtypeStruct((8, group), f32),
             jax.ShapeDtypeStruct((width, width), f32),
         ),
+        7,
         "grads",
-    )(anchors, members, weight_t, terms, tots, jnp.broadcast_to(mask, (8, group)))
+    )(place, anchors, members, weight_t, terms, tots, jnp.broadcast_to(mask, (8, group)))
     node_loss = lax.dynamic_slice_in_dim(loss[0], zl * nodes, nodes)
     return node_loss, reduce_all(grad)
 

time: 297 us -> 244 us (0.82)
  waiting for transfers between devices: 104 us -> 69.8 us
  blocking collectives: 97.6 us -> 67.8 us
  starting transfers between devices: 49.5 us -> 56.9 us
    all_to_all x6 -> x5, waiting for transfers between devices: 90.2 us -> 50 us  [swap(): return lax.all_to_all(x, axis, 0, 0, tiled=True)]
    all_to_all x3 -> x4, blocking collectives: 97.6 us -> 67.8 us  [swap(): return lax.all_to_all(x, axis, 0, 0, tiled=True)]
    all_to_all x6 -> x5, starting transfers between devices: 25.7 us -> 33.6 us  [swap(): return lax.all_to_all(x, axis, 0, 0, tiled=True)]
    ppermute x7, waiting for transfers between devices: 13.5 us -> 19.8 us  [shift(): return lax.ppermute(x, axis, [(i, (i + by) % size) for i in range(size)])]
    unnamed x18 -> x22, local copies, waits for them, and re-layouts: 4.61 us -> 6.41 us
  transfers between devices with their start and end apart: 13 -> 12, of which waited for: 8 -> 10; matrix products, arithmetic and copies ran while one was open for 0% -> 1% of each run, Pallas kernels for 6% -> 6%
where the time goes in v2:
time: 244 us; the launch traced here: 243 us
  waiting for transfers between devices  69.8 us (29%)
  blocking collectives  67.8 us (28%)
  starting transfers between devices  56.9 us (23%)
  Pallas kernels  34.7 us (14%)
  local copies, waits for them, and re-layouts  12.1 us (5%)
    all_to_all x4, blocking collectives, swap(): return lax.all_to_all(x, axis, 0, 0, tiled=True)  67.8 us
    all_to_all x5, waiting for transfers between devices, swap(): return lax.all_to_all(x, axis, 0, 0, tiled=True)  50 us
    all_to_all x5, starting transfers between devices, swap(): return lax.all_to_all(x, axis, 0, 0, tiled=True)  33.6 us
    ppermute x7, starting transfers between devices, shift(): return lax.ppermute(x, axis, [(i, (i + by) % size) for i in range(size)])  23.2 us
    ppermute x7, waiting for transfers between devices, shift(): return lax.ppermute(x, axis, [(i, (i + by) % size) for i in range(size)])  19.8 us
    pallas_call x1, Pallas kernels, count_negatives(): pl.pallas_call(functools.partial(counts_kernel, blocks), out_shape=jax.Sh...  15.8 us
    pallas_call x1, Pallas kernels, shards(): vmem_call(functools.partial(grads_kernel, coef), (jax.ShapeDtypeStruct((8...  8.37 us
    unnamed x22, local copies, waits for them, and re-layouts  6.41 us
  transfers between devices with their start and end apart: 12, of which 10 were waited for; matrix products, arithmetic and copies ran while one was open for 1% of the time, Pallas kernels for 6%

profile of v2, /device:TPU:1, one launch (start us, length us, event | category | flops | bytes accessed | tf_op | source)
XLA Modules:
  0.0 243.0 jit_solution(8690046376335332865)
XLA Ops:
  2.5 15.7 %all-to-all-start = ((bf16[12,96,128]{2,1,0:T(8,128)(2,1)}), bf16[12,96,128]{2,1,0:T(8,128)(2,1)S(1)}, u32[]{:S(2)}, u32[]{:S(2)}) async-start(bf16[12,96,128]{2,1,0:T(8,128)(2,1)} %bitcast.4), calls=%async_computation | async-start | bytes 589824 | tf_op jit(solution)/shard_map/all_to_all | solution.py:211
  18.3 3.3 %collective-permute-start = (bf16[1552,128]{1,0:T(8,128)(2,1)S(1)}, bf16[1552,128]{1,0:T(8,128)(2,1)S(1)}, u32[]{:S(2)}, u32[]{:S(2)}) collective-permute-start(bf16[1552,128]{1,0:T(8,128)(2,1)S(1)} %pad_maximum_fusion.1.refs_0_), channel_id=1, source_target_pairs={{0,256},{256,512},{512,0},{1,257},{257,513},{513,1},{2,258},{258,5... | collective-permute-start | bytes 1191944 | tf_op jit(solution)/shard_map/ppermute | solution.py:220
  21.6 2.9 %collective-permute-start.1 = (bf16[1552,128]{1,0:T(8,128)(2,1)S(1)}, bf16[1552,128]{1,0:T(8,128)(2,1)}, u32[]{:S(2)}, u32[]{:S(2)}) collective-permute-start(bf16[1552,128]{1,0:T(8,128)(2,1)S(1)} %pad_maximum_fusion.1.refs_0_), channel_id=1, source_target_pairs={{0,512},{256,0},{512,256},{1,513},{257,1},{513,257},{2,514},{258,2... | collective-permute-start | bytes 1191944 | tf_op jit(solution)/shard_map/ppermute | solution.py:220
  24.5 15.8 %counts.1 = s16[24,128,128]{2,1,0:T(8,128)(2,1)S(1)} custom-call(s32[128,1024]{1,0:T(8,128)S(1)} %copy-done.4), custom_call_target="tpu_custom_call" | custom-call | flops 4294967296 | bytes 2097152 | tf_op jit(solution)/shard_map/counts/pallas_call | solution.py:60
  41.0 5.4 %collective-permute-done.1.refs_2_ = bf16[1552,128]{1,0:T(8,128)(2,1)} collective-permute-done((bf16[1552,128]{1,0:T(8,128)(2,1)S(1)}, bf16[1552,128]{1,0:T(8,128)(2,1)}, u32[]{:S(2)}, u32[]{:S(2)}) %collective-permute-start.1) | collective-permute-done | bytes 397344 | tf_op jit(solution)/shard_map/ppermute | solution.py:220
  46.7 18.5 %all_to_all.45.own_ref = bf16[4,12,96,128]{3,2,1,0:T(8,128)(2,1)S(1)} all-to-all(bf16[4,12,96,128]{3,2,1,0:T(8,128)(2,1)S(1)} %broadcast_in_dim.56), channel_id=1, replica_groups=mesh['zl'=3,'y'=8,'x'=4,'zh'=4,'core'=2] {'x'}, dimensions={0} | all-to-all | bytes 2359296 | tf_op jit(solution)/shard_map/all_to_all | solution.py:211
  65.1 4.7 %collective-permute-start.2 = (bf16[4,12,96,128]{3,2,1,0:T(8,128)(2,1)S(1)}, bf16[4,12,96,128]{3,2,1,0:T(8,128)(2,1)S(1)}, u32[]{:S(2)}, u32[]{:S(2)}) collective-permute-start(bf16[4,12,96,128]{3,2,1,0:T(8,128)(2,1)S(1)} %all_to_all.45.own_ref), channel_id=1, source_target_pairs={{0,1},{1,0},{2,3},{3,2},{4,5},{5,4},{6,7},{7,6},{8,9},{9,8},{10,11... | collective-permute-start | bytes 3538952 | tf_op jit(solution)/shard_map/ppermute | solution.py:220
  70.6 1.6 collective-permute-done.2.other_ref
  73.3 5.0 %tile_sums.1 = bf16[8,3,2,96,128]{4,3,2,1,0:T(8,128)(2,1)} custom-call(s32[3,4,12]{2,1,0:T(4,128)S(1)} %maximum_convert_fusion.meta_ref, s32[2]{0:T(128)S(1)} %pad_add_fusion.1.place_ref, bf16[4,12,96,128]{3,2,1,0:T(8,128)(2,1)S(1)} %all_to_all.45.own_ref, bf16[4,12,96,128]{3,2,1,0:T(8,128)(2,1)S(1)} %collective-permute-done.2.other_ref, ...), custom_call_target="tpu_custom_call" | custom-call | tf_op jit(solution)/shard_map/tile_sums/pallas_call | solution.py:106
  78.3 7.1 %all-to-all-start.2 = ((bf16[8,3,2,96,128]{4,3,2,1,0:T(8,128)(2,1)}), bf16[8,3,2,96,128]{4,3,2,1,0:T(8,128)(2,1)S(1)}, u32[]{:S(2)}, u32[]{:S(2)}) async-start(bf16[8,3,2,96,128]{4,3,2,1,0:T(8,128)(2,1)} %tile_sums.1), calls=%async_computation.2 | async-start | bytes 2359296 | tf_op jit(solution)/shard_map/all_to_all | solution.py:211
  85.6 3.0 %collective-permute-start.3 = (s16[8,128,128]{2,1,0:T(8,128)(2,1)S(1)}, s16[8,128,128]{2,1,0:T(8,128)(2,1)S(1)}, u32[]{:S(2)}, u32[]{:S(2)}) collective-permute-start(s16[8,128,128]{2,1,0:T(8,128)(2,1)S(1)} %get-tuple-element.34), channel_id=1, source_target_pairs={{0,256},{256,512},{512,0},{1,257},{257,513},{513,1},{2,258},{258,5... | collective-permute-start | bytes 786440 | tf_op jit(solution)/shard_map/ppermute | solution.py:220
  88.5 3.2 %collective-permute-start.4 = (s16[8,128,128]{2,1,0:T(8,128)(2,1)S(1)}, s16[8,128,128]{2,1,0:T(8,128)(2,1)S(1)}, u32[]{:S(2)}, u32[]{:S(2)}) collective-permute-start(s16[8,128,128]{2,1,0:T(8,128)(2,1)S(1)} %get-tuple-element.33), channel_id=1, source_target_pairs={{0,512},{256,0},{512,256},{1,513},{257,1},{513,257},{2,514},{258,2... | collective-permute-start | bytes 786440 | tf_op jit(solution)/shard_map/ppermute | solution.py:220
  91.9 4.8 %collective-permute-done.3 = s16[8,128,128]{2,1,0:T(8,128)(2,1)S(1)} collective-permute-done((s16[8,128,128]{2,1,0:T(8,128)(2,1)S(1)}, s16[8,128,128]{2,1,0:T(8,128)(2,1)S(1)}, u32[]{:S(2)}, u32[]{:S(2)}) %collective-permute-start.3) | collective-permute-done | bytes 262176 | tf_op jit(solution)/shard_map/ppermute | solution.py:220
  96.7 4.7 %collective-permute-done.4 = s16[8,128,128]{2,1,0:T(8,128)(2,1)S(1)} collective-permute-done((s16[8,128,128]{2,1,0:T(8,128)(2,1)S(1)}, s16[8,128,128]{2,1,0:T(8,128)(2,1)S(1)}, u32[]{:S(2)}, u32[]{:S(2)}) %collective-permute-start.4) | collective-permute-done | bytes 262176 | tf_op jit(solution)/shard_map/ppermute | solution.py:220
  101.5 15.1 %all-to-all-done.2 = bf16[8,3,2,96,128]{4,3,2,1,0:T(8,128)(2,1)S(1)} async-done(((bf16[8,3,2,96,128]{4,3,2,1,0:T(8,128)(2,1)}), bf16[8,3,2,96,128]{4,3,2,1,0:T(8,128)(2,1)S(1)}, u32[]{:S(2)}, u32[]{:S(2)}) %all-to-all-start.2) | async-done | bytes 1179680 | tf_op jit(solution)/shard_map/all_to_all | solution.py:211
  116.8 7.2 %all_to_all.46 = bf16[3,2,96,128]{3,2,1,0:T(8,128)(2,1)S(1)} all-to-all(bf16[3,2,96,128]{3,2,1,0:T(8,128)(2,1)S(1)} %multiply_convert_fusion), channel_id=1, replica_groups=mesh['zl'=3,'y'=8,'x'=4,'zh'=4,'core'=2] {'zl'}, dimensions={0} | all-to-all | bytes 294912 | tf_op jit(solution)/shard_map/all_to_all | solution.py:211
  124.1 1.2 broadcast_in_dim.57
  125.3 3.7 %all-to-all-start.4 = ((bf16[8,2,256,128]{3,2,1,0:T(8,128)(2,1)}), bf16[8,2,256,128]{3,2,1,0:T(8,128)(2,1)S(1)}, u32[]{:S(2)}, u32[]{:S(2)}) async-start(bf16[8,2,256,128]{3,2,1,0:T(8,128)(2,1)} %broadcast_in_dim.57), calls=%async_computation.4 | async-start | bytes 2097152 | tf_op jit(solution)/shard_map/all_to_all | solution.py:211
  129.0 2.4 collective-permute-start.5
  131.3 3.8 %collective-permute-start.6 = (bf16[3,2,96,128]{3,2,1,0:T(8,128)(2,1)S(1)}, bf16[3,2,96,128]{3,2,1,0:T(8,128)(2,1)S(1)}, u32[]{:S(2)}, u32[]{:S(2)}) collective-permute-start(bf16[3,2,96,128]{3,2,1,0:T(8,128)(2,1)S(1)} %multiply_convert_fusion), channel_id=1, source_target_pairs={{0,512},{256,0},{512,256},{1,513},{257,1},{513,257},{2,514},{258,2... | collective-permute-start | bytes 442376 | tf_op jit(solution)/shard_map/ppermute | solution.py:220
  135.8 2.8 %collective-permute-done.6 = bf16[3,2,96,128]{3,2,1,0:T(8,128)(2,1)S(1)} collective-permute-done((bf16[3,2,96,128]{3,2,1,0:T(8,128)(2,1)S(1)}, bf16[3,2,96,128]{3,2,1,0:T(8,128)(2,1)S(1)}, u32[]{:S(2)}, u32[]{:S(2)}) %collective-permute-start.6) | collective-permute-done | bytes 147488 | tf_op jit(solution)/shard_map/ppermute | solution.py:220
  138.6 19.5 %all-to-all-done.4.a_ref = bf16[8,2,256,128]{3,2,1,0:T(8,128)(2,1)S(1)} async-done(((bf16[8,2,256,128]{3,2,1,0:T(8,128)(2,1)}), bf16[8,2,256,128]{3,2,1,0:T(8,128)(2,1)S(1)}, u32[]{:S(2)}, u32[]{:S(2)}) %all-to-all-start.4) | async-done | bytes 1048608 | tf_op jit(solution)/shard_map/all_to_all | solution.py:211
  158.1 5.5 %scores.1 = (f32[8,384]{1,0:T(8,128)S(1)}, f32[2,1024,384]{2,1,0:T(8,128)S(1)}) custom-call(s32[2]{0:T(128)S(1)} %pad_add_fusion.1.place_ref, bf16[3,3,2,96,128]{4,3,2,1,0:T(8,128)(2,1)S(1)} %pad_maximum_fusion.n_ref, bf16[8,2,256,128]{3,2,1,0:T(8,128)(2,1)S(1)} %all-to-all-done.4.a_ref, bf16[256,288]{1,0:T(8,128)(2,1)S(1)} %pad.19.w_ref, ...), custom_call_target="tpu_custom_call" | custom-call | tf_op jit(solution)/shard_map/scores/pallas_call | solution.py:285
  163.6 1.6 copy-done
  165.8 3.3 %all-to-all-start.5 = ((f32[3,8,384]{2,1,0:T(8,128)}), f32[3,8,384]{2,1,0:T(8,128)S(1)}, u32[]{:S(2)}, u32[]{:S(2)}) async-start(f32[3,8,384]{2,1,0:T(8,128)} %broadcast_in_dim.58), calls=%async_computation.5 | async-start | bytes 73728 | tf_op jit(solution)/shard_map/all_to_all | solution.py:211
  169.1 3.6 %all-to-all-done.5.tot_ref = f32[3,8,384]{2,1,0:T(8,128)S(1)} async-done(((f32[3,8,384]{2,1,0:T(8,128)}), f32[3,8,384]{2,1,0:T(8,128)S(1)}, u32[]{:S(2)}, u32[]{:S(2)}) %all-to-all-start.5) | async-done | bytes 36896 | tf_op jit(solution)/shard_map/all_to_all | solution.py:211
  172.8 1.9 copy-done.1
  174.6 8.4 %grads.1 = (f32[8,384]{1,0:T(8,128)S(1)}, f32[256,256]{1,0:T(8,128)S(1)}) custom-call(s32[2]{0:T(128)S(1)} %pad_add_fusion.1.place_ref, bf16[3,3,2,96,128]{4,3,2,1,0:T(8,128)(2,1)S(1)} %pad_maximum_fusion.n_ref, bf16[8,2,256,128]{3,2,1,0:T(8,128)(2,1)S(1)} %all-to-all-done.4.a_ref, bf16[256,288]{1,0:T(8,128)(2,1)S(1)} %pad.19.w_ref, ...), custom_call_target="tpu_custom_call" | custom-call | tf_op jit(solution)/shard_map/grads/pallas_call | solution.py:297
  183.0 13.4 %all_to_all.47 = f32[32,16,128]{2,1,0:T(8,128)S(1)} all-to-all(f32[32,16,128]{2,1,0:T(8,128)S(1)} %reshape.44), channel_id=1, replica_groups=mesh['zl'=3,'y'=8,'x'=4,'zh'=4,'core'=2] {'y','x'}, dimensions={0} | all-to-all | bytes 524288 | tf_op jit(solution)/shard_map/all_to_all | solution.py:211
  196.5 28.8 %all_to_all.48 = f32[24,16,128]{2,1,0:T(8,128)S(1)} all-to-all(f32[24,16,128]{2,1,0:T(8,128)S(1)} %broadcast_in_dim.60), channel_id=1, replica_groups=mesh['zl'=3,'y'=8,'x'=4,'zh'=4,'core'=2] {'zl','zh','core'}, dimensions={0} | all-to-all | bytes 393216 | tf_op jit(solution)/shard_map/all_to_all | solution.py:211
  226.0 3.9 %all-to-all-start.8 = ((f32[32,16,128]{2,1,0:T(8,128)}), f32[32,16,128]{2,1,0:T(8,128)S(1)}, u32[]{:S(2)}, u32[]{:S(2)}) async-start(f32[32,16,128]{2,1,0:T(8,128)} %broadcast_in_dim.61), calls=%async_computation.8 | async-start | bytes 524288 | tf_op jit(solution)/shard_map/all_to_all | solution.py:211
  230.4 11.8 %all-to-all-done.8 = f32[32,16,128]{2,1,0:T(8,128)S(1)} async-done(((f32[32,16,128]{2,1,0:T(8,128)}), f32[32,16,128]{2,1,0:T(8,128)S(1)}, u32[]{:S(2)}, u32[]{:S(2)}) %all-to-all-start.8) | async-done | bytes 262176 | tf_op jit(solution)/shard_map/all_to_all | solution.py:211
  (56 shorter events, 8.5 us)
Async XLA Ops:
  0.6 17.6 %copy-start.9 = (s32[12]{0:T(128)S(1)}, s32[12]{0:T(128)}, u32[]{:S(2)}) copy-start(s32[12]{0:T(128)} %param.10) | copy-start | bytes 148
  0.6 17.6 %copy-start.8 = (s32[2,12]{1,0:T(2,128)S(1)}, s32[2,12]{1,0:T(2,128)}, u32[]{:S(2)}) copy-start(s32[2,12]{1,0:T(2,128)} %param.11) | copy-start | bytes 292
  0.7 17.6 %copy-start.5 = (bf16[12,128,128]{2,1,0:T(8,128)(2,1)S(1)}, bf16[12,128,128]{2,1,0:T(8,128)(2,1)}, u32[]{:S(2)}) copy-start(bf16[12,128,128]{2,1,0:T(8,128)(2,1)} %param.9) | copy-start | bytes 1179652
  0.7 23.8 %copy-start.4 = (s32[128,1024]{1,0:T(8,128)S(1)}, s32[128,1024]{1,0:T(8,128)}, u32[]{:S(2)}) copy-start(s32[128,1024]{1,0:T(8,128)} %neg_ref.1) | copy-start | bytes 1572868
  2.5 44.0 %all-to-all-start = ((bf16[12,96,128]{2,1,0:T(8,128)(2,1)}), bf16[12,96,128]{2,1,0:T(8,128)(2,1)S(1)}, u32[]{:S(2)}, u32[]{:S(2)}) async-start(bf16[12,96,128]{2,1,0:T(8,128)(2,1)} %bitcast.4), calls=%async_computation | async-start | bytes 589824 | tf_op jit(solution)/shard_map/all_to_all | solution.py:211
  18.3 22.0 %collective-permute-start = (bf16[1552,128]{1,0:T(8,128)(2,1)S(1)}, bf16[1552,128]{1,0:T(8,128)(2,1)S(1)}, u32[]{:S(2)}, u32[]{:S(2)}) collective-permute-start(bf16[1552,128]{1,0:T(8,128)(2,1)S(1)} %pad_maximum_fusion.1.refs_0_), channel_id=1, source_target_pairs={{0,256},{256,512},{512,0},{1,257},{257,513},{513,1},{2,258},{258,5... | collective-permute-start | bytes 1191944 | tf_op jit(solution)/shard_map/ppermute | solution.py:220
  21.6 24.8 %collective-permute-start.1 = (bf16[1552,128]{1,0:T(8,128)(2,1)S(1)}, bf16[1552,128]{1,0:T(8,128)(2,1)}, u32[]{:S(2)}, u32[]{:S(2)}) collective-permute-start(bf16[1552,128]{1,0:T(8,128)(2,1)S(1)} %pad_maximum_fusion.1.refs_0_), channel_id=1, source_target_pairs={{0,512},{256,0},{512,256},{1,513},{257,1},{513,257},{2,514},{258,2... | collective-permute-start | bytes 1191944 | tf_op jit(solution)/shard_map/ppermute | solution.py:220
  40.3 0.7 copy-start.2
  65.1 7.2 %collective-permute-start.2 = (bf16[4,12,96,128]{3,2,1,0:T(8,128)(2,1)S(1)}, bf16[4,12,96,128]{3,2,1,0:T(8,128)(2,1)S(1)}, u32[]{:S(2)}, u32[]{:S(2)}) collective-permute-start(bf16[4,12,96,128]{3,2,1,0:T(8,128)(2,1)S(1)} %all_to_all.45.own_ref), channel_id=1, source_target_pairs={{0,1},{1,0},{2,3},{3,2},{4,5},{5,4},{6,7},{7,6},{8,9},{9,8},{10,11... | collective-permute-start | bytes 3538952 | tf_op jit(solution)/shard_map/ppermute | solution.py:220
  72.3 1.0 copy-start.3
  78.3 38.3 %all-to-all-start.2 = ((bf16[8,3,2,96,128]{4,3,2,1,0:T(8,128)(2,1)}), bf16[8,3,2,96,128]{4,3,2,1,0:T(8,128)(2,1)S(1)}, u32[]{:S(2)}, u32[]{:S(2)}) async-start(bf16[8,3,2,96,128]{4,3,2,1,0:T(8,128)(2,1)} %tile_sums.1), calls=%async_computation.2 | async-start | bytes 2359296 | tf_op jit(solution)/shard_map/all_to_all | solution.py:211
  85.4 6.3 %copy-start.7 = (s32[2,256]{1,0:T(2,128)S(1)}, s32[2,256]{1,0:T(2,128)}, u32[]{:S(2)}) copy-start(s32[2,256]{1,0:T(2,128)} %param.12) | copy-start | bytes 6148
  85.6 11.1 %collective-permute-start.3 = (s16[8,128,128]{2,1,0:T(8,128)(2,1)S(1)}, s16[8,128,128]{2,1,0:T(8,128)(2,1)S(1)}, u32[]{:S(2)}, u32[]{:S(2)}) collective-permute-start(s16[8,128,128]{2,1,0:T(8,128)(2,1)S(1)} %get-tuple-element.34), channel_id=1, source_target_pairs={{0,256},{256,512},{512,0},{1,257},{257,513},{513,1},{2,258},{258,5... | collective-permute-start | bytes 786440 | tf_op jit(solution)/shard_map/ppermute | solution.py:220
  88.5 12.9 %collective-permute-start.4 = (s16[8,128,128]{2,1,0:T(8,128)(2,1)S(1)}, s16[8,128,128]{2,1,0:T(8,128)(2,1)S(1)}, u32[]{:S(2)}, u32[]{:S(2)}) collective-permute-start(s16[8,128,128]{2,1,0:T(8,128)(2,1)S(1)} %get-tuple-element.33), channel_id=1, source_target_pairs={{0,512},{256,0},{512,256},{1,513},{257,1},{513,257},{2,514},{258,2... | collective-permute-start | bytes 786440 | tf_op jit(solution)/shard_map/ppermute | solution.py:220
  125.3 9.9 %copy-start.6 = (bf16[256,256]{1,0:T(8,128)(2,1)S(1)}, bf16[256,256]{1,0:T(8,128)(2,1)}, u32[]{:S(2)}) copy-start(bf16[256,256]{1,0:T(8,128)(2,1)} %param.8) | copy-start | bytes 393220
  125.3 32.8 %all-to-all-start.4 = ((bf16[8,2,256,128]{3,2,1,0:T(8,128)(2,1)}), bf16[8,2,256,128]{3,2,1,0:T(8,128)(2,1)S(1)}, u32[]{:S(2)}, u32[]{:S(2)}) async-start(bf16[8,2,256,128]{3,2,1,0:T(8,128)(2,1)} %broadcast_in_dim.57), calls=%async_computation.4 | async-start | bytes 2097152 | tf_op jit(solution)/shard_map/all_to_all | solution.py:211
  129.0 6.8 %collective-permute-start.5 = (bf16[3,2,96,128]{3,2,1,0:T(8,128)(2,1)S(1)}, bf16[3,2,96,128]{3,2,1,0:T(8,128)(2,1)S(1)}, u32[]{:S(2)}, u32[]{:S(2)}) collective-permute-start(bf16[3,2,96,128]{3,2,1,0:T(8,128)(2,1)S(1)} %multiply_convert_fusion), channel_id=1, source_target_pairs={{0,256},{256,512},{512,0},{1,257},{257,513},{513,1},{2,258},{258,5... | collective-permute-start | bytes 442376 | tf_op jit(solution)/shard_map/ppermute | solution.py:220
  131.3 7.2 %collective-permute-start.6 = (bf16[3,2,96,128]{3,2,1,0:T(8,128)(2,1)S(1)}, bf16[3,2,96,128]{3,2,1,0:T(8,128)(2,1)S(1)}, u32[]{:S(2)}, u32[]{:S(2)}) collective-permute-start(bf16[3,2,96,128]{3,2,1,0:T(8,128)(2,1)S(1)} %multiply_convert_fusion), channel_id=1, source_target_pairs={{0,512},{256,0},{512,256},{1,513},{257,1},{513,257},{2,514},{258,2... | collective-permute-start | bytes 442376 | tf_op jit(solution)/shard_map/ppermute | solution.py:220
  163.6 1.6 copy-start
  165.8 6.9 %all-to-all-start.5 = ((f32[3,8,384]{2,1,0:T(8,128)}), f32[3,8,384]{2,1,0:T(8,128)S(1)}, u32[]{:S(2)}, u32[]{:S(2)}) async-start(f32[3,8,384]{2,1,0:T(8,128)} %broadcast_in_dim.58), calls=%async_computation.5 | async-start | bytes 73728 | tf_op jit(solution)/shard_map/all_to_all | solution.py:211
  172.7 1.9 copy-start.1
  226.0 16.2 %all-to-all-start.8 = ((f32[32,16,128]{2,1,0:T(8,128)}), f32[32,16,128]{2,1,0:T(8,128)S(1)}, u32[]{:S(2)}, u32[]{:S(2)}) async-start(f32[32,16,128]{2,1,0:T(8,128)} %broadcast_in_dim.61), calls=%async_computation.8 | async-start | bytes 524288 | tf_op jit(solution)/shard_map/all_to_all | solution.py:211

commit v3 on v2

v3 whole, which is shorter than its diff:
```python
import functools

import jax
import jax.numpy as jnp
from jax import lax
from jax.experimental import pallas as pl
from jax.experimental.pallas import tpu as pltpu
from jax.sharding import Mesh
from jax.sharding import PartitionSpec as P

tau = 0.5
eps = 1e-06
T = 128
ZL = 3
YL = 4
f32 = jnp.float32
bf16 = jnp.bfloat16
NT = (((1,), (1,)), ((), ()))
NN = (((1,), (0,)), ((), ()))
Y = ("yh", "yl")
ROW = ("zl",) + Y
COL = ("x", "zh", "core")
HBM = pl.BlockSpec(memory_space=pltpu.HBM)
PARAMS = dict(vmem_limit_bytes=24 * 1024 * 1024)


def dot(a, b, dims):
    return lax.dot_general(a, b, dims, preferred_element_type=f32)


def counts_kernel(blocks, neg_ref, out_ref, acc_ref):
    nodes, negs = neg_ref.shape
    rows = 8 * ((blocks + 7) // 8)
    low_iota = lax.broadcasted_iota(jnp.int32, (T, negs), 0)
    high_iota = lax.broadcasted_iota(jnp.int32, (rows, negs), 0)

    def step(i, carry):
        base = pl.multiple_of(i * 8, 8)
        index = neg_ref[pl.ds(base, 8), :]
        low = index & (T - 1)
        high = index >> 7
        for j in range(8):
            low_hot = jnp.where(low[j : j + 1, :] == low_iota, 1.0, 0.0).astype(bf16)
            high_hot = jnp.where(high[j : j + 1, :] == high_iota, 1.0, 0.0).astype(bf16)
            found = dot(high_hot, low_hot, NT)
            acc_ref[pl.ds(base + j, rows, stride=nodes), :] = found
        return carry

    lax.fori_loop(0, nodes // 8, step, 0)

    def turn(h, carry):
        block = acc_ref[pl.ds(pl.multiple_of(h * nodes, nodes), nodes), :]
        out_ref[h] = block.T.astype(jnp.int32).astype(jnp.int16)
        return carry

    lax.fori_loop(0, blocks, turn, 0)


def count_negatives(negatives, blocks):
    nodes = negatives.shape[0]
    rows = 8 * ((blocks + 7) // 8)
    return pl.pallas_call(
        functools.partial(counts_kernel, blocks),
        out_shape=jax.ShapeDtypeStruct((blocks, T, nodes), jnp.int16),
        scratch_shapes=[pltpu.VMEM((rows * nodes, T), f32)],
        compiler_params=pltpu.CompilerParams(**PARAMS),
        cost_estimate=pl.CostEstimate(
            flops=2 * 16 * nodes * T * T * 64, bytes_accessed=2 << 20, transcendentals=0
        ),
        name="counts",
    )(negatives)


def behind(place, s, size):
    return lax.rem(place + size - s, size)


def tiles_kernel(cols, meta_ref, place_ref, own_ref, other_ref, *refs):
    tile_refs, (out_ref, acc_ref) = refs[:YL], refs[YL:]
    zsize = own_ref.shape[1] // YL
    acc_ref[...] = jnp.zeros_like(acc_ref)
    core, yl = place_ref[0], place_ref[2]
    for s in range(YL):

        def slot(k, carry, s=s):
            trow, tcol = meta_ref[s, 0, k], meta_ref[s, 1, k]

            @pl.when(trow >= 0)
            def _():
                chip = lax.div(tcol, 2)
                at = lax.div(chip, zsize), behind(yl, s, YL) * zsize + lax.rem(chip, zsize)
                mine = lax.rem(tcol, 2) == core
                rows = jnp.where(mine, own_ref[at], other_ref[at])
                product = dot(rows, tile_refs[s][pl.ds(pl.multiple_of(k * T, T), T), :], NT)
                for v in range(2):
                    kept = meta_ref[s, 2 + v, k].astype(f32)
                    acc_ref[trow, v] += kept * product

            return carry

        lax.fori_loop(0, meta_ref.shape[2], slot, 0)
    out_ref[...] = acc_ref[...].astype(bf16)


def tile_sums(meta, place, own, other, tiles, cols, blocks):
    shape = (blocks, 2, own.shape[2], T)
    return pl.pallas_call(
        functools.partial(tiles_kernel, cols),
        out_shape=jax.ShapeDtypeStruct(shape, bf16),
        in_specs=[pl.BlockSpec(memory_space=pltpu.SMEM)] * 2
        + [pl.BlockSpec(memory_space=pltpu.VMEM)] * (2 + YL),
        scratch_shapes=[pltpu.VMEM(shape, f32)],
        compiler_params=pltpu.CompilerParams(**PARAMS),
        name="tile_sums",
    )(meta, place, own, other, *tiles)


def anchors_of(n_ref, zl, v):
    return jnp.concatenate([n_ref[behind(zl, z, ZL), v] for z in range(ZL)], 1)


def embed(weight_t, agg):
    z = dot(weight_t, agg, NN)
    rinv = lax.rsqrt(jnp.sum(z * z, 0, keepdims=True) + eps)
    return z * rinv, rinv


def scores_kernel(place_ref, n_ref, a_ref, w_ref, c_ref, tot_ref, e_ref, terms, sems):
    weight_t = w_ref[...]
    ysize = a_ref.shape[0]
    zl = place_ref[1]
    anchors = [embed(weight_t, anchors_of(n_ref, zl, v))[0].astype(bf16) for v in range(2)]
    tot_ref[...] = jnp.zeros_like(tot_ref)

    def keep(y):
        return pltpu.make_async_copy(terms.at[y], e_ref.at[y], sems.at[y])

    def member(y, carry):
        count = jnp.concatenate(
            [c_ref[behind(zl, z, ZL), y].astype(jnp.int32).astype(f32) for z in range(ZL)], 1
        )
        for v in range(2):
            emb = embed(weight_t, a_ref[y, 1 - v])[0]
            score = dot(emb.T.astype(bf16), anchors[v], NN)
            term = count * jnp.exp(score * (1.0 / tau))
            terms[y, v] = term
            tot_ref[v : v + 1, :] += jnp.sum(term, 0, keepdims=True)
        keep(y).start()
        return carry

    lax.fori_loop(0, ysize, member, 0)
    for y in range(ysize):
        keep(y).wait()


def split_dot(agg, dz):
    high = dz.astype(bf16)
    low = (dz - high.astype(f32)).astype(bf16)
    return dot(agg, high, NT) + dot(agg, low, NT)


def grads_kernel(coef, place_ref, n_ref, a_ref, w_ref, e_ref, tot_ref, mask_ref, loss_ref, grad_ref, terms, sems):
    weight_t = w_ref[...]
    ysize = a_ref.shape[0]

    def fetch(y):
        return pltpu.make_async_copy(e_ref.at[y], terms.at[y], sems.at[y])

    for y in range(ysize):
        fetch(y).start()
    agg_n = [anchors_of(n_ref, place_ref[1], v) for v in range(2)]
    emb_n, rinv_n = zip(*[embed(weight_t, agg) for agg in agg_n])
    low_n = [emb.astype(bf16) for emb in emb_n]
    full_n = [emb.astype(f32) for emb in low_n]
    pos = jnp.sum(full_n[0] * full_n[1], 0, keepdims=True) * (1.0 / tau)
    own = jnp.exp(pos)
    tot = [own + sum(tot_ref[z, v : v + 1, :] for z in range(ZL)) for v in range(2)]
    loss = 0.5 * ((jnp.log(tot[0]) - pos) + (jnp.log(tot[1]) - pos))
    loss_ref[...] = jnp.broadcast_to(loss, loss_ref.shape)
    inverse = [1.0 / t for t in tot]
    both = (own * inverse[0] + own * inverse[1] - 2.0) * mask_ref[0:1, :]

    def back(emb, rinv, d):
        return (d - emb * jnp.sum(emb * d, 0, keepdims=True)) * rinv

    grad_ref[...] = jnp.zeros_like(grad_ref)

    def member(y, carry):
        parts = [embed(weight_t, a_ref[y, v]) for v in range(2)]
        low = [emb.astype(bf16) for emb, _ in parts]
        fetch(y).wait()
        q = [(terms[y, v] * inverse[v]).astype(bf16) for v in range(2)]
        d_one = coef * dot(low_n[1], q[1], NT)
        d_two = coef * dot(low_n[0], q[0], NT)
        for v, d in ((0, d_one), (1, d_two)):
            dz = back(parts[v][0], parts[v][1], d)
            grad_ref[...] += split_dot(a_ref[y, v], dz)
        return carry[0] + dot(low[1], q[0], NN), carry[1] + dot(low[0], q[1], NN)

    sums = (jnp.zeros_like(pos) + jnp.zeros((weight_t.shape[0], 1), f32),) * 2
    sums = lax.fori_loop(0, ysize, member, sums)
    for v in range(2):
        d = coef * (both * full_n[1 - v] + sums[v])
        dz = back(emb_n[v], rinv_n[v], d)
        grad_ref[...] += split_dot(agg_n[v], dz)


def group_call(kernel, out_shape, in_specs, out_specs, terms, name):
    return pl.pallas_call(
        kernel,
        out_shape=out_shape,
        in_specs=in_specs,
        out_specs=out_specs,
        scratch_shapes=[pltpu.VMEM(terms, f32), pltpu.SemaphoreType.DMA((terms[0],))],
        compiler_params=pltpu.CompilerParams(**PARAMS),
        name=name,
    )


def swap(x, axis):
    return lax.all_to_all(x, axis, 0, 0, tiled=True)


def share(x, axis):
    return swap(jnp.broadcast_to(x[None], (lax.axis_size(axis),) + x.shape), axis)


def shift(x, axis, by):
    size = lax.axis_size(axis)
    return lax.ppermute(x, axis, [(i, (i + by) % size) for i in range(size)])


def around(x, pick, axis):
    return [pick(x, 0)] + [shift(pick(x, s), axis, s) for s in range(1, lax.axis_size(axis))]


def reduce_all(grad):
    rows, width = grad.shape
    planes = ("core",), Y + ("x",)
    part = grad.reshape(-1, T)
    for axes in planes:
        got = swap(part.reshape(lax.axis_size(axes), -1, T), axes)
        part = jnp.sum(got, 0)
    part = jnp.sum(share(part, ("zl", "zh")), 0)
    for axes in planes[::-1]:
        part = share(part, axes).reshape(-1, T)
    return part.reshape(rows, width)


def packed(tiles, tile_pos, edge_keep, cols):
    slots = tile_pos.shape[0]
    held = tile_pos >= 0
    trow = jnp.where(held, tile_pos // cols, -1)
    tcol = jnp.where(held, tile_pos % cols, 0)
    meta = jnp.concatenate([trow[None], tcol[None], edge_keep], 0).astype(bf16)
    meta = jnp.pad(meta, ((0, 16 - meta.shape[0]), (0, T - slots)))
    return jnp.concatenate([tiles.reshape(slots * T, T), meta], 0)


def shards(features, weight, tiles, tile_pos, edge_keep, feature_keep, negatives):
    nodes, width = features.shape
    slots = tiles.shape[0]
    xsize, zsize = lax.axis_size("x"), lax.axis_size("zh")
    ysize = lax.axis_size(Y)
    cols = xsize * zsize * lax.axis_size("core")
    zl = lax.axis_index("zl")
    place = jnp.stack([lax.axis_index("core"), zl, lax.axis_index("yl")])
    total = lax.axis_size(ROW) * cols * nodes
    part_width = width // YL
    whole = lambda x, s: x

    turned = features.T.reshape(YL, 1, part_width, nodes)
    sent = jnp.broadcast_to(turned, (YL, zsize, part_width, nodes))
    near = swap(sent.reshape(YL * zsize, part_width, nodes), ("yl", "zh"))
    held = packed(tiles, tile_pos, edge_keep, cols)
    first, last = shift(held, "yl", 1), shift(held, "yl", 3)
    near, first, last = lax.optimization_barrier((near, first, last))
    own = share(near, "x")
    across = shift(held, "yl", 2)
    own, across = lax.optimization_barrier((own, across))
    all_tiles = [held, first, across, last]
    other = shift(own, "core", 1)
    metas = jnp.stack([x[slots * T : slots * T + 4, :slots] for x in all_tiles]).astype(jnp.int32)

    part = tile_sums(metas, place, own, other, all_tiles, cols, ZL * ysize)
    part, negatives = lax.optimization_barrier((part, negatives))
    got = swap(part, ROW)
    counts = count_negatives(negatives, ZL * ysize)
    got, counts = lax.optimization_barrier((got, counts))
    got = got.reshape(ZL, ysize // YL, YL, 2, part_width, nodes).astype(f32)
    agg = jnp.sum(got, (0, 1)).transpose(1, 0, 2, 3).reshape(2, width, nodes)
    agg = (agg * feature_keep.astype(f32)[:, :, None]).astype(bf16)
    agg, counts = lax.optimization_barrier((agg, counts))
    members = share(agg, Y)
    anchors = jnp.stack(around(agg, whole, "zl"))
    ahead = lambda x, s: lax.dynamic_index_in_dim(x, lax.rem(zl + s, ZL), 0, keepdims=False)
    counts = jnp.stack(around(counts.reshape(ZL, ysize, nodes, nodes), ahead, "zl"))

    weight_t = weight.T
    group = ZL * nodes
    smem, vmem = pl.BlockSpec(memory_space=pltpu.SMEM), pl.BlockSpec(memory_space=pltpu.VMEM)
    rows = jax.ShapeDtypeStruct((8, group), f32)
    terms_shape = (ysize, 2, nodes, group)
    tot, terms = group_call(
        scores_kernel,
        (rows, jax.ShapeDtypeStruct(terms_shape, f32)),
        [smem] + [vmem] * 4,
        (vmem, HBM),
        terms_shape,
        "scores",
    )(place, anchors, members, weight_t, counts)
    tots = share(tot, "zl")
    mask = (jnp.arange(group) // nodes == zl).astype(f32)
    coef = 1.0 / (2.0 * tau * float(total) ** 0.5)
    loss, grad = group_call(
        functools.partial(grads_kernel, coef),
        (rows, jax.ShapeDtypeStruct((width, width), f32)),
        [smem] + [vmem] * 3 + [HBM] + [vmem] * 2,
        (vmem, vmem),
        terms_shape,
        "grads",
    )(place, anchors, members, weight_t, terms, tots, jnp.broadcast_to(mask, (8, group)))
    node_loss = lax.dynamic_slice_in_dim(loss[0], zl * nodes, nodes)
    return node_loss, reduce_all(grad)


def solution(mesh):
    rows, cols = mesh.devices.shape
    shape = (ZL, rows // (ZL * YL), YL, cols // 8, 4, 2)
    fine = Mesh(mesh.devices.reshape(shape), ROW + COL)
    every = ROW + COL
    in_specs = (
        P(every, None),
        P(),
        P(every, None, None),
        P(every),
        P(None, every),
        P(),
        P(every, None),
    )
    out_specs = (P(every), P())
    return jax.shard_map(shards, mesh=fine, in_specs=in_specs, out_specs=out_specs, check_vma=False)
```

time: 244 us -> 243 us (level)
  blocking collectives: 67.8 us -> 47.6 us
  starting transfers between devices: 56.9 us -> 70.8 us
  Pallas kernels: 34.7 us -> 39.1 us
    all_to_all x5 -> x6, waiting for transfers between devices: 50 us -> 21.4 us  [swap(): return lax.all_to_all(x, axis, 0, 0, tiled=True)]
    ppermute x7 -> x8, waiting for transfers between devices: 19.8 us -> 46.7 us  [shift(): return lax.ppermute(x, axis, [(i, (i + by) % size) for i in range(size)])]
    all_to_all x4, blocking collectives: 67.8 us -> 47.6 us  [swap(): return lax.all_to_all(x, axis, 0, 0, tiled=True)]
    all_to_all x5 -> x6, starting transfers between devices: 33.6 us -> 44.1 us  [swap(): return lax.all_to_all(x, axis, 0, 0, tiled=True)]
    pallas_call x3, Pallas kernels: 18.9 us -> 23.4 us  [the longest x1 11.7 us: shards(): group_call(functools.partial(grads_kernel, coef), (rows, jax.ShapeDtypeSt...]
    ppermute x7 -> x8, starting transfers between devices: 23.2 us -> 26.6 us  [shift(): return lax.ppermute(x, axis, [(i, (i + by) % size) for i in range(size)])]
    unnamed x22 -> x14, local copies, waits for them, and re-layouts: 6.41 us -> 5.63 us
  transfers between devices with their start and end apart: 12 -> 14, of which waited for: 10 -> 10; matrix products, arithmetic and copies ran while one was open for 1% -> 2% of each run, Pallas kernels for 6% -> 7%
where the time goes in v3:
time: 243 us; the launch traced here: 242 us
  starting transfers between devices  70.8 us (29%)
  waiting for transfers between devices  68.1 us (28%)
  blocking collectives  47.6 us (20%)
  Pallas kernels  39.1 us (16%)
  local copies, waits for them, and re-layouts  12.2 us (5%)
  other arithmetic  2.92 us (1%)
    all_to_all x4, blocking collectives, swap(): return lax.all_to_all(x, axis, 0, 0, tiled=True)  47.6 us
    ppermute x8, waiting for transfers between devices, shift(): return lax.ppermute(x, axis, [(i, (i + by) % size) for i in range(size)])  46.7 us
    all_to_all x6, starting transfers between devices, swap(): return lax.all_to_all(x, axis, 0, 0, tiled=True)  44.1 us
    ppermute x8, starting transfers between devices, shift(): return lax.ppermute(x, axis, [(i, (i + by) % size) for i in range(size)])  26.6 us
    all_to_all x6, waiting for transfers between devices, swap(): return lax.all_to_all(x, axis, 0, 0, tiled=True)  21.4 us
    pallas_call x1, Pallas kernels, count_negatives(): pl.pallas_call(functools.partial(counts_kernel, blocks), out_shape=jax.Sh...  15.8 us
    pallas_call x1, Pallas kernels, shards(): group_call(functools.partial(grads_kernel, coef), (rows, jax.ShapeDtypeSt...  11.7 us
    pallas_call x1, Pallas kernels, shards(): group_call(scores_kernel, (rows, jax.ShapeDtypeStruct(terms_shape, f32)),...  6.97 us
  transfers between devices with their start and end apart: 14, of which 10 were waited for; matrix products, arithmetic and copies ran while one was open for 2% of the time, Pallas kernels for 7%

profile of v3, /device:TPU:1, one launch (start us, length us, event | category | flops | bytes accessed | tf_op | source)
XLA Modules:
  0.0 241.7 jit_solution(16552956144795025479)
XLA Ops:
  2.4 18.2 %all-to-all-start = ((bf16[16,64,128]{2,1,0:T(8,128)(2,1)}), bf16[16,64,128]{2,1,0:T(8,128)(2,1)S(1)}, u32[]{:S(2)}, u32[]{:S(2)}) async-start(bf16[16,64,128]{2,1,0:T(8,128)(2,1)} %bitcast.8), calls=%async_computation | async-start | bytes 524288 | tf_op jit(solution)/shard_map/all_to_all | solution.py:221
  23.0 3.3 %collective-permute-start = (bf16[1552,128]{1,0:T(8,128)(2,1)S(1)}, bf16[1552,128]{1,0:T(8,128)(2,1)S(1)}, u32[]{:S(2)}, u32[]{:S(2)}) collective-permute-start(bf16[1552,128]{1,0:T(8,128)(2,1)S(1)} %pad_maximum_fusion.refs_0_), channel_id=1, source_target_pairs={{0,32},{32,64},{64,96},{96,0},{1,33},{33,65},{65,97},{97,1},{2,34}... | collective-permute-start | bytes 1191944 | tf_op jit(solution)/shard_map/ppermute | solution.py:230
  26.3 3.8 %collective-permute-start.1 = (bf16[1552,128]{1,0:T(8,128)(2,1)S(1)}, bf16[1552,128]{1,0:T(8,128)(2,1)S(1)}, u32[]{:S(2)}, u32[]{:S(2)}) collective-permute-start(bf16[1552,128]{1,0:T(8,128)(2,1)S(1)} %pad_maximum_fusion.refs_0_), channel_id=1, source_target_pairs={{0,96},{32,0},{64,32},{96,64},{1,97},{33,1},{65,33},{97,65},{2,98}... | collective-permute-start | bytes 1191944 | tf_op jit(solution)/shard_map/ppermute | solution.py:230
  30.1 10.2 %collective-permute-done.refs_1_ = bf16[1552,128]{1,0:T(8,128)(2,1)S(1)} collective-permute-done((bf16[1552,128]{1,0:T(8,128)(2,1)S(1)}, bf16[1552,128]{1,0:T(8,128)(2,1)S(1)}, u32[]{:S(2)}, u32[]{:S(2)}) %collective-permute-start) | collective-permute-done | bytes 397344 | tf_op jit(solution)/shard_map/ppermute | solution.py:230
  40.3 8.2 %collective-permute-done.1.refs_3_ = bf16[1552,128]{1,0:T(8,128)(2,1)S(1)} collective-permute-done((bf16[1552,128]{1,0:T(8,128)(2,1)S(1)}, bf16[1552,128]{1,0:T(8,128)(2,1)S(1)}, u32[]{:S(2)}, u32[]{:S(2)}) %collective-permute-start.1) | collective-permute-done | bytes 397344 | tf_op jit(solution)/shard_map/ppermute | solution.py:230
  49.7 4.0 %all-to-all-start.1 = ((bf16[4,16,64,128]{3,2,1,0:T(8,128)(2,1)}), bf16[4,16,64,128]{3,2,1,0:T(8,128)(2,1)S(1)}, u32[]{:S(2)}, u32[]{:S(2)}) async-start(bf16[4,16,64,128]{3,2,1,0:T(8,128)(2,1)} %broadcast_in_dim.63), calls=%async_computation.1 | async-start | bytes 2097152 | tf_op jit(solution)/shard_map/all_to_all | solution.py:221
  53.8 2.6 %collective-permute-start.2 = (bf16[1552,128]{1,0:T(8,128)(2,1)S(1)}, bf16[1552,128]{1,0:T(8,128)(2,1)}, u32[]{:S(2)}, u32[]{:S(2)}) collective-permute-start(bf16[1552,128]{1,0:T(8,128)(2,1)S(1)} %pad_maximum_fusion.refs_0_), channel_id=1, source_target_pairs={{0,64},{32,96},{64,0},{96,32},{1,65},{33,97},{65,1},{97,33},{2,66}... | collective-permute-start | bytes 1191944 | tf_op jit(solution)/shard_map/ppermute | solution.py:230
  56.4 19.0 %collective-permute-done.2.refs_2_ = bf16[1552,128]{1,0:T(8,128)(2,1)} collective-permute-done((bf16[1552,128]{1,0:T(8,128)(2,1)S(1)}, bf16[1552,128]{1,0:T(8,128)(2,1)}, u32[]{:S(2)}, u32[]{:S(2)}) %collective-permute-start.2) | collective-permute-done | bytes 397344 | tf_op jit(solution)/shard_map/ppermute | solution.py:230
  75.4 3.4 %collective-permute-start.3 = (bf16[4,16,64,128]{3,2,1,0:T(8,128)(2,1)S(1)}, bf16[4,16,64,128]{3,2,1,0:T(8,128)(2,1)S(1)}, u32[]{:S(2)}, u32[]{:S(2)}) collective-permute-start(bf16[4,16,64,128]{3,2,1,0:T(8,128)(2,1)S(1)} %all-to-all-done.1.own_ref), channel_id=1, source_target_pairs={{0,1},{1,0},{2,3},{3,2},{4,5},{5,4},{6,7},{7,6},{8,9},{9,8},{10,11... | collective-permute-start | bytes 3145736 | tf_op jit(solution)/shard_map/ppermute | solution.py:230
  81.1 4.7 %tile_sums.1 = bf16[24,2,64,128]{3,2,1,0:T(8,128)(2,1)} custom-call(s32[4,4,12]{2,1,0:T(4,128)S(1)} %maximum_convert_fusion.meta_ref, s32[3]{0:T(128)S(1)} %pad_add_fusion.1.place_ref, bf16[4,16,64,128]{3,2,1,0:T(8,128)(2,1)S(1)} %all-to-all-done.1.own_ref, bf16[4,16,64,128]{3,2,1,0:T(8,128)(2,1)S(1)} %collective-permute-done.3.other_ref, ...), custom_call_target="tpu_custom_call" | custom-call | tf_op jit(solution)/shard_map/tile_sums/pallas_call | solution.py:107
  85.8 6.5 %all-to-all-start.2 = ((bf16[24,2,64,128]{3,2,1,0:T(8,128)(2,1)}), bf16[24,2,64,128]{3,2,1,0:T(8,128)(2,1)S(1)}, u32[]{:S(2)}, u32[]{:S(2)}) async-start(bf16[24,2,64,128]{3,2,1,0:T(8,128)(2,1)} %tile_sums.1), calls=%async_computation.2 | async-start | bytes 1572864 | tf_op jit(solution)/shard_map/all_to_all | solution.py:221
  93.4 15.8 %counts.1 = s16[24,128,128]{2,1,0:T(8,128)(2,1)S(1)} custom-call(s32[128,1024]{1,0:T(8,128)S(1)} %copy-done.2), custom_call_target="tpu_custom_call" | custom-call | flops 4294967296 | bytes 2097152 | tf_op jit(solution)/shard_map/counts/pallas_call | solution.py:62
  112.1 6.7 %all-to-all-start.3 = ((bf16[8,2,256,128]{3,2,1,0:T(8,128)(2,1)}), bf16[8,2,256,128]{3,2,1,0:T(8,128)(2,1)S(1)}, u32[]{:S(2)}, u32[]{:S(2)}) async-start(bf16[8,2,256,128]{3,2,1,0:T(8,128)(2,1)} %broadcast_in_dim.64), calls=%async_computation.3 | async-start | bytes 2097152 | tf_op jit(solution)/shard_map/all_to_all | solution.py:221
  118.9 5.4 %collective-permute-start.6 = (s16[8,128,128]{2,1,0:T(8,128)(2,1)S(1)}, s16[8,128,128]{2,1,0:T(8,128)(2,1)S(1)}, u32[]{:S(2)}, u32[]{:S(2)}) collective-permute-start(s16[8,128,128]{2,1,0:T(8,128)(2,1)S(1)} %get-tuple-element.36), channel_id=1, source_target_pairs={{0,256},{256,512},{512,0},{1,257},{257,513},{513,1},{2,258},{258,5... | collective-permute-start | bytes 786440 | tf_op jit(solution)/shard_map/ppermute | solution.py:230
  124.3 1.9 collective-permute-start.7
  126.2 3.4 %collective-permute-start.4 = (bf16[2,256,128]{2,1,0:T(8,128)(2,1)S(1)}, bf16[2,256,128]{2,1,0:T(8,128)(2,1)S(1)}, u32[]{:S(2)}, u32[]{:S(2)}) collective-permute-start(bf16[2,256,128]{2,1,0:T(8,128)(2,1)S(1)} %fusion), channel_id=1, source_target_pairs={{0,256},{256,512},{512,0},{1,257},{257,513},{513,1},{2,258},{258,5... | collective-permute-start | bytes 393224 | tf_op jit(solution)/shard_map/ppermute | solution.py:230
  129.6 2.8 %collective-permute-start.5 = (bf16[2,256,128]{2,1,0:T(8,128)(2,1)S(1)}, bf16[2,256,128]{2,1,0:T(8,128)(2,1)S(1)}, u32[]{:S(2)}, u32[]{:S(2)}) collective-permute-start(bf16[2,256,128]{2,1,0:T(8,128)(2,1)S(1)} %fusion), channel_id=1, source_target_pairs={{0,512},{256,0},{512,256},{1,513},{257,1},{513,257},{2,514},{258,2... | collective-permute-start | bytes 393224 | tf_op jit(solution)/shard_map/ppermute | solution.py:230
  132.5 4.6 %collective-permute-done.4 = bf16[2,256,128]{2,1,0:T(8,128)(2,1)S(1)} collective-permute-done((bf16[2,256,128]{2,1,0:T(8,128)(2,1)S(1)}, bf16[2,256,128]{2,1,0:T(8,128)(2,1)S(1)}, u32[]{:S(2)}, u32[]{:S(2)}) %collective-permute-start.4) | collective-permute-done | bytes 131104 | tf_op jit(solution)/shard_map/ppermute | solution.py:230
  137.2 3.1 %collective-permute-done.5 = bf16[2,256,128]{2,1,0:T(8,128)(2,1)S(1)} collective-permute-done((bf16[2,256,128]{2,1,0:T(8,128)(2,1)S(1)}, bf16[2,256,128]{2,1,0:T(8,128)(2,1)S(1)}, u32[]{:S(2)}, u32[]{:S(2)}) %collective-permute-start.5) | collective-permute-done | bytes 131104 | tf_op jit(solution)/shard_map/ppermute | solution.py:230
  140.4 7.6 %all-to-all-done.3.a_ref = bf16[8,2,256,128]{3,2,1,0:T(8,128)(2,1)S(1)} async-done(((bf16[8,2,256,128]{3,2,1,0:T(8,128)(2,1)}), bf16[8,2,256,128]{3,2,1,0:T(8,128)(2,1)S(1)}, u32[]{:S(2)}, u32[]{:S(2)}) %all-to-all-start.3) | async-done | bytes 1048608 | tf_op jit(solution)/shard_map/all_to_all | solution.py:221
  148.0 7.0 %scores.1 = (f32[8,384]{1,0:T(8,128)S(1)}, f32[8,2,128,384]{3,2,1,0:T(8,128)S(1)}) custom-call(s32[3]{0:T(128)S(1)} %pad_add_fusion.1.place_ref, bf16[3,2,256,128]{3,2,1,0:T(8,128)(2,1)S(1)} %pad_maximum_fusion.1.n_ref, bf16[8,2,256,128]{3,2,1,0:T(8,128)(2,1)S(1)} %all-to-all-done.3.a_ref, bf16[256,256]{1,0:T(8,128)(2,1)S(1)} %bitcast.44, ...), custom_call_target="tpu_custom_call" | custom-call | tf_op jit(solution)/shard_map/scores/pallas_call | solution.py:304
  155.0 1.6 copy-done
  157.2 4.8 %all-to-all-start.4 = ((f32[3,8,384]{2,1,0:T(8,128)}), f32[3,8,384]{2,1,0:T(8,128)S(1)}, u32[]{:S(2)}, u32[]{:S(2)}) async-start(f32[3,8,384]{2,1,0:T(8,128)} %broadcast_in_dim.65), calls=%async_computation.4 | async-start | bytes 73728 | tf_op jit(solution)/shard_map/all_to_all | solution.py:221
  162.0 3.6 %all-to-all-done.4.tot_ref = f32[3,8,384]{2,1,0:T(8,128)S(1)} async-done(((f32[3,8,384]{2,1,0:T(8,128)}), f32[3,8,384]{2,1,0:T(8,128)S(1)}, u32[]{:S(2)}, u32[]{:S(2)}) %all-to-all-start.4) | async-done | bytes 36896 | tf_op jit(solution)/shard_map/all_to_all | solution.py:221
  165.7 1.9 copy-done.1
  167.6 11.7 %grads.1 = (f32[8,384]{1,0:T(8,128)S(1)}, f32[256,256]{1,0:T(8,128)S(1)}) custom-call(s32[3]{0:T(128)S(1)} %pad_add_fusion.1.place_ref, bf16[3,2,256,128]{3,2,1,0:T(8,128)(2,1)S(1)} %pad_maximum_fusion.1.n_ref, bf16[8,2,256,128]{3,2,1,0:T(8,128)(2,1)S(1)} %all-to-all-done.3.a_ref, bf16[256,256]{1,0:T(8,128)(2,1)S(1)} %bitcast.45, ...), custom_call_target="tpu_custom_call" | custom-call | tf_op jit(solution)/shard_map/grads/pallas_call | solution.py:315
  179.3 5.5 %all_to_all.50 = f32[2,256,128]{2,1,0:T(8,128)S(1)} all-to-all(f32[2,256,128]{2,1,0:T(8,128)S(1)} %reshape_reshape.6), channel_id=1, replica_groups=mesh['zl'=3,'yh'=2,'yl'=4,'x'=4,'zh'=4,'core'=2] {'core'}, dimensions={0} | all-to-all | bytes 524288 | tf_op jit(solution)/shard_map/all_to_all | solution.py:221
  184.8 14.0 %all_to_all.51 = f32[32,8,128]{2,1,0:T(8,128)S(1)} all-to-all(f32[32,8,128]{2,1,0:T(8,128)S(1)} %bitcast.51), channel_id=1, replica_groups=mesh['zl'=3,'yh'=2,'yl'=4,'x'=4,'zh'=4,'core'=2] {'yh','yl','x'}, dimensions={0} | all-to-all | bytes 262144 | tf_op jit(solution)/shard_map/all_to_all | solution.py:221
  198.9 19.8 %all_to_all.52 = f32[12,8,128]{2,1,0:T(8,128)S(1)} all-to-all(f32[12,8,128]{2,1,0:T(8,128)S(1)} %broadcast_in_dim.67), channel_id=1, replica_groups=mesh['zl'=3,'yh'=2,'yl'=4,'x'=4,'zh'=4,'core'=2] {'zl','zh'}, dimensions={0} | all-to-all | bytes 98304 | tf_op jit(solution)/shard_map/all_to_all | solution.py:221
  219.4 3.9 %all-to-all-start.8 = ((f32[32,8,128]{2,1,0:T(8,128)}), f32[32,8,128]{2,1,0:T(8,128)S(1)}, u32[]{:S(2)}, u32[]{:S(2)}) async-start(f32[32,8,128]{2,1,0:T(8,128)} %broadcast_in_dim.68), calls=%async_computation.8 | async-start | bytes 262144 | tf_op jit(solution)/shard_map/all_to_all | solution.py:221
  223.8 8.8 %all-to-all-done.8 = f32[32,8,128]{2,1,0:T(8,128)S(1)} async-done(((f32[32,8,128]{2,1,0:T(8,128)}), f32[32,8,128]{2,1,0:T(8,128)S(1)}, u32[]{:S(2)}, u32[]{:S(2)}) %all-to-all-start.8) | async-done | bytes 131104 | tf_op jit(solution)/shard_map/all_to_all | solution.py:221
  232.6 8.3 %all_to_all.53 = f32[2,256,128]{2,1,0:T(8,128)S(1)} all-to-all(f32[2,256,128]{2,1,0:T(8,128)S(1)} %broadcast_in_dim.70), channel_id=1, replica_groups=mesh['zl'=3,'yh'=2,'yl'=4,'x'=4,'zh'=4,'core'=2] {'core'}, dimensions={0} | all-to-all | bytes 524288 | tf_op jit(solution)/shard_map/all_to_all | solution.py:221
  (51 shorter events, 14.5 us)
Async XLA Ops:
  0.6 78.3 %copy-start.5 = (s32[2,12]{1,0:T(2,128)S(1)}, s32[2,12]{1,0:T(2,128)}, u32[]{:S(2)}) copy-start(s32[2,12]{1,0:T(2,128)} %param.11) | copy-start | bytes 292
  2.4 46.1 %all-to-all-start = ((bf16[16,64,128]{2,1,0:T(8,128)(2,1)}), bf16[16,64,128]{2,1,0:T(8,128)(2,1)S(1)}, u32[]{:S(2)}, u32[]{:S(2)}) async-start(bf16[16,64,128]{2,1,0:T(8,128)(2,1)} %bitcast.8), calls=%async_computation | async-start | bytes 524288 | tf_op jit(solution)/shard_map/all_to_all | solution.py:221
  23.0 17.3 %collective-permute-start = (bf16[1552,128]{1,0:T(8,128)(2,1)S(1)}, bf16[1552,128]{1,0:T(8,128)(2,1)S(1)}, u32[]{:S(2)}, u32[]{:S(2)}) collective-permute-start(bf16[1552,128]{1,0:T(8,128)(2,1)S(1)} %pad_maximum_fusion.refs_0_), channel_id=1, source_target_pairs={{0,32},{32,64},{64,96},{96,0},{1,33},{33,65},{65,97},{97,1},{2,34}... | collective-permute-start | bytes 1191944 | tf_op jit(solution)/shard_map/ppermute | solution.py:230
  26.3 22.2 %collective-permute-start.1 = (bf16[1552,128]{1,0:T(8,128)(2,1)S(1)}, bf16[1552,128]{1,0:T(8,128)(2,1)S(1)}, u32[]{:S(2)}, u32[]{:S(2)}) collective-permute-start(bf16[1552,128]{1,0:T(8,128)(2,1)S(1)} %pad_maximum_fusion.refs_0_), channel_id=1, source_target_pairs={{0,96},{32,0},{64,32},{96,64},{1,97},{33,1},{65,33},{97,65},{2,98}... | collective-permute-start | bytes 1191944 | tf_op jit(solution)/shard_map/ppermute | solution.py:230
  49.7 25.7 %all-to-all-start.1 = ((bf16[4,16,64,128]{3,2,1,0:T(8,128)(2,1)}), bf16[4,16,64,128]{3,2,1,0:T(8,128)(2,1)S(1)}, u32[]{:S(2)}, u32[]{:S(2)}) async-start(bf16[4,16,64,128]{3,2,1,0:T(8,128)(2,1)} %broadcast_in_dim.63), calls=%async_computation.1 | async-start | bytes 2097152 | tf_op jit(solution)/shard_map/all_to_all | solution.py:221
  53.8 38.6 %copy-start.4 = (s32[2,256]{1,0:T(2,128)S(1)}, s32[2,256]{1,0:T(2,128)}, u32[]{:S(2)}) copy-start(s32[2,256]{1,0:T(2,128)} %param.12) | copy-start | bytes 6148
  53.8 21.6 %collective-permute-start.2 = (bf16[1552,128]{1,0:T(8,128)(2,1)S(1)}, bf16[1552,128]{1,0:T(8,128)(2,1)}, u32[]{:S(2)}, u32[]{:S(2)}) collective-permute-start(bf16[1552,128]{1,0:T(8,128)(2,1)S(1)} %pad_maximum_fusion.refs_0_), channel_id=1, source_target_pairs={{0,64},{32,96},{64,0},{96,32},{1,65},{33,97},{65,1},{97,33},{2,66}... | collective-permute-start | bytes 1191944 | tf_op jit(solution)/shard_map/ppermute | solution.py:230
  75.4 5.7 %collective-permute-start.3 = (bf16[4,16,64,128]{3,2,1,0:T(8,128)(2,1)S(1)}, bf16[4,16,64,128]{3,2,1,0:T(8,128)(2,1)S(1)}, u32[]{:S(2)}, u32[]{:S(2)}) collective-permute-start(bf16[4,16,64,128]{3,2,1,0:T(8,128)(2,1)S(1)} %all-to-all-done.1.own_ref), channel_id=1, source_target_pairs={{0,1},{1,0},{2,3},{3,2},{4,5},{5,4},{6,7},{7,6},{8,9},{9,8},{10,11... | collective-permute-start | bytes 3145736 | tf_op jit(solution)/shard_map/ppermute | solution.py:230
  85.8 24.8 %all-to-all-start.2 = ((bf16[24,2,64,128]{3,2,1,0:T(8,128)(2,1)}), bf16[24,2,64,128]{3,2,1,0:T(8,128)(2,1)S(1)}, u32[]{:S(2)}, u32[]{:S(2)}) async-start(bf16[24,2,64,128]{3,2,1,0:T(8,128)(2,1)} %tile_sums.1), calls=%async_computation.2 | async-start | bytes 1572864 | tf_op jit(solution)/shard_map/all_to_all | solution.py:221
  92.4 1.0 copy-start.2
  110.7 21.7 %copy-start.3 = (bf16[256,256]{1,0:T(8,128)(2,1)S(1)}, bf16[256,256]{1,0:T(8,128)(2,1)}, u32[]{:S(2)}) copy-start(bf16[256,256]{1,0:T(8,128)(2,1)} %param.8) | copy-start | bytes 393220
  112.1 35.9 %all-to-all-start.3 = ((bf16[8,2,256,128]{3,2,1,0:T(8,128)(2,1)}), bf16[8,2,256,128]{3,2,1,0:T(8,128)(2,1)S(1)}, u32[]{:S(2)}, u32[]{:S(2)}) async-start(bf16[8,2,256,128]{3,2,1,0:T(8,128)(2,1)} %broadcast_in_dim.64), calls=%async_computation.3 | async-start | bytes 2097152 | tf_op jit(solution)/shard_map/all_to_all | solution.py:221
  118.9 21.5 %collective-permute-start.6 = (s16[8,128,128]{2,1,0:T(8,128)(2,1)S(1)}, s16[8,128,128]{2,1,0:T(8,128)(2,1)S(1)}, u32[]{:S(2)}, u32[]{:S(2)}) collective-permute-start(s16[8,128,128]{2,1,0:T(8,128)(2,1)S(1)} %get-tuple-element.36), channel_id=1, source_target_pairs={{0,256},{256,512},{512,0},{1,257},{257,513},{513,1},{2,258},{258,5... | collective-permute-start | bytes 786440 | tf_op jit(solution)/shard_map/ppermute | solution.py:230
  124.3 16.0 %collective-permute-start.7 = (s16[8,128,128]{2,1,0:T(8,128)(2,1)S(1)}, s16[8,128,128]{2,1,0:T(8,128)(2,1)S(1)}, u32[]{:S(2)}, u32[]{:S(2)}) collective-permute-start(s16[8,128,128]{2,1,0:T(8,128)(2,1)S(1)} %get-tuple-element.35), channel_id=1, source_target_pairs={{0,512},{256,0},{512,256},{1,513},{257,1},{513,257},{2,514},{258,2... | collective-permute-start | bytes 786440 | tf_op jit(solution)/shard_map/ppermute | solution.py:230
  126.2 10.9 %collective-permute-start.4 = (bf16[2,256,128]{2,1,0:T(8,128)(2,1)S(1)}, bf16[2,256,128]{2,1,0:T(8,128)(2,1)S(1)}, u32[]{:S(2)}, u32[]{:S(2)}) collective-permute-start(bf16[2,256,128]{2,1,0:T(8,128)(2,1)S(1)} %fusion), channel_id=1, source_target_pairs={{0,256},{256,512},{512,0},{1,257},{257,513},{513,1},{2,258},{258,5... | collective-permute-start | bytes 393224 | tf_op jit(solution)/shard_map/ppermute | solution.py:230
  129.6 10.7 %collective-permute-start.5 = (bf16[2,256,128]{2,1,0:T(8,128)(2,1)S(1)}, bf16[2,256,128]{2,1,0:T(8,128)(2,1)S(1)}, u32[]{:S(2)}, u32[]{:S(2)}) collective-permute-start(bf16[2,256,128]{2,1,0:T(8,128)(2,1)S(1)} %fusion), channel_id=1, source_target_pairs={{0,512},{256,0},{512,256},{1,513},{257,1},{513,257},{2,514},{258,2... | collective-permute-start | bytes 393224 | tf_op jit(solution)/shard_map/ppermute | solution.py:230
  155.0 1.6 copy-start
  157.2 8.5 %all-to-all-start.4 = ((f32[3,8,384]{2,1,0:T(8,128)}), f32[3,8,384]{2,1,0:T(8,128)S(1)}, u32[]{:S(2)}, u32[]{:S(2)}) async-start(f32[3,8,384]{2,1,0:T(8,128)} %broadcast_in_dim.65), calls=%async_computation.4 | async-start | bytes 73728 | tf_op jit(solution)/shard_map/all_to_all | solution.py:221
  165.7 1.9 copy-start.1
  219.4 13.2 %all-to-all-start.8 = ((f32[32,8,128]{2,1,0:T(8,128)}), f32[32,8,128]{2,1,0:T(8,128)S(1)}, u32[]{:S(2)}, u32[]{:S(2)}) async-start(f32[32,8,128]{2,1,0:T(8,128)} %broadcast_in_dim.68), calls=%async_computation.8 | async-start | bytes 262144 | tf_op jit(solution)/shard_map/all_to_all | solution.py:221

commit v4 on v3

v4 whole, which is shorter than its diff:
```python
import functools

import jax
import jax.numpy as jnp
from jax import lax
from jax.experimental import pallas as pl
from jax.experimental.pallas import tpu as pltpu
from jax.sharding import Mesh
from jax.sharding import PartitionSpec as P

tau = 0.5
eps = 1e-06
T = 128
ZL = 3
FS = 96
f32 = jnp.float32
bf16 = jnp.bfloat16
NT = (((1,), (1,)), ((), ()))
NN = (((1,), (0,)), ((), ()))
ROW = ("zl", "y")
COL = ("x", "zh", "core")
PARAMS = dict(vmem_limit_bytes=24 * 1024 * 1024)


def dot(a, b, dims):
    return lax.dot_general(a, b, dims, preferred_element_type=f32)


def counts_kernel(blocks, neg_ref, out_ref, acc_ref):
    nodes, negs = neg_ref.shape
    rows = 8 * ((blocks + 7) // 8)
    low_iota = lax.broadcasted_iota(jnp.int32, (T, negs), 0)
    high_iota = lax.broadcasted_iota(jnp.int32, (rows, negs), 0)

    def step(i, carry):
        base = pl.multiple_of(i * 8, 8)
        index = neg_ref[pl.ds(base, 8), :]
        low = index & (T - 1)
        high = index >> 7
        for j in range(8):
            low_hot = jnp.where(low[j : j + 1, :] == low_iota, 1.0, 0.0).astype(bf16)
            high_hot = jnp.where(high[j : j + 1, :] == high_iota, 1.0, 0.0).astype(bf16)
            found = dot(high_hot, low_hot, NT)
            acc_ref[pl.ds(base + j, rows, stride=nodes), :] = found
        return carry

    lax.fori_loop(0, nodes // 8, step, 0)

    def turn(h, carry):
        block = acc_ref[pl.ds(pl.multiple_of(h * nodes, nodes), nodes), :]
        out_ref[h] = block.T.astype(jnp.int32).astype(jnp.int16)
        return carry

    lax.fori_loop(0, blocks, turn, 0)


def count_negatives(negatives, blocks):
    nodes = negatives.shape[0]
    rows = 8 * ((blocks + 7) // 8)
    return pl.pallas_call(
        functools.partial(counts_kernel, blocks),
        out_shape=jax.ShapeDtypeStruct((blocks, T, nodes), jnp.int16),
        scratch_shapes=[pltpu.VMEM((rows * nodes, T), f32)],
        compiler_params=pltpu.CompilerParams(**PARAMS),
        cost_estimate=pl.CostEstimate(
            flops=2 * 16 * nodes * T * T * 64, bytes_accessed=2 << 20, transcendentals=0
        ),
        name="counts",
    )(negatives)


def behind(place, s):
    return lax.rem(place + ZL - s, ZL)


def tiles_kernel(cols, meta_ref, place_ref, own_ref, other_ref, *refs):
    tile_refs, (out_ref, acc_ref) = refs[:ZL], refs[ZL:]
    zsize = own_ref.shape[1] // ZL
    acc_ref[...] = jnp.zeros_like(acc_ref)
    core, zl = place_ref[0], place_ref[1]
    for s in range(ZL):

        def slot(k, carry, s=s):
            trow, tcol = meta_ref[s, 0, k], meta_ref[s, 1, k]

            @pl.when(trow >= 0)
            def _():
                chip = lax.div(tcol, 2)
                at = lax.div(chip, zsize), behind(zl, s) * zsize + lax.rem(chip, zsize)
                mine = lax.rem(tcol, 2) == core
                rows = jnp.where(mine, own_ref[at], other_ref[at])
                product = dot(rows, tile_refs[s][pl.ds(pl.multiple_of(k * T, T), T), :], NT)
                for v in range(2):
                    kept = meta_ref[s, 2 + v, k].astype(f32)
                    acc_ref[trow, v] += kept * product

            return carry

        lax.fori_loop(0, meta_ref.shape[2], slot, 0)
    out_ref[...] = acc_ref[...].astype(bf16)


def tile_sums(meta, place, own, other, tiles, cols, blocks):
    shape = (blocks, 2, own.shape[2], T)
    return pl.pallas_call(
        functools.partial(tiles_kernel, cols),
        out_shape=jax.ShapeDtypeStruct(shape, bf16),
        in_specs=[pl.BlockSpec(memory_space=pltpu.SMEM)] * 2
        + [pl.BlockSpec(memory_space=pltpu.VMEM)] * (2 + ZL),
        scratch_shapes=[pltpu.VMEM(shape, f32)],
        compiler_params=pltpu.CompilerParams(**PARAMS),
        name="tile_sums",
    )(meta, place, own, other, *tiles)


def anchors_of(n_ref, zl, v):
    return jnp.concatenate([n_ref[behind(zl, z), v] for z in range(ZL)], 1)


def embed(weight_t, agg):
    z = dot(weight_t, agg, NN)
    rinv = lax.rsqrt(jnp.sum(z * z, 0, keepdims=True) + eps)
    return z * rinv, rinv


def pair_of(a_ref, p, v):
    return jnp.concatenate([a_ref[2 * p, v], a_ref[2 * p + 1, v]], 1)


def scores_kernel(place_ref, n_ref, a_ref, w_ref, c_ref, tot_ref, e_ref, low_ref):
    weight_t = w_ref[...]
    zl = place_ref[1]
    anchors = [embed(weight_t, anchors_of(n_ref, zl, v))[0].astype(bf16) for v in range(2)]
    tot_ref[...] = jnp.zeros_like(tot_ref)

    def pair(p, carry):
        count = jnp.concatenate(
            [
                jnp.concatenate([c_ref[behind(zl, z), 2 * p + i] for z in range(ZL)], 1)
                for i in range(2)
            ],
            0,
        )
        count = count.astype(jnp.int32).astype(f32)
        for v in range(2):
            emb = embed(weight_t, pair_of(a_ref, p, 1 - v))[0]
            low_ref[p, 1 - v] = emb.astype(bf16)
            score = dot(emb.T.astype(bf16), anchors[v], NN)
            term = count * jnp.exp(score * (1.0 / tau))
            e_ref[p, v] = term.astype(bf16)
            tot_ref[v : v + 1, :] += jnp.sum(term, 0, keepdims=True)
        return carry

    lax.fori_loop(0, e_ref.shape[0], pair, 0)


def pull_kernel(e_ref, low_ref, sums_ref):
    sums_ref[...] = jnp.zeros_like(sums_ref)

    def pair(p, carry):
        for v in range(2):
            sums_ref[v] += dot(low_ref[p, 1 - v], e_ref[p, v], NN)
        return carry

    lax.fori_loop(0, e_ref.shape[0], pair, 0)


def split_dot(agg, dz):
    high = dz.astype(bf16)
    low = (dz - high.astype(f32)).astype(bf16)
    return dot(agg, high, NT) + dot(agg, low, NT)


def grads_kernel(
    coef, place_ref, n_ref, a_ref, w_ref, e_ref, sums_ref, tot_ref, mask_ref, loss_ref, grad_ref
):
    weight_t = w_ref[...]
    agg_n = [anchors_of(n_ref, place_ref[1], v) for v in range(2)]
    emb_n, rinv_n = zip(*[embed(weight_t, agg) for agg in agg_n])
    full_n = [emb.astype(bf16).astype(f32) for emb in emb_n]
    pos = jnp.sum(full_n[0] * full_n[1], 0, keepdims=True) * (1.0 / tau)
    own = jnp.exp(pos)
    tot = [own + sum(tot_ref[z, v : v + 1, :] for z in range(ZL)) for v in range(2)]
    loss = 0.5 * ((jnp.log(tot[0]) - pos) + (jnp.log(tot[1]) - pos))
    loss_ref[...] = jnp.broadcast_to(loss, loss_ref.shape)
    inverse = [1.0 / t for t in tot]
    both = (own * inverse[0] + own * inverse[1] - 2.0) * mask_ref[0:1, :]
    scaled = [(full_n[v] * inverse[v]).astype(bf16) for v in range(2)]

    def back(emb, rinv, d):
        return (d - emb * jnp.sum(emb * d, 0, keepdims=True)) * rinv

    grad_ref[...] = jnp.zeros_like(grad_ref)

    def pair(p, carry):
        for v in range(2):
            agg = pair_of(a_ref, p, v)
            emb, rinv = embed(weight_t, agg)
            d = coef * dot(scaled[1 - v], e_ref[p, 1 - v], NT)
            grad_ref[...] += split_dot(agg, back(emb, rinv, d))
        return carry

    lax.fori_loop(0, e_ref.shape[0], pair, 0)
    for v in range(2):
        d = coef * (both * full_n[1 - v] + sums_ref[v] * inverse[v])
        grad_ref[...] += split_dot(agg_n[v], back(emb_n[v], rinv_n[v], d))


def group_call(kernel, out_shape, inputs, scalars, name):
    return pl.pallas_call(
        kernel,
        out_shape=out_shape,
        in_specs=[pl.BlockSpec(memory_space=pltpu.SMEM)] * scalars
        + [pl.BlockSpec(memory_space=pltpu.VMEM)] * (inputs - scalars),
        compiler_params=pltpu.CompilerParams(**PARAMS),
        cost_estimate=pl.CostEstimate(flops=1 << 31, bytes_accessed=4 << 20, transcendentals=0),
        name=name,
    )


def swap(x, axis):
    return lax.all_to_all(x, axis, 0, 0, tiled=True)


def share(x, axis):
    return swap(jnp.broadcast_to(x[None], (lax.axis_size(axis),) + x.shape), axis)


def shift(x, axis, by):
    size = lax.axis_size(axis)
    return lax.ppermute(x, axis, [(i, (i + by) % size) for i in range(size)])


def around(x, pick, axis):
    return [pick(x, 0)] + [shift(pick(x, s), axis, s) for s in range(1, lax.axis_size(axis))]


def reduce_all(grad):
    rows, width = grad.shape
    planes = ("core",), ("y", "x")
    part = grad.reshape(-1, T)
    for axes in planes:
        got = swap(part.reshape(lax.axis_size(axes), -1, T), axes)
        part = jnp.sum(got, 0)
    part = jnp.sum(share(part, ("zl", "zh")), 0)
    for axes in planes[::-1]:
        part = share(part, axes).reshape(-1, T)
    return part.reshape(rows, width)


def packed(tiles, tile_pos, edge_keep, cols):
    slots = tile_pos.shape[0]
    held = tile_pos >= 0
    trow = jnp.where(held, tile_pos // cols, -1)
    tcol = jnp.where(held, tile_pos % cols, 0)
    meta = jnp.concatenate([trow[None], tcol[None], edge_keep], 0).astype(bf16)
    meta = jnp.pad(meta, ((0, 16 - meta.shape[0]), (0, T - slots)))
    return jnp.concatenate([tiles.reshape(slots * T, T), meta], 0)


def shards(features, weight, tiles, tile_pos, edge_keep, feature_keep, negatives):
    nodes, width = features.shape
    slots = tiles.shape[0]
    xsize, zsize = lax.axis_size("x"), lax.axis_size("zh")
    ysize = lax.axis_size("y")
    cols = xsize * zsize * lax.axis_size("core")
    zl = lax.axis_index("zl")
    place = jnp.stack([lax.axis_index("core"), zl])
    total = lax.axis_size(ROW) * cols * nodes
    pad = ZL * FS - width
    whole = lambda x, s: x

    turned = jnp.pad(features.T, ((0, pad), (0, 0))).reshape(ZL, 1, FS, nodes)
    sent = jnp.broadcast_to(turned, (ZL, zsize, FS, nodes)).reshape(ZL * zsize, FS, nodes)
    near = swap(sent, ("zl", "zh"))
    all_tiles = around(packed(tiles, tile_pos, edge_keep, cols), whole, "zl")
    own = share(near, "x")
    own, all_tiles = lax.optimization_barrier((own, all_tiles))
    other = shift(own, "core", 1)
    metas = jnp.stack([x[slots * T : slots * T + 4, :slots] for x in all_tiles]).astype(jnp.int32)

    part = tile_sums(metas, place, own, other, all_tiles, cols, ZL * ysize)
    part, negatives = lax.optimization_barrier((part, negatives))
    got = swap(part, ROW)
    counts = count_negatives(negatives, ZL * ysize)
    got, counts = lax.optimization_barrier((got, counts))
    agg = jnp.sum(got.reshape(ZL, ysize, 2, FS, nodes).astype(f32), 1)
    agg = agg.transpose(1, 0, 2, 3).reshape(2, ZL * FS, nodes)[:, :width]
    agg = (agg * feature_keep.astype(f32)[:, :, None]).astype(bf16)
    agg, counts = lax.optimization_barrier((agg, counts))
    members = share(agg, "y")
    anchors = jnp.stack(around(agg, whole, "zl"))
    ahead = lambda x, s: lax.dynamic_index_in_dim(x, lax.rem(zl + s, ZL), 0, keepdims=False)
    counts = jnp.stack(around(counts.reshape(ZL, ysize, nodes, nodes), ahead, "zl"))

    weight_t = weight.T
    group = ZL * nodes
    rows = jax.ShapeDtypeStruct((8, group), f32)
    tot, terms, low = group_call(
        scores_kernel,
        (
            rows,
            jax.ShapeDtypeStruct((ysize // 2, 2, 2 * nodes, group), bf16),
            jax.ShapeDtypeStruct((ysize // 2, 2, width, 2 * nodes), bf16),
        ),
        5,
        1,
        "scores",
    )(place, anchors, members, weight_t, counts)
    tots = share(tot, "zl")
    sums = group_call(
        pull_kernel, jax.ShapeDtypeStruct((2, width, group), f32), 2, 0, "pull"
    )(terms, low)
    mask = (jnp.arange(group) // nodes == zl).astype(f32)
    mask = jnp.broadcast_to(mask, (8, group))
    coef = 1.0 / (2.0 * tau * float(total) ** 0.5)
    loss, grad = group_call(
        functools.partial(grads_kernel, coef),
        (rows, jax.ShapeDtypeStruct((width, width), f32)),
        8,
        1,
        "grads",
    )(place, anchors, members, weight_t, terms, sums, tots, mask)
    node_loss = lax.dynamic_slice_in_dim(loss[0], zl * nodes, nodes)
    return node_loss, reduce_all(grad)


def solution(mesh):
    rows, cols = mesh.devices.shape
    fine = Mesh(mesh.devices.reshape(ZL, rows // ZL, cols // 8, 4, 2), ROW + COL)
    every = ROW + COL
    in_specs = (
        P(every, None),
        P(),
        P(every, None, None),
        P(every),
        P(None, every),
        P(),
        P(every, None),
    )
    out_specs = (P(every), P())
    return jax.shard_map(shards, mesh=fine, in_specs=in_specs, out_specs=out_specs, check_vma=False)
```

time: 243 us -> 229 us (0.942)
  Pallas kernels: 39.1 us -> 31.4 us
  starting transfers between devices: 70.8 us -> 65.9 us
  waiting for transfers between devices: 68.1 us -> 65.6 us
    ppermute x8 -> x7, waiting for transfers between devices: 46.7 us -> 25.6 us  [shift(): return lax.ppermute(x, axis, [(i, (i + by) % size) for i in range(size)])]
    all_to_all x6, waiting for transfers between devices: 21.4 us -> 40 us  [swap(): return lax.all_to_all(x, axis, 0, 0, tiled=True)]
    pallas_call x1, Pallas kernels: 11.7 us -> 6.01 us  [shards(): group_call(functools.partial(grads_kernel, coef), (rows, jax.ShapeDtypeSt...]
    ppermute x8 -> x7, starting transfers between devices: 26.6 us -> 22.7 us  [shift(): return lax.ppermute(x, axis, [(i, (i + by) % size) for i in range(size)])]
    unnamed x14 -> x26, local copies, waits for them, and re-layouts: 5.63 us -> 7.76 us
    pallas_call x1 -> x2, Pallas kernels: 6.97 us -> 5.81 us  [the longest x1 4.59 us: shards(): group_call(scores_kernel, (rows, jax.ShapeDtypeStruct((ysize // 2, 2, 2 *...]
  transfers between devices with their start and end apart: 14 -> 13, of which waited for: 10 -> 10; matrix products, arithmetic and copies ran while one was open for 2% -> 1% of each run, Pallas kernels for 7% -> 7%
where the time goes in v4:
time: 229 us; the launch traced here: 228 us
  starting transfers between devices  65.9 us (29%)
  waiting for transfers between devices  65.6 us (29%)
  blocking collectives  49.1 us (21%)
  Pallas kernels  31.4 us (14%)
  local copies, waits for them, and re-layouts  13.7 us (6%)
    all_to_all x4, blocking collectives, swap(): return lax.all_to_all(x, axis, 0, 0, tiled=True)  49.1 us
    all_to_all x6, starting transfers between devices, swap(): return lax.all_to_all(x, axis, 0, 0, tiled=True)  43.1 us
    all_to_all x6, waiting for transfers between devices, swap(): return lax.all_to_all(x, axis, 0, 0, tiled=True)  40 us
    ppermute x7, waiting for transfers between devices, shift(): return lax.ppermute(x, axis, [(i, (i + by) % size) for i in range(size)])  25.6 us
    ppermute x7, starting transfers between devices, shift(): return lax.ppermute(x, axis, [(i, (i + by) % size) for i in range(size)])  22.7 us
    pallas_call x1, Pallas kernels, count_negatives(): pl.pallas_call(functools.partial(counts_kernel, blocks), out_shape=jax.Sh...  15.8 us
    unnamed x26, local copies, waits for them, and re-layouts  7.76 us
    pallas_call x1, Pallas kernels, shards(): group_call(functools.partial(grads_kernel, coef), (rows, jax.ShapeDtypeSt...  6.01 us
  transfers between devices with their start and end apart: 13, of which 10 were waited for; matrix products, arithmetic and copies ran while one was open for 1% of the time, Pallas kernels for 7%

profile of v4, /device:TPU:1, one launch (start us, length us, event | category | flops | bytes accessed | tf_op | source)
XLA Modules:
  0.0 228.3 jit_solution(14076250502331593373)
XLA Ops:
  2.4 15.7 %all-to-all-start = ((bf16[12,96,128]{2,1,0:T(8,128)(2,1)}), bf16[12,96,128]{2,1,0:T(8,128)(2,1)S(1)}, u32[]{:S(2)}, u32[]{:S(2)}) async-start(bf16[12,96,128]{2,1,0:T(8,128)(2,1)} %bitcast.4), calls=%async_computation | async-start | bytes 589824 | tf_op jit(solution)/shard_map/all_to_all | solution.py:222
  18.1 14.4 %all-to-all-done = bf16[12,96,128]{2,1,0:T(8,128)(2,1)S(1)} async-done(((bf16[12,96,128]{2,1,0:T(8,128)(2,1)}), bf16[12,96,128]{2,1,0:T(8,128)(2,1)S(1)}, u32[]{:S(2)}, u32[]{:S(2)}) %all-to-all-start) | async-done | bytes 294944 | tf_op jit(solution)/shard_map/all_to_all | solution.py:222
  33.7 4.1 %all-to-all-start.1 = ((bf16[4,12,96,128]{3,2,1,0:T(8,128)(2,1)}), bf16[4,12,96,128]{3,2,1,0:T(8,128)(2,1)S(1)}, u32[]{:S(2)}, u32[]{:S(2)}) async-start(bf16[4,12,96,128]{3,2,1,0:T(8,128)(2,1)} %broadcast_in_dim.31), calls=%async_computation.1 | async-start | bytes 2359296 | tf_op jit(solution)/shard_map/all_to_all | solution.py:222
  37.9 1.9 collective-permute-start
  39.8 4.3 %collective-permute-start.1 = (bf16[1552,128]{1,0:T(8,128)(2,1)S(1)}, bf16[1552,128]{1,0:T(8,128)(2,1)S(1)}, u32[]{:S(2)}, u32[]{:S(2)}) collective-permute-start(bf16[1552,128]{1,0:T(8,128)(2,1)S(1)} %pad_maximum_fusion.refs_0_), channel_id=1, source_target_pairs={{0,512},{256,0},{512,256},{1,513},{257,1},{513,257},{2,514},{258,2... | collective-permute-start | bytes 1191944 | tf_op jit(solution)/shard_map/ppermute | solution.py:231
  44.1 3.6 %collective-permute-done.refs_1_ = bf16[1552,128]{1,0:T(8,128)(2,1)S(1)} collective-permute-done((bf16[1552,128]{1,0:T(8,128)(2,1)S(1)}, bf16[1552,128]{1,0:T(8,128)(2,1)S(1)}, u32[]{:S(2)}, u32[]{:S(2)}) %collective-permute-start) | collective-permute-done | bytes 397344 | tf_op jit(solution)/shard_map/ppermute | solution.py:231
  47.7 11.7 %collective-permute-done.1.refs_2_ = bf16[1552,128]{1,0:T(8,128)(2,1)S(1)} collective-permute-done((bf16[1552,128]{1,0:T(8,128)(2,1)S(1)}, bf16[1552,128]{1,0:T(8,128)(2,1)S(1)}, u32[]{:S(2)}, u32[]{:S(2)}) %collective-permute-start.1) | collective-permute-done | bytes 397344 | tf_op jit(solution)/shard_map/ppermute | solution.py:231
  59.4 3.3 %collective-permute-start.2 = (bf16[4,12,96,128]{3,2,1,0:T(8,128)(2,1)S(1)}, bf16[4,12,96,128]{3,2,1,0:T(8,128)(2,1)S(1)}, u32[]{:S(2)}, u32[]{:S(2)}) collective-permute-start(bf16[4,12,96,128]{3,2,1,0:T(8,128)(2,1)S(1)} %all-to-all-done.1.own_ref), channel_id=1, source_target_pairs={{0,1},{1,0},{2,3},{3,2},{4,5},{5,4},{6,7},{7,6},{8,9},{9,8},{10,11... | collective-permute-start | bytes 3538952 | tf_op jit(solution)/shard_map/ppermute | solution.py:231
  62.8 2.3 %collective-permute-done.2.other_ref = bf16[4,12,96,128]{3,2,1,0:T(8,128)(2,1)S(1)} collective-permute-done((bf16[4,12,96,128]{3,2,1,0:T(8,128)(2,1)S(1)}, bf16[4,12,96,128]{3,2,1,0:T(8,128)(2,1)S(1)}, u32[]{:S(2)}, u32[]{:S(2)}) %collective-permute-start.2) | collective-permute-done | bytes 1179680 | tf_op jit(solution)/shard_map/ppermute | solution.py:231
  65.2 3.8 %tile_sums.1 = bf16[24,2,96,128]{3,2,1,0:T(8,128)(2,1)} custom-call(s32[3,4,12]{2,1,0:T(4,128)S(1)} %maximum_convert_fusion.meta_ref, s32[2]{0:T(128)S(1)} %pad_add_fusion.1.place_ref, bf16[4,12,96,128]{3,2,1,0:T(8,128)(2,1)S(1)} %all-to-all-done.1.own_ref, bf16[4,12,96,128]{3,2,1,0:T(8,128)(2,1)S(1)} %collective-permute-done.2.other_ref, ...), custom_call_target="tpu_custom_call" | custom-call | tf_op jit(solution)/shard_map/tile_sums/pallas_call | solution.py:105
  69.0 7.2 %all-to-all-start.2 = ((bf16[24,2,96,128]{3,2,1,0:T(8,128)(2,1)}), bf16[24,2,96,128]{3,2,1,0:T(8,128)(2,1)S(1)}, u32[]{:S(2)}, u32[]{:S(2)}) async-start(bf16[24,2,96,128]{3,2,1,0:T(8,128)(2,1)} %tile_sums.1), calls=%async_computation.2 | async-start | bytes 2359296 | tf_op jit(solution)/shard_map/all_to_all | solution.py:222
  76.2 15.8 %counts.1 = s16[24,128,128]{2,1,0:T(8,128)(2,1)S(1)} custom-call(s32[128,1024]{1,0:T(8,128)S(1)} %copy-done), custom_call_target="tpu_custom_call" | custom-call | flops 4294967296 | bytes 2097152 | tf_op jit(solution)/shard_map/counts/pallas_call | solution.py:60
  92.0 10.8 %all-to-all-done.2 = bf16[24,2,96,128]{3,2,1,0:T(8,128)(2,1)S(1)} async-done(((bf16[24,2,96,128]{3,2,1,0:T(8,128)(2,1)}), bf16[24,2,96,128]{3,2,1,0:T(8,128)(2,1)S(1)}, u32[]{:S(2)}, u32[]{:S(2)}) %all-to-all-start.2) | async-done | bytes 1179680 | tf_op jit(solution)/shard_map/all_to_all | solution.py:222
  104.3 7.7 %all-to-all-start.3 = ((bf16[8,2,256,128]{3,2,1,0:T(8,128)(2,1)}), bf16[8,2,256,128]{3,2,1,0:T(8,128)(2,1)S(1)}, u32[]{:S(2)}, u32[]{:S(2)}) async-start(bf16[8,2,256,128]{3,2,1,0:T(8,128)(2,1)} %broadcast_in_dim.64), calls=%async_computation.3 | async-start | bytes 2097152 | tf_op jit(solution)/shard_map/all_to_all | solution.py:222
  112.2 5.2 %collective-permute-start.5 = (s16[8,128,128]{2,1,0:T(8,128)(2,1)S(1)}, s16[8,128,128]{2,1,0:T(8,128)(2,1)S(1)}, u32[]{:S(2)}, u32[]{:S(2)}) collective-permute-start(s16[8,128,128]{2,1,0:T(8,128)(2,1)S(1)} %get-tuple-element.34), channel_id=1, source_target_pairs={{0,256},{256,512},{512,0},{1,257},{257,513},{513,1},{2,258},{258,5... | collective-permute-start | bytes 786440 | tf_op jit(solution)/shard_map/ppermute | solution.py:231
  117.3 1.9 collective-permute-start.6
  119.3 3.4 %collective-permute-start.3 = (bf16[2,256,128]{2,1,0:T(8,128)(2,1)S(1)}, bf16[2,256,128]{2,1,0:T(8,128)(2,1)S(1)}, u32[]{:S(2)}, u32[]{:S(2)}) collective-permute-start(bf16[2,256,128]{2,1,0:T(8,128)(2,1)S(1)} %fusion), channel_id=1, source_target_pairs={{0,256},{256,512},{512,0},{1,257},{257,513},{513,1},{2,258},{258,5... | collective-permute-start | bytes 393224 | tf_op jit(solution)/shard_map/ppermute | solution.py:231
  122.6 2.8 %collective-permute-start.4 = (bf16[2,256,128]{2,1,0:T(8,128)(2,1)S(1)}, bf16[2,256,128]{2,1,0:T(8,128)(2,1)S(1)}, u32[]{:S(2)}, u32[]{:S(2)}) collective-permute-start(bf16[2,256,128]{2,1,0:T(8,128)(2,1)S(1)} %fusion), channel_id=1, source_target_pairs={{0,512},{256,0},{512,256},{1,513},{257,1},{513,257},{2,514},{258,2... | collective-permute-start | bytes 393224 | tf_op jit(solution)/shard_map/ppermute | solution.py:231
  125.6 4.6 %collective-permute-done.3 = bf16[2,256,128]{2,1,0:T(8,128)(2,1)S(1)} collective-permute-done((bf16[2,256,128]{2,1,0:T(8,128)(2,1)S(1)}, bf16[2,256,128]{2,1,0:T(8,128)(2,1)S(1)}, u32[]{:S(2)}, u32[]{:S(2)}) %collective-permute-start.3) | collective-permute-done | bytes 131104 | tf_op jit(solution)/shard_map/ppermute | solution.py:231
  130.2 3.3 %collective-permute-done.4 = bf16[2,256,128]{2,1,0:T(8,128)(2,1)S(1)} collective-permute-done((bf16[2,256,128]{2,1,0:T(8,128)(2,1)S(1)}, bf16[2,256,128]{2,1,0:T(8,128)(2,1)S(1)}, u32[]{:S(2)}, u32[]{:S(2)}) %collective-permute-start.4) | collective-permute-done | bytes 131104 | tf_op jit(solution)/shard_map/ppermute | solution.py:231
  135.3 6.0 %all-to-all-done.3.a_ref = bf16[8,2,256,128]{3,2,1,0:T(8,128)(2,1)S(1)} async-done(((bf16[8,2,256,128]{3,2,1,0:T(8,128)(2,1)}), bf16[8,2,256,128]{3,2,1,0:T(8,128)(2,1)S(1)}, u32[]{:S(2)}, u32[]{:S(2)}) %all-to-all-start.3) | async-done | bytes 1048608 | tf_op jit(solution)/shard_map/all_to_all | solution.py:222
  141.2 4.6 %scores.1 = (f32[8,384]{1,0:T(8,128)S(1)}, bf16[4,2,256,384]{3,2,1,0:T(8,128)(2,1)S(1)}, bf16[4,2,256,256]{3,2,1,0:T(8,128)(2,1)S(1)}) custom-call(s32[2]{0:T(128)S(1)} %pad_add_fusion.1.place_ref, bf16[3,2,256,128]{3,2,1,0:T(8,128)(2,1)S(1)} %pad_maximum_fusion.1.n_ref, bf16[8,2,256,128]{3,2,1,0:T(8,128)(2,1)S(1)} %all-to-all-done.3.a_ref, ...), custom_call_target="tpu_custom_call" | custom-call | flops 2147483648 | bytes 4194304 | tf_op jit(solution)/shard_map/scores/pallas_call | solution.py:299
  147.6 4.5 %all-to-all-start.4 = ((f32[3,8,384]{2,1,0:T(8,128)}), f32[3,8,384]{2,1,0:T(8,128)S(1)}, u32[]{:S(2)}, u32[]{:S(2)}) async-start(f32[3,8,384]{2,1,0:T(8,128)} %broadcast_in_dim.65), calls=%async_computation.4 | async-start | bytes 73728 | tf_op jit(solution)/shard_map/all_to_all | solution.py:222
  152.1 1.4 copy-done.2
  155.8 1.4 copy-done.3
  158.3 6.0 %grads.1 = (f32[8,384]{1,0:T(8,128)S(1)}, f32[256,256]{1,0:T(8,128)S(1)}) custom-call(s32[2]{0:T(128)S(1)} %pad_add_fusion.1.place_ref, bf16[3,2,256,128]{3,2,1,0:T(8,128)(2,1)S(1)} %pad_maximum_fusion.1.n_ref, bf16[8,2,256,128]{3,2,1,0:T(8,128)(2,1)S(1)} %all-to-all-done.3.a_ref, bf16[256,256]{1,0:T(8,128)(2,1)S(1)} %bitcast.37, ...), custom_call_target="tpu_custom_call" | custom-call | flops 2147483648 | bytes 4194304 | tf_op jit(solution)/shard_map/grads/pallas_call | solution.py:317
  164.4 5.5 %all_to_all.50 = f32[2,256,128]{2,1,0:T(8,128)S(1)} all-to-all(f32[2,256,128]{2,1,0:T(8,128)S(1)} %reshape_reshape.6), channel_id=1, replica_groups=mesh['zl'=3,'y'=8,'x'=4,'zh'=4,'core'=2] {'core'}, dimensions={0} | all-to-all | bytes 524288 | tf_op jit(solution)/shard_map/all_to_all | solution.py:222
  169.9 13.5 %all_to_all.51 = f32[32,8,128]{2,1,0:T(8,128)S(1)} all-to-all(f32[32,8,128]{2,1,0:T(8,128)S(1)} %bitcast.43), channel_id=1, replica_groups=mesh['zl'=3,'y'=8,'x'=4,'zh'=4,'core'=2] {'y','x'}, dimensions={0} | all-to-all | bytes 262144 | tf_op jit(solution)/shard_map/all_to_all | solution.py:222
  183.4 21.9 %all_to_all.52 = f32[12,8,128]{2,1,0:T(8,128)S(1)} all-to-all(f32[12,8,128]{2,1,0:T(8,128)S(1)} %broadcast_in_dim.67), channel_id=1, replica_groups=mesh['zl'=3,'y'=8,'x'=4,'zh'=4,'core'=2] {'zl','zh'}, dimensions={0} | all-to-all | bytes 98304 | tf_op jit(solution)/shard_map/all_to_all | solution.py:222
  206.0 3.9 %all-to-all-start.8 = ((f32[32,8,128]{2,1,0:T(8,128)}), f32[32,8,128]{2,1,0:T(8,128)S(1)}, u32[]{:S(2)}, u32[]{:S(2)}) async-start(f32[32,8,128]{2,1,0:T(8,128)} %broadcast_in_dim.68), calls=%async_computation.8 | async-start | bytes 262144 | tf_op jit(solution)/shard_map/all_to_all | solution.py:222
  210.4 8.8 %all-to-all-done.8 = f32[32,8,128]{2,1,0:T(8,128)S(1)} async-done(((f32[32,8,128]{2,1,0:T(8,128)}), f32[32,8,128]{2,1,0:T(8,128)S(1)}, u32[]{:S(2)}, u32[]{:S(2)}) %all-to-all-start.8) | async-done | bytes 131104 | tf_op jit(solution)/shard_map/all_to_all | solution.py:222
  219.2 8.3 %all_to_all.53 = f32[2,256,128]{2,1,0:T(8,128)S(1)} all-to-all(f32[2,256,128]{2,1,0:T(8,128)S(1)} %broadcast_in_dim.70), channel_id=1, replica_groups=mesh['zl'=3,'y'=8,'x'=4,'zh'=4,'core'=2] {'core'}, dimensions={0} | all-to-all | bytes 524288 | tf_op jit(solution)/shard_map/all_to_all | solution.py:222
  (61 shorter events, 13.8 us)
Async XLA Ops:
  0.6 17.5 %copy-start.10 = (s32[2,12]{1,0:T(2,128)S(1)}, s32[2,12]{1,0:T(2,128)}, u32[]{:S(2)}) copy-start(s32[2,12]{1,0:T(2,128)} %param.11) | copy-start | bytes 292
  2.4 30.1 %all-to-all-start = ((bf16[12,96,128]{2,1,0:T(8,128)(2,1)}), bf16[12,96,128]{2,1,0:T(8,128)(2,1)S(1)}, u32[]{:S(2)}, u32[]{:S(2)}) async-start(bf16[12,96,128]{2,1,0:T(8,128)(2,1)} %bitcast.4), calls=%async_computation | async-start | bytes 589824 | tf_op jit(solution)/shard_map/all_to_all | solution.py:222
  33.7 4.2 %copy-start.11 = (s32[12]{0:T(128)S(1)}, s32[12]{0:T(128)}, u32[]{:S(2)}) copy-start(s32[12]{0:T(128)} %param.10) | copy-start | bytes 148
  33.7 4.2 %copy-start.6 = (bf16[12,128,128]{2,1,0:T(8,128)(2,1)S(1)}, bf16[12,128,128]{2,1,0:T(8,128)(2,1)}, u32[]{:S(2)}) copy-start(bf16[12,128,128]{2,1,0:T(8,128)(2,1)} %param.9) | copy-start | bytes 1179652
  33.7 25.8 %all-to-all-start.1 = ((bf16[4,12,96,128]{3,2,1,0:T(8,128)(2,1)}), bf16[4,12,96,128]{3,2,1,0:T(8,128)(2,1)S(1)}, u32[]{:S(2)}, u32[]{:S(2)}) async-start(bf16[4,12,96,128]{3,2,1,0:T(8,128)(2,1)} %broadcast_in_dim.31), calls=%async_computation.1 | async-start | bytes 2359296 | tf_op jit(solution)/shard_map/all_to_all | solution.py:222
  37.9 9.8 %collective-permute-start = (bf16[1552,128]{1,0:T(8,128)(2,1)S(1)}, bf16[1552,128]{1,0:T(8,128)(2,1)S(1)}, u32[]{:S(2)}, u32[]{:S(2)}) collective-permute-start(bf16[1552,128]{1,0:T(8,128)(2,1)S(1)} %pad_maximum_fusion.refs_0_), channel_id=1, source_target_pairs={{0,256},{256,512},{512,0},{1,257},{257,513},{513,1},{2,258},{258,5... | collective-permute-start | bytes 1191944 | tf_op jit(solution)/shard_map/ppermute | solution.py:231
  39.8 19.6 %collective-permute-start.1 = (bf16[1552,128]{1,0:T(8,128)(2,1)S(1)}, bf16[1552,128]{1,0:T(8,128)(2,1)S(1)}, u32[]{:S(2)}, u32[]{:S(2)}) collective-permute-start(bf16[1552,128]{1,0:T(8,128)(2,1)S(1)} %pad_maximum_fusion.refs_0_), channel_id=1, source_target_pairs={{0,512},{256,0},{512,256},{1,513},{257,1},{513,257},{2,514},{258,2... | collective-permute-start | bytes 1191944 | tf_op jit(solution)/shard_map/ppermute | solution.py:231
  59.4 5.7 %collective-permute-start.2 = (bf16[4,12,96,128]{3,2,1,0:T(8,128)(2,1)S(1)}, bf16[4,12,96,128]{3,2,1,0:T(8,128)(2,1)S(1)}, u32[]{:S(2)}, u32[]{:S(2)}) collective-permute-start(bf16[4,12,96,128]{3,2,1,0:T(8,128)(2,1)S(1)} %all-to-all-done.1.own_ref), channel_id=1, source_target_pairs={{0,1},{1,0},{2,3},{3,2},{4,5},{5,4},{6,7},{7,6},{8,9},{9,8},{10,11... | collective-permute-start | bytes 3538952 | tf_op jit(solution)/shard_map/ppermute | solution.py:231
  69.0 7.2 %copy-start.9 = (s32[2,256]{1,0:T(2,128)S(1)}, s32[2,256]{1,0:T(2,128)}, u32[]{:S(2)}) copy-start(s32[2,256]{1,0:T(2,128)} %param.12) | copy-start | bytes 6148
  69.0 7.2 %copy-start = (s32[128,1024]{1,0:T(8,128)S(1)}, s32[128,1024]{1,0:T(8,128)}, u32[]{:S(2)}) copy-start(s32[128,1024]{1,0:T(8,128)} %neg_ref) | copy-start | bytes 1572868
  69.0 33.8 %all-to-all-start.2 = ((bf16[24,2,96,128]{3,2,1,0:T(8,128)(2,1)}), bf16[24,2,96,128]{3,2,1,0:T(8,128)(2,1)S(1)}, u32[]{:S(2)}, u32[]{:S(2)}) async-start(bf16[24,2,96,128]{3,2,1,0:T(8,128)(2,1)} %tile_sums.1), calls=%async_computation.2 | async-start | bytes 2359296 | tf_op jit(solution)/shard_map/all_to_all | solution.py:222
  104.3 36.9 %all-to-all-start.3 = ((bf16[8,2,256,128]{3,2,1,0:T(8,128)(2,1)}), bf16[8,2,256,128]{3,2,1,0:T(8,128)(2,1)S(1)}, u32[]{:S(2)}, u32[]{:S(2)}) async-start(bf16[8,2,256,128]{3,2,1,0:T(8,128)(2,1)} %broadcast_in_dim.64), calls=%async_computation.3 | async-start | bytes 2097152 | tf_op jit(solution)/shard_map/all_to_all | solution.py:222
  112.0 13.4 %copy-start.8 = (bf16[256,256]{1,0:T(8,128)(2,1)S(1)}, bf16[256,256]{1,0:T(8,128)(2,1)}, u32[]{:S(2)}) copy-start(bf16[256,256]{1,0:T(8,128)(2,1)} %param.8) | copy-start | bytes 393220
  112.2 21.4 %collective-permute-start.5 = (s16[8,128,128]{2,1,0:T(8,128)(2,1)S(1)}, s16[8,128,128]{2,1,0:T(8,128)(2,1)S(1)}, u32[]{:S(2)}, u32[]{:S(2)}) collective-permute-start(s16[8,128,128]{2,1,0:T(8,128)(2,1)S(1)} %get-tuple-element.34), channel_id=1, source_target_pairs={{0,256},{256,512},{512,0},{1,257},{257,513},{513,1},{2,258},{258,5... | collective-permute-start | bytes 786440 | tf_op jit(solution)/shard_map/ppermute | solution.py:231
  117.3 16.2 %collective-permute-start.6 = (s16[8,128,128]{2,1,0:T(8,128)(2,1)S(1)}, s16[8,128,128]{2,1,0:T(8,128)(2,1)S(1)}, u32[]{:S(2)}, u32[]{:S(2)}) collective-permute-start(s16[8,128,128]{2,1,0:T(8,128)(2,1)S(1)} %get-tuple-element.33), channel_id=1, source_target_pairs={{0,512},{256,0},{512,256},{1,513},{257,1},{513,257},{2,514},{258,2... | collective-permute-start | bytes 786440 | tf_op jit(solution)/shard_map/ppermute | solution.py:231
  119.3 10.9 %collective-permute-start.3 = (bf16[2,256,128]{2,1,0:T(8,128)(2,1)S(1)}, bf16[2,256,128]{2,1,0:T(8,128)(2,1)S(1)}, u32[]{:S(2)}, u32[]{:S(2)}) collective-permute-start(bf16[2,256,128]{2,1,0:T(8,128)(2,1)S(1)} %fusion), channel_id=1, source_target_pairs={{0,256},{256,512},{512,0},{1,257},{257,513},{513,1},{2,258},{258,5... | collective-permute-start | bytes 393224 | tf_op jit(solution)/shard_map/ppermute | solution.py:231
  122.6 10.8 %collective-permute-start.4 = (bf16[2,256,128]{2,1,0:T(8,128)(2,1)S(1)}, bf16[2,256,128]{2,1,0:T(8,128)(2,1)S(1)}, u32[]{:S(2)}, u32[]{:S(2)}) collective-permute-start(bf16[2,256,128]{2,1,0:T(8,128)(2,1)S(1)} %fusion), channel_id=1, source_target_pairs={{0,512},{256,0},{512,256},{1,513},{257,1},{513,257},{2,514},{258,2... | collective-permute-start | bytes 393224 | tf_op jit(solution)/shard_map/ppermute | solution.py:231
  133.5 0.7 copy-start.7
  145.8 1.2 copy-start.1
  147.6 8.2 %all-to-all-start.4 = ((f32[3,8,384]{2,1,0:T(8,128)}), f32[3,8,384]{2,1,0:T(8,128)S(1)}, u32[]{:S(2)}, u32[]{:S(2)}) async-start(f32[3,8,384]{2,1,0:T(8,128)} %broadcast_in_dim.65), calls=%async_computation.4 | async-start | bytes 73728 | tf_op jit(solution)/shard_map/all_to_all | solution.py:222
  152.1 1.4 copy-start.2
  154.8 0.9 copy-start.4
  155.8 1.4 copy-start.3
  157.2 1.1 copy-start.5
  206.0 13.2 %all-to-all-start.8 = ((f32[32,8,128]{2,1,0:T(8,128)}), f32[32,8,128]{2,1,0:T(8,128)S(1)}, u32[]{:S(2)}, u32[]{:S(2)}) async-start(f32[32,8,128]{2,1,0:T(8,128)} %broadcast_in_dim.68), calls=%async_computation.8 | async-start | bytes 262144 | tf_op jit(solution)/shard_map/all_to_all | solution.py:222

commit v5 on v4

--- a/solution.py
+++ b/solution.py
@@ -12,7 +12,7 @@
 eps = 1e-06
 T = 128
 ZL = 3
-FS = 96
+FS = 88
 f32 = jnp.float32
 bf16 = jnp.bfloat16
 NT = (((1,), (1,)), ((), ()))
@@ -172,15 +172,16 @@
 
 
 def grads_kernel(
-    coef, place_ref, n_ref, a_ref, w_ref, e_ref, sums_ref, tot_ref, mask_ref, loss_ref, grad_ref
+    coef, place_ref, n_ref, a_ref, w_ref, e_ref, sums_ref, mask_ref, *refs
 ):
+    *tot_refs, loss_ref, grad_ref = refs
     weight_t = w_ref[...]
     agg_n = [anchors_of(n_ref, place_ref[1], v) for v in range(2)]
     emb_n, rinv_n = zip(*[embed(weight_t, agg) for agg in agg_n])
     full_n = [emb.astype(bf16).astype(f32) for emb in emb_n]
     pos = jnp.sum(full_n[0] * full_n[1], 0, keepdims=True) * (1.0 / tau)
     own = jnp.exp(pos)
-    tot = [own + sum(tot_ref[z, v : v + 1, :] for z in range(ZL)) for v in range(2)]
+    tot = [own + sum(t[v : v + 1, :] for t in tot_refs) for v in range(2)]
     loss = 0.5 * ((jnp.log(tot[0]) - pos) + (jnp.log(tot[1]) - pos))
     loss_ref[...] = jnp.broadcast_to(loss, loss_ref.shape)
     inverse = [1.0 / t for t in tot]
@@ -273,9 +274,13 @@
     turned = jnp.pad(features.T, ((0, pad), (0, 0))).reshape(ZL, 1, FS, nodes)
     sent = jnp.broadcast_to(turned, (ZL, zsize, FS, nodes)).reshape(ZL * zsize, FS, nodes)
     near = swap(sent, ("zl", "zh"))
-    all_tiles = around(packed(tiles, tile_pos, edge_keep, cols), whole, "zl")
+    held = packed(tiles, tile_pos, edge_keep, cols)
+    next_tiles = shift(held, "zl", 1)
+    near, next_tiles = lax.optimization_barrier((near, next_tiles))
     own = share(near, "x")
-    own, all_tiles = lax.optimization_barrier((own, all_tiles))
+    last_tiles = shift(held, "zl", 2)
+    own, last_tiles = lax.optimization_barrier((own, last_tiles))
+    all_tiles = [held, next_tiles, last_tiles]
     other = shift(own, "core", 1)
     metas = jnp.stack([x[slots * T : slots * T + 4, :slots] for x in all_tiles]).astype(jnp.int32)
 
@@ -307,7 +312,7 @@
         1,
         "scores",
     )(place, anchors, members, weight_t, counts)
-    tots = share(tot, "zl")
+    tots = around(tot, whole, "zl")
     sums = group_call(
         pull_kernel, jax.ShapeDtypeStruct((2, width, group), f32), 2, 0, "pull"
     )(terms, low)
@@ -317,10 +322,10 @@
     loss, grad = group_call(
         functools.partial(grads_kernel, coef),
         (rows, jax.ShapeDtypeStruct((width, width), f32)),
-        8,
+        7 + ZL,
         1,
         "grads",
-    )(place, anchors, members, weight_t, terms, sums, tots, mask)
+    )(place, anchors, members, weight_t, terms, sums, mask, *tots)
     node_loss = lax.dynamic_slice_in_dim(loss[0], zl * nodes, nodes)
     return node_loss, reduce_all(grad)
 

time: 229 us -> 222 us (0.969)
  local copies, waits for them, and re-layouts: 13.7 us -> 6.29 us
  starting transfers between devices: 65.9 us -> 69.2 us
    all_to_all x6 -> x5, waiting for transfers between devices: 40 us -> 29.7 us  [swap(): return lax.all_to_all(x, axis, 0, 0, tiled=True)]
    ppermute x7 -> x9, waiting for transfers between devices: 25.6 us -> 35.7 us  [shift(): return lax.ppermute(x, axis, [(i, (i + by) % size) for i in range(size)])]
    ppermute x7 -> x9, starting transfers between devices: 22.7 us -> 30.9 us  [shift(): return lax.ppermute(x, axis, [(i, (i + by) % size) for i in range(size)])]
    unnamed x26 -> x14, local copies, waits for them, and re-layouts: 7.76 us -> 1.12 us
    all_to_all x6 -> x5, starting transfers between devices: 43.1 us -> 38.3 us  [swap(): return lax.all_to_all(x, axis, 0, 0, tiled=True)]
  transfers between devices with their start and end apart: 13 -> 14, of which waited for: 10 -> 10; matrix products, arithmetic and copies ran while one was open for 1% -> 0% of each run, Pallas kernels for 7% -> 8%
where the time goes in v5:
time: 222 us; the launch traced here: 221 us
  starting transfers between devices  69.2 us (31%)
  waiting for transfers between devices  65.5 us (30%)
  blocking collectives  48.1 us (22%)
  Pallas kernels  30.6 us (14%)
  local copies, waits for them, and re-layouts  6.29 us (3%)
    all_to_all x4, blocking collectives, swap(): return lax.all_to_all(x, axis, 0, 0, tiled=True)  48.1 us
    all_to_all x5, starting transfers between devices, swap(): return lax.all_to_all(x, axis, 0, 0, tiled=True)  38.3 us
    ppermute x9, waiting for transfers between devices, shift(): return lax.ppermute(x, axis, [(i, (i + by) % size) for i in range(size)])  35.7 us
    ppermute x9, starting transfers between devices, shift(): return lax.ppermute(x, axis, [(i, (i + by) % size) for i in range(size)])  30.9 us
    all_to_all x5, waiting for transfers between devices, swap(): return lax.all_to_all(x, axis, 0, 0, tiled=True)  29.7 us
    pallas_call x1, Pallas kernels, count_negatives(): pl.pallas_call(functools.partial(counts_kernel, blocks), out_shape=jax.Sh...  15.8 us
    pallas_call x1, Pallas kernels, shards(): group_call(functools.partial(grads_kernel, coef), (rows, jax.ShapeDtypeSt...  6.01 us
    pallas_call x1, Pallas kernels, shards(): group_call(scores_kernel, (rows, jax.ShapeDtypeStruct((ysize // 2, 2, 2 *...  4.58 us
  transfers between devices with their start and end apart: 14, of which 10 were waited for; matrix products, arithmetic and copies ran while one was open for 0% of the time, Pallas kernels for 8%

profile of v5, /device:TPU:1, one launch (start us, length us, event | category | flops | bytes accessed | tf_op | source)
XLA Modules:
  0.0 221.3 jit_solution(122365709043505670)
XLA Ops:
  2.4 15.7 %all-to-all-start = ((bf16[12,88,128]{2,1,0:T(8,128)(2,1)}), bf16[12,88,128]{2,1,0:T(8,128)(2,1)S(1)}, u32[]{:S(2)}, u32[]{:S(2)}) async-start(bf16[12,88,128]{2,1,0:T(8,128)(2,1)} %bitcast.7), calls=%async_computation | async-start | bytes 540672 | tf_op jit(solution)/shard_map/all_to_all | solution.py:223
  18.3 3.3 %collective-permute-start = (bf16[1552,128]{1,0:T(8,128)(2,1)S(1)}, bf16[1552,128]{1,0:T(8,128)(2,1)S(1)}, u32[]{:S(2)}, u32[]{:S(2)}) collective-permute-start(bf16[1552,128]{1,0:T(8,128)(2,1)S(1)} %pad_maximum_fusion.refs_0_), channel_id=1, source_target_pairs={{0,256},{256,512},{512,0},{1,257},{257,513},{513,1},{2,258},{258,5... | collective-permute-start | bytes 1191944 | tf_op jit(solution)/shard_map/ppermute | solution.py:232
  21.6 16.3 %collective-permute-done.refs_1_ = bf16[1552,128]{1,0:T(8,128)(2,1)S(1)} collective-permute-done((bf16[1552,128]{1,0:T(8,128)(2,1)S(1)}, bf16[1552,128]{1,0:T(8,128)(2,1)S(1)}, u32[]{:S(2)}, u32[]{:S(2)}) %collective-permute-start) | collective-permute-done | bytes 397344 | tf_op jit(solution)/shard_map/ppermute | solution.py:232
  39.1 4.0 %all-to-all-start.1 = ((bf16[4,12,88,128]{3,2,1,0:T(8,128)(2,1)}), bf16[4,12,88,128]{3,2,1,0:T(8,128)(2,1)S(1)}, u32[]{:S(2)}, u32[]{:S(2)}) async-start(bf16[4,12,88,128]{3,2,1,0:T(8,128)(2,1)} %broadcast_in_dim.57), calls=%async_computation.1 | async-start | bytes 2162688 | tf_op jit(solution)/shard_map/all_to_all | solution.py:223
  43.1 2.8 %collective-permute-start.1 = (bf16[1552,128]{1,0:T(8,128)(2,1)S(1)}, bf16[1552,128]{1,0:T(8,128)(2,1)S(1)}, u32[]{:S(2)}, u32[]{:S(2)}) collective-permute-start(bf16[1552,128]{1,0:T(8,128)(2,1)S(1)} %pad_maximum_fusion.refs_0_), channel_id=1, source_target_pairs={{0,512},{256,0},{512,256},{1,513},{257,1},{513,257},{2,514},{258,2... | collective-permute-start | bytes 1191944 | tf_op jit(solution)/shard_map/ppermute | solution.py:232
  45.9 7.9 %collective-permute-done.1.refs_2_ = bf16[1552,128]{1,0:T(8,128)(2,1)S(1)} collective-permute-done((bf16[1552,128]{1,0:T(8,128)(2,1)S(1)}, bf16[1552,128]{1,0:T(8,128)(2,1)S(1)}, u32[]{:S(2)}, u32[]{:S(2)}) %collective-permute-start.1) | collective-permute-done | bytes 397344 | tf_op jit(solution)/shard_map/ppermute | solution.py:232
  53.8 2.9 %all-to-all-done.1.own_ref = bf16[4,12,88,128]{3,2,1,0:T(8,128)(2,1)S(1)} async-done(((bf16[4,12,88,128]{3,2,1,0:T(8,128)(2,1)}), bf16[4,12,88,128]{3,2,1,0:T(8,128)(2,1)S(1)}, u32[]{:S(2)}, u32[]{:S(2)}) %all-to-all-start.1) | async-done | bytes 1081376 | tf_op jit(solution)/shard_map/all_to_all | solution.py:223
  56.7 4.7 %collective-permute-start.2 = (bf16[4,12,88,128]{3,2,1,0:T(8,128)(2,1)S(1)}, bf16[4,12,88,128]{3,2,1,0:T(8,128)(2,1)S(1)}, u32[]{:S(2)}, u32[]{:S(2)}) collective-permute-start(bf16[4,12,88,128]{3,2,1,0:T(8,128)(2,1)S(1)} %all-to-all-done.1.own_ref), channel_id=1, source_target_pairs={{0,1},{1,0},{2,3},{3,2},{4,5},{5,4},{6,7},{7,6},{8,9},{9,8},{10,11... | collective-permute-start | bytes 3244040 | tf_op jit(solution)/shard_map/ppermute | solution.py:232
  61.5 2.2 collective-permute-done.2.other_ref
  63.7 3.0 %tile_sums.1 = bf16[24,2,88,128]{3,2,1,0:T(8,128)(2,1)} custom-call(s32[3,4,12]{2,1,0:T(4,128)S(1)} %maximum_convert_fusion.meta_ref, s32[2]{0:T(128)S(1)} %pad_add_fusion.1.place_ref, bf16[4,12,88,128]{3,2,1,0:T(8,128)(2,1)S(1)} %all-to-all-done.1.own_ref, bf16[4,12,88,128]{3,2,1,0:T(8,128)(2,1)S(1)} %collective-permute-done.2.other_ref, ...), custom_call_target="tpu_custom_call" | custom-call | tf_op jit(solution)/shard_map/tile_sums/pallas_call | solution.py:105
  66.7 8.7 %all-to-all-start.2 = ((bf16[24,2,88,128]{3,2,1,0:T(8,128)(2,1)}), bf16[24,2,88,128]{3,2,1,0:T(8,128)(2,1)S(1)}, u32[]{:S(2)}, u32[]{:S(2)}) async-start(bf16[24,2,88,128]{3,2,1,0:T(8,128)(2,1)} %tile_sums.1), calls=%async_computation.2 | async-start | bytes 2162688 | tf_op jit(solution)/shard_map/all_to_all | solution.py:223
  75.5 15.8 %counts.1 = s16[24,128,128]{2,1,0:T(8,128)(2,1)S(1)} custom-call(s32[128,1024]{1,0:T(8,128)S(1)} %copy-done), custom_call_target="tpu_custom_call" | custom-call | flops 4294967296 | bytes 2097152 | tf_op jit(solution)/shard_map/counts/pallas_call | solution.py:60
  91.3 10.4 %all-to-all-done.2 = bf16[24,2,88,128]{3,2,1,0:T(8,128)(2,1)S(1)} async-done(((bf16[24,2,88,128]{3,2,1,0:T(8,128)(2,1)}), bf16[24,2,88,128]{3,2,1,0:T(8,128)(2,1)S(1)}, u32[]{:S(2)}, u32[]{:S(2)}) %all-to-all-start.2) | async-done | bytes 1081376 | tf_op jit(solution)/shard_map/all_to_all | solution.py:223
  103.2 5.9 %all-to-all-start.3 = ((bf16[8,2,256,128]{3,2,1,0:T(8,128)(2,1)}), bf16[8,2,256,128]{3,2,1,0:T(8,128)(2,1)S(1)}, u32[]{:S(2)}, u32[]{:S(2)}) async-start(bf16[8,2,256,128]{3,2,1,0:T(8,128)(2,1)} %broadcast_in_dim.58), calls=%async_computation.3 | async-start | bytes 2097152 | tf_op jit(solution)/shard_map/all_to_all | solution.py:223
  109.2 5.0 %collective-permute-start.5 = (s16[8,128,128]{2,1,0:T(8,128)(2,1)S(1)}, s16[8,128,128]{2,1,0:T(8,128)(2,1)S(1)}, u32[]{:S(2)}, u32[]{:S(2)}) collective-permute-start(s16[8,128,128]{2,1,0:T(8,128)(2,1)S(1)} %get-tuple-element.36), channel_id=1, source_target_pairs={{0,256},{256,512},{512,0},{1,257},{257,513},{513,1},{2,258},{258,5... | collective-permute-start | bytes 786440 | tf_op jit(solution)/shard_map/ppermute | solution.py:232
  114.3 1.9 collective-permute-start.6
  116.2 3.4 %collective-permute-start.3 = (bf16[2,256,128]{2,1,0:T(8,128)(2,1)S(1)}, bf16[2,256,128]{2,1,0:T(8,128)(2,1)S(1)}, u32[]{:S(2)}, u32[]{:S(2)}) collective-permute-start(bf16[2,256,128]{2,1,0:T(8,128)(2,1)S(1)} %fusion), channel_id=1, source_target_pairs={{0,256},{256,512},{512,0},{1,257},{257,513},{513,1},{2,258},{258,5... | collective-permute-start | bytes 393224 | tf_op jit(solution)/shard_map/ppermute | solution.py:232
  119.6 2.8 %collective-permute-start.4 = (bf16[2,256,128]{2,1,0:T(8,128)(2,1)S(1)}, bf16[2,256,128]{2,1,0:T(8,128)(2,1)S(1)}, u32[]{:S(2)}, u32[]{:S(2)}) collective-permute-start(bf16[2,256,128]{2,1,0:T(8,128)(2,1)S(1)} %fusion), channel_id=1, source_target_pairs={{0,512},{256,0},{512,256},{1,513},{257,1},{513,257},{2,514},{258,2... | collective-permute-start | bytes 393224 | tf_op jit(solution)/shard_map/ppermute | solution.py:232
  122.6 4.6 %collective-permute-done.3 = bf16[2,256,128]{2,1,0:T(8,128)(2,1)S(1)} collective-permute-done((bf16[2,256,128]{2,1,0:T(8,128)(2,1)S(1)}, bf16[2,256,128]{2,1,0:T(8,128)(2,1)S(1)}, u32[]{:S(2)}, u32[]{:S(2)}) %collective-permute-start.3) | collective-permute-done | bytes 131104 | tf_op jit(solution)/shard_map/ppermute | solution.py:232
  127.1 3.4 %collective-permute-done.4 = bf16[2,256,128]{2,1,0:T(8,128)(2,1)S(1)} collective-permute-done((bf16[2,256,128]{2,1,0:T(8,128)(2,1)S(1)}, bf16[2,256,128]{2,1,0:T(8,128)(2,1)S(1)}, u32[]{:S(2)}, u32[]{:S(2)}) %collective-permute-start.4) | collective-permute-done | bytes 131104 | tf_op jit(solution)/shard_map/ppermute | solution.py:232
  130.7 7.6 %all-to-all-done.3.a_ref = bf16[8,2,256,128]{3,2,1,0:T(8,128)(2,1)S(1)} async-done(((bf16[8,2,256,128]{3,2,1,0:T(8,128)(2,1)}), bf16[8,2,256,128]{3,2,1,0:T(8,128)(2,1)S(1)}, u32[]{:S(2)}, u32[]{:S(2)}) %all-to-all-start.3) | async-done | bytes 1048608 | tf_op jit(solution)/shard_map/all_to_all | solution.py:223
  138.3 4.6 %scores.1 = (f32[8,384]{1,0:T(8,128)S(1)}, bf16[4,2,256,384]{3,2,1,0:T(8,128)(2,1)S(1)}, bf16[4,2,256,256]{3,2,1,0:T(8,128)(2,1)S(1)}) custom-call(s32[2]{0:T(128)S(1)} %pad_add_fusion.1.place_ref, bf16[3,2,256,128]{3,2,1,0:T(8,128)(2,1)S(1)} %pad_maximum_fusion.1.n_ref, bf16[8,2,256,128]{3,2,1,0:T(8,128)(2,1)S(1)} %all-to-all-done.3.a_ref, ...), custom_call_target="tpu_custom_call" | custom-call | flops 2147483648 | bytes 4194304 | tf_op jit(solution)/shard_map/scores/pallas_call | solution.py:304
  142.9 5.0 %collective-permute-start.7 = (f32[8,384]{1,0:T(8,128)S(1)}, f32[8,384]{1,0:T(8,128)S(1)}, u32[]{:S(2)}, u32[]{:S(2)}) collective-permute-start(f32[8,384]{1,0:T(8,128)S(1)} %get-tuple-element.29.refs_0_), channel_id=1, source_target_pairs={{0,256},{256,512},{512,0},{1,257},{257,513},{513,1},{2,258},{258,5... | collective-permute-start | bytes 36872 | tf_op jit(solution)/shard_map/ppermute | solution.py:232
  147.9 1.9 collective-permute-start.8
  151.1 1.3 collective-permute-done.8.refs_2_
  152.4 6.0 %grads.1 = (f32[8,384]{1,0:T(8,128)S(1)}, f32[256,256]{1,0:T(8,128)S(1)}) custom-call(s32[2]{0:T(128)S(1)} %pad_add_fusion.1.place_ref, bf16[3,2,256,128]{3,2,1,0:T(8,128)(2,1)S(1)} %pad_maximum_fusion.1.n_ref, bf16[8,2,256,128]{3,2,1,0:T(8,128)(2,1)S(1)} %all-to-all-done.3.a_ref, bf16[256,256]{1,0:T(8,128)(2,1)S(1)} %bitcast.39, ...), custom_call_target="tpu_custom_call" | custom-call | flops 2147483648 | bytes 4194304 | tf_op jit(solution)/shard_map/grads/pallas_call | solution.py:322
  158.4 5.5 %all_to_all.45 = f32[2,256,128]{2,1,0:T(8,128)S(1)} all-to-all(f32[2,256,128]{2,1,0:T(8,128)S(1)} %reshape_reshape.6), channel_id=1, replica_groups=mesh['zl'=3,'y'=8,'x'=4,'zh'=4,'core'=2] {'core'}, dimensions={0} | all-to-all | bytes 524288 | tf_op jit(solution)/shard_map/all_to_all | solution.py:223
  164.0 12.6 %all_to_all.46 = f32[32,8,128]{2,1,0:T(8,128)S(1)} all-to-all(f32[32,8,128]{2,1,0:T(8,128)S(1)} %bitcast.45), channel_id=1, replica_groups=mesh['zl'=3,'y'=8,'x'=4,'zh'=4,'core'=2] {'y','x'}, dimensions={0} | all-to-all | bytes 262144 | tf_op jit(solution)/shard_map/all_to_all | solution.py:223
  176.6 21.7 %all_to_all.47 = f32[12,8,128]{2,1,0:T(8,128)S(1)} all-to-all(f32[12,8,128]{2,1,0:T(8,128)S(1)} %broadcast_in_dim.60), channel_id=1, replica_groups=mesh['zl'=3,'y'=8,'x'=4,'zh'=4,'core'=2] {'zl','zh'}, dimensions={0} | all-to-all | bytes 98304 | tf_op jit(solution)/shard_map/all_to_all | solution.py:223
  199.0 3.9 %all-to-all-start.7 = ((f32[32,8,128]{2,1,0:T(8,128)}), f32[32,8,128]{2,1,0:T(8,128)S(1)}, u32[]{:S(2)}, u32[]{:S(2)}) async-start(f32[32,8,128]{2,1,0:T(8,128)} %broadcast_in_dim.61), calls=%async_computation.7 | async-start | bytes 262144 | tf_op jit(solution)/shard_map/all_to_all | solution.py:223
  203.4 8.8 %all-to-all-done.7 = f32[32,8,128]{2,1,0:T(8,128)S(1)} async-done(((f32[32,8,128]{2,1,0:T(8,128)}), f32[32,8,128]{2,1,0:T(8,128)S(1)}, u32[]{:S(2)}, u32[]{:S(2)}) %all-to-all-start.7) | async-done | bytes 131104 | tf_op jit(solution)/shard_map/all_to_all | solution.py:223
  212.2 8.3 %all_to_all.48 = f32[2,256,128]{2,1,0:T(8,128)S(1)} all-to-all(f32[2,256,128]{2,1,0:T(8,128)S(1)} %broadcast_in_dim.63), channel_id=1, replica_groups=mesh['zl'=3,'y'=8,'x'=4,'zh'=4,'core'=2] {'core'}, dimensions={0} | all-to-all | bytes 524288 | tf_op jit(solution)/shard_map/all_to_all | solution.py:223
  (52 shorter events, 8.1 us)
Async XLA Ops:
  0.6 17.5 %copy-start.4 = (s32[12]{0:T(128)S(1)}, s32[12]{0:T(128)}, u32[]{:S(2)}) copy-start(s32[12]{0:T(128)} %param.10) | copy-start | bytes 148
  0.6 17.5 %copy-start.5 = (s32[2,12]{1,0:T(2,128)S(1)}, s32[2,12]{1,0:T(2,128)}, u32[]{:S(2)}) copy-start(s32[2,12]{1,0:T(2,128)} %param.11) | copy-start | bytes 292
  0.7 17.6 %copy-start.1 = (bf16[12,128,128]{2,1,0:T(8,128)(2,1)S(1)}, bf16[12,128,128]{2,1,0:T(8,128)(2,1)}, u32[]{:S(2)}) copy-start(bf16[12,128,128]{2,1,0:T(8,128)(2,1)} %param.9) | copy-start | bytes 1179652
  2.4 35.5 %all-to-all-start = ((bf16[12,88,128]{2,1,0:T(8,128)(2,1)}), bf16[12,88,128]{2,1,0:T(8,128)(2,1)S(1)}, u32[]{:S(2)}, u32[]{:S(2)}) async-start(bf16[12,88,128]{2,1,0:T(8,128)(2,1)} %bitcast.7), calls=%async_computation | async-start | bytes 540672 | tf_op jit(solution)/shard_map/all_to_all | solution.py:223
  18.3 19.7 %collective-permute-start = (bf16[1552,128]{1,0:T(8,128)(2,1)S(1)}, bf16[1552,128]{1,0:T(8,128)(2,1)S(1)}, u32[]{:S(2)}, u32[]{:S(2)}) collective-permute-start(bf16[1552,128]{1,0:T(8,128)(2,1)S(1)} %pad_maximum_fusion.refs_0_), channel_id=1, source_target_pairs={{0,256},{256,512},{512,0},{1,257},{257,513},{513,1},{2,258},{258,5... | collective-permute-start | bytes 1191944 | tf_op jit(solution)/shard_map/ppermute | solution.py:232
  39.1 17.6 %all-to-all-start.1 = ((bf16[4,12,88,128]{3,2,1,0:T(8,128)(2,1)}), bf16[4,12,88,128]{3,2,1,0:T(8,128)(2,1)S(1)}, u32[]{:S(2)}, u32[]{:S(2)}) async-start(bf16[4,12,88,128]{3,2,1,0:T(8,128)(2,1)} %broadcast_in_dim.57), calls=%async_computation.1 | async-start | bytes 2162688 | tf_op jit(solution)/shard_map/all_to_all | solution.py:223
  43.1 10.7 %collective-permute-start.1 = (bf16[1552,128]{1,0:T(8,128)(2,1)S(1)}, bf16[1552,128]{1,0:T(8,128)(2,1)S(1)}, u32[]{:S(2)}, u32[]{:S(2)}) collective-permute-start(bf16[1552,128]{1,0:T(8,128)(2,1)S(1)} %pad_maximum_fusion.refs_0_), channel_id=1, source_target_pairs={{0,512},{256,0},{512,256},{1,513},{257,1},{513,257},{2,514},{258,2... | collective-permute-start | bytes 1191944 | tf_op jit(solution)/shard_map/ppermute | solution.py:232
  56.7 7.0 %collective-permute-start.2 = (bf16[4,12,88,128]{3,2,1,0:T(8,128)(2,1)S(1)}, bf16[4,12,88,128]{3,2,1,0:T(8,128)(2,1)S(1)}, u32[]{:S(2)}, u32[]{:S(2)}) collective-permute-start(bf16[4,12,88,128]{3,2,1,0:T(8,128)(2,1)S(1)} %all-to-all-done.1.own_ref), channel_id=1, source_target_pairs={{0,1},{1,0},{2,3},{3,2},{4,5},{5,4},{6,7},{7,6},{8,9},{9,8},{10,11... | collective-permute-start | bytes 3244040 | tf_op jit(solution)/shard_map/ppermute | solution.py:232
  66.7 8.7 %copy-start.3 = (s32[2,256]{1,0:T(2,128)S(1)}, s32[2,256]{1,0:T(2,128)}, u32[]{:S(2)}) copy-start(s32[2,256]{1,0:T(2,128)} %param.12) | copy-start | bytes 6148
  66.7 8.8 %copy-start = (s32[128,1024]{1,0:T(8,128)S(1)}, s32[128,1024]{1,0:T(8,128)}, u32[]{:S(2)}) copy-start(s32[128,1024]{1,0:T(8,128)} %neg_ref) | copy-start | bytes 1572868
  66.7 35.0 %all-to-all-start.2 = ((bf16[24,2,88,128]{3,2,1,0:T(8,128)(2,1)}), bf16[24,2,88,128]{3,2,1,0:T(8,128)(2,1)S(1)}, u32[]{:S(2)}, u32[]{:S(2)}) async-start(bf16[24,2,88,128]{3,2,1,0:T(8,128)(2,1)} %tile_sums.1), calls=%async_computation.2 | async-start | bytes 2162688 | tf_op jit(solution)/shard_map/all_to_all | solution.py:223
  103.2 35.1 %all-to-all-start.3 = ((bf16[8,2,256,128]{3,2,1,0:T(8,128)(2,1)}), bf16[8,2,256,128]{3,2,1,0:T(8,128)(2,1)S(1)}, u32[]{:S(2)}, u32[]{:S(2)}) async-start(bf16[8,2,256,128]{3,2,1,0:T(8,128)(2,1)} %broadcast_in_dim.58), calls=%async_computation.3 | async-start | bytes 2097152 | tf_op jit(solution)/shard_map/all_to_all | solution.py:223
  109.1 13.3 %copy-start.2 = (bf16[256,256]{1,0:T(8,128)(2,1)S(1)}, bf16[256,256]{1,0:T(8,128)(2,1)}, u32[]{:S(2)}) copy-start(bf16[256,256]{1,0:T(8,128)(2,1)} %param.8) | copy-start | bytes 393220
  109.2 21.4 %collective-permute-start.5 = (s16[8,128,128]{2,1,0:T(8,128)(2,1)S(1)}, s16[8,128,128]{2,1,0:T(8,128)(2,1)S(1)}, u32[]{:S(2)}, u32[]{:S(2)}) collective-permute-start(s16[8,128,128]{2,1,0:T(8,128)(2,1)S(1)} %get-tuple-element.36), channel_id=1, source_target_pairs={{0,256},{256,512},{512,0},{1,257},{257,513},{513,1},{2,258},{258,5... | collective-permute-start | bytes 786440 | tf_op jit(solution)/shard_map/ppermute | solution.py:232
  114.3 16.3 %collective-permute-start.6 = (s16[8,128,128]{2,1,0:T(8,128)(2,1)S(1)}, s16[8,128,128]{2,1,0:T(8,128)(2,1)S(1)}, u32[]{:S(2)}, u32[]{:S(2)}) collective-permute-start(s16[8,128,128]{2,1,0:T(8,128)(2,1)S(1)} %get-tuple-element.35), channel_id=1, source_target_pairs={{0,512},{256,0},{512,256},{1,513},{257,1},{513,257},{2,514},{258,2... | collective-permute-start | bytes 786440 | tf_op jit(solution)/shard_map/ppermute | solution.py:232
  116.2 10.9 %collective-permute-start.3 = (bf16[2,256,128]{2,1,0:T(8,128)(2,1)S(1)}, bf16[2,256,128]{2,1,0:T(8,128)(2,1)S(1)}, u32[]{:S(2)}, u32[]{:S(2)}) collective-permute-start(bf16[2,256,128]{2,1,0:T(8,128)(2,1)S(1)} %fusion), channel_id=1, source_target_pairs={{0,256},{256,512},{512,0},{1,257},{257,513},{513,1},{2,258},{258,5... | collective-permute-start | bytes 393224 | tf_op jit(solution)/shard_map/ppermute | solution.py:232
  119.6 11.0 %collective-permute-start.4 = (bf16[2,256,128]{2,1,0:T(8,128)(2,1)S(1)}, bf16[2,256,128]{2,1,0:T(8,128)(2,1)S(1)}, u32[]{:S(2)}, u32[]{:S(2)}) collective-permute-start(bf16[2,256,128]{2,1,0:T(8,128)(2,1)S(1)} %fusion), channel_id=1, source_target_pairs={{0,512},{256,0},{512,256},{1,513},{257,1},{513,257},{2,514},{258,2... | collective-permute-start | bytes 393224 | tf_op jit(solution)/shard_map/ppermute | solution.py:232
  142.9 8.2 %collective-permute-start.7 = (f32[8,384]{1,0:T(8,128)S(1)}, f32[8,384]{1,0:T(8,128)S(1)}, u32[]{:S(2)}, u32[]{:S(2)}) collective-permute-start(f32[8,384]{1,0:T(8,128)S(1)} %get-tuple-element.29.refs_0_), channel_id=1, source_target_pairs={{0,256},{256,512},{512,0},{1,257},{257,513},{513,1},{2,258},{258,5... | collective-permute-start | bytes 36872 | tf_op jit(solution)/shard_map/ppermute | solution.py:232
  147.9 4.4 %collective-permute-start.8 = (f32[8,384]{1,0:T(8,128)S(1)}, f32[8,384]{1,0:T(8,128)S(1)}, u32[]{:S(2)}, u32[]{:S(2)}) collective-permute-start(f32[8,384]{1,0:T(8,128)S(1)} %get-tuple-element.29.refs_0_), channel_id=1, source_target_pairs={{0,512},{256,0},{512,256},{1,513},{257,1},{513,257},{2,514},{258,2... | collective-permute-start | bytes 36872 | tf_op jit(solution)/shard_map/ppermute | solution.py:232
  199.0 13.2 %all-to-all-start.7 = ((f32[32,8,128]{2,1,0:T(8,128)}), f32[32,8,128]{2,1,0:T(8,128)S(1)}, u32[]{:S(2)}, u32[]{:S(2)}) async-start(f32[32,8,128]{2,1,0:T(8,128)} %broadcast_in_dim.61), calls=%async_computation.7 | async-start | bytes 262144 | tf_op jit(solution)/shard_map/all_to_all | solution.py:223

commit v6 on v5

--- a/solution.py
+++ b/solution.py
@@ -12,12 +12,15 @@
 eps = 1e-06
 T = 128
 ZL = 3
+YQ = 4
 FS = 88
 f32 = jnp.float32
 bf16 = jnp.bfloat16
 NT = (((1,), (1,)), ((), ()))
 NN = (((1,), (0,)), ((), ()))
-ROW = ("zl", "y")
+Y = ("yq", "yp")
+ROW = ("zl",) + Y
+MEMBERS = ("zl", "yp")
 COL = ("x", "zh", "core")
 PARAMS = dict(vmem_limit_bytes=24 * 1024 * 1024)
 
@@ -37,11 +40,17 @@
         index = neg_ref[pl.ds(base, 8), :]
         low = index & (T - 1)
         high = index >> 7
-        for j in range(8):
-            low_hot = jnp.where(low[j : j + 1, :] == low_iota, 1.0, 0.0).astype(bf16)
-            high_hot = jnp.where(high[j : j + 1, :] == high_iota, 1.0, 0.0).astype(bf16)
+        for j in range(0, 8, 2):
+            low_hot, high_hot = (
+                jnp.concatenate(
+                    [jnp.where(part[j + i : j + i + 1, :] == iota, 1.0, 0.0) for i in range(2)], 0
+                ).astype(bf16)
+                for part, iota in ((low, low_iota), (high, high_iota))
+            )
             found = dot(high_hot, low_hot, NT)
-            acc_ref[pl.ds(base + j, rows, stride=nodes), :] = found
+            for i in range(2):
+                own = found[i * rows : (i + 1) * rows, i * T : (i + 1) * T]
+                acc_ref[pl.ds(base + j + i, rows, stride=nodes), :] = own
         return carry
 
     lax.fori_loop(0, nodes // 8, step, 0)
@@ -69,34 +78,43 @@
     )(negatives)
 
 
-def behind(place, s):
-    return lax.rem(place + ZL - s, ZL)
+def behind(place, s, size):
+    return lax.rem(place + size - s, size)
 
 
 def tiles_kernel(cols, meta_ref, place_ref, own_ref, other_ref, *refs):
     tile_refs, (out_ref, acc_ref) = refs[:ZL], refs[ZL:]
     zsize = own_ref.shape[1] // ZL
+    slots = meta_ref.shape[2]
     acc_ref[...] = jnp.zeros_like(acc_ref)
     core, zl = place_ref[0], place_ref[1]
     for s in range(ZL):
 
-        def slot(k, carry, s=s):
-            trow, tcol = meta_ref[s, 0, k], meta_ref[s, 1, k]
-
-            @pl.when(trow >= 0)
+        def few(i, carry, s=s):
+            @pl.when(meta_ref[s, 0, i * 4] >= 0)
             def _():
-                chip = lax.div(tcol, 2)
-                at = lax.div(chip, zsize), behind(zl, s) * zsize + lax.rem(chip, zsize)
-                mine = lax.rem(tcol, 2) == core
-                rows = jnp.where(mine, own_ref[at], other_ref[at])
-                product = dot(rows, tile_refs[s][pl.ds(pl.multiple_of(k * T, T), T), :], NT)
-                for v in range(2):
-                    kept = meta_ref[s, 2 + v, k].astype(f32)
-                    acc_ref[trow, v] += kept * product
+                products = []
+                for j in range(4):
+                    k = i * 4 + j
+                    tcol = meta_ref[s, 1, k]
+                    chip = lax.div(tcol, 2)
+                    at = lax.div(chip, zsize), behind(zl, s, ZL) * zsize + lax.rem(chip, zsize)
+                    mine = lax.rem(tcol, 2) == core
+                    rows = jnp.where(mine, own_ref[at], other_ref[at])
+                    tile = tile_refs[s][pl.ds(pl.multiple_of(k * T, T), T), :]
+                    products.append(dot(rows, tile, NT))
+                for j in range(4):
+                    k = i * 4 + j
+                    trow = meta_ref[s, 0, k]
+                    held = jnp.where(trow >= 0, 1, 0)
+                    at = jnp.maximum(trow, 0)
+                    for v in range(2):
+                        kept = (held * meta_ref[s, 2 + v, k]).astype(f32)
+                        acc_ref[at, v] += kept * products[j]
 
             return carry
 
-        lax.fori_loop(0, meta_ref.shape[2], slot, 0)
+        lax.fori_loop(0, slots // 4, few, 0)
     out_ref[...] = acc_ref[...].astype(bf16)
 
 
@@ -113,8 +131,8 @@
     )(meta, place, own, other, *tiles)
 
 
-def anchors_of(n_ref, zl, v):
-    return jnp.concatenate([n_ref[behind(zl, z), v] for z in range(ZL)], 1)
+def anchors_of(n_ref, yq, v):
+    return jnp.concatenate([n_ref[behind(yq, q, YQ), v] for q in range(YQ)], 1)
 
 
 def embed(weight_t, agg):
@@ -129,14 +147,14 @@
 
 def scores_kernel(place_ref, n_ref, a_ref, w_ref, c_ref, tot_ref, e_ref, low_ref):
     weight_t = w_ref[...]
-    zl = place_ref[1]
-    anchors = [embed(weight_t, anchors_of(n_ref, zl, v))[0].astype(bf16) for v in range(2)]
+    yq = place_ref[2]
+    anchors = [embed(weight_t, anchors_of(n_ref, yq, v))[0].astype(bf16) for v in range(2)]
     tot_ref[...] = jnp.zeros_like(tot_ref)
 
     def pair(p, carry):
         count = jnp.concatenate(
             [
-                jnp.concatenate([c_ref[behind(zl, z), 2 * p + i] for z in range(ZL)], 1)
+                jnp.concatenate([c_ref[behind(yq, q, YQ), 2 * p + i] for q in range(YQ)], 1)
                 for i in range(2)
             ],
             0,
@@ -176,7 +194,7 @@
 ):
     *tot_refs, loss_ref, grad_ref = refs
     weight_t = w_ref[...]
-    agg_n = [anchors_of(n_ref, place_ref[1], v) for v in range(2)]
+    agg_n = [anchors_of(n_ref, place_ref[2], v) for v in range(2)]
     emb_n, rinv_n = zip(*[embed(weight_t, agg) for agg in agg_n])
     full_n = [emb.astype(bf16).astype(f32) for emb in emb_n]
     pos = jnp.sum(full_n[0] * full_n[1], 0, keepdims=True) * (1.0 / tau)
@@ -238,7 +256,7 @@
 
 def reduce_all(grad):
     rows, width = grad.shape
-    planes = ("core",), ("y", "x")
+    planes = ("core",), Y + ("x",)
     part = grad.reshape(-1, T)
     for axes in planes:
         got = swap(part.reshape(lax.axis_size(axes), -1, T), axes)
@@ -263,10 +281,10 @@
     nodes, width = features.shape
     slots = tiles.shape[0]
     xsize, zsize = lax.axis_size("x"), lax.axis_size("zh")
-    ysize = lax.axis_size("y")
+    ysize, psize = lax.axis_size(Y), lax.axis_size("yp")
     cols = xsize * zsize * lax.axis_size("core")
-    zl = lax.axis_index("zl")
-    place = jnp.stack([lax.axis_index("core"), zl])
+    zl, yq = lax.axis_index("zl"), lax.axis_index("yq")
+    place = jnp.stack([lax.axis_index("core"), zl, yq])
     total = lax.axis_size(ROW) * cols * nodes
     pad = ZL * FS - width
     whole = lambda x, s: x
@@ -276,63 +294,63 @@
     near = swap(sent, ("zl", "zh"))
     held = packed(tiles, tile_pos, edge_keep, cols)
     next_tiles = shift(held, "zl", 1)
-    near, next_tiles = lax.optimization_barrier((near, next_tiles))
+    counts = count_negatives(negatives, ZL * ysize)
+    near, next_tiles, counts = lax.optimization_barrier((near, next_tiles, counts))
     own = share(near, "x")
     last_tiles = shift(held, "zl", 2)
-    own, last_tiles = lax.optimization_barrier((own, last_tiles))
+    counts = counts.reshape(ZL, YQ, psize, nodes, nodes)
+    ahead = lambda x, s: lax.dynamic_index_in_dim(x, lax.rem(yq + s, YQ), 1, keepdims=False)
+    counts = around(counts, ahead, "yq")
+    own, last_tiles, counts = lax.optimization_barrier((own, last_tiles, counts))
     all_tiles = [held, next_tiles, last_tiles]
     other = shift(own, "core", 1)
     metas = jnp.stack([x[slots * T : slots * T + 4, :slots] for x in all_tiles]).astype(jnp.int32)
 
     part = tile_sums(metas, place, own, other, all_tiles, cols, ZL * ysize)
-    part, negatives = lax.optimization_barrier((part, negatives))
+    part, counts = lax.optimization_barrier((part, counts))
     got = swap(part, ROW)
-    counts = count_negatives(negatives, ZL * ysize)
-    got, counts = lax.optimization_barrier((got, counts))
+    counts = jnp.stack(counts).reshape(YQ, ZL * psize, nodes, nodes)
     agg = jnp.sum(got.reshape(ZL, ysize, 2, FS, nodes).astype(f32), 1)
     agg = agg.transpose(1, 0, 2, 3).reshape(2, ZL * FS, nodes)[:, :width]
     agg = (agg * feature_keep.astype(f32)[:, :, None]).astype(bf16)
-    agg, counts = lax.optimization_barrier((agg, counts))
-    members = share(agg, "y")
-    anchors = jnp.stack(around(agg, whole, "zl"))
-    ahead = lambda x, s: lax.dynamic_index_in_dim(x, lax.rem(zl + s, ZL), 0, keepdims=False)
-    counts = jnp.stack(around(counts.reshape(ZL, ysize, nodes, nodes), ahead, "zl"))
+    members = share(agg, MEMBERS)
+    anchors = jnp.stack(around(agg, whole, "yq"))
 
     weight_t = weight.T
-    group = ZL * nodes
+    group, pairs = YQ * nodes, ZL * psize // 2
     rows = jax.ShapeDtypeStruct((8, group), f32)
     tot, terms, low = group_call(
         scores_kernel,
         (
             rows,
-            jax.ShapeDtypeStruct((ysize // 2, 2, 2 * nodes, group), bf16),
-            jax.ShapeDtypeStruct((ysize // 2, 2, width, 2 * nodes), bf16),
+            jax.ShapeDtypeStruct((pairs, 2, 2 * nodes, group), bf16),
+            jax.ShapeDtypeStruct((pairs, 2, width, 2 * nodes), bf16),
         ),
         5,
         1,
         "scores",
     )(place, anchors, members, weight_t, counts)
-    tots = around(tot, whole, "zl")
+    tots = around(tot, whole, "yq")
     sums = group_call(
         pull_kernel, jax.ShapeDtypeStruct((2, width, group), f32), 2, 0, "pull"
     )(terms, low)
-    mask = (jnp.arange(group) // nodes == zl).astype(f32)
+    mask = (jnp.arange(group) // nodes == yq).astype(f32)
     mask = jnp.broadcast_to(mask, (8, group))
     coef = 1.0 / (2.0 * tau * float(total) ** 0.5)
     loss, grad = group_call(
         functools.partial(grads_kernel, coef),
         (rows, jax.ShapeDtypeStruct((width, width), f32)),
-        7 + ZL,
+        7 + YQ,
         1,
         "grads",
     )(place, anchors, members, weight_t, terms, sums, mask, *tots)
-    node_loss = lax.dynamic_slice_in_dim(loss[0], zl * nodes, nodes)
+    node_loss = lax.dynamic_slice_in_dim(loss[0], yq * nodes, nodes)
     return node_loss, reduce_all(grad)
 
 
 def solution(mesh):
     rows, cols = mesh.devices.shape
-    fine = Mesh(mesh.devices.reshape(ZL, rows // ZL, cols // 8, 4, 2), ROW + COL)
+    fine = Mesh(mesh.devices.reshape(ZL, YQ, rows // (ZL * YQ), cols // 8, 4, 2), ROW + COL)
     every = ROW + COL
     in_specs = (
         P(every, None),

time: 222 us -> 240 us (1.081)
  starting transfers between devices: 69.2 us -> 87.7 us
  waiting for transfers between devices: 65.5 us -> 59.3 us
  blocking collectives: 48.1 us -> 52.7 us
    ppermute x9 -> x12, starting transfers between devices: 30.9 us -> 47.9 us  [shift(): return lax.ppermute(x, axis, [(i, (i + by) % size) for i in range(size)])]
    ppermute x9 -> x12, waiting for transfers between devices: 35.7 us -> 28.1 us  [shift(): return lax.ppermute(x, axis, [(i, (i + by) % size) for i in range(size)])]
    all_to_all x4, blocking collectives: 48.1 us -> 52.7 us  [swap(): return lax.all_to_all(x, axis, 0, 0, tiled=True)]
  transfers between devices with their start and end apart: 14 -> 17, of which waited for: 10 -> 10; matrix products, arithmetic and copies ran while one was open for 0% -> 1% of each run, Pallas kernels for 8% -> 7%
where the time goes in v6:
time: 240 us; the launch traced here: 239 us
  starting transfers between devices  87.7 us (37%)
  waiting for transfers between devices  59.3 us (25%)
  blocking collectives  52.7 us (22%)
  Pallas kernels  28.3 us (12%)
  local copies, waits for them, and re-layouts  7.4 us (3%)
  other arithmetic  2.64 us (1%)
    all_to_all x4, blocking collectives, swap(): return lax.all_to_all(x, axis, 0, 0, tiled=True)  52.7 us
    ppermute x12, starting transfers between devices, shift(): return lax.ppermute(x, axis, [(i, (i + by) % size) for i in range(size)])  47.9 us
    all_to_all x5, starting transfers between devices, swap(): return lax.all_to_all(x, axis, 0, 0, tiled=True)  39.8 us
    all_to_all x5, waiting for transfers between devices, swap(): return lax.all_to_all(x, axis, 0, 0, tiled=True)  31.2 us
    ppermute x12, waiting for transfers between devices, shift(): return lax.ppermute(x, axis, [(i, (i + by) % size) for i in range(size)])  28.1 us
    pallas_call x1, Pallas kernels, count_negatives(): pl.pallas_call(functools.partial(counts_kernel, blocks), out_shape=jax.Sh...  15.3 us
    pallas_call x1, Pallas kernels, shards(): group_call(functools.partial(grads_kernel, coef), (rows, jax.ShapeDtypeSt...  5.21 us
  transfers between devices with their start and end apart: 17, of which 10 were waited for; matrix products, arithmetic and copies ran while one was open for 1% of the time, Pallas kernels for 7%

profile of v6, /device:TPU:1, one launch (start us, length us, event | category | flops | bytes accessed | tf_op | source)
XLA Modules:
  0.0 239.1 jit_solution(3443633812064468142)
XLA Ops:
  2.5 15.7 %all-to-all-start = ((bf16[12,88,128]{2,1,0:T(8,128)(2,1)}), bf16[12,88,128]{2,1,0:T(8,128)(2,1)S(1)}, u32[]{:S(2)}, u32[]{:S(2)}) async-start(bf16[12,88,128]{2,1,0:T(8,128)(2,1)} %bitcast.8), calls=%async_computation | async-start | bytes 540672 | tf_op jit(solution)/shard_map/all_to_all | solution.py:241
  19.3 3.3 %collective-permute-start = (bf16[1552,128]{1,0:T(8,128)(2,1)S(1)}, bf16[1552,128]{1,0:T(8,128)(2,1)S(1)}, u32[]{:S(2)}, u32[]{:S(2)}) collective-permute-start(bf16[1552,128]{1,0:T(8,128)(2,1)S(1)} %pad_maximum_fusion.1.refs_0_), channel_id=1, source_target_pairs={{0,256},{256,512},{512,0},{1,257},{257,513},{513,1},{2,258},{258,5... | collective-permute-start | bytes 1191944 | tf_op jit(solution)/shard_map/ppermute | solution.py:250
  22.7 15.3 %counts.1 = s16[24,128,128]{2,1,0:T(8,128)(2,1)S(1)} custom-call(s32[128,1024]{1,0:T(8,128)S(1)} %copy-done), custom_call_target="tpu_custom_call" | custom-call | flops 4294967296 | bytes 2097152 | tf_op jit(solution)/shard_map/counts/pallas_call | solution.py:69
  39.3 4.0 %all-to-all-start.1 = ((bf16[4,12,88,128]{3,2,1,0:T(8,128)(2,1)}), bf16[4,12,88,128]{3,2,1,0:T(8,128)(2,1)S(1)}, u32[]{:S(2)}, u32[]{:S(2)}) async-start(bf16[4,12,88,128]{3,2,1,0:T(8,128)(2,1)} %broadcast_in_dim.57), calls=%async_computation.1 | async-start | bytes 2162688 | tf_op jit(solution)/shard_map/all_to_all | solution.py:241
  43.3 2.7 %collective-permute-start.1 = (bf16[1552,128]{1,0:T(8,128)(2,1)S(1)}, bf16[1552,128]{1,0:T(8,128)(2,1)S(1)}, u32[]{:S(2)}, u32[]{:S(2)}) collective-permute-start(bf16[1552,128]{1,0:T(8,128)(2,1)S(1)} %pad_maximum_fusion.1.refs_0_), channel_id=1, source_target_pairs={{0,512},{256,0},{512,256},{1,513},{257,1},{513,257},{2,514},{258,2... | collective-permute-start | bytes 1191944 | tf_op jit(solution)/shard_map/ppermute | solution.py:250
  46.1 4.2 %collective-permute-start.2 = (s16[3,2,128,128]{3,2,1,0:T(8,128)(2,1)S(1)}, s16[3,2,128,128]{3,2,1,0:T(8,128)(2,1)S(1)}, u32[]{:S(2)}, u32[]{:S(2)}) collective-permute-start(s16[3,2,128,128]{3,2,1,0:T(8,128)(2,1)S(1)} %get-tuple-element.44), channel_id=1, source_target_pairs={{0,64},{64,128},{128,192},{192,0},{1,65},{65,129},{129,193},{193,1... | collective-permute-start | bytes 589832 | tf_op jit(solution)/shard_map/ppermute | solution.py:250
  50.3 5.7 %collective-permute-start.3 = (s16[3,2,128,128]{3,2,1,0:T(8,128)(2,1)S(1)}, s16[3,2,128,128]{3,2,1,0:T(8,128)(2,1)S(1)}, u32[]{:S(2)}, u32[]{:S(2)}) collective-permute-start(s16[3,2,128,128]{3,2,1,0:T(8,128)(2,1)S(1)} %get-tuple-element.43), channel_id=1, source_target_pairs={{0,128},{64,192},{128,0},{192,64},{1,129},{65,193},{129,1},{193,65... | collective-permute-start | bytes 589832 | tf_op jit(solution)/shard_map/ppermute | solution.py:250
  56.0 5.0 %collective-permute-start.4 = (s16[3,2,128,128]{3,2,1,0:T(8,128)(2,1)S(1)}, s16[3,2,128,128]{3,2,1,0:T(8,128)(2,1)S(1)}, u32[]{:S(2)}, u32[]{:S(2)}) collective-permute-start(s16[3,2,128,128]{3,2,1,0:T(8,128)(2,1)S(1)} %get-tuple-element.42), channel_id=1, source_target_pairs={{0,192},{64,0},{128,64},{192,128},{1,193},{65,1},{129,65},{193,129... | collective-permute-start | bytes 589832 | tf_op jit(solution)/shard_map/ppermute | solution.py:250
  61.0 5.6 %collective-permute-done.3 = s16[3,2,128,128]{3,2,1,0:T(8,128)(2,1)S(1)} collective-permute-done((s16[3,2,128,128]{3,2,1,0:T(8,128)(2,1)S(1)}, s16[3,2,128,128]{3,2,1,0:T(8,128)(2,1)S(1)}, u32[]{:S(2)}, u32[]{:S(2)}) %collective-permute-start.3) | collective-permute-done | bytes 196640 | tf_op jit(solution)/shard_map/ppermute | solution.py:250
  66.6 8.1 %collective-permute-done.4 = s16[3,2,128,128]{3,2,1,0:T(8,128)(2,1)S(1)} collective-permute-done((s16[3,2,128,128]{3,2,1,0:T(8,128)(2,1)S(1)}, s16[3,2,128,128]{3,2,1,0:T(8,128)(2,1)S(1)}, u32[]{:S(2)}, u32[]{:S(2)}) %collective-permute-start.4) | collective-permute-done | bytes 196640 | tf_op jit(solution)/shard_map/ppermute | solution.py:250
  75.3 2.4 collective-permute-start.5
  80.0 3.1 %tile_sums.1 = bf16[24,2,88,128]{3,2,1,0:T(8,128)(2,1)} custom-call(s32[3,4,12]{2,1,0:T(4,128)S(1)} %maximum_convert_fusion.meta_ref, s32[3]{0:T(128)S(1)} %pad_add_fusion.1.place_ref, bf16[4,12,88,128]{3,2,1,0:T(8,128)(2,1)S(1)} %all-to-all-done.1.own_ref, bf16[4,12,88,128]{3,2,1,0:T(8,128)(2,1)S(1)} %collective-permute-done.5.other_ref, ...), custom_call_target="tpu_custom_call" | custom-call | tf_op jit(solution)/shard_map/tile_sums/pallas_call | solution.py:123
  83.1 7.0 %all-to-all-start.2 = ((bf16[24,2,88,128]{3,2,1,0:T(8,128)(2,1)}), bf16[24,2,88,128]{3,2,1,0:T(8,128)(2,1)S(1)}, u32[]{:S(2)}, u32[]{:S(2)}) async-start(bf16[24,2,88,128]{3,2,1,0:T(8,128)(2,1)} %tile_sums.1), calls=%async_computation.2 | async-start | bytes 2162688 | tf_op jit(solution)/shard_map/all_to_all | solution.py:241
  90.2 22.4 %all-to-all-done.2 = bf16[24,2,88,128]{3,2,1,0:T(8,128)(2,1)S(1)} async-done(((bf16[24,2,88,128]{3,2,1,0:T(8,128)(2,1)}), bf16[24,2,88,128]{3,2,1,0:T(8,128)(2,1)S(1)}, u32[]{:S(2)}, u32[]{:S(2)}) %all-to-all-start.2) | async-done | bytes 1081376 | tf_op jit(solution)/shard_map/all_to_all | solution.py:241
  113.9 9.2 %all-to-all-start.3 = ((bf16[6,2,256,128]{3,2,1,0:T(8,128)(2,1)}), bf16[6,2,256,128]{3,2,1,0:T(8,128)(2,1)S(1)}, u32[]{:S(2)}, u32[]{:S(2)}) async-start(bf16[6,2,256,128]{3,2,1,0:T(8,128)(2,1)} %broadcast_in_dim.58), calls=%async_computation.3 | async-start | bytes 1572864 | tf_op jit(solution)/shard_map/all_to_all | solution.py:241
  123.3 4.1 %collective-permute-start.6 = (bf16[2,256,128]{2,1,0:T(8,128)(2,1)S(1)}, bf16[2,256,128]{2,1,0:T(8,128)(2,1)S(1)}, u32[]{:S(2)}, u32[]{:S(2)}) collective-permute-start(bf16[2,256,128]{2,1,0:T(8,128)(2,1)S(1)} %fusion), channel_id=1, source_target_pairs={{0,64},{64,128},{128,192},{192,0},{1,65},{65,129},{129,193},{193,1... | collective-permute-start | bytes 393224 | tf_op jit(solution)/shard_map/ppermute | solution.py:250
  127.4 6.1 %collective-permute-start.7 = (bf16[2,256,128]{2,1,0:T(8,128)(2,1)S(1)}, bf16[2,256,128]{2,1,0:T(8,128)(2,1)S(1)}, u32[]{:S(2)}, u32[]{:S(2)}) collective-permute-start(bf16[2,256,128]{2,1,0:T(8,128)(2,1)S(1)} %fusion), channel_id=1, source_target_pairs={{0,128},{64,192},{128,0},{192,64},{1,129},{65,193},{129,1},{193,65... | collective-permute-start | bytes 393224 | tf_op jit(solution)/shard_map/ppermute | solution.py:250
  133.5 2.1 collective-permute-start.8
  135.7 5.5 %collective-permute-done.6 = bf16[2,256,128]{2,1,0:T(8,128)(2,1)S(1)} collective-permute-done((bf16[2,256,128]{2,1,0:T(8,128)(2,1)S(1)}, bf16[2,256,128]{2,1,0:T(8,128)(2,1)S(1)}, u32[]{:S(2)}, u32[]{:S(2)}) %collective-permute-start.6) | collective-permute-done | bytes 131104 | tf_op jit(solution)/shard_map/ppermute | solution.py:250
  141.2 4.1 %collective-permute-done.7 = bf16[2,256,128]{2,1,0:T(8,128)(2,1)S(1)} collective-permute-done((bf16[2,256,128]{2,1,0:T(8,128)(2,1)S(1)}, bf16[2,256,128]{2,1,0:T(8,128)(2,1)S(1)}, u32[]{:S(2)}, u32[]{:S(2)}) %collective-permute-start.7) | collective-permute-done | bytes 131104 | tf_op jit(solution)/shard_map/ppermute | solution.py:250
  145.7 3.7 %scores.1 = (f32[8,512]{1,0:T(8,128)S(1)}, bf16[3,2,256,512]{3,2,1,0:T(8,128)(2,1)S(1)}, bf16[3,2,256,256]{3,2,1,0:T(8,128)(2,1)S(1)}) custom-call(s32[3]{0:T(128)S(1)} %pad_add_fusion.1.place_ref, bf16[4,2,256,128]{3,2,1,0:T(8,128)(2,1)S(1)} %pad_maximum_fusion.n_ref, bf16[6,2,256,128]{3,2,1,0:T(8,128)(2,1)S(1)} %all-to-all-done.3.a_ref, ...), custom_call_target="tpu_custom_call" | custom-call | flops 2147483648 | bytes 4194304 | tf_op jit(solution)/shard_map/scores/pallas_call | solution.py:322
  149.4 2.9 %collective-permute-start.10 = (f32[8,512]{1,0:T(8,128)S(1)}, f32[8,512]{1,0:T(8,128)S(1)}, u32[]{:S(2)}, u32[]{:S(2)}) collective-permute-start(f32[8,512]{1,0:T(8,128)S(1)} %get-tuple-element.37.refs_0_), channel_id=1, source_target_pairs={{0,128},{64,192},{128,0},{192,64},{1,129},{65,193},{129,1},{193,65... | collective-permute-start | bytes 49160 | tf_op jit(solution)/shard_map/ppermute | solution.py:250
  152.4 7.4 %collective-permute-start.11 = (f32[8,512]{1,0:T(8,128)S(1)}, f32[8,512]{1,0:T(8,128)S(1)}, u32[]{:S(2)}, u32[]{:S(2)}) collective-permute-start(f32[8,512]{1,0:T(8,128)S(1)} %get-tuple-element.37.refs_0_), channel_id=1, source_target_pairs={{0,192},{64,0},{128,64},{192,128},{1,193},{65,1},{129,65},{193,129... | collective-permute-start | bytes 49160 | tf_op jit(solution)/shard_map/ppermute | solution.py:250
  159.8 2.1 collective-permute-start.9
  162.9 3.5 %collective-permute-done.9.refs_1_ = f32[8,512]{1,0:T(8,128)S(1)} collective-permute-done((f32[8,512]{1,0:T(8,128)S(1)}, f32[8,512]{1,0:T(8,128)S(1)}, u32[]{:S(2)}, u32[]{:S(2)}) %collective-permute-start.9) | collective-permute-done | bytes 16416 | tf_op jit(solution)/shard_map/ppermute | solution.py:250
  166.4 5.2 %grads.1 = (f32[8,512]{1,0:T(8,128)S(1)}, f32[256,256]{1,0:T(8,128)S(1)}) custom-call(s32[3]{0:T(128)S(1)} %pad_add_fusion.1.place_ref, bf16[4,2,256,128]{3,2,1,0:T(8,128)(2,1)S(1)} %pad_maximum_fusion.n_ref, bf16[6,2,256,128]{3,2,1,0:T(8,128)(2,1)S(1)} %all-to-all-done.3.a_ref, bf16[256,256]{1,0:T(8,128)(2,1)S(1)} %bitcast.48, ...), custom_call_target="tpu_custom_call" | custom-call | flops 2147483648 | bytes 4194304 | tf_op jit(solution)/shard_map/grads/pallas_call | solution.py:340
  171.6 7.9 %all_to_all.45 = f32[2,256,128]{2,1,0:T(8,128)S(1)} all-to-all(f32[2,256,128]{2,1,0:T(8,128)S(1)} %reshape_reshape.6), channel_id=1, replica_groups=mesh['zl'=3,'yq'=4,'yp'=2,'x'=4,'zh'=4,'core'=2] {'core'}, dimensions={0} | all-to-all | bytes 524288 | tf_op jit(solution)/shard_map/all_to_all | solution.py:241
  179.5 16.6 %all_to_all.46 = f32[32,8,128]{2,1,0:T(8,128)S(1)} all-to-all(f32[32,8,128]{2,1,0:T(8,128)S(1)} %bitcast.55), channel_id=1, replica_groups=mesh['zl'=3,'yq'=4,'yp'=2,'x'=4,'zh'=4,'core'=2] {'yq','yp','x'}, dimensions={0} | all-to-all | bytes 262144 | tf_op jit(solution)/shard_map/all_to_all | solution.py:241
  196.1 20.0 %all_to_all.47 = f32[12,8,128]{2,1,0:T(8,128)S(1)} all-to-all(f32[12,8,128]{2,1,0:T(8,128)S(1)} %broadcast_in_dim.60), channel_id=1, replica_groups=mesh['zl'=3,'yq'=4,'yp'=2,'x'=4,'zh'=4,'core'=2] {'zl','zh'}, dimensions={0} | all-to-all | bytes 98304 | tf_op jit(solution)/shard_map/all_to_all | solution.py:241
  216.8 3.9 %all-to-all-start.7 = ((f32[32,8,128]{2,1,0:T(8,128)}), f32[32,8,128]{2,1,0:T(8,128)S(1)}, u32[]{:S(2)}, u32[]{:S(2)}) async-start(f32[32,8,128]{2,1,0:T(8,128)} %broadcast_in_dim.61), calls=%async_computation.7 | async-start | bytes 262144 | tf_op jit(solution)/shard_map/all_to_all | solution.py:241
  221.2 8.8 %all-to-all-done.7 = f32[32,8,128]{2,1,0:T(8,128)S(1)} async-done(((f32[32,8,128]{2,1,0:T(8,128)}), f32[32,8,128]{2,1,0:T(8,128)S(1)}, u32[]{:S(2)}, u32[]{:S(2)}) %all-to-all-start.7) | async-done | bytes 131104 | tf_op jit(solution)/shard_map/all_to_all | solution.py:241
  230.0 8.3 %all_to_all.48 = f32[2,256,128]{2,1,0:T(8,128)S(1)} all-to-all(f32[2,256,128]{2,1,0:T(8,128)S(1)} %broadcast_in_dim.63), channel_id=1, replica_groups=mesh['zl'=3,'yq'=4,'yp'=2,'x'=4,'zh'=4,'core'=2] {'core'}, dimensions={0} | all-to-all | bytes 524288 | tf_op jit(solution)/shard_map/all_to_all | solution.py:241
  (73 shorter events, 12.4 us)
Async XLA Ops:
  0.6 17.5 %copy-start.11 = (s32[12]{0:T(128)S(1)}, s32[12]{0:T(128)}, u32[]{:S(2)}) copy-start(s32[12]{0:T(128)} %param.10) | copy-start | bytes 148
  0.6 18.1 %copy-start.12 = (s32[2,12]{1,0:T(2,128)S(1)}, s32[2,12]{1,0:T(2,128)}, u32[]{:S(2)}) copy-start(s32[2,12]{1,0:T(2,128)} %param.11) | copy-start | bytes 292
  0.7 18.6 %copy-start.1 = (bf16[12,128,128]{2,1,0:T(8,128)(2,1)S(1)}, bf16[12,128,128]{2,1,0:T(8,128)(2,1)}, u32[]{:S(2)}) copy-start(bf16[12,128,128]{2,1,0:T(8,128)(2,1)} %param.9) | copy-start | bytes 1179652
  0.7 22.0 %copy-start = (s32[128,1024]{1,0:T(8,128)S(1)}, s32[128,1024]{1,0:T(8,128)}, u32[]{:S(2)}) copy-start(s32[128,1024]{1,0:T(8,128)} %neg_ref.1) | copy-start | bytes 1572868
  2.5 35.7 %all-to-all-start = ((bf16[12,88,128]{2,1,0:T(8,128)(2,1)}), bf16[12,88,128]{2,1,0:T(8,128)(2,1)S(1)}, u32[]{:S(2)}, u32[]{:S(2)}) async-start(bf16[12,88,128]{2,1,0:T(8,128)(2,1)} %bitcast.8), calls=%async_computation | async-start | bytes 540672 | tf_op jit(solution)/shard_map/all_to_all | solution.py:241
  18.7 0.6 copy-start.9
  19.3 18.8 %collective-permute-start = (bf16[1552,128]{1,0:T(8,128)(2,1)S(1)}, bf16[1552,128]{1,0:T(8,128)(2,1)S(1)}, u32[]{:S(2)}, u32[]{:S(2)}) collective-permute-start(bf16[1552,128]{1,0:T(8,128)(2,1)S(1)} %pad_maximum_fusion.1.refs_0_), channel_id=1, source_target_pairs={{0,256},{256,512},{512,0},{1,257},{257,513},{513,1},{2,258},{258,5... | collective-permute-start | bytes 1191944 | tf_op jit(solution)/shard_map/ppermute | solution.py:250
  39.3 35.4 %all-to-all-start.1 = ((bf16[4,12,88,128]{3,2,1,0:T(8,128)(2,1)}), bf16[4,12,88,128]{3,2,1,0:T(8,128)(2,1)S(1)}, u32[]{:S(2)}, u32[]{:S(2)}) async-start(bf16[4,12,88,128]{3,2,1,0:T(8,128)(2,1)} %broadcast_in_dim.57), calls=%async_computation.1 | async-start | bytes 2162688 | tf_op jit(solution)/shard_map/all_to_all | solution.py:241
  43.3 17.7 %collective-permute-start.1 = (bf16[1552,128]{1,0:T(8,128)(2,1)S(1)}, bf16[1552,128]{1,0:T(8,128)(2,1)S(1)}, u32[]{:S(2)}, u32[]{:S(2)}) collective-permute-start(bf16[1552,128]{1,0:T(8,128)(2,1)S(1)} %pad_maximum_fusion.1.refs_0_), channel_id=1, source_target_pairs={{0,512},{256,0},{512,256},{1,513},{257,1},{513,257},{2,514},{258,2... | collective-permute-start | bytes 1191944 | tf_op jit(solution)/shard_map/ppermute | solution.py:250
  46.1 14.9 %collective-permute-start.2 = (s16[3,2,128,128]{3,2,1,0:T(8,128)(2,1)S(1)}, s16[3,2,128,128]{3,2,1,0:T(8,128)(2,1)S(1)}, u32[]{:S(2)}, u32[]{:S(2)}) collective-permute-start(s16[3,2,128,128]{3,2,1,0:T(8,128)(2,1)S(1)} %get-tuple-element.44), channel_id=1, source_target_pairs={{0,64},{64,128},{128,192},{192,0},{1,65},{65,129},{129,193},{193,1... | collective-permute-start | bytes 589832 | tf_op jit(solution)/shard_map/ppermute | solution.py:250
  50.3 16.2 %collective-permute-start.3 = (s16[3,2,128,128]{3,2,1,0:T(8,128)(2,1)S(1)}, s16[3,2,128,128]{3,2,1,0:T(8,128)(2,1)S(1)}, u32[]{:S(2)}, u32[]{:S(2)}) collective-permute-start(s16[3,2,128,128]{3,2,1,0:T(8,128)(2,1)S(1)} %get-tuple-element.43), channel_id=1, source_target_pairs={{0,128},{64,192},{128,0},{192,64},{1,129},{65,193},{129,1},{193,65... | collective-permute-start | bytes 589832 | tf_op jit(solution)/shard_map/ppermute | solution.py:250
  56.0 18.6 %collective-permute-start.4 = (s16[3,2,128,128]{3,2,1,0:T(8,128)(2,1)S(1)}, s16[3,2,128,128]{3,2,1,0:T(8,128)(2,1)S(1)}, u32[]{:S(2)}, u32[]{:S(2)}) collective-permute-start(s16[3,2,128,128]{3,2,1,0:T(8,128)(2,1)S(1)} %get-tuple-element.42), channel_id=1, source_target_pairs={{0,192},{64,0},{128,64},{192,128},{1,193},{65,1},{129,65},{193,129... | collective-permute-start | bytes 589832 | tf_op jit(solution)/shard_map/ppermute | solution.py:250
  61.0 13.6 %copy-start.2 = (s16[3,2,128,128]{3,2,1,0:T(8,128)(2,1)}, s16[3,2,128,128]{3,2,1,0:T(8,128)(2,1)S(1)}, u32[]{:S(2)}) copy-start(s16[3,2,128,128]{3,2,1,0:T(8,128)(2,1)S(1)} %collective-permute-done.2) | copy-start | bytes 589828
  66.6 8.1 %copy-start.4 = (s16[3,2,128,128]{3,2,1,0:T(8,128)(2,1)}, s16[3,2,128,128]{3,2,1,0:T(8,128)(2,1)S(1)}, u32[]{:S(2)}) copy-start(s16[3,2,128,128]{3,2,1,0:T(8,128)(2,1)S(1)} %collective-permute-done.3) | copy-start | bytes 589828
  74.6 0.7 copy-start.6
  75.3 4.7 %collective-permute-start.5 = (bf16[4,12,88,128]{3,2,1,0:T(8,128)(2,1)S(1)}, bf16[4,12,88,128]{3,2,1,0:T(8,128)(2,1)S(1)}, u32[]{:S(2)}, u32[]{:S(2)}) collective-permute-start(bf16[4,12,88,128]{3,2,1,0:T(8,128)(2,1)S(1)} %all-to-all-done.1.own_ref), channel_id=1, source_target_pairs={{0,1},{1,0},{2,3},{3,2},{4,5},{5,4},{6,7},{7,6},{8,9},{9,8},{10,11... | collective-permute-start | bytes 3244040 | tf_op jit(solution)/shard_map/ppermute | solution.py:250
  83.1 7.0 %copy-start.10 = (s32[2,256]{1,0:T(2,128)S(1)}, s32[2,256]{1,0:T(2,128)}, u32[]{:S(2)}) copy-start(s32[2,256]{1,0:T(2,128)} %param.12) | copy-start | bytes 6148
  83.1 29.4 %all-to-all-start.2 = ((bf16[24,2,88,128]{3,2,1,0:T(8,128)(2,1)}), bf16[24,2,88,128]{3,2,1,0:T(8,128)(2,1)S(1)}, u32[]{:S(2)}, u32[]{:S(2)}) async-start(bf16[24,2,88,128]{3,2,1,0:T(8,128)(2,1)} %tile_sums.1), calls=%async_computation.2 | async-start | bytes 2162688 | tf_op jit(solution)/shard_map/all_to_all | solution.py:241
  112.8 10.2 %copy-start.8 = (bf16[256,256]{1,0:T(8,128)(2,1)S(1)}, bf16[256,256]{1,0:T(8,128)(2,1)}, u32[]{:S(2)}) copy-start(bf16[256,256]{1,0:T(8,128)(2,1)} %param.8) | copy-start | bytes 393220
  113.9 9.3 %copy-start.3 = (s16[3,2,128,128]{3,2,1,0:T(8,128)(2,1)S(1)}, s16[3,2,128,128]{3,2,1,0:T(8,128)(2,1)}, u32[]{:S(2)}) copy-start(s16[3,2,128,128]{3,2,1,0:T(8,128)(2,1)} %copy-done.2) | copy-start | bytes 589828
  113.9 9.3 %copy-start.5 = (s16[3,2,128,128]{3,2,1,0:T(8,128)(2,1)S(1)}, s16[3,2,128,128]{3,2,1,0:T(8,128)(2,1)}, u32[]{:S(2)}) copy-start(s16[3,2,128,128]{3,2,1,0:T(8,128)(2,1)} %copy-done.4) | copy-start | bytes 589828
  113.9 9.3 %copy-start.7 = (s16[3,2,128,128]{3,2,1,0:T(8,128)(2,1)S(1)}, s16[3,2,128,128]{3,2,1,0:T(8,128)(2,1)}, u32[]{:S(2)}) copy-start(s16[3,2,128,128]{3,2,1,0:T(8,128)(2,1)} %copy-done.6) | copy-start | bytes 589828
  113.9 31.8 %all-to-all-start.3 = ((bf16[6,2,256,128]{3,2,1,0:T(8,128)(2,1)}), bf16[6,2,256,128]{3,2,1,0:T(8,128)(2,1)S(1)}, u32[]{:S(2)}, u32[]{:S(2)}) async-start(bf16[6,2,256,128]{3,2,1,0:T(8,128)(2,1)} %broadcast_in_dim.58), calls=%async_computation.3 | async-start | bytes 1572864 | tf_op jit(solution)/shard_map/all_to_all | solution.py:241
  123.3 17.9 %collective-permute-start.6 = (bf16[2,256,128]{2,1,0:T(8,128)(2,1)S(1)}, bf16[2,256,128]{2,1,0:T(8,128)(2,1)S(1)}, u32[]{:S(2)}, u32[]{:S(2)}) collective-permute-start(bf16[2,256,128]{2,1,0:T(8,128)(2,1)S(1)} %fusion), channel_id=1, source_target_pairs={{0,64},{64,128},{128,192},{192,0},{1,65},{65,129},{129,193},{193,1... | collective-permute-start | bytes 393224 | tf_op jit(solution)/shard_map/ppermute | solution.py:250
  127.4 17.9 %collective-permute-start.7 = (bf16[2,256,128]{2,1,0:T(8,128)(2,1)S(1)}, bf16[2,256,128]{2,1,0:T(8,128)(2,1)S(1)}, u32[]{:S(2)}, u32[]{:S(2)}) collective-permute-start(bf16[2,256,128]{2,1,0:T(8,128)(2,1)S(1)} %fusion), channel_id=1, source_target_pairs={{0,128},{64,192},{128,0},{192,64},{1,129},{65,193},{129,1},{193,65... | collective-permute-start | bytes 393224 | tf_op jit(solution)/shard_map/ppermute | solution.py:250
  133.5 12.2 %collective-permute-start.8 = (bf16[2,256,128]{2,1,0:T(8,128)(2,1)S(1)}, bf16[2,256,128]{2,1,0:T(8,128)(2,1)S(1)}, u32[]{:S(2)}, u32[]{:S(2)}) collective-permute-start(bf16[2,256,128]{2,1,0:T(8,128)(2,1)S(1)} %fusion), channel_id=1, source_target_pairs={{0,192},{64,0},{128,64},{192,128},{1,193},{65,1},{129,65},{193,129... | collective-permute-start | bytes 393224 | tf_op jit(solution)/shard_map/ppermute | solution.py:250
  149.4 13.4 %collective-permute-start.10 = (f32[8,512]{1,0:T(8,128)S(1)}, f32[8,512]{1,0:T(8,128)S(1)}, u32[]{:S(2)}, u32[]{:S(2)}) collective-permute-start(f32[8,512]{1,0:T(8,128)S(1)} %get-tuple-element.37.refs_0_), channel_id=1, source_target_pairs={{0,128},{64,192},{128,0},{192,64},{1,129},{65,193},{129,1},{193,65... | collective-permute-start | bytes 49160 | tf_op jit(solution)/shard_map/ppermute | solution.py:250
  152.4 10.5 %collective-permute-start.11 = (f32[8,512]{1,0:T(8,128)S(1)}, f32[8,512]{1,0:T(8,128)S(1)}, u32[]{:S(2)}, u32[]{:S(2)}) collective-permute-start(f32[8,512]{1,0:T(8,128)S(1)} %get-tuple-element.37.refs_0_), channel_id=1, source_target_pairs={{0,192},{64,0},{128,64},{192,128},{1,193},{65,1},{129,65},{193,129... | collective-permute-start | bytes 49160 | tf_op jit(solution)/shard_map/ppermute | solution.py:250
  159.8 6.6 %collective-permute-start.9 = (f32[8,512]{1,0:T(8,128)S(1)}, f32[8,512]{1,0:T(8,128)S(1)}, u32[]{:S(2)}, u32[]{:S(2)}) collective-permute-start(f32[8,512]{1,0:T(8,128)S(1)} %get-tuple-element.37.refs_0_), channel_id=1, source_target_pairs={{0,64},{64,128},{128,192},{192,0},{1,65},{65,129},{129,193},{193,1... | collective-permute-start | bytes 49160 | tf_op jit(solution)/shard_map/ppermute | solution.py:250
  216.8 13.2 %all-to-all-start.7 = ((f32[32,8,128]{2,1,0:T(8,128)}), f32[32,8,128]{2,1,0:T(8,128)S(1)}, u32[]{:S(2)}, u32[]{:S(2)}) async-start(f32[32,8,128]{2,1,0:T(8,128)} %broadcast_in_dim.61), calls=%async_computation.7 | async-start | bytes 262144 | tf_op jit(solution)/shard_map/all_to_all | solution.py:241

commit v7 on v5

--- a/solution.py
+++ b/solution.py
@@ -37,11 +37,17 @@
         index = neg_ref[pl.ds(base, 8), :]
         low = index & (T - 1)
         high = index >> 7
-        for j in range(8):
-            low_hot = jnp.where(low[j : j + 1, :] == low_iota, 1.0, 0.0).astype(bf16)
-            high_hot = jnp.where(high[j : j + 1, :] == high_iota, 1.0, 0.0).astype(bf16)
+        for j in range(0, 8, 2):
+            low_hot, high_hot = (
+                jnp.concatenate(
+                    [jnp.where(part[j + i : j + i + 1, :] == iota, 1.0, 0.0) for i in range(2)], 0
+                ).astype(bf16)
+                for part, iota in ((low, low_iota), (high, high_iota))
+            )
             found = dot(high_hot, low_hot, NT)
-            acc_ref[pl.ds(base + j, rows, stride=nodes), :] = found
+            for i in range(2):
+                own = found[i * rows : (i + 1) * rows, i * T : (i + 1) * T]
+                acc_ref[pl.ds(base + j + i, rows, stride=nodes), :] = own
         return carry
 
     lax.fori_loop(0, nodes // 8, step, 0)
@@ -76,27 +82,36 @@
 def tiles_kernel(cols, meta_ref, place_ref, own_ref, other_ref, *refs):
     tile_refs, (out_ref, acc_ref) = refs[:ZL], refs[ZL:]
     zsize = own_ref.shape[1] // ZL
+    slots = meta_ref.shape[2]
     acc_ref[...] = jnp.zeros_like(acc_ref)
     core, zl = place_ref[0], place_ref[1]
     for s in range(ZL):
 
-        def slot(k, carry, s=s):
-            trow, tcol = meta_ref[s, 0, k], meta_ref[s, 1, k]
-
-            @pl.when(trow >= 0)
+        def few(i, carry, s=s):
+            @pl.when(meta_ref[s, 0, i * 4] >= 0)
             def _():
-                chip = lax.div(tcol, 2)
-                at = lax.div(chip, zsize), behind(zl, s) * zsize + lax.rem(chip, zsize)
-                mine = lax.rem(tcol, 2) == core
-                rows = jnp.where(mine, own_ref[at], other_ref[at])
-                product = dot(rows, tile_refs[s][pl.ds(pl.multiple_of(k * T, T), T), :], NT)
-                for v in range(2):
-                    kept = meta_ref[s, 2 + v, k].astype(f32)
-                    acc_ref[trow, v] += kept * product
+                products = []
+                for j in range(4):
+                    k = i * 4 + j
+                    tcol = meta_ref[s, 1, k]
+                    chip = lax.div(tcol, 2)
+                    at = lax.div(chip, zsize), behind(zl, s) * zsize + lax.rem(chip, zsize)
+                    mine = lax.rem(tcol, 2) == core
+                    rows = jnp.where(mine, own_ref[at], other_ref[at])
+                    tile = tile_refs[s][pl.ds(pl.multiple_of(k * T, T), T), :]
+                    products.append(dot(rows, tile, NT))
+                for j in range(4):
+                    k = i * 4 + j
+                    trow = meta_ref[s, 0, k]
+                    held = jnp.where(trow >= 0, 1, 0)
+                    at = jnp.maximum(trow, 0)
+                    for v in range(2):
+                        kept = (held * meta_ref[s, 2 + v, k]).astype(f32)
+                        acc_ref[at, v] += kept * products[j]
 
             return carry
 
-        lax.fori_loop(0, meta_ref.shape[2], slot, 0)
+        lax.fori_loop(0, slots // 4, few, 0)
     out_ref[...] = acc_ref[...].astype(bf16)
 
 
@@ -151,7 +166,7 @@
             tot_ref[v : v + 1, :] += jnp.sum(term, 0, keepdims=True)
         return carry
 
-    lax.fori_loop(0, e_ref.shape[0], pair, 0)
+    lax.fori_loop(0, e_ref.shape[0], pair, 0, unroll=True)
 
 
 def pull_kernel(e_ref, low_ref, sums_ref):
@@ -162,7 +177,7 @@
             sums_ref[v] += dot(low_ref[p, 1 - v], e_ref[p, v], NN)
         return carry
 
-    lax.fori_loop(0, e_ref.shape[0], pair, 0)
+    lax.fori_loop(0, e_ref.shape[0], pair, 0, unroll=True)
 
 
 def split_dot(agg, dz):
@@ -201,7 +216,7 @@
             grad_ref[...] += split_dot(agg, back(emb, rinv, d))
         return carry
 
-    lax.fori_loop(0, e_ref.shape[0], pair, 0)
+    lax.fori_loop(0, e_ref.shape[0], pair, 0, unroll=True)
     for v in range(2):
         d = coef * (both * full_n[1 - v] + sums_ref[v] * inverse[v])
         grad_ref[...] += split_dot(agg_n[v], back(emb_n[v], rinv_n[v], d))

time: 222 us -> 219 us (0.986)
  Pallas kernels: 30.6 us -> 26.5 us
  transfers between devices with their start and end apart: 14 -> 14, of which waited for: 10 -> 10; matrix products, arithmetic and copies ran while one was open for 0% -> 0% of each run, Pallas kernels for 8% -> 7%
where the time goes in v7:
time: 219 us; the launch traced here: 218 us
  starting transfers between devices  70.8 us (32%)
  waiting for transfers between devices  65.1 us (30%)
  blocking collectives  47.7 us (22%)
  Pallas kernels  26.5 us (12%)
  local copies, waits for them, and re-layouts  6.29 us (3%)
    all_to_all x4, blocking collectives, swap(): return lax.all_to_all(x, axis, 0, 0, tiled=True)  47.7 us
    all_to_all x5, starting transfers between devices, swap(): return lax.all_to_all(x, axis, 0, 0, tiled=True)  38.6 us
    ppermute x9, waiting for transfers between devices, shift(): return lax.ppermute(x, axis, [(i, (i + by) % size) for i in range(size)])  35.8 us
    ppermute x9, starting transfers between devices, shift(): return lax.ppermute(x, axis, [(i, (i + by) % size) for i in range(size)])  32.2 us
    all_to_all x5, waiting for transfers between devices, swap(): return lax.all_to_all(x, axis, 0, 0, tiled=True)  29.3 us
    pallas_call x1, Pallas kernels, count_negatives(): pl.pallas_call(functools.partial(counts_kernel, blocks), out_shape=jax.Sh...  15.3 us
  transfers between devices with their start and end apart: 14, of which 10 were waited for; matrix products, arithmetic and copies ran while one was open for 0% of the time, Pallas kernels for 7%

profile of v7, /device:TPU:1, one launch (start us, length us, event | category | flops | bytes accessed | tf_op | source)
XLA Modules:
  0.0 218.0 jit_solution(1665733700066445771)
XLA Ops:
  2.4 15.7 %all-to-all-start = ((bf16[12,88,128]{2,1,0:T(8,128)(2,1)}), bf16[12,88,128]{2,1,0:T(8,128)(2,1)S(1)}, u32[]{:S(2)}, u32[]{:S(2)}) async-start(bf16[12,88,128]{2,1,0:T(8,128)(2,1)} %bitcast.7), calls=%async_computation | async-start | bytes 540672 | tf_op jit(solution)/shard_map/all_to_all | solution.py:238
  18.3 3.3 %collective-permute-start = (bf16[1552,128]{1,0:T(8,128)(2,1)S(1)}, bf16[1552,128]{1,0:T(8,128)(2,1)S(1)}, u32[]{:S(2)}, u32[]{:S(2)}) collective-permute-start(bf16[1552,128]{1,0:T(8,128)(2,1)S(1)} %pad_maximum_fusion.refs_0_), channel_id=1, source_target_pairs={{0,256},{256,512},{512,0},{1,257},{257,513},{513,1},{2,258},{258,5... | collective-permute-start | bytes 1191944 | tf_op jit(solution)/shard_map/ppermute | solution.py:247
  21.6 16.3 %collective-permute-done.refs_1_ = bf16[1552,128]{1,0:T(8,128)(2,1)S(1)} collective-permute-done((bf16[1552,128]{1,0:T(8,128)(2,1)S(1)}, bf16[1552,128]{1,0:T(8,128)(2,1)S(1)}, u32[]{:S(2)}, u32[]{:S(2)}) %collective-permute-start) | collective-permute-done | bytes 397344 | tf_op jit(solution)/shard_map/ppermute | solution.py:247
  39.1 4.0 %all-to-all-start.1 = ((bf16[4,12,88,128]{3,2,1,0:T(8,128)(2,1)}), bf16[4,12,88,128]{3,2,1,0:T(8,128)(2,1)S(1)}, u32[]{:S(2)}, u32[]{:S(2)}) async-start(bf16[4,12,88,128]{3,2,1,0:T(8,128)(2,1)} %broadcast_in_dim.57), calls=%async_computation.1 | async-start | bytes 2162688 | tf_op jit(solution)/shard_map/all_to_all | solution.py:238
  43.1 2.8 %collective-permute-start.1 = (bf16[1552,128]{1,0:T(8,128)(2,1)S(1)}, bf16[1552,128]{1,0:T(8,128)(2,1)S(1)}, u32[]{:S(2)}, u32[]{:S(2)}) collective-permute-start(bf16[1552,128]{1,0:T(8,128)(2,1)S(1)} %pad_maximum_fusion.refs_0_), channel_id=1, source_target_pairs={{0,512},{256,0},{512,256},{1,513},{257,1},{513,257},{2,514},{258,2... | collective-permute-start | bytes 1191944 | tf_op jit(solution)/shard_map/ppermute | solution.py:247
  45.9 7.9 %collective-permute-done.1.refs_2_ = bf16[1552,128]{1,0:T(8,128)(2,1)S(1)} collective-permute-done((bf16[1552,128]{1,0:T(8,128)(2,1)S(1)}, bf16[1552,128]{1,0:T(8,128)(2,1)S(1)}, u32[]{:S(2)}, u32[]{:S(2)}) %collective-permute-start.1) | collective-permute-done | bytes 397344 | tf_op jit(solution)/shard_map/ppermute | solution.py:247
  53.8 2.9 %all-to-all-done.1.own_ref = bf16[4,12,88,128]{3,2,1,0:T(8,128)(2,1)S(1)} async-done(((bf16[4,12,88,128]{3,2,1,0:T(8,128)(2,1)}), bf16[4,12,88,128]{3,2,1,0:T(8,128)(2,1)S(1)}, u32[]{:S(2)}, u32[]{:S(2)}) %all-to-all-start.1) | async-done | bytes 1081376 | tf_op jit(solution)/shard_map/all_to_all | solution.py:238
  56.7 4.7 %collective-permute-start.2 = (bf16[4,12,88,128]{3,2,1,0:T(8,128)(2,1)S(1)}, bf16[4,12,88,128]{3,2,1,0:T(8,128)(2,1)S(1)}, u32[]{:S(2)}, u32[]{:S(2)}) collective-permute-start(bf16[4,12,88,128]{3,2,1,0:T(8,128)(2,1)S(1)} %all-to-all-done.1.own_ref), channel_id=1, source_target_pairs={{0,1},{1,0},{2,3},{3,2},{4,5},{5,4},{6,7},{7,6},{8,9},{9,8},{10,11... | collective-permute-start | bytes 3244040 | tf_op jit(solution)/shard_map/ppermute | solution.py:247
  61.5 2.2 %collective-permute-done.2.other_ref = bf16[4,12,88,128]{3,2,1,0:T(8,128)(2,1)S(1)} collective-permute-done((bf16[4,12,88,128]{3,2,1,0:T(8,128)(2,1)S(1)}, bf16[4,12,88,128]{3,2,1,0:T(8,128)(2,1)S(1)}, u32[]{:S(2)}, u32[]{:S(2)}) %collective-permute-start.2) | collective-permute-done | bytes 1081376 | tf_op jit(solution)/shard_map/ppermute | solution.py:247
  63.7 2.7 %tile_sums.1 = bf16[24,2,88,128]{3,2,1,0:T(8,128)(2,1)} custom-call(s32[3,4,12]{2,1,0:T(4,128)S(1)} %maximum_convert_fusion.meta_ref, s32[2]{0:T(128)S(1)} %pad_add_fusion.1.place_ref, bf16[4,12,88,128]{3,2,1,0:T(8,128)(2,1)S(1)} %all-to-all-done.1.own_ref, bf16[4,12,88,128]{3,2,1,0:T(8,128)(2,1)S(1)} %collective-permute-done.2.other_ref, ...), custom_call_target="tpu_custom_call" | custom-call | tf_op jit(solution)/shard_map/tile_sums/pallas_call | solution.py:120
  66.4 8.3 %all-to-all-start.2 = ((bf16[24,2,88,128]{3,2,1,0:T(8,128)(2,1)}), bf16[24,2,88,128]{3,2,1,0:T(8,128)(2,1)S(1)}, u32[]{:S(2)}, u32[]{:S(2)}) async-start(bf16[24,2,88,128]{3,2,1,0:T(8,128)(2,1)} %tile_sums.1), calls=%async_computation.2 | async-start | bytes 2162688 | tf_op jit(solution)/shard_map/all_to_all | solution.py:238
  74.7 15.3 %counts.1 = s16[24,128,128]{2,1,0:T(8,128)(2,1)S(1)} custom-call(s32[128,1024]{1,0:T(8,128)S(1)} %copy-done), custom_call_target="tpu_custom_call" | custom-call | flops 4294967296 | bytes 2097152 | tf_op jit(solution)/shard_map/counts/pallas_call | solution.py:66
  90.0 10.1 %all-to-all-done.2 = bf16[24,2,88,128]{3,2,1,0:T(8,128)(2,1)S(1)} async-done(((bf16[24,2,88,128]{3,2,1,0:T(8,128)(2,1)}), bf16[24,2,88,128]{3,2,1,0:T(8,128)(2,1)S(1)}, u32[]{:S(2)}, u32[]{:S(2)}) %all-to-all-start.2) | async-done | bytes 1081376 | tf_op jit(solution)/shard_map/all_to_all | solution.py:238
  101.6 6.7 %all-to-all-start.3 = ((bf16[8,2,256,128]{3,2,1,0:T(8,128)(2,1)}), bf16[8,2,256,128]{3,2,1,0:T(8,128)(2,1)S(1)}, u32[]{:S(2)}, u32[]{:S(2)}) async-start(bf16[8,2,256,128]{3,2,1,0:T(8,128)(2,1)} %broadcast_in_dim.58), calls=%async_computation.3 | async-start | bytes 2097152 | tf_op jit(solution)/shard_map/all_to_all | solution.py:238
  108.4 5.7 %collective-permute-start.5 = (s16[8,128,128]{2,1,0:T(8,128)(2,1)S(1)}, s16[8,128,128]{2,1,0:T(8,128)(2,1)S(1)}, u32[]{:S(2)}, u32[]{:S(2)}) collective-permute-start(s16[8,128,128]{2,1,0:T(8,128)(2,1)S(1)} %get-tuple-element.36), channel_id=1, source_target_pairs={{0,256},{256,512},{512,0},{1,257},{257,513},{513,1},{2,258},{258,5... | collective-permute-start | bytes 786440 | tf_op jit(solution)/shard_map/ppermute | solution.py:247
  114.1 1.9 collective-permute-start.6
  116.0 3.4 %collective-permute-start.3 = (bf16[2,256,128]{2,1,0:T(8,128)(2,1)S(1)}, bf16[2,256,128]{2,1,0:T(8,128)(2,1)S(1)}, u32[]{:S(2)}, u32[]{:S(2)}) collective-permute-start(bf16[2,256,128]{2,1,0:T(8,128)(2,1)S(1)} %fusion), channel_id=1, source_target_pairs={{0,256},{256,512},{512,0},{1,257},{257,513},{513,1},{2,258},{258,5... | collective-permute-start | bytes 393224 | tf_op jit(solution)/shard_map/ppermute | solution.py:247
  119.4 2.8 %collective-permute-start.4 = (bf16[2,256,128]{2,1,0:T(8,128)(2,1)S(1)}, bf16[2,256,128]{2,1,0:T(8,128)(2,1)S(1)}, u32[]{:S(2)}, u32[]{:S(2)}) collective-permute-start(bf16[2,256,128]{2,1,0:T(8,128)(2,1)S(1)} %fusion), channel_id=1, source_target_pairs={{0,512},{256,0},{512,256},{1,513},{257,1},{513,257},{2,514},{258,2... | collective-permute-start | bytes 393224 | tf_op jit(solution)/shard_map/ppermute | solution.py:247
  122.4 4.7 %collective-permute-done.3 = bf16[2,256,128]{2,1,0:T(8,128)(2,1)S(1)} collective-permute-done((bf16[2,256,128]{2,1,0:T(8,128)(2,1)S(1)}, bf16[2,256,128]{2,1,0:T(8,128)(2,1)S(1)}, u32[]{:S(2)}, u32[]{:S(2)}) %collective-permute-start.3) | collective-permute-done | bytes 131104 | tf_op jit(solution)/shard_map/ppermute | solution.py:247
  127.1 2.8 %collective-permute-done.4 = bf16[2,256,128]{2,1,0:T(8,128)(2,1)S(1)} collective-permute-done((bf16[2,256,128]{2,1,0:T(8,128)(2,1)S(1)}, bf16[2,256,128]{2,1,0:T(8,128)(2,1)S(1)}, u32[]{:S(2)}, u32[]{:S(2)}) %collective-permute-start.4) | collective-permute-done | bytes 131104 | tf_op jit(solution)/shard_map/ppermute | solution.py:247
  130.1 7.4 %all-to-all-done.3.a_ref = bf16[8,2,256,128]{3,2,1,0:T(8,128)(2,1)S(1)} async-done(((bf16[8,2,256,128]{3,2,1,0:T(8,128)(2,1)}), bf16[8,2,256,128]{3,2,1,0:T(8,128)(2,1)S(1)}, u32[]{:S(2)}, u32[]{:S(2)}) %all-to-all-start.3) | async-done | bytes 1048608 | tf_op jit(solution)/shard_map/all_to_all | solution.py:238
  137.5 3.8 %scores.1 = (f32[8,384]{1,0:T(8,128)S(1)}, bf16[4,2,256,384]{3,2,1,0:T(8,128)(2,1)S(1)}, bf16[4,2,256,256]{3,2,1,0:T(8,128)(2,1)S(1)}) custom-call(s32[2]{0:T(128)S(1)} %pad_add_fusion.1.place_ref, bf16[3,2,256,128]{3,2,1,0:T(8,128)(2,1)S(1)} %pad_maximum_fusion.1.n_ref, bf16[8,2,256,128]{3,2,1,0:T(8,128)(2,1)S(1)} %all-to-all-done.3.a_ref, ...), custom_call_target="tpu_custom_call" | custom-call | flops 2147483648 | bytes 4194304 | tf_op jit(solution)/shard_map/scores/pallas_call | solution.py:319
  141.3 5.7 %collective-permute-start.7 = (f32[8,384]{1,0:T(8,128)S(1)}, f32[8,384]{1,0:T(8,128)S(1)}, u32[]{:S(2)}, u32[]{:S(2)}) collective-permute-start(f32[8,384]{1,0:T(8,128)S(1)} %get-tuple-element.29.refs_0_), channel_id=1, source_target_pairs={{0,256},{256,512},{512,0},{1,257},{257,513},{513,1},{2,258},{258,5... | collective-permute-start | bytes 36872 | tf_op jit(solution)/shard_map/ppermute | solution.py:247
  147.0 1.9 collective-permute-start.8
  149.6 1.8 collective-permute-done.8.refs_2_
  151.4 4.1 %grads.1 = (f32[8,384]{1,0:T(8,128)S(1)}, f32[256,256]{1,0:T(8,128)S(1)}) custom-call(s32[2]{0:T(128)S(1)} %pad_add_fusion.1.place_ref, bf16[3,2,256,128]{3,2,1,0:T(8,128)(2,1)S(1)} %pad_maximum_fusion.1.n_ref, bf16[8,2,256,128]{3,2,1,0:T(8,128)(2,1)S(1)} %all-to-all-done.3.a_ref, bf16[256,256]{1,0:T(8,128)(2,1)S(1)} %bitcast.39, ...), custom_call_target="tpu_custom_call" | custom-call | flops 2147483648 | bytes 4194304 | tf_op jit(solution)/shard_map/grads/pallas_call | solution.py:337
  155.5 5.5 %all_to_all.45 = f32[2,256,128]{2,1,0:T(8,128)S(1)} all-to-all(f32[2,256,128]{2,1,0:T(8,128)S(1)} %reshape_reshape.6), channel_id=1, replica_groups=mesh['zl'=3,'y'=8,'x'=4,'zh'=4,'core'=2] {'core'}, dimensions={0} | all-to-all | bytes 524288 | tf_op jit(solution)/shard_map/all_to_all | solution.py:238
  161.0 12.8 %all_to_all.46 = f32[32,8,128]{2,1,0:T(8,128)S(1)} all-to-all(f32[32,8,128]{2,1,0:T(8,128)S(1)} %bitcast.45), channel_id=1, replica_groups=mesh['zl'=3,'y'=8,'x'=4,'zh'=4,'core'=2] {'y','x'}, dimensions={0} | all-to-all | bytes 262144 | tf_op jit(solution)/shard_map/all_to_all | solution.py:238
  173.9 21.1 %all_to_all.47 = f32[12,8,128]{2,1,0:T(8,128)S(1)} all-to-all(f32[12,8,128]{2,1,0:T(8,128)S(1)} %broadcast_in_dim.60), channel_id=1, replica_groups=mesh['zl'=3,'y'=8,'x'=4,'zh'=4,'core'=2] {'zl','zh'}, dimensions={0} | all-to-all | bytes 98304 | tf_op jit(solution)/shard_map/all_to_all | solution.py:238
  195.7 3.9 %all-to-all-start.7 = ((f32[32,8,128]{2,1,0:T(8,128)}), f32[32,8,128]{2,1,0:T(8,128)S(1)}, u32[]{:S(2)}, u32[]{:S(2)}) async-start(f32[32,8,128]{2,1,0:T(8,128)} %broadcast_in_dim.61), calls=%async_computation.7 | async-start | bytes 262144 | tf_op jit(solution)/shard_map/all_to_all | solution.py:238
  200.1 8.8 %all-to-all-done.7 = f32[32,8,128]{2,1,0:T(8,128)S(1)} async-done(((f32[32,8,128]{2,1,0:T(8,128)}), f32[32,8,128]{2,1,0:T(8,128)S(1)}, u32[]{:S(2)}, u32[]{:S(2)}) %all-to-all-start.7) | async-done | bytes 131104 | tf_op jit(solution)/shard_map/all_to_all | solution.py:238
  208.9 8.3 %all_to_all.48 = f32[2,256,128]{2,1,0:T(8,128)S(1)} all-to-all(f32[2,256,128]{2,1,0:T(8,128)S(1)} %broadcast_in_dim.63), channel_id=1, replica_groups=mesh['zl'=3,'y'=8,'x'=4,'zh'=4,'core'=2] {'core'}, dimensions={0} | all-to-all | bytes 524288 | tf_op jit(solution)/shard_map/all_to_all | solution.py:238
  (52 shorter events, 7.6 us)
Async XLA Ops:
  0.6 17.5 %copy-start.4 = (s32[12]{0:T(128)S(1)}, s32[12]{0:T(128)}, u32[]{:S(2)}) copy-start(s32[12]{0:T(128)} %param.10) | copy-start | bytes 148
  0.6 17.5 %copy-start.5 = (s32[2,12]{1,0:T(2,128)S(1)}, s32[2,12]{1,0:T(2,128)}, u32[]{:S(2)}) copy-start(s32[2,12]{1,0:T(2,128)} %param.11) | copy-start | bytes 292
  0.7 17.6 %copy-start.1 = (bf16[12,128,128]{2,1,0:T(8,128)(2,1)S(1)}, bf16[12,128,128]{2,1,0:T(8,128)(2,1)}, u32[]{:S(2)}) copy-start(bf16[12,128,128]{2,1,0:T(8,128)(2,1)} %param.9) | copy-start | bytes 1179652
  2.4 35.5 %all-to-all-start = ((bf16[12,88,128]{2,1,0:T(8,128)(2,1)}), bf16[12,88,128]{2,1,0:T(8,128)(2,1)S(1)}, u32[]{:S(2)}, u32[]{:S(2)}) async-start(bf16[12,88,128]{2,1,0:T(8,128)(2,1)} %bitcast.7), calls=%async_computation | async-start | bytes 540672 | tf_op jit(solution)/shard_map/all_to_all | solution.py:238
  18.3 19.7 %collective-permute-start = (bf16[1552,128]{1,0:T(8,128)(2,1)S(1)}, bf16[1552,128]{1,0:T(8,128)(2,1)S(1)}, u32[]{:S(2)}, u32[]{:S(2)}) collective-permute-start(bf16[1552,128]{1,0:T(8,128)(2,1)S(1)} %pad_maximum_fusion.refs_0_), channel_id=1, source_target_pairs={{0,256},{256,512},{512,0},{1,257},{257,513},{513,1},{2,258},{258,5... | collective-permute-start | bytes 1191944 | tf_op jit(solution)/shard_map/ppermute | solution.py:247
  39.1 17.6 %all-to-all-start.1 = ((bf16[4,12,88,128]{3,2,1,0:T(8,128)(2,1)}), bf16[4,12,88,128]{3,2,1,0:T(8,128)(2,1)S(1)}, u32[]{:S(2)}, u32[]{:S(2)}) async-start(bf16[4,12,88,128]{3,2,1,0:T(8,128)(2,1)} %broadcast_in_dim.57), calls=%async_computation.1 | async-start | bytes 2162688 | tf_op jit(solution)/shard_map/all_to_all | solution.py:238
  43.1 10.7 %collective-permute-start.1 = (bf16[1552,128]{1,0:T(8,128)(2,1)S(1)}, bf16[1552,128]{1,0:T(8,128)(2,1)S(1)}, u32[]{:S(2)}, u32[]{:S(2)}) collective-permute-start(bf16[1552,128]{1,0:T(8,128)(2,1)S(1)} %pad_maximum_fusion.refs_0_), channel_id=1, source_target_pairs={{0,512},{256,0},{512,256},{1,513},{257,1},{513,257},{2,514},{258,2... | collective-permute-start | bytes 1191944 | tf_op jit(solution)/shard_map/ppermute | solution.py:247
  56.7 7.0 %collective-permute-start.2 = (bf16[4,12,88,128]{3,2,1,0:T(8,128)(2,1)S(1)}, bf16[4,12,88,128]{3,2,1,0:T(8,128)(2,1)S(1)}, u32[]{:S(2)}, u32[]{:S(2)}) collective-permute-start(bf16[4,12,88,128]{3,2,1,0:T(8,128)(2,1)S(1)} %all-to-all-done.1.own_ref), channel_id=1, source_target_pairs={{0,1},{1,0},{2,3},{3,2},{4,5},{5,4},{6,7},{7,6},{8,9},{9,8},{10,11... | collective-permute-start | bytes 3244040 | tf_op jit(solution)/shard_map/ppermute | solution.py:247
  66.4 8.3 %copy-start.3 = (s32[2,256]{1,0:T(2,128)S(1)}, s32[2,256]{1,0:T(2,128)}, u32[]{:S(2)}) copy-start(s32[2,256]{1,0:T(2,128)} %param.12) | copy-start | bytes 6148
  66.4 8.3 %copy-start = (s32[128,1024]{1,0:T(8,128)S(1)}, s32[128,1024]{1,0:T(8,128)}, u32[]{:S(2)}) copy-start(s32[128,1024]{1,0:T(8,128)} %neg_ref) | copy-start | bytes 1572868
  66.4 33.8 %all-to-all-start.2 = ((bf16[24,2,88,128]{3,2,1,0:T(8,128)(2,1)}), bf16[24,2,88,128]{3,2,1,0:T(8,128)(2,1)S(1)}, u32[]{:S(2)}, u32[]{:S(2)}) async-start(bf16[24,2,88,128]{3,2,1,0:T(8,128)(2,1)} %tile_sums.1), calls=%async_computation.2 | async-start | bytes 2162688 | tf_op jit(solution)/shard_map/all_to_all | solution.py:238
  101.6 35.9 %all-to-all-start.3 = ((bf16[8,2,256,128]{3,2,1,0:T(8,128)(2,1)}), bf16[8,2,256,128]{3,2,1,0:T(8,128)(2,1)S(1)}, u32[]{:S(2)}, u32[]{:S(2)}) async-start(bf16[8,2,256,128]{3,2,1,0:T(8,128)(2,1)} %broadcast_in_dim.58), calls=%async_computation.3 | async-start | bytes 2097152 | tf_op jit(solution)/shard_map/all_to_all | solution.py:238
  108.3 13.9 %copy-start.2 = (bf16[256,256]{1,0:T(8,128)(2,1)S(1)}, bf16[256,256]{1,0:T(8,128)(2,1)}, u32[]{:S(2)}) copy-start(bf16[256,256]{1,0:T(8,128)(2,1)} %param.8) | copy-start | bytes 393220
  108.4 21.5 %collective-permute-start.5 = (s16[8,128,128]{2,1,0:T(8,128)(2,1)S(1)}, s16[8,128,128]{2,1,0:T(8,128)(2,1)S(1)}, u32[]{:S(2)}, u32[]{:S(2)}) collective-permute-start(s16[8,128,128]{2,1,0:T(8,128)(2,1)S(1)} %get-tuple-element.36), channel_id=1, source_target_pairs={{0,256},{256,512},{512,0},{1,257},{257,513},{513,1},{2,258},{258,5... | collective-permute-start | bytes 786440 | tf_op jit(solution)/shard_map/ppermute | solution.py:247
  114.1 15.9 %collective-permute-start.6 = (s16[8,128,128]{2,1,0:T(8,128)(2,1)S(1)}, s16[8,128,128]{2,1,0:T(8,128)(2,1)S(1)}, u32[]{:S(2)}, u32[]{:S(2)}) collective-permute-start(s16[8,128,128]{2,1,0:T(8,128)(2,1)S(1)} %get-tuple-element.35), channel_id=1, source_target_pairs={{0,512},{256,0},{512,256},{1,513},{257,1},{513,257},{2,514},{258,2... | collective-permute-start | bytes 786440 | tf_op jit(solution)/shard_map/ppermute | solution.py:247
  116.0 11.1 %collective-permute-start.3 = (bf16[2,256,128]{2,1,0:T(8,128)(2,1)S(1)}, bf16[2,256,128]{2,1,0:T(8,128)(2,1)S(1)}, u32[]{:S(2)}, u32[]{:S(2)}) collective-permute-start(bf16[2,256,128]{2,1,0:T(8,128)(2,1)S(1)} %fusion), channel_id=1, source_target_pairs={{0,256},{256,512},{512,0},{1,257},{257,513},{513,1},{2,258},{258,5... | collective-permute-start | bytes 393224 | tf_op jit(solution)/shard_map/ppermute | solution.py:247
  119.4 10.5 %collective-permute-start.4 = (bf16[2,256,128]{2,1,0:T(8,128)(2,1)S(1)}, bf16[2,256,128]{2,1,0:T(8,128)(2,1)S(1)}, u32[]{:S(2)}, u32[]{:S(2)}) collective-permute-start(bf16[2,256,128]{2,1,0:T(8,128)(2,1)S(1)} %fusion), channel_id=1, source_target_pairs={{0,512},{256,0},{512,256},{1,513},{257,1},{513,257},{2,514},{258,2... | collective-permute-start | bytes 393224 | tf_op jit(solution)/shard_map/ppermute | solution.py:247
  141.3 8.3 %collective-permute-start.7 = (f32[8,384]{1,0:T(8,128)S(1)}, f32[8,384]{1,0:T(8,128)S(1)}, u32[]{:S(2)}, u32[]{:S(2)}) collective-permute-start(f32[8,384]{1,0:T(8,128)S(1)} %get-tuple-element.29.refs_0_), channel_id=1, source_target_pairs={{0,256},{256,512},{512,0},{1,257},{257,513},{513,1},{2,258},{258,5... | collective-permute-start | bytes 36872 | tf_op jit(solution)/shard_map/ppermute | solution.py:247
  147.0 4.4 %collective-permute-start.8 = (f32[8,384]{1,0:T(8,128)S(1)}, f32[8,384]{1,0:T(8,128)S(1)}, u32[]{:S(2)}, u32[]{:S(2)}) collective-permute-start(f32[8,384]{1,0:T(8,128)S(1)} %get-tuple-element.29.refs_0_), channel_id=1, source_target_pairs={{0,512},{256,0},{512,256},{1,513},{257,1},{513,257},{2,514},{258,2... | collective-permute-start | bytes 36872 | tf_op jit(solution)/shard_map/ppermute | solution.py:247
  195.7 13.2 %all-to-all-start.7 = ((f32[32,8,128]{2,1,0:T(8,128)}), f32[32,8,128]{2,1,0:T(8,128)S(1)}, u32[]{:S(2)}, u32[]{:S(2)}) async-start(f32[32,8,128]{2,1,0:T(8,128)} %broadcast_in_dim.61), calls=%async_computation.7 | async-start | bytes 262144 | tf_op jit(solution)/shard_map/all_to_all | solution.py:238

commit v8 on v7

--- a/solution.py
+++ b/solution.py
@@ -291,7 +291,8 @@
     near = swap(sent, ("zl", "zh"))
     held = packed(tiles, tile_pos, edge_keep, cols)
     next_tiles = shift(held, "zl", 1)
-    near, next_tiles = lax.optimization_barrier((near, next_tiles))
+    counts = count_negatives(negatives, ZL * ysize)
+    near, next_tiles, counts = lax.optimization_barrier((near, next_tiles, counts))
     own = share(near, "x")
     last_tiles = shift(held, "zl", 2)
     own, last_tiles = lax.optimization_barrier((own, last_tiles))
@@ -300,18 +301,16 @@
     metas = jnp.stack([x[slots * T : slots * T + 4, :slots] for x in all_tiles]).astype(jnp.int32)
 
     part = tile_sums(metas, place, own, other, all_tiles, cols, ZL * ysize)
-    part, negatives = lax.optimization_barrier((part, negatives))
+    part, counts = lax.optimization_barrier((part, counts))
     got = swap(part, ROW)
-    counts = count_negatives(negatives, ZL * ysize)
+    ahead = lambda x, s: lax.dynamic_index_in_dim(x, lax.rem(zl + s, ZL), 0, keepdims=False)
+    counts = jnp.stack(around(counts.reshape(ZL, ysize, nodes, nodes), ahead, "zl"))
     got, counts = lax.optimization_barrier((got, counts))
     agg = jnp.sum(got.reshape(ZL, ysize, 2, FS, nodes).astype(f32), 1)
     agg = agg.transpose(1, 0, 2, 3).reshape(2, ZL * FS, nodes)[:, :width]
     agg = (agg * feature_keep.astype(f32)[:, :, None]).astype(bf16)
-    agg, counts = lax.optimization_barrier((agg, counts))
     members = share(agg, "y")
     anchors = jnp.stack(around(agg, whole, "zl"))
-    ahead = lambda x, s: lax.dynamic_index_in_dim(x, lax.rem(zl + s, ZL), 0, keepdims=False)
-    counts = jnp.stack(around(counts.reshape(ZL, ysize, nodes, nodes), ahead, "zl"))
 
     weight_t = weight.T
     group = ZL * nodes

time: 219 us -> 220 us (level)
  waiting for transfers between devices: 65.1 us -> 69.4 us
  starting transfers between devices: 70.8 us -> 67.8 us
  blocking collectives: 47.7 us -> 45.5 us
    ppermute x9, waiting for transfers between devices: 35.8 us -> 39.3 us  [shift(): return lax.ppermute(x, axis, [(i, (i + by) % size) for i in range(size)])]
    ppermute x9, starting transfers between devices: 32.2 us -> 29.4 us  [shift(): return lax.ppermute(x, axis, [(i, (i + by) % size) for i in range(size)])]
  transfers between devices with their start and end apart: 14 -> 14, of which waited for: 10 -> 11; matrix products, arithmetic and copies ran while one was open for 0% -> 1% of each run, Pallas kernels for 7% -> 7%
where the time goes in v8:
time: 220 us; the launch traced here: 219 us
  waiting for transfers between devices  69.4 us (32%)
  starting transfers between devices  67.8 us (31%)
  blocking collectives  45.5 us (21%)
  Pallas kernels  27.2 us (12%)
  local copies, waits for them, and re-layouts  7.65 us (3%)
    all_to_all x4, blocking collectives, swap(): return lax.all_to_all(x, axis, 0, 0, tiled=True)  45.5 us
    ppermute x9, waiting for transfers between devices, shift(): return lax.ppermute(x, axis, [(i, (i + by) % size) for i in range(size)])  39.3 us
    all_to_all x5, starting transfers between devices, swap(): return lax.all_to_all(x, axis, 0, 0, tiled=True)  38.4 us
    all_to_all x5, waiting for transfers between devices, swap(): return lax.all_to_all(x, axis, 0, 0, tiled=True)  30 us
    ppermute x9, starting transfers between devices, shift(): return lax.ppermute(x, axis, [(i, (i + by) % size) for i in range(size)])  29.4 us
    pallas_call x1, Pallas kernels, count_negatives(): pl.pallas_call(functools.partial(counts_kernel, blocks), out_shape=jax.Sh...  15.3 us
  transfers between devices with their start and end apart: 14, of which 11 were waited for; matrix products, arithmetic and copies ran while one was open for 1% of the time, Pallas kernels for 7%

profile of v8, /device:TPU:1, one launch (start us, length us, event | category | flops | bytes accessed | tf_op | source)
XLA Modules:
  0.0 219.3 jit_solution(7896355730648189364)
XLA Ops:
  2.5 15.7 %all-to-all-start = ((bf16[12,88,128]{2,1,0:T(8,128)(2,1)}), bf16[12,88,128]{2,1,0:T(8,128)(2,1)S(1)}, u32[]{:S(2)}, u32[]{:S(2)}) async-start(bf16[12,88,128]{2,1,0:T(8,128)(2,1)} %bitcast.7), calls=%async_computation | async-start | bytes 540672 | tf_op jit(solution)/shard_map/all_to_all | solution.py:238
  18.3 3.3 %collective-permute-start = (bf16[1552,128]{1,0:T(8,128)(2,1)S(1)}, bf16[1552,128]{1,0:T(8,128)(2,1)}, u32[]{:S(2)}, u32[]{:S(2)}) collective-permute-start(bf16[1552,128]{1,0:T(8,128)(2,1)S(1)} %pad_maximum_fusion.refs_0_), channel_id=1, source_target_pairs={{0,256},{256,512},{512,0},{1,257},{257,513},{513,1},{2,258},{258,5... | collective-permute-start | bytes 1191944 | tf_op jit(solution)/shard_map/ppermute | solution.py:247
  21.6 15.3 %counts.1 = s16[24,128,128]{2,1,0:T(8,128)(2,1)S(1)} custom-call(s32[128,1024]{1,0:T(8,128)S(1)} %copy-done), custom_call_target="tpu_custom_call" | custom-call | flops 4294967296 | bytes 2097152 | tf_op jit(solution)/shard_map/counts/pallas_call | solution.py:66
  36.9 1.1 collective-permute-done.refs_1_
  39.2 4.0 %all-to-all-start.1 = ((bf16[4,12,88,128]{3,2,1,0:T(8,128)(2,1)}), bf16[4,12,88,128]{3,2,1,0:T(8,128)(2,1)S(1)}, u32[]{:S(2)}, u32[]{:S(2)}) async-start(bf16[4,12,88,128]{3,2,1,0:T(8,128)(2,1)} %broadcast_in_dim.57), calls=%async_computation.1 | async-start | bytes 2162688 | tf_op jit(solution)/shard_map/all_to_all | solution.py:238
  43.2 2.8 %collective-permute-start.1 = (bf16[1552,128]{1,0:T(8,128)(2,1)S(1)}, bf16[1552,128]{1,0:T(8,128)(2,1)}, u32[]{:S(2)}, u32[]{:S(2)}) collective-permute-start(bf16[1552,128]{1,0:T(8,128)(2,1)S(1)} %pad_maximum_fusion.refs_0_), channel_id=1, source_target_pairs={{0,512},{256,0},{512,256},{1,513},{257,1},{513,257},{2,514},{258,2... | collective-permute-start | bytes 1191944 | tf_op jit(solution)/shard_map/ppermute | solution.py:247
  46.1 8.0 %collective-permute-done.1.refs_2_ = bf16[1552,128]{1,0:T(8,128)(2,1)} collective-permute-done((bf16[1552,128]{1,0:T(8,128)(2,1)S(1)}, bf16[1552,128]{1,0:T(8,128)(2,1)}, u32[]{:S(2)}, u32[]{:S(2)}) %collective-permute-start.1) | collective-permute-done | bytes 397344 | tf_op jit(solution)/shard_map/ppermute | solution.py:247
  54.1 2.8 %all-to-all-done.1.own_ref = bf16[4,12,88,128]{3,2,1,0:T(8,128)(2,1)S(1)} async-done(((bf16[4,12,88,128]{3,2,1,0:T(8,128)(2,1)}), bf16[4,12,88,128]{3,2,1,0:T(8,128)(2,1)S(1)}, u32[]{:S(2)}, u32[]{:S(2)}) %all-to-all-start.1) | async-done | bytes 1081376 | tf_op jit(solution)/shard_map/all_to_all | solution.py:238
  56.8 4.7 %collective-permute-start.2 = (bf16[4,12,88,128]{3,2,1,0:T(8,128)(2,1)S(1)}, bf16[4,12,88,128]{3,2,1,0:T(8,128)(2,1)S(1)}, u32[]{:S(2)}, u32[]{:S(2)}) collective-permute-start(bf16[4,12,88,128]{3,2,1,0:T(8,128)(2,1)S(1)} %all-to-all-done.1.own_ref), channel_id=1, source_target_pairs={{0,1},{1,0},{2,3},{3,2},{4,5},{5,4},{6,7},{7,6},{8,9},{9,8},{10,11... | collective-permute-start | bytes 3244040 | tf_op jit(solution)/shard_map/ppermute | solution.py:247
  63.8 3.3 %tile_sums.1 = bf16[24,2,88,128]{3,2,1,0:T(8,128)(2,1)} custom-call(s32[3,4,12]{2,1,0:T(4,128)S(1)} %maximum_convert_fusion.meta_ref, s32[2]{0:T(128)S(1)} %pad_add_fusion.1.place_ref, bf16[4,12,88,128]{3,2,1,0:T(8,128)(2,1)S(1)} %all-to-all-done.1.own_ref, bf16[4,12,88,128]{3,2,1,0:T(8,128)(2,1)S(1)} %collective-permute-done.2.other_ref, ...), custom_call_target="tpu_custom_call" | custom-call | tf_op jit(solution)/shard_map/tile_sums/pallas_call | solution.py:120
  67.2 7.5 %all-to-all-start.2 = ((bf16[24,2,88,128]{3,2,1,0:T(8,128)(2,1)}), bf16[24,2,88,128]{3,2,1,0:T(8,128)(2,1)S(1)}, u32[]{:S(2)}, u32[]{:S(2)}) async-start(bf16[24,2,88,128]{3,2,1,0:T(8,128)(2,1)} %tile_sums.1), calls=%async_computation.2 | async-start | bytes 2162688 | tf_op jit(solution)/shard_map/all_to_all | solution.py:238
  74.8 3.2 %collective-permute-start.3 = (s16[8,128,128]{2,1,0:T(8,128)(2,1)S(1)}, s16[8,128,128]{2,1,0:T(8,128)(2,1)S(1)}, u32[]{:S(2)}, u32[]{:S(2)}) collective-permute-start(s16[8,128,128]{2,1,0:T(8,128)(2,1)S(1)} %get-tuple-element.34), channel_id=1, source_target_pairs={{0,256},{256,512},{512,0},{1,257},{257,513},{513,1},{2,258},{258,5... | collective-permute-start | bytes 786440 | tf_op jit(solution)/shard_map/ppermute | solution.py:247
  78.1 3.0 %collective-permute-start.4 = (s16[8,128,128]{2,1,0:T(8,128)(2,1)S(1)}, s16[8,128,128]{2,1,0:T(8,128)(2,1)S(1)}, u32[]{:S(2)}, u32[]{:S(2)}) collective-permute-start(s16[8,128,128]{2,1,0:T(8,128)(2,1)S(1)} %get-tuple-element.33), channel_id=1, source_target_pairs={{0,512},{256,0},{512,256},{1,513},{257,1},{513,257},{2,514},{258,2... | collective-permute-start | bytes 786440 | tf_op jit(solution)/shard_map/ppermute | solution.py:247
  81.1 17.7 %collective-permute-done.3 = s16[8,128,128]{2,1,0:T(8,128)(2,1)S(1)} collective-permute-done((s16[8,128,128]{2,1,0:T(8,128)(2,1)S(1)}, s16[8,128,128]{2,1,0:T(8,128)(2,1)S(1)}, u32[]{:S(2)}, u32[]{:S(2)}) %collective-permute-start.3) | collective-permute-done | bytes 262176 | tf_op jit(solution)/shard_map/ppermute | solution.py:247
  98.7 5.7 %collective-permute-done.4 = s16[8,128,128]{2,1,0:T(8,128)(2,1)S(1)} collective-permute-done((s16[8,128,128]{2,1,0:T(8,128)(2,1)S(1)}, s16[8,128,128]{2,1,0:T(8,128)(2,1)S(1)}, u32[]{:S(2)}, u32[]{:S(2)}) %collective-permute-start.4) | collective-permute-done | bytes 262176 | tf_op jit(solution)/shard_map/ppermute | solution.py:247
  104.8 1.2 broadcast_in_dim.58
  106.0 7.3 %all-to-all-start.3 = ((bf16[8,2,256,128]{3,2,1,0:T(8,128)(2,1)}), bf16[8,2,256,128]{3,2,1,0:T(8,128)(2,1)S(1)}, u32[]{:S(2)}, u32[]{:S(2)}) async-start(bf16[8,2,256,128]{3,2,1,0:T(8,128)(2,1)} %broadcast_in_dim.58), calls=%async_computation.3 | async-start | bytes 2097152 | tf_op jit(solution)/shard_map/all_to_all | solution.py:238
  113.4 4.2 %collective-permute-start.5 = (bf16[2,256,128]{2,1,0:T(8,128)(2,1)S(1)}, bf16[2,256,128]{2,1,0:T(8,128)(2,1)S(1)}, u32[]{:S(2)}, u32[]{:S(2)}) collective-permute-start(bf16[2,256,128]{2,1,0:T(8,128)(2,1)S(1)} %fusion), channel_id=1, source_target_pairs={{0,256},{256,512},{512,0},{1,257},{257,513},{513,1},{2,258},{258,5... | collective-permute-start | bytes 393224 | tf_op jit(solution)/shard_map/ppermute | solution.py:247
  117.6 2.0 collective-permute-start.6
  120.0 4.1 %collective-permute-done.6 = bf16[2,256,128]{2,1,0:T(8,128)(2,1)S(1)} collective-permute-done((bf16[2,256,128]{2,1,0:T(8,128)(2,1)S(1)}, bf16[2,256,128]{2,1,0:T(8,128)(2,1)S(1)}, u32[]{:S(2)}, u32[]{:S(2)}) %collective-permute-start.6) | collective-permute-done | bytes 131104 | tf_op jit(solution)/shard_map/ppermute | solution.py:247
  124.1 18.4 %all-to-all-done.3.a_ref = bf16[8,2,256,128]{3,2,1,0:T(8,128)(2,1)S(1)} async-done(((bf16[8,2,256,128]{3,2,1,0:T(8,128)(2,1)}), bf16[8,2,256,128]{3,2,1,0:T(8,128)(2,1)S(1)}, u32[]{:S(2)}, u32[]{:S(2)}) %all-to-all-start.3) | async-done | bytes 1048608 | tf_op jit(solution)/shard_map/all_to_all | solution.py:238
  142.5 3.8 %scores.1 = (f32[8,384]{1,0:T(8,128)S(1)}, bf16[4,2,256,384]{3,2,1,0:T(8,128)(2,1)S(1)}, bf16[4,2,256,256]{3,2,1,0:T(8,128)(2,1)S(1)}) custom-call(s32[2]{0:T(128)S(1)} %pad_add_fusion.1.place_ref, bf16[3,2,256,128]{3,2,1,0:T(8,128)(2,1)S(1)} %pad_maximum_fusion.1.n_ref, bf16[8,2,256,128]{3,2,1,0:T(8,128)(2,1)S(1)} %all-to-all-done.3.a_ref, ...), custom_call_target="tpu_custom_call" | custom-call | flops 2147483648 | bytes 4194304 | tf_op jit(solution)/shard_map/scores/pallas_call | solution.py:318
  146.3 4.2 %collective-permute-start.7 = (f32[8,384]{1,0:T(8,128)S(1)}, f32[8,384]{1,0:T(8,128)S(1)}, u32[]{:S(2)}, u32[]{:S(2)}) collective-permute-start(f32[8,384]{1,0:T(8,128)S(1)} %get-tuple-element.27.refs_0_), channel_id=1, source_target_pairs={{0,256},{256,512},{512,0},{1,257},{257,513},{513,1},{2,258},{258,5... | collective-permute-start | bytes 36872 | tf_op jit(solution)/shard_map/ppermute | solution.py:247
  150.4 2.0 collective-permute-start.8
  153.2 1.7 collective-permute-done.8.refs_2_
  154.9 4.0 %grads.1 = (f32[8,384]{1,0:T(8,128)S(1)}, f32[256,256]{1,0:T(8,128)S(1)}) custom-call(s32[2]{0:T(128)S(1)} %pad_add_fusion.1.place_ref, bf16[3,2,256,128]{3,2,1,0:T(8,128)(2,1)S(1)} %pad_maximum_fusion.1.n_ref, bf16[8,2,256,128]{3,2,1,0:T(8,128)(2,1)S(1)} %all-to-all-done.3.a_ref, bf16[256,256]{1,0:T(8,128)(2,1)S(1)} %bitcast.40, ...), custom_call_target="tpu_custom_call" | custom-call | flops 2147483648 | bytes 4194304 | tf_op jit(solution)/shard_map/grads/pallas_call | solution.py:336
  158.9 5.5 %all_to_all.45 = f32[2,256,128]{2,1,0:T(8,128)S(1)} all-to-all(f32[2,256,128]{2,1,0:T(8,128)S(1)} %reshape_reshape.6), channel_id=1, replica_groups=mesh['zl'=3,'y'=8,'x'=4,'zh'=4,'core'=2] {'core'}, dimensions={0} | all-to-all | bytes 524288 | tf_op jit(solution)/shard_map/all_to_all | solution.py:238
  164.5 12.8 %all_to_all.46 = f32[32,8,128]{2,1,0:T(8,128)S(1)} all-to-all(f32[32,8,128]{2,1,0:T(8,128)S(1)} %bitcast.46), channel_id=1, replica_groups=mesh['zl'=3,'y'=8,'x'=4,'zh'=4,'core'=2] {'y','x'}, dimensions={0} | all-to-all | bytes 262144 | tf_op jit(solution)/shard_map/all_to_all | solution.py:238
  177.3 19.4 %all_to_all.47 = f32[12,8,128]{2,1,0:T(8,128)S(1)} all-to-all(f32[12,8,128]{2,1,0:T(8,128)S(1)} %broadcast_in_dim.60), channel_id=1, replica_groups=mesh['zl'=3,'y'=8,'x'=4,'zh'=4,'core'=2] {'zl','zh'}, dimensions={0} | all-to-all | bytes 98304 | tf_op jit(solution)/shard_map/all_to_all | solution.py:238
  197.4 3.9 %all-to-all-start.7 = ((f32[32,8,128]{2,1,0:T(8,128)}), f32[32,8,128]{2,1,0:T(8,128)S(1)}, u32[]{:S(2)}, u32[]{:S(2)}) async-start(f32[32,8,128]{2,1,0:T(8,128)} %broadcast_in_dim.61), calls=%async_computation.7 | async-start | bytes 262144 | tf_op jit(solution)/shard_map/all_to_all | solution.py:238
  201.8 8.9 %all-to-all-done.7 = f32[32,8,128]{2,1,0:T(8,128)S(1)} async-done(((f32[32,8,128]{2,1,0:T(8,128)}), f32[32,8,128]{2,1,0:T(8,128)S(1)}, u32[]{:S(2)}, u32[]{:S(2)}) %all-to-all-start.7) | async-done | bytes 131104 | tf_op jit(solution)/shard_map/all_to_all | solution.py:238
  210.7 7.8 %all_to_all.48 = f32[2,256,128]{2,1,0:T(8,128)S(1)} all-to-all(f32[2,256,128]{2,1,0:T(8,128)S(1)} %broadcast_in_dim.63), channel_id=1, replica_groups=mesh['zl'=3,'y'=8,'x'=4,'zh'=4,'core'=2] {'core'}, dimensions={0} | all-to-all | bytes 524288 | tf_op jit(solution)/shard_map/all_to_all | solution.py:238
  (53 shorter events, 9.1 us)
Async XLA Ops:
  0.6 17.5 %copy-start.4 = (s32[12]{0:T(128)S(1)}, s32[12]{0:T(128)}, u32[]{:S(2)}) copy-start(s32[12]{0:T(128)} %param.10) | copy-start | bytes 148
  0.6 17.6 %copy-start.5 = (s32[2,12]{1,0:T(2,128)S(1)}, s32[2,12]{1,0:T(2,128)}, u32[]{:S(2)}) copy-start(s32[2,12]{1,0:T(2,128)} %param.11) | copy-start | bytes 292
  0.7 17.6 %copy-start.1 = (bf16[12,128,128]{2,1,0:T(8,128)(2,1)S(1)}, bf16[12,128,128]{2,1,0:T(8,128)(2,1)}, u32[]{:S(2)}) copy-start(bf16[12,128,128]{2,1,0:T(8,128)(2,1)} %param.9) | copy-start | bytes 1179652
  0.7 21.0 %copy-start = (s32[128,1024]{1,0:T(8,128)S(1)}, s32[128,1024]{1,0:T(8,128)}, u32[]{:S(2)}) copy-start(s32[128,1024]{1,0:T(8,128)} %neg_ref.1) | copy-start | bytes 1572868
  2.5 35.6 %all-to-all-start = ((bf16[12,88,128]{2,1,0:T(8,128)(2,1)}), bf16[12,88,128]{2,1,0:T(8,128)(2,1)S(1)}, u32[]{:S(2)}, u32[]{:S(2)}) async-start(bf16[12,88,128]{2,1,0:T(8,128)(2,1)} %bitcast.7), calls=%async_computation | async-start | bytes 540672 | tf_op jit(solution)/shard_map/all_to_all | solution.py:238
  18.3 19.8 %collective-permute-start = (bf16[1552,128]{1,0:T(8,128)(2,1)S(1)}, bf16[1552,128]{1,0:T(8,128)(2,1)}, u32[]{:S(2)}, u32[]{:S(2)}) collective-permute-start(bf16[1552,128]{1,0:T(8,128)(2,1)S(1)} %pad_maximum_fusion.refs_0_), channel_id=1, source_target_pairs={{0,256},{256,512},{512,0},{1,257},{257,513},{513,1},{2,258},{258,5... | collective-permute-start | bytes 1191944 | tf_op jit(solution)/shard_map/ppermute | solution.py:247
  39.2 17.6 %all-to-all-start.1 = ((bf16[4,12,88,128]{3,2,1,0:T(8,128)(2,1)}), bf16[4,12,88,128]{3,2,1,0:T(8,128)(2,1)S(1)}, u32[]{:S(2)}, u32[]{:S(2)}) async-start(bf16[4,12,88,128]{3,2,1,0:T(8,128)(2,1)} %broadcast_in_dim.57), calls=%async_computation.1 | async-start | bytes 2162688 | tf_op jit(solution)/shard_map/all_to_all | solution.py:238
  43.2 10.8 %collective-permute-start.1 = (bf16[1552,128]{1,0:T(8,128)(2,1)S(1)}, bf16[1552,128]{1,0:T(8,128)(2,1)}, u32[]{:S(2)}, u32[]{:S(2)}) collective-permute-start(bf16[1552,128]{1,0:T(8,128)(2,1)S(1)} %pad_maximum_fusion.refs_0_), channel_id=1, source_target_pairs={{0,512},{256,0},{512,256},{1,513},{257,1},{513,257},{2,514},{258,2... | collective-permute-start | bytes 1191944 | tf_op jit(solution)/shard_map/ppermute | solution.py:247
  56.8 7.0 %collective-permute-start.2 = (bf16[4,12,88,128]{3,2,1,0:T(8,128)(2,1)S(1)}, bf16[4,12,88,128]{3,2,1,0:T(8,128)(2,1)S(1)}, u32[]{:S(2)}, u32[]{:S(2)}) collective-permute-start(bf16[4,12,88,128]{3,2,1,0:T(8,128)(2,1)S(1)} %all-to-all-done.1.own_ref), channel_id=1, source_target_pairs={{0,1},{1,0},{2,3},{3,2},{4,5},{5,4},{6,7},{7,6},{8,9},{9,8},{10,11... | collective-permute-start | bytes 3244040 | tf_op jit(solution)/shard_map/ppermute | solution.py:247
  67.2 37.3 %all-to-all-start.2 = ((bf16[24,2,88,128]{3,2,1,0:T(8,128)(2,1)}), bf16[24,2,88,128]{3,2,1,0:T(8,128)(2,1)S(1)}, u32[]{:S(2)}, u32[]{:S(2)}) async-start(bf16[24,2,88,128]{3,2,1,0:T(8,128)(2,1)} %tile_sums.1), calls=%async_computation.2 | async-start | bytes 2162688 | tf_op jit(solution)/shard_map/all_to_all | solution.py:238
  74.7 6.3 %copy-start.3 = (s32[2,256]{1,0:T(2,128)S(1)}, s32[2,256]{1,0:T(2,128)}, u32[]{:S(2)}) copy-start(s32[2,256]{1,0:T(2,128)} %param.12) | copy-start | bytes 6148
  74.8 23.9 %collective-permute-start.3 = (s16[8,128,128]{2,1,0:T(8,128)(2,1)S(1)}, s16[8,128,128]{2,1,0:T(8,128)(2,1)S(1)}, u32[]{:S(2)}, u32[]{:S(2)}) collective-permute-start(s16[8,128,128]{2,1,0:T(8,128)(2,1)S(1)} %get-tuple-element.34), channel_id=1, source_target_pairs={{0,256},{256,512},{512,0},{1,257},{257,513},{513,1},{2,258},{258,5... | collective-permute-start | bytes 786440 | tf_op jit(solution)/shard_map/ppermute | solution.py:247
  78.1 26.3 %collective-permute-start.4 = (s16[8,128,128]{2,1,0:T(8,128)(2,1)S(1)}, s16[8,128,128]{2,1,0:T(8,128)(2,1)S(1)}, u32[]{:S(2)}, u32[]{:S(2)}) collective-permute-start(s16[8,128,128]{2,1,0:T(8,128)(2,1)S(1)} %get-tuple-element.33), channel_id=1, source_target_pairs={{0,512},{256,0},{512,256},{1,513},{257,1},{513,257},{2,514},{258,2... | collective-permute-start | bytes 786440 | tf_op jit(solution)/shard_map/ppermute | solution.py:247
  106.0 7.3 %copy-start.2 = (bf16[256,256]{1,0:T(8,128)(2,1)S(1)}, bf16[256,256]{1,0:T(8,128)(2,1)}, u32[]{:S(2)}) copy-start(bf16[256,256]{1,0:T(8,128)(2,1)} %param.8) | copy-start | bytes 393220
  106.0 36.5 %all-to-all-start.3 = ((bf16[8,2,256,128]{3,2,1,0:T(8,128)(2,1)}), bf16[8,2,256,128]{3,2,1,0:T(8,128)(2,1)S(1)}, u32[]{:S(2)}, u32[]{:S(2)}) async-start(bf16[8,2,256,128]{3,2,1,0:T(8,128)(2,1)} %broadcast_in_dim.58), calls=%async_computation.3 | async-start | bytes 2097152 | tf_op jit(solution)/shard_map/all_to_all | solution.py:238
  113.4 6.6 %collective-permute-start.5 = (bf16[2,256,128]{2,1,0:T(8,128)(2,1)S(1)}, bf16[2,256,128]{2,1,0:T(8,128)(2,1)S(1)}, u32[]{:S(2)}, u32[]{:S(2)}) collective-permute-start(bf16[2,256,128]{2,1,0:T(8,128)(2,1)S(1)} %fusion), channel_id=1, source_target_pairs={{0,256},{256,512},{512,0},{1,257},{257,513},{513,1},{2,258},{258,5... | collective-permute-start | bytes 393224 | tf_op jit(solution)/shard_map/ppermute | solution.py:247
  117.6 6.5 %collective-permute-start.6 = (bf16[2,256,128]{2,1,0:T(8,128)(2,1)S(1)}, bf16[2,256,128]{2,1,0:T(8,128)(2,1)S(1)}, u32[]{:S(2)}, u32[]{:S(2)}) collective-permute-start(bf16[2,256,128]{2,1,0:T(8,128)(2,1)S(1)} %fusion), channel_id=1, source_target_pairs={{0,512},{256,0},{512,256},{1,513},{257,1},{513,257},{2,514},{258,2... | collective-permute-start | bytes 393224 | tf_op jit(solution)/shard_map/ppermute | solution.py:247
  146.3 6.9 %collective-permute-start.7 = (f32[8,384]{1,0:T(8,128)S(1)}, f32[8,384]{1,0:T(8,128)S(1)}, u32[]{:S(2)}, u32[]{:S(2)}) collective-permute-start(f32[8,384]{1,0:T(8,128)S(1)} %get-tuple-element.27.refs_0_), channel_id=1, source_target_pairs={{0,256},{256,512},{512,0},{1,257},{257,513},{513,1},{2,258},{258,5... | collective-permute-start | bytes 36872 | tf_op jit(solution)/shard_map/ppermute | solution.py:247
  150.4 4.4 %collective-permute-start.8 = (f32[8,384]{1,0:T(8,128)S(1)}, f32[8,384]{1,0:T(8,128)S(1)}, u32[]{:S(2)}, u32[]{:S(2)}) collective-permute-start(f32[8,384]{1,0:T(8,128)S(1)} %get-tuple-element.27.refs_0_), channel_id=1, source_target_pairs={{0,512},{256,0},{512,256},{1,513},{257,1},{513,257},{2,514},{258,2... | collective-permute-start | bytes 36872 | tf_op jit(solution)/shard_map/ppermute | solution.py:247
  197.4 13.3 %all-to-all-start.7 = ((f32[32,8,128]{2,1,0:T(8,128)}), f32[32,8,128]{2,1,0:T(8,128)S(1)}, u32[]{:S(2)}, u32[]{:S(2)}) async-start(f32[32,8,128]{2,1,0:T(8,128)} %broadcast_in_dim.61), calls=%async_computation.7 | async-start | bytes 262144 | tf_op jit(solution)/shard_map/all_to_all | solution.py:238

commit v9 on v7

--- a/solution.py
+++ b/solution.py
@@ -253,15 +253,11 @@
 
 def reduce_all(grad):
     rows, width = grad.shape
-    planes = ("core",), ("y", "x")
-    part = grad.reshape(-1, T)
-    for axes in planes:
-        got = swap(part.reshape(lax.axis_size(axes), -1, T), axes)
-        part = jnp.sum(got, 0)
+    plane = ("y", "x")
+    part = jnp.sum(swap(grad.reshape(lax.axis_size(plane), -1, width), plane), 0)
+    part = part + shift(part, "core", 1)
     part = jnp.sum(share(part, ("zl", "zh")), 0)
-    for axes in planes[::-1]:
-        part = share(part, axes).reshape(-1, T)
-    return part.reshape(rows, width)
+    return share(part, plane).reshape(rows, width)
 
 
 def packed(tiles, tile_pos, edge_keep, cols):

time: 219 us -> 216 us (0.986)
  blocking collectives: 47.7 us -> 36.6 us
  starting transfers between devices: 70.8 us -> 75.7 us
    all_to_all x4 -> x2, blocking collectives: 47.7 us -> 36.6 us  [swap(): return lax.all_to_all(x, axis, 0, 0, tiled=True)]
    ppermute x9 -> x10, starting transfers between devices: 32.2 us -> 37.1 us  [shift(): return lax.ppermute(x, axis, [(i, (i + by) % size) for i in range(size)])]
    ppermute x9 -> x10, waiting for transfers between devices: 35.8 us -> 36.6 us  [shift(): return lax.ppermute(x, axis, [(i, (i + by) % size) for i in range(size)])]
  transfers between devices with their start and end apart: 14 -> 15, of which waited for: 10 -> 11; matrix products, arithmetic and copies ran while one was open for 0% -> 0% of each run, Pallas kernels for 7% -> 7%
where the time goes in v9:
time: 216 us; the launch traced here: 214 us
  starting transfers between devices  75.7 us (35%)
  waiting for transfers between devices  66.8 us (31%)
  blocking collectives  36.6 us (17%)
  Pallas kernels  26.5 us (12%)
  local copies, waits for them, and re-layouts  6.26 us (3%)
    all_to_all x5, starting transfers between devices, swap(): return lax.all_to_all(x, axis, 0, 0, tiled=True)  38.6 us
    ppermute x10, starting transfers between devices, shift(): return lax.ppermute(x, axis, [(i, (i + by) % size) for i in range(size)])  37.1 us
    all_to_all x2, blocking collectives, swap(): return lax.all_to_all(x, axis, 0, 0, tiled=True)  36.6 us
    ppermute x10, waiting for transfers between devices, shift(): return lax.ppermute(x, axis, [(i, (i + by) % size) for i in range(size)])  36.6 us
    all_to_all x5, waiting for transfers between devices, swap(): return lax.all_to_all(x, axis, 0, 0, tiled=True)  30.2 us
    pallas_call x1, Pallas kernels, count_negatives(): pl.pallas_call(functools.partial(counts_kernel, blocks), out_shape=jax.Sh...  15.3 us
  transfers between devices with their start and end apart: 15, of which 11 were waited for; matrix products, arithmetic and copies ran while one was open for 0% of the time, Pallas kernels for 7%

profile of v9, /device:TPU:1, one launch (start us, length us, event | category | flops | bytes accessed | tf_op | source)
XLA Modules:
  0.0 213.6 jit_solution(15894073497932288614)
XLA Ops:
  2.4 15.7 %all-to-all-start = ((bf16[12,88,128]{2,1,0:T(8,128)(2,1)}), bf16[12,88,128]{2,1,0:T(8,128)(2,1)S(1)}, u32[]{:S(2)}, u32[]{:S(2)}) async-start(bf16[12,88,128]{2,1,0:T(8,128)(2,1)} %bitcast.7), calls=%async_computation | async-start | bytes 540672 | tf_op jit(solution)/shard_map/all_to_all | solution.py:238
  18.3 3.3 %collective-permute-start = (bf16[1552,128]{1,0:T(8,128)(2,1)S(1)}, bf16[1552,128]{1,0:T(8,128)(2,1)S(1)}, u32[]{:S(2)}, u32[]{:S(2)}) collective-permute-start(bf16[1552,128]{1,0:T(8,128)(2,1)S(1)} %pad_maximum_fusion.refs_0_), channel_id=1, source_target_pairs={{0,256},{256,512},{512,0},{1,257},{257,513},{513,1},{2,258},{258,5... | collective-permute-start | bytes 1191944 | tf_op jit(solution)/shard_map/ppermute | solution.py:247
  21.6 16.3 %collective-permute-done.refs_1_ = bf16[1552,128]{1,0:T(8,128)(2,1)S(1)} collective-permute-done((bf16[1552,128]{1,0:T(8,128)(2,1)S(1)}, bf16[1552,128]{1,0:T(8,128)(2,1)S(1)}, u32[]{:S(2)}, u32[]{:S(2)}) %collective-permute-start) | collective-permute-done | bytes 397344 | tf_op jit(solution)/shard_map/ppermute | solution.py:247
  39.1 4.0 %all-to-all-start.1 = ((bf16[4,12,88,128]{3,2,1,0:T(8,128)(2,1)}), bf16[4,12,88,128]{3,2,1,0:T(8,128)(2,1)S(1)}, u32[]{:S(2)}, u32[]{:S(2)}) async-start(bf16[4,12,88,128]{3,2,1,0:T(8,128)(2,1)} %broadcast_in_dim.50), calls=%async_computation.1 | async-start | bytes 2162688 | tf_op jit(solution)/shard_map/all_to_all | solution.py:238
  43.1 2.8 %collective-permute-start.1 = (bf16[1552,128]{1,0:T(8,128)(2,1)S(1)}, bf16[1552,128]{1,0:T(8,128)(2,1)S(1)}, u32[]{:S(2)}, u32[]{:S(2)}) collective-permute-start(bf16[1552,128]{1,0:T(8,128)(2,1)S(1)} %pad_maximum_fusion.refs_0_), channel_id=1, source_target_pairs={{0,512},{256,0},{512,256},{1,513},{257,1},{513,257},{2,514},{258,2... | collective-permute-start | bytes 1191944 | tf_op jit(solution)/shard_map/ppermute | solution.py:247
  45.9 7.9 %collective-permute-done.1.refs_2_ = bf16[1552,128]{1,0:T(8,128)(2,1)S(1)} collective-permute-done((bf16[1552,128]{1,0:T(8,128)(2,1)S(1)}, bf16[1552,128]{1,0:T(8,128)(2,1)S(1)}, u32[]{:S(2)}, u32[]{:S(2)}) %collective-permute-start.1) | collective-permute-done | bytes 397344 | tf_op jit(solution)/shard_map/ppermute | solution.py:247
  53.8 2.9 %all-to-all-done.1.own_ref = bf16[4,12,88,128]{3,2,1,0:T(8,128)(2,1)S(1)} async-done(((bf16[4,12,88,128]{3,2,1,0:T(8,128)(2,1)}), bf16[4,12,88,128]{3,2,1,0:T(8,128)(2,1)S(1)}, u32[]{:S(2)}, u32[]{:S(2)}) %all-to-all-start.1) | async-done | bytes 1081376 | tf_op jit(solution)/shard_map/all_to_all | solution.py:238
  56.7 4.7 %collective-permute-start.2 = (bf16[4,12,88,128]{3,2,1,0:T(8,128)(2,1)S(1)}, bf16[4,12,88,128]{3,2,1,0:T(8,128)(2,1)S(1)}, u32[]{:S(2)}, u32[]{:S(2)}) collective-permute-start(bf16[4,12,88,128]{3,2,1,0:T(8,128)(2,1)S(1)} %all-to-all-done.1.own_ref), channel_id=1, source_target_pairs={{0,1},{1,0},{2,3},{3,2},{4,5},{5,4},{6,7},{7,6},{8,9},{9,8},{10,11... | collective-permute-start | bytes 3244040 | tf_op jit(solution)/shard_map/ppermute | solution.py:247
  61.5 2.2 %collective-permute-done.2.other_ref = bf16[4,12,88,128]{3,2,1,0:T(8,128)(2,1)S(1)} collective-permute-done((bf16[4,12,88,128]{3,2,1,0:T(8,128)(2,1)S(1)}, bf16[4,12,88,128]{3,2,1,0:T(8,128)(2,1)S(1)}, u32[]{:S(2)}, u32[]{:S(2)}) %collective-permute-start.2) | collective-permute-done | bytes 1081376 | tf_op jit(solution)/shard_map/ppermute | solution.py:247
  63.7 2.7 %tile_sums.1 = bf16[24,2,88,128]{3,2,1,0:T(8,128)(2,1)} custom-call(s32[3,4,12]{2,1,0:T(4,128)S(1)} %maximum_convert_fusion.meta_ref, s32[2]{0:T(128)S(1)} %pad_add_fusion.1.place_ref, bf16[4,12,88,128]{3,2,1,0:T(8,128)(2,1)S(1)} %all-to-all-done.1.own_ref, bf16[4,12,88,128]{3,2,1,0:T(8,128)(2,1)S(1)} %collective-permute-done.2.other_ref, ...), custom_call_target="tpu_custom_call" | custom-call | tf_op jit(solution)/shard_map/tile_sums/pallas_call | solution.py:120
  66.4 8.1 %all-to-all-start.2 = ((bf16[24,2,88,128]{3,2,1,0:T(8,128)(2,1)}), bf16[24,2,88,128]{3,2,1,0:T(8,128)(2,1)S(1)}, u32[]{:S(2)}, u32[]{:S(2)}) async-start(bf16[24,2,88,128]{3,2,1,0:T(8,128)(2,1)} %tile_sums.1), calls=%async_computation.2 | async-start | bytes 2162688 | tf_op jit(solution)/shard_map/all_to_all | solution.py:238
  74.5 15.3 %counts.1 = s16[24,128,128]{2,1,0:T(8,128)(2,1)S(1)} custom-call(s32[128,1024]{1,0:T(8,128)S(1)} %copy-done), custom_call_target="tpu_custom_call" | custom-call | flops 4294967296 | bytes 2097152 | tf_op jit(solution)/shard_map/counts/pallas_call | solution.py:66
  89.8 9.6 %all-to-all-done.2 = bf16[24,2,88,128]{3,2,1,0:T(8,128)(2,1)S(1)} async-done(((bf16[24,2,88,128]{3,2,1,0:T(8,128)(2,1)}), bf16[24,2,88,128]{3,2,1,0:T(8,128)(2,1)S(1)}, u32[]{:S(2)}, u32[]{:S(2)}) %all-to-all-start.2) | async-done | bytes 1081376 | tf_op jit(solution)/shard_map/all_to_all | solution.py:238
  99.7 1.2 broadcast_in_dim.51
  100.9 6.9 %all-to-all-start.3 = ((bf16[8,2,256,128]{3,2,1,0:T(8,128)(2,1)}), bf16[8,2,256,128]{3,2,1,0:T(8,128)(2,1)S(1)}, u32[]{:S(2)}, u32[]{:S(2)}) async-start(bf16[8,2,256,128]{3,2,1,0:T(8,128)(2,1)} %broadcast_in_dim.51), calls=%async_computation.3 | async-start | bytes 2097152 | tf_op jit(solution)/shard_map/all_to_all | solution.py:238
  107.9 5.4 %collective-permute-start.5 = (s16[8,128,128]{2,1,0:T(8,128)(2,1)S(1)}, s16[8,128,128]{2,1,0:T(8,128)(2,1)S(1)}, u32[]{:S(2)}, u32[]{:S(2)}) collective-permute-start(s16[8,128,128]{2,1,0:T(8,128)(2,1)S(1)} %get-tuple-element.36), channel_id=1, source_target_pairs={{0,256},{256,512},{512,0},{1,257},{257,513},{513,1},{2,258},{258,5... | collective-permute-start | bytes 786440 | tf_op jit(solution)/shard_map/ppermute | solution.py:247
  113.4 1.9 collective-permute-start.6
  115.3 3.4 %collective-permute-start.3 = (bf16[2,256,128]{2,1,0:T(8,128)(2,1)S(1)}, bf16[2,256,128]{2,1,0:T(8,128)(2,1)S(1)}, u32[]{:S(2)}, u32[]{:S(2)}) collective-permute-start(bf16[2,256,128]{2,1,0:T(8,128)(2,1)S(1)} %fusion), channel_id=1, source_target_pairs={{0,256},{256,512},{512,0},{1,257},{257,513},{513,1},{2,258},{258,5... | collective-permute-start | bytes 393224 | tf_op jit(solution)/shard_map/ppermute | solution.py:247
  118.7 2.8 %collective-permute-start.4 = (bf16[2,256,128]{2,1,0:T(8,128)(2,1)S(1)}, bf16[2,256,128]{2,1,0:T(8,128)(2,1)S(1)}, u32[]{:S(2)}, u32[]{:S(2)}) collective-permute-start(bf16[2,256,128]{2,1,0:T(8,128)(2,1)S(1)} %fusion), channel_id=1, source_target_pairs={{0,512},{256,0},{512,256},{1,513},{257,1},{513,257},{2,514},{258,2... | collective-permute-start | bytes 393224 | tf_op jit(solution)/shard_map/ppermute | solution.py:247
  121.6 4.6 %collective-permute-done.3 = bf16[2,256,128]{2,1,0:T(8,128)(2,1)S(1)} collective-permute-done((bf16[2,256,128]{2,1,0:T(8,128)(2,1)S(1)}, bf16[2,256,128]{2,1,0:T(8,128)(2,1)S(1)}, u32[]{:S(2)}, u32[]{:S(2)}) %collective-permute-start.3) | collective-permute-done | bytes 131104 | tf_op jit(solution)/shard_map/ppermute | solution.py:247
  126.2 3.0 %collective-permute-done.4 = bf16[2,256,128]{2,1,0:T(8,128)(2,1)S(1)} collective-permute-done((bf16[2,256,128]{2,1,0:T(8,128)(2,1)S(1)}, bf16[2,256,128]{2,1,0:T(8,128)(2,1)S(1)}, u32[]{:S(2)}, u32[]{:S(2)}) %collective-permute-start.4) | collective-permute-done | bytes 131104 | tf_op jit(solution)/shard_map/ppermute | solution.py:247
  129.4 7.6 %all-to-all-done.3.a_ref = bf16[8,2,256,128]{3,2,1,0:T(8,128)(2,1)S(1)} async-done(((bf16[8,2,256,128]{3,2,1,0:T(8,128)(2,1)}), bf16[8,2,256,128]{3,2,1,0:T(8,128)(2,1)S(1)}, u32[]{:S(2)}, u32[]{:S(2)}) %all-to-all-start.3) | async-done | bytes 1048608 | tf_op jit(solution)/shard_map/all_to_all | solution.py:238
  137.0 3.8 %scores.1 = (f32[8,384]{1,0:T(8,128)S(1)}, bf16[4,2,256,384]{3,2,1,0:T(8,128)(2,1)S(1)}, bf16[4,2,256,256]{3,2,1,0:T(8,128)(2,1)S(1)}) custom-call(s32[2]{0:T(128)S(1)} %pad_add_fusion.1.place_ref, bf16[3,2,256,128]{3,2,1,0:T(8,128)(2,1)S(1)} %pad_maximum_fusion.1.n_ref, bf16[8,2,256,128]{3,2,1,0:T(8,128)(2,1)S(1)} %all-to-all-done.3.a_ref, ...), custom_call_target="tpu_custom_call" | custom-call | flops 2147483648 | bytes 4194304 | tf_op jit(solution)/shard_map/scores/pallas_call | solution.py:315
  140.8 5.4 %collective-permute-start.7 = (f32[8,384]{1,0:T(8,128)S(1)}, f32[8,384]{1,0:T(8,128)S(1)}, u32[]{:S(2)}, u32[]{:S(2)}) collective-permute-start(f32[8,384]{1,0:T(8,128)S(1)} %get-tuple-element.29.refs_0_), channel_id=1, source_target_pairs={{0,256},{256,512},{512,0},{1,257},{257,513},{513,1},{2,258},{258,5... | collective-permute-start | bytes 36872 | tf_op jit(solution)/shard_map/ppermute | solution.py:247
  146.3 1.9 collective-permute-start.8
  148.9 1.8 collective-permute-done.8.refs_2_
  150.7 4.1 %grads.1 = (f32[8,384]{1,0:T(8,128)S(1)}, f32[256,256]{1,0:T(8,128)S(1)}) custom-call(s32[2]{0:T(128)S(1)} %pad_add_fusion.1.place_ref, bf16[3,2,256,128]{3,2,1,0:T(8,128)(2,1)S(1)} %pad_maximum_fusion.1.n_ref, bf16[8,2,256,128]{3,2,1,0:T(8,128)(2,1)S(1)} %all-to-all-done.3.a_ref, bf16[256,256]{1,0:T(8,128)(2,1)S(1)} %bitcast.40, ...), custom_call_target="tpu_custom_call" | custom-call | flops 2147483648 | bytes 4194304 | tf_op jit(solution)/shard_map/grads/pallas_call | solution.py:333
  154.8 13.6 %all_to_all.35 = f32[32,8,256]{2,1,0:T(8,128)S(1)} all-to-all(f32[32,8,256]{2,1,0:T(8,128)S(1)} %bitcast.38), channel_id=1, replica_groups=mesh['zl'=3,'y'=8,'x'=4,'zh'=4,'core'=2] {'y','x'}, dimensions={0} | all-to-all | bytes 524288 | tf_op jit(solution)/shard_map/all_to_all | solution.py:238
  168.4 5.4 %collective-permute-start.9 = (f32[8,256]{1,0:T(8,128)S(1)}, f32[8,256]{1,0:T(8,128)S(1)}, u32[]{:S(2)}, u32[]{:S(2)}) collective-permute-start(f32[8,256]{1,0:T(8,128)S(1)} %reduce_sum.28), channel_id=1, source_target_pairs={{0,1},{1,0},{2,3},{3,2},{4,5},{5,4},{6,7},{7,6},{8,9},{9,8},{10,11... | collective-permute-start | bytes 24584 | tf_op jit(solution)/shard_map/ppermute | solution.py:247
  174.6 23.1 %all_to_all.36 = f32[12,8,256]{2,1,0:T(8,128)S(1)} all-to-all(f32[12,8,256]{2,1,0:T(8,128)S(1)} %broadcast_in_dim.53), channel_id=1, replica_groups=mesh['zl'=3,'y'=8,'x'=4,'zh'=4,'core'=2] {'zl','zh'}, dimensions={0} | all-to-all | bytes 196608 | tf_op jit(solution)/shard_map/all_to_all | solution.py:238
  198.4 3.9 %all-to-all-start.6 = ((f32[32,8,256]{2,1,0:T(8,128)}), f32[32,8,256]{2,1,0:T(8,128)S(1)}, u32[]{:S(2)}, u32[]{:S(2)}) async-start(f32[32,8,256]{2,1,0:T(8,128)} %broadcast_in_dim.54), calls=%async_computation.6 | async-start | bytes 524288 | tf_op jit(solution)/shard_map/all_to_all | solution.py:238
  202.8 10.0 %all-to-all-done.6 = f32[32,8,256]{2,1,0:T(8,128)S(1)} async-done(((f32[32,8,256]{2,1,0:T(8,128)}), f32[32,8,256]{2,1,0:T(8,128)S(1)}, u32[]{:S(2)}, u32[]{:S(2)}) %all-to-all-start.6) | async-done | bytes 262176 | tf_op jit(solution)/shard_map/all_to_all | solution.py:238
  (50 shorter events, 7.2 us)
Async XLA Ops:
  0.6 17.5 %copy-start.4 = (s32[12]{0:T(128)S(1)}, s32[12]{0:T(128)}, u32[]{:S(2)}) copy-start(s32[12]{0:T(128)} %param.10) | copy-start | bytes 148
  0.6 17.5 %copy-start.5 = (s32[2,12]{1,0:T(2,128)S(1)}, s32[2,12]{1,0:T(2,128)}, u32[]{:S(2)}) copy-start(s32[2,12]{1,0:T(2,128)} %param.11) | copy-start | bytes 292
  0.7 17.6 %copy-start.1 = (bf16[12,128,128]{2,1,0:T(8,128)(2,1)S(1)}, bf16[12,128,128]{2,1,0:T(8,128)(2,1)}, u32[]{:S(2)}) copy-start(bf16[12,128,128]{2,1,0:T(8,128)(2,1)} %param.9) | copy-start | bytes 1179652
  2.4 35.5 %all-to-all-start = ((bf16[12,88,128]{2,1,0:T(8,128)(2,1)}), bf16[12,88,128]{2,1,0:T(8,128)(2,1)S(1)}, u32[]{:S(2)}, u32[]{:S(2)}) async-start(bf16[12,88,128]{2,1,0:T(8,128)(2,1)} %bitcast.7), calls=%async_computation | async-start | bytes 540672 | tf_op jit(solution)/shard_map/all_to_all | solution.py:238
  18.3 19.7 %collective-permute-start = (bf16[1552,128]{1,0:T(8,128)(2,1)S(1)}, bf16[1552,128]{1,0:T(8,128)(2,1)S(1)}, u32[]{:S(2)}, u32[]{:S(2)}) collective-permute-start(bf16[1552,128]{1,0:T(8,128)(2,1)S(1)} %pad_maximum_fusion.refs_0_), channel_id=1, source_target_pairs={{0,256},{256,512},{512,0},{1,257},{257,513},{513,1},{2,258},{258,5... | collective-permute-start | bytes 1191944 | tf_op jit(solution)/shard_map/ppermute | solution.py:247
  39.1 17.6 %all-to-all-start.1 = ((bf16[4,12,88,128]{3,2,1,0:T(8,128)(2,1)}), bf16[4,12,88,128]{3,2,1,0:T(8,128)(2,1)S(1)}, u32[]{:S(2)}, u32[]{:S(2)}) async-start(bf16[4,12,88,128]{3,2,1,0:T(8,128)(2,1)} %broadcast_in_dim.50), calls=%async_computation.1 | async-start | bytes 2162688 | tf_op jit(solution)/shard_map/all_to_all | solution.py:238
  43.1 10.7 %collective-permute-start.1 = (bf16[1552,128]{1,0:T(8,128)(2,1)S(1)}, bf16[1552,128]{1,0:T(8,128)(2,1)S(1)}, u32[]{:S(2)}, u32[]{:S(2)}) collective-permute-start(bf16[1552,128]{1,0:T(8,128)(2,1)S(1)} %pad_maximum_fusion.refs_0_), channel_id=1, source_target_pairs={{0,512},{256,0},{512,256},{1,513},{257,1},{513,257},{2,514},{258,2... | collective-permute-start | bytes 1191944 | tf_op jit(solution)/shard_map/ppermute | solution.py:247
  56.7 7.0 %collective-permute-start.2 = (bf16[4,12,88,128]{3,2,1,0:T(8,128)(2,1)S(1)}, bf16[4,12,88,128]{3,2,1,0:T(8,128)(2,1)S(1)}, u32[]{:S(2)}, u32[]{:S(2)}) collective-permute-start(bf16[4,12,88,128]{3,2,1,0:T(8,128)(2,1)S(1)} %all-to-all-done.1.own_ref), channel_id=1, source_target_pairs={{0,1},{1,0},{2,3},{3,2},{4,5},{5,4},{6,7},{7,6},{8,9},{9,8},{10,11... | collective-permute-start | bytes 3244040 | tf_op jit(solution)/shard_map/ppermute | solution.py:247
  66.4 8.1 %copy-start.3 = (s32[2,256]{1,0:T(2,128)S(1)}, s32[2,256]{1,0:T(2,128)}, u32[]{:S(2)}) copy-start(s32[2,256]{1,0:T(2,128)} %param.12) | copy-start | bytes 6148
  66.4 8.1 %copy-start = (s32[128,1024]{1,0:T(8,128)S(1)}, s32[128,1024]{1,0:T(8,128)}, u32[]{:S(2)}) copy-start(s32[128,1024]{1,0:T(8,128)} %neg_ref) | copy-start | bytes 1572868
  66.4 33.0 %all-to-all-start.2 = ((bf16[24,2,88,128]{3,2,1,0:T(8,128)(2,1)}), bf16[24,2,88,128]{3,2,1,0:T(8,128)(2,1)S(1)}, u32[]{:S(2)}, u32[]{:S(2)}) async-start(bf16[24,2,88,128]{3,2,1,0:T(8,128)(2,1)} %tile_sums.1), calls=%async_computation.2 | async-start | bytes 2162688 | tf_op jit(solution)/shard_map/all_to_all | solution.py:238
  100.9 36.1 %all-to-all-start.3 = ((bf16[8,2,256,128]{3,2,1,0:T(8,128)(2,1)}), bf16[8,2,256,128]{3,2,1,0:T(8,128)(2,1)S(1)}, u32[]{:S(2)}, u32[]{:S(2)}) async-start(bf16[8,2,256,128]{3,2,1,0:T(8,128)(2,1)} %broadcast_in_dim.51), calls=%async_computation.3 | async-start | bytes 2097152 | tf_op jit(solution)/shard_map/all_to_all | solution.py:238
  107.8 13.7 %copy-start.2 = (bf16[256,256]{1,0:T(8,128)(2,1)S(1)}, bf16[256,256]{1,0:T(8,128)(2,1)}, u32[]{:S(2)}) copy-start(bf16[256,256]{1,0:T(8,128)(2,1)} %param.8) | copy-start | bytes 393220
  107.9 21.3 %collective-permute-start.5 = (s16[8,128,128]{2,1,0:T(8,128)(2,1)S(1)}, s16[8,128,128]{2,1,0:T(8,128)(2,1)S(1)}, u32[]{:S(2)}, u32[]{:S(2)}) collective-permute-start(s16[8,128,128]{2,1,0:T(8,128)(2,1)S(1)} %get-tuple-element.36), channel_id=1, source_target_pairs={{0,256},{256,512},{512,0},{1,257},{257,513},{513,1},{2,258},{258,5... | collective-permute-start | bytes 786440 | tf_op jit(solution)/shard_map/ppermute | solution.py:247
  113.4 15.9 %collective-permute-start.6 = (s16[8,128,128]{2,1,0:T(8,128)(2,1)S(1)}, s16[8,128,128]{2,1,0:T(8,128)(2,1)S(1)}, u32[]{:S(2)}, u32[]{:S(2)}) collective-permute-start(s16[8,128,128]{2,1,0:T(8,128)(2,1)S(1)} %get-tuple-element.35), channel_id=1, source_target_pairs={{0,512},{256,0},{512,256},{1,513},{257,1},{513,257},{2,514},{258,2... | collective-permute-start | bytes 786440 | tf_op jit(solution)/shard_map/ppermute | solution.py:247
  115.3 10.9 %collective-permute-start.3 = (bf16[2,256,128]{2,1,0:T(8,128)(2,1)S(1)}, bf16[2,256,128]{2,1,0:T(8,128)(2,1)S(1)}, u32[]{:S(2)}, u32[]{:S(2)}) collective-permute-start(bf16[2,256,128]{2,1,0:T(8,128)(2,1)S(1)} %fusion), channel_id=1, source_target_pairs={{0,256},{256,512},{512,0},{1,257},{257,513},{513,1},{2,258},{258,5... | collective-permute-start | bytes 393224 | tf_op jit(solution)/shard_map/ppermute | solution.py:247
  118.7 10.5 %collective-permute-start.4 = (bf16[2,256,128]{2,1,0:T(8,128)(2,1)S(1)}, bf16[2,256,128]{2,1,0:T(8,128)(2,1)S(1)}, u32[]{:S(2)}, u32[]{:S(2)}) collective-permute-start(bf16[2,256,128]{2,1,0:T(8,128)(2,1)S(1)} %fusion), channel_id=1, source_target_pairs={{0,512},{256,0},{512,256},{1,513},{257,1},{513,257},{2,514},{258,2... | collective-permute-start | bytes 393224 | tf_op jit(solution)/shard_map/ppermute | solution.py:247
  140.8 8.1 %collective-permute-start.7 = (f32[8,384]{1,0:T(8,128)S(1)}, f32[8,384]{1,0:T(8,128)S(1)}, u32[]{:S(2)}, u32[]{:S(2)}) collective-permute-start(f32[8,384]{1,0:T(8,128)S(1)} %get-tuple-element.29.refs_0_), channel_id=1, source_target_pairs={{0,256},{256,512},{512,0},{1,257},{257,513},{513,1},{2,258},{258,5... | collective-permute-start | bytes 36872 | tf_op jit(solution)/shard_map/ppermute | solution.py:247
  146.3 4.4 %collective-permute-start.8 = (f32[8,384]{1,0:T(8,128)S(1)}, f32[8,384]{1,0:T(8,128)S(1)}, u32[]{:S(2)}, u32[]{:S(2)}) collective-permute-start(f32[8,384]{1,0:T(8,128)S(1)} %get-tuple-element.29.refs_0_), channel_id=1, source_target_pairs={{0,512},{256,0},{512,256},{1,513},{257,1},{513,257},{2,514},{258,2... | collective-permute-start | bytes 36872 | tf_op jit(solution)/shard_map/ppermute | solution.py:247
  168.4 6.2 %collective-permute-start.9 = (f32[8,256]{1,0:T(8,128)S(1)}, f32[8,256]{1,0:T(8,128)S(1)}, u32[]{:S(2)}, u32[]{:S(2)}) collective-permute-start(f32[8,256]{1,0:T(8,128)S(1)} %reduce_sum.28), channel_id=1, source_target_pairs={{0,1},{1,0},{2,3},{3,2},{4,5},{5,4},{6,7},{7,6},{8,9},{9,8},{10,11... | collective-permute-start | bytes 24584 | tf_op jit(solution)/shard_map/ppermute | solution.py:247
  198.4 14.5 %all-to-all-start.6 = ((f32[32,8,256]{2,1,0:T(8,128)}), f32[32,8,256]{2,1,0:T(8,128)S(1)}, u32[]{:S(2)}, u32[]{:S(2)}) async-start(f32[32,8,256]{2,1,0:T(8,128)} %broadcast_in_dim.54), calls=%async_computation.6 | async-start | bytes 524288 | tf_op jit(solution)/shard_map/all_to_all | solution.py:238

commit v10 on v9

--- a/solution.py
+++ b/solution.py
@@ -12,6 +12,7 @@
 eps = 1e-06
 T = 128
 ZL = 3
+EARLY = 8
 FS = 88
 f32 = jnp.float32
 bf16 = jnp.bfloat16
@@ -80,16 +81,17 @@
 
 
 def tiles_kernel(cols, meta_ref, place_ref, own_ref, other_ref, *refs):
-    tile_refs, (out_ref, acc_ref) = refs[:ZL], refs[ZL:]
+    tile_refs, (out_ref, acc_ref) = refs[: 2 * ZL], refs[2 * ZL :]
     zsize = own_ref.shape[1] // ZL
     slots = meta_ref.shape[2]
     acc_ref[...] = jnp.zeros_like(acc_ref)
     core, zl = place_ref[0], place_ref[1]
     for s in range(ZL):
-
-        def few(i, carry, s=s):
+        for i in range(slots // 4):
+            late = i * 4 >= EARLY
+
             @pl.when(meta_ref[s, 0, i * 4] >= 0)
-            def _():
+            def _(s=s, i=i, late=late):
                 products = []
                 for j in range(4):
                     k = i * 4 + j
@@ -98,7 +100,8 @@
                     at = lax.div(chip, zsize), behind(zl, s) * zsize + lax.rem(chip, zsize)
                     mine = lax.rem(tcol, 2) == core
                     rows = jnp.where(mine, own_ref[at], other_ref[at])
-                    tile = tile_refs[s][pl.ds(pl.multiple_of(k * T, T), T), :]
+                    start = (k - EARLY if late else k) * T
+                    tile = tile_refs[2 * s + late][start : start + T, :]
                     products.append(dot(rows, tile, NT))
                 for j in range(4):
                     k = i * 4 + j
@@ -109,10 +112,26 @@
                         kept = (held * meta_ref[s, 2 + v, k]).astype(f32)
                         acc_ref[at, v] += kept * products[j]
 
-            return carry
-
-        lax.fori_loop(0, slots // 4, few, 0)
     out_ref[...] = acc_ref[...].astype(bf16)
+
+
+def cut_kernel(x_ref, out_ref):
+    copies = out_ref.shape[0] // ZL
+    turned = x_ref[...].astype(f32).T
+    for s in range(ZL):
+        rows = turned[s * FS : (s + 1) * FS]
+        if rows.shape[0] < FS:
+            rows = jnp.concatenate([rows, jnp.zeros((FS - rows.shape[0], T), f32)], 0)
+        for i in range(copies):
+            out_ref[s * copies + i] = rows.astype(bf16)
+
+
+def cut_features(features, copies):
+    return pl.pallas_call(
+        cut_kernel,
+        out_shape=jax.ShapeDtypeStruct((ZL * copies, FS, features.shape[0]), bf16),
+        name="cut_features",
+    )(features)
 
 
 def tile_sums(meta, place, own, other, tiles, cols, blocks):
@@ -121,7 +140,7 @@
         functools.partial(tiles_kernel, cols),
         out_shape=jax.ShapeDtypeStruct(shape, bf16),
         in_specs=[pl.BlockSpec(memory_space=pltpu.SMEM)] * 2
-        + [pl.BlockSpec(memory_space=pltpu.VMEM)] * (2 + ZL),
+        + [pl.BlockSpec(memory_space=pltpu.VMEM)] * (2 + 2 * ZL),
         scratch_shapes=[pltpu.VMEM(shape, f32)],
         compiler_params=pltpu.CompilerParams(**PARAMS),
         name="tile_sums",
@@ -267,7 +286,7 @@
     tcol = jnp.where(held, tile_pos % cols, 0)
     meta = jnp.concatenate([trow[None], tcol[None], edge_keep], 0).astype(bf16)
     meta = jnp.pad(meta, ((0, 16 - meta.shape[0]), (0, T - slots)))
-    return jnp.concatenate([tiles.reshape(slots * T, T), meta], 0)
+    return jnp.concatenate([tiles[EARLY:].reshape((slots - EARLY) * T, T), meta], 0)
 
 
 def shards(features, weight, tiles, tile_pos, edge_keep, feature_keep, negatives):
@@ -279,21 +298,25 @@
     zl = lax.axis_index("zl")
     place = jnp.stack([lax.axis_index("core"), zl])
     total = lax.axis_size(ROW) * cols * nodes
-    pad = ZL * FS - width
     whole = lambda x, s: x
 
-    turned = jnp.pad(features.T, ((0, pad), (0, 0))).reshape(ZL, 1, FS, nodes)
-    sent = jnp.broadcast_to(turned, (ZL, zsize, FS, nodes)).reshape(ZL * zsize, FS, nodes)
-    near = swap(sent, ("zl", "zh"))
-    held = packed(tiles, tile_pos, edge_keep, cols)
-    next_tiles = shift(held, "zl", 1)
-    near, next_tiles = lax.optimization_barrier((near, next_tiles))
+    near = swap(cut_features(features, zsize), ("zl", "zh"))
+    some, rest = tiles[:EARLY].reshape(EARLY * T, T), packed(tiles, tile_pos, edge_keep, cols)
+    next_some = shift(some, "zl", 1)
+    near, next_some = lax.optimization_barrier((near, next_some))
     own = share(near, "x")
-    last_tiles = shift(held, "zl", 2)
-    own, last_tiles = lax.optimization_barrier((own, last_tiles))
-    all_tiles = [held, next_tiles, last_tiles]
+    next_rest, last_some, last_rest = (
+        shift(rest, "zl", 1),
+        shift(some, "zl", 2),
+        shift(rest, "zl", 2),
+    )
+    own, next_rest, last_some, last_rest = lax.optimization_barrier(
+        (own, next_rest, last_some, last_rest)
+    )
+    all_tiles = [some, rest, next_some, next_rest, last_some, last_rest]
     other = shift(own, "core", 1)
-    metas = jnp.stack([x[slots * T : slots * T + 4, :slots] for x in all_tiles]).astype(jnp.int32)
+    late = (slots - EARLY) * T
+    metas = jnp.stack([x[late : late + 4, :slots] for x in all_tiles[1::2]]).astype(jnp.int32)
 
     part = tile_sums(metas, place, own, other, all_tiles, cols, ZL * ysize)
     part, negatives = lax.optimization_barrier((part, negatives))

time: 216 us -> 213 us (0.986)
  waiting for transfers between devices: 66.8 us -> 55.5 us
  starting transfers between devices: 75.7 us -> 84.3 us
    ppermute x10 -> x12, waiting for transfers between devices: 36.6 us -> 24.2 us  [shift(): return lax.ppermute(x, axis, [(i, (i + by) % size) for i in range(size)])]
    ppermute x10 -> x12, starting transfers between devices: 37.1 us -> 44.7 us  [shift(): return lax.ppermute(x, axis, [(i, (i + by) % size) for i in range(size)])]
  transfers between devices with their start and end apart: 15 -> 17, of which waited for: 11 -> 12; matrix products, arithmetic and copies ran while one was open for 0% -> 1% of each run, Pallas kernels for 7% -> 8%
where the time goes in v10:
time: 213 us; the launch traced here: 211 us
  starting transfers between devices  84.3 us (40%)
  waiting for transfers between devices  55.5 us (26%)
  blocking collectives  35.6 us (17%)
  Pallas kernels  28.1 us (13%)
  local copies, waits for them, and re-layouts  5.52 us (3%)
    ppermute x12, starting transfers between devices, shift(): return lax.ppermute(x, axis, [(i, (i + by) % size) for i in range(size)])  44.7 us
    all_to_all x5, starting transfers between devices, swap(): return lax.all_to_all(x, axis, 0, 0, tiled=True)  39.6 us
    all_to_all x2, blocking collectives, swap(): return lax.all_to_all(x, axis, 0, 0, tiled=True)  35.6 us
    all_to_all x5, waiting for transfers between devices, swap(): return lax.all_to_all(x, axis, 0, 0, tiled=True)  31.3 us
    ppermute x12, waiting for transfers between devices, shift(): return lax.ppermute(x, axis, [(i, (i + by) % size) for i in range(size)])  24.2 us
    pallas_call x1, Pallas kernels, count_negatives(): pl.pallas_call(functools.partial(counts_kernel, blocks), out_shape=jax.Sh...  15.3 us
  transfers between devices with their start and end apart: 17, of which 12 were waited for; matrix products, arithmetic and copies ran while one was open for 1% of the time, Pallas kernels for 8%

profile of v10, /device:TPU:1, one launch (start us, length us, event | category | flops | bytes accessed | tf_op | source)
XLA Modules:
  0.0 210.6 jit_solution(3694242533489804550)
XLA Ops:
  2.3 15.7 %all-to-all-start = ((bf16[12,88,128]{2,1,0:T(8,128)(2,1)}), bf16[12,88,128]{2,1,0:T(8,128)(2,1)S(1)}, u32[]{:S(2)}, u32[]{:S(2)}) async-start(bf16[12,88,128]{2,1,0:T(8,128)(2,1)} %cut_features.1), calls=%async_computation | async-start | bytes 540672 | tf_op jit(solution)/shard_map/all_to_all | solution.py:257
  19.0 3.3 %collective-permute-start = (bf16[1024,128]{1,0:T(8,128)(2,1)S(1)}, bf16[1024,128]{1,0:T(8,128)(2,1)S(1)}, u32[]{:S(2)}, u32[]{:S(2)}) collective-permute-start(bf16[1024,128]{1,0:T(8,128)(2,1)S(1)} %bitcast.35), channel_id=1, source_target_pairs={{0,256},{256,512},{512,0},{1,257},{257,513},{513,1},{2,258},{258,5... | collective-permute-start | bytes 786440 | tf_op jit(solution)/shard_map/ppermute | solution.py:266
  22.3 2.8 %collective-permute-start.2 = (bf16[1024,128]{1,0:T(8,128)(2,1)S(1)}, bf16[1024,128]{1,0:T(8,128)(2,1)S(1)}, u32[]{:S(2)}, u32[]{:S(2)}) collective-permute-start(bf16[1024,128]{1,0:T(8,128)(2,1)S(1)} %bitcast.36), channel_id=1, source_target_pairs={{0,512},{256,0},{512,256},{1,513},{257,1},{513,257},{2,514},{258,2... | collective-permute-start | bytes 786440 | tf_op jit(solution)/shard_map/ppermute | solution.py:266
  25.2 9.9 %collective-permute-done.refs_2_ = bf16[1024,128]{1,0:T(8,128)(2,1)S(1)} collective-permute-done((bf16[1024,128]{1,0:T(8,128)(2,1)S(1)}, bf16[1024,128]{1,0:T(8,128)(2,1)S(1)}, u32[]{:S(2)}, u32[]{:S(2)}) %collective-permute-start) | collective-permute-done | bytes 262176 | tf_op jit(solution)/shard_map/ppermute | solution.py:266
  36.2 4.1 %all-to-all-start.1 = ((bf16[4,12,88,128]{3,2,1,0:T(8,128)(2,1)}), bf16[4,12,88,128]{3,2,1,0:T(8,128)(2,1)S(1)}, u32[]{:S(2)}, u32[]{:S(2)}) async-start(bf16[4,12,88,128]{3,2,1,0:T(8,128)(2,1)} %broadcast_in_dim.19), calls=%async_computation.1 | async-start | bytes 2162688 | tf_op jit(solution)/shard_map/all_to_all | solution.py:257
  40.5 1.9 collective-permute-start.1
  42.4 4.3 %collective-permute-start.3 = (bf16[528,128]{1,0:T(8,128)(2,1)S(1)}, bf16[528,128]{1,0:T(8,128)(2,1)S(1)}, u32[]{:S(2)}, u32[]{:S(2)}) collective-permute-start(bf16[528,128]{1,0:T(8,128)(2,1)S(1)} %pad_maximum_fusion.1.refs_1_), channel_id=1, source_target_pairs={{0,512},{256,0},{512,256},{1,513},{257,1},{513,257},{2,514},{258,2... | collective-permute-start | bytes 405512 | tf_op jit(solution)/shard_map/ppermute | solution.py:266
  47.2 1.7 collective-permute-done.3.refs_5_
  48.9 4.0 %all-to-all-done.1.own_ref = bf16[4,12,88,128]{3,2,1,0:T(8,128)(2,1)S(1)} async-done(((bf16[4,12,88,128]{3,2,1,0:T(8,128)(2,1)}), bf16[4,12,88,128]{3,2,1,0:T(8,128)(2,1)S(1)}, u32[]{:S(2)}, u32[]{:S(2)}) %all-to-all-start.1) | async-done | bytes 1081376 | tf_op jit(solution)/shard_map/all_to_all | solution.py:257
  52.8 5.8 %collective-permute-start.4 = (bf16[4,12,88,128]{3,2,1,0:T(8,128)(2,1)S(1)}, bf16[4,12,88,128]{3,2,1,0:T(8,128)(2,1)S(1)}, u32[]{:S(2)}, u32[]{:S(2)}) collective-permute-start(bf16[4,12,88,128]{3,2,1,0:T(8,128)(2,1)S(1)} %all-to-all-done.1.own_ref), channel_id=1, source_target_pairs={{0,1},{1,0},{2,3},{3,2},{4,5},{5,4},{6,7},{7,6},{8,9},{9,8},{10,11... | collective-permute-start | bytes 3244040 | tf_op jit(solution)/shard_map/ppermute | solution.py:266
  58.8 2.2 %collective-permute-done.4.other_ref = bf16[4,12,88,128]{3,2,1,0:T(8,128)(2,1)S(1)} collective-permute-done((bf16[4,12,88,128]{3,2,1,0:T(8,128)(2,1)S(1)}, bf16[4,12,88,128]{3,2,1,0:T(8,128)(2,1)S(1)}, u32[]{:S(2)}, u32[]{:S(2)}) %collective-permute-start.4) | collective-permute-done | bytes 1081376 | tf_op jit(solution)/shard_map/ppermute | solution.py:266
  61.0 2.6 %tile_sums.1 = bf16[24,2,88,128]{3,2,1,0:T(8,128)(2,1)} custom-call(s32[3,4,12]{2,1,0:T(4,128)S(1)} %maximum_convert_fusion.meta_ref, s32[2]{0:T(128)S(1)} %pad_add_fusion.1.place_ref, bf16[4,12,88,128]{3,2,1,0:T(8,128)(2,1)S(1)} %all-to-all-done.1.own_ref, bf16[4,12,88,128]{3,2,1,0:T(8,128)(2,1)S(1)} %collective-permute-done.4.other_ref, ...), custom_call_target="tpu_custom_call" | custom-call | tf_op jit(solution)/shard_map/tile_sums/pallas_call | solution.py:139
  63.6 9.0 %all-to-all-start.2 = ((bf16[24,2,88,128]{3,2,1,0:T(8,128)(2,1)}), bf16[24,2,88,128]{3,2,1,0:T(8,128)(2,1)S(1)}, u32[]{:S(2)}, u32[]{:S(2)}) async-start(bf16[24,2,88,128]{3,2,1,0:T(8,128)(2,1)} %tile_sums.1), calls=%async_computation.2 | async-start | bytes 2162688 | tf_op jit(solution)/shard_map/all_to_all | solution.py:257
  72.6 15.3 %counts.1 = s16[24,128,128]{2,1,0:T(8,128)(2,1)S(1)} custom-call(s32[128,1024]{1,0:T(8,128)S(1)} %copy-done), custom_call_target="tpu_custom_call" | custom-call | flops 4294967296 | bytes 2097152 | tf_op jit(solution)/shard_map/counts/pallas_call | solution.py:67
  87.9 9.6 %all-to-all-done.2 = bf16[24,2,88,128]{3,2,1,0:T(8,128)(2,1)S(1)} async-done(((bf16[24,2,88,128]{3,2,1,0:T(8,128)(2,1)}), bf16[24,2,88,128]{3,2,1,0:T(8,128)(2,1)S(1)}, u32[]{:S(2)}, u32[]{:S(2)}) %all-to-all-start.2) | async-done | bytes 1081376 | tf_op jit(solution)/shard_map/all_to_all | solution.py:257
  99.0 6.9 %all-to-all-start.3 = ((bf16[8,2,256,128]{3,2,1,0:T(8,128)(2,1)}), bf16[8,2,256,128]{3,2,1,0:T(8,128)(2,1)S(1)}, u32[]{:S(2)}, u32[]{:S(2)}) async-start(bf16[8,2,256,128]{3,2,1,0:T(8,128)(2,1)} %broadcast_in_dim.42), calls=%async_computation.3 | async-start | bytes 2097152 | tf_op jit(solution)/shard_map/all_to_all | solution.py:257
  106.0 5.4 %collective-permute-start.7 = (s16[8,128,128]{2,1,0:T(8,128)(2,1)S(1)}, s16[8,128,128]{2,1,0:T(8,128)(2,1)S(1)}, u32[]{:S(2)}, u32[]{:S(2)}) collective-permute-start(s16[8,128,128]{2,1,0:T(8,128)(2,1)S(1)} %get-tuple-element.40), channel_id=1, source_target_pairs={{0,256},{256,512},{512,0},{1,257},{257,513},{513,1},{2,258},{258,5... | collective-permute-start | bytes 786440 | tf_op jit(solution)/shard_map/ppermute | solution.py:266
  111.5 1.9 collective-permute-start.8
  113.4 3.4 %collective-permute-start.5 = (bf16[2,256,128]{2,1,0:T(8,128)(2,1)S(1)}, bf16[2,256,128]{2,1,0:T(8,128)(2,1)S(1)}, u32[]{:S(2)}, u32[]{:S(2)}) collective-permute-start(bf16[2,256,128]{2,1,0:T(8,128)(2,1)S(1)} %fusion), channel_id=1, source_target_pairs={{0,256},{256,512},{512,0},{1,257},{257,513},{513,1},{2,258},{258,5... | collective-permute-start | bytes 393224 | tf_op jit(solution)/shard_map/ppermute | solution.py:266
  116.7 2.8 %collective-permute-start.6 = (bf16[2,256,128]{2,1,0:T(8,128)(2,1)S(1)}, bf16[2,256,128]{2,1,0:T(8,128)(2,1)S(1)}, u32[]{:S(2)}, u32[]{:S(2)}) collective-permute-start(bf16[2,256,128]{2,1,0:T(8,128)(2,1)S(1)} %fusion), channel_id=1, source_target_pairs={{0,512},{256,0},{512,256},{1,513},{257,1},{513,257},{2,514},{258,2... | collective-permute-start | bytes 393224 | tf_op jit(solution)/shard_map/ppermute | solution.py:266
  119.7 4.6 %collective-permute-done.5 = bf16[2,256,128]{2,1,0:T(8,128)(2,1)S(1)} collective-permute-done((bf16[2,256,128]{2,1,0:T(8,128)(2,1)S(1)}, bf16[2,256,128]{2,1,0:T(8,128)(2,1)S(1)}, u32[]{:S(2)}, u32[]{:S(2)}) %collective-permute-start.5) | collective-permute-done | bytes 131104 | tf_op jit(solution)/shard_map/ppermute | solution.py:266
  124.3 3.0 %collective-permute-done.6 = bf16[2,256,128]{2,1,0:T(8,128)(2,1)S(1)} collective-permute-done((bf16[2,256,128]{2,1,0:T(8,128)(2,1)S(1)}, bf16[2,256,128]{2,1,0:T(8,128)(2,1)S(1)}, u32[]{:S(2)}, u32[]{:S(2)}) %collective-permute-start.6) | collective-permute-done | bytes 131104 | tf_op jit(solution)/shard_map/ppermute | solution.py:266
  127.5 7.6 %all-to-all-done.3.a_ref = bf16[8,2,256,128]{3,2,1,0:T(8,128)(2,1)S(1)} async-done(((bf16[8,2,256,128]{3,2,1,0:T(8,128)(2,1)}), bf16[8,2,256,128]{3,2,1,0:T(8,128)(2,1)S(1)}, u32[]{:S(2)}, u32[]{:S(2)}) %all-to-all-start.3) | async-done | bytes 1048608 | tf_op jit(solution)/shard_map/all_to_all | solution.py:257
  135.1 3.8 %scores.1 = (f32[8,384]{1,0:T(8,128)S(1)}, bf16[4,2,256,384]{3,2,1,0:T(8,128)(2,1)S(1)}, bf16[4,2,256,256]{3,2,1,0:T(8,128)(2,1)S(1)}) custom-call(s32[2]{0:T(128)S(1)} %pad_add_fusion.1.place_ref, bf16[3,2,256,128]{3,2,1,0:T(8,128)(2,1)S(1)} %pad_maximum_fusion.n_ref, bf16[8,2,256,128]{3,2,1,0:T(8,128)(2,1)S(1)} %all-to-all-done.3.a_ref, ...), custom_call_target="tpu_custom_call" | custom-call | flops 2147483648 | bytes 4194304 | tf_op jit(solution)/shard_map/scores/pallas_call | solution.py:338
  138.9 3.7 %collective-permute-start.10 = (f32[8,384]{1,0:T(8,128)S(1)}, f32[8,384]{1,0:T(8,128)S(1)}, u32[]{:S(2)}, u32[]{:S(2)}) collective-permute-start(f32[8,384]{1,0:T(8,128)S(1)} %get-tuple-element.33.refs_0_), channel_id=1, source_target_pairs={{0,512},{256,0},{512,256},{1,513},{257,1},{513,257},{2,514},{258,2... | collective-permute-start | bytes 36872 | tf_op jit(solution)/shard_map/ppermute | solution.py:266
  142.6 3.6 %collective-permute-start.9 = (f32[8,384]{1,0:T(8,128)S(1)}, f32[8,384]{1,0:T(8,128)S(1)}, u32[]{:S(2)}, u32[]{:S(2)}) collective-permute-start(f32[8,384]{1,0:T(8,128)S(1)} %get-tuple-element.33.refs_0_), channel_id=1, source_target_pairs={{0,256},{256,512},{512,0},{1,257},{257,513},{513,1},{2,258},{258,5... | collective-permute-start | bytes 36872 | tf_op jit(solution)/shard_map/ppermute | solution.py:266
  148.5 4.1 %grads.1 = (f32[8,384]{1,0:T(8,128)S(1)}, f32[256,256]{1,0:T(8,128)S(1)}) custom-call(s32[2]{0:T(128)S(1)} %pad_add_fusion.1.place_ref, bf16[3,2,256,128]{3,2,1,0:T(8,128)(2,1)S(1)} %pad_maximum_fusion.n_ref, bf16[8,2,256,128]{3,2,1,0:T(8,128)(2,1)S(1)} %all-to-all-done.3.a_ref, bf16[256,256]{1,0:T(8,128)(2,1)S(1)} %bitcast.41, ...), custom_call_target="tpu_custom_call" | custom-call | flops 2147483648 | bytes 4194304 | tf_op jit(solution)/shard_map/grads/pallas_call | solution.py:356
  152.6 13.4 %all_to_all.35 = f32[32,8,256]{2,1,0:T(8,128)S(1)} all-to-all(f32[32,8,256]{2,1,0:T(8,128)S(1)} %bitcast.39), channel_id=1, replica_groups=mesh['zl'=3,'y'=8,'x'=4,'zh'=4,'core'=2] {'y','x'}, dimensions={0} | all-to-all | bytes 524288 | tf_op jit(solution)/shard_map/all_to_all | solution.py:257
  166.0 5.7 %collective-permute-start.11 = (f32[8,256]{1,0:T(8,128)S(1)}, f32[8,256]{1,0:T(8,128)S(1)}, u32[]{:S(2)}, u32[]{:S(2)}) collective-permute-start(f32[8,256]{1,0:T(8,128)S(1)} %reduce_sum.28), channel_id=1, source_target_pairs={{0,1},{1,0},{2,3},{3,2},{4,5},{5,4},{6,7},{7,6},{8,9},{9,8},{10,11... | collective-permute-start | bytes 24584 | tf_op jit(solution)/shard_map/ppermute | solution.py:266
  172.5 22.2 %all_to_all.36 = f32[12,8,256]{2,1,0:T(8,128)S(1)} all-to-all(f32[12,8,256]{2,1,0:T(8,128)S(1)} %broadcast_in_dim.44), channel_id=1, replica_groups=mesh['zl'=3,'y'=8,'x'=4,'zh'=4,'core'=2] {'zl','zh'}, dimensions={0} | all-to-all | bytes 196608 | tf_op jit(solution)/shard_map/all_to_all | solution.py:257
  195.5 3.9 %all-to-all-start.6 = ((f32[32,8,256]{2,1,0:T(8,128)}), f32[32,8,256]{2,1,0:T(8,128)S(1)}, u32[]{:S(2)}, u32[]{:S(2)}) async-start(f32[32,8,256]{2,1,0:T(8,128)} %broadcast_in_dim.45), calls=%async_computation.6 | async-start | bytes 524288 | tf_op jit(solution)/shard_map/all_to_all | solution.py:257
  199.9 10.0 %all-to-all-done.6 = f32[32,8,256]{2,1,0:T(8,128)S(1)} async-done(((f32[32,8,256]{2,1,0:T(8,128)}), f32[32,8,256]{2,1,0:T(8,128)S(1)}, u32[]{:S(2)}, u32[]{:S(2)}) %all-to-all-start.6) | async-done | bytes 262176 | tf_op jit(solution)/shard_map/all_to_all | solution.py:257
  (52 shorter events, 11.3 us)
Async XLA Ops:
  0.6 24.5 %copy-start.4 = (s32[2,12]{1,0:T(2,128)S(1)}, s32[2,12]{1,0:T(2,128)}, u32[]{:S(2)}) copy-start(s32[2,12]{1,0:T(2,128)} %param.11) | copy-start | bytes 292
  2.3 32.8 %all-to-all-start = ((bf16[12,88,128]{2,1,0:T(8,128)(2,1)}), bf16[12,88,128]{2,1,0:T(8,128)(2,1)S(1)}, u32[]{:S(2)}, u32[]{:S(2)}) async-start(bf16[12,88,128]{2,1,0:T(8,128)(2,1)} %cut_features.1), calls=%async_computation | async-start | bytes 540672 | tf_op jit(solution)/shard_map/all_to_all | solution.py:257
  19.0 16.1 %collective-permute-start = (bf16[1024,128]{1,0:T(8,128)(2,1)S(1)}, bf16[1024,128]{1,0:T(8,128)(2,1)S(1)}, u32[]{:S(2)}, u32[]{:S(2)}) collective-permute-start(bf16[1024,128]{1,0:T(8,128)(2,1)S(1)} %bitcast.35), channel_id=1, source_target_pairs={{0,256},{256,512},{512,0},{1,257},{257,513},{513,1},{2,258},{258,5... | collective-permute-start | bytes 786440 | tf_op jit(solution)/shard_map/ppermute | solution.py:266
  22.3 26.5 %collective-permute-start.2 = (bf16[1024,128]{1,0:T(8,128)(2,1)S(1)}, bf16[1024,128]{1,0:T(8,128)(2,1)S(1)}, u32[]{:S(2)}, u32[]{:S(2)}) collective-permute-start(bf16[1024,128]{1,0:T(8,128)(2,1)S(1)} %bitcast.36), channel_id=1, source_target_pairs={{0,512},{256,0},{512,256},{1,513},{257,1},{513,257},{2,514},{258,2... | collective-permute-start | bytes 786440 | tf_op jit(solution)/shard_map/ppermute | solution.py:266
  36.2 4.2 %copy-start.3 = (s32[12]{0:T(128)S(1)}, s32[12]{0:T(128)}, u32[]{:S(2)}) copy-start(s32[12]{0:T(128)} %param.10) | copy-start | bytes 148
  36.2 4.2 %slice-start = ((bf16[12,128,128]{2,1,0:T(8,128)(2,1)}), bf16[4,128,128]{2,1,0:T(8,128)(2,1)S(1)}, s32[]{:S(2)}) async-start(bf16[12,128,128]{2,1,0:T(8,128)(2,1)} %param.9), calls=%async_computation.7 | async-start | bytes 262144 | tf_op jit(solution)/shard_map/slice | solution.py:289
  36.2 16.6 %all-to-all-start.1 = ((bf16[4,12,88,128]{3,2,1,0:T(8,128)(2,1)}), bf16[4,12,88,128]{3,2,1,0:T(8,128)(2,1)S(1)}, u32[]{:S(2)}, u32[]{:S(2)}) async-start(bf16[4,12,88,128]{3,2,1,0:T(8,128)(2,1)} %broadcast_in_dim.19), calls=%async_computation.1 | async-start | bytes 2162688 | tf_op jit(solution)/shard_map/all_to_all | solution.py:257
  40.5 6.7 %collective-permute-start.1 = (bf16[528,128]{1,0:T(8,128)(2,1)S(1)}, bf16[528,128]{1,0:T(8,128)(2,1)S(1)}, u32[]{:S(2)}, u32[]{:S(2)}) collective-permute-start(bf16[528,128]{1,0:T(8,128)(2,1)S(1)} %pad_maximum_fusion.1.refs_1_), channel_id=1, source_target_pairs={{0,256},{256,512},{512,0},{1,257},{257,513},{513,1},{2,258},{258,5... | collective-permute-start | bytes 405512 | tf_op jit(solution)/shard_map/ppermute | solution.py:266
  42.4 6.5 %collective-permute-start.3 = (bf16[528,128]{1,0:T(8,128)(2,1)S(1)}, bf16[528,128]{1,0:T(8,128)(2,1)S(1)}, u32[]{:S(2)}, u32[]{:S(2)}) collective-permute-start(bf16[528,128]{1,0:T(8,128)(2,1)S(1)} %pad_maximum_fusion.1.refs_1_), channel_id=1, source_target_pairs={{0,512},{256,0},{512,256},{1,513},{257,1},{513,257},{2,514},{258,2... | collective-permute-start | bytes 405512 | tf_op jit(solution)/shard_map/ppermute | solution.py:266
  52.8 8.2 %collective-permute-start.4 = (bf16[4,12,88,128]{3,2,1,0:T(8,128)(2,1)S(1)}, bf16[4,12,88,128]{3,2,1,0:T(8,128)(2,1)S(1)}, u32[]{:S(2)}, u32[]{:S(2)}) collective-permute-start(bf16[4,12,88,128]{3,2,1,0:T(8,128)(2,1)S(1)} %all-to-all-done.1.own_ref), channel_id=1, source_target_pairs={{0,1},{1,0},{2,3},{3,2},{4,5},{5,4},{6,7},{7,6},{8,9},{9,8},{10,11... | collective-permute-start | bytes 3244040 | tf_op jit(solution)/shard_map/ppermute | solution.py:266
  63.6 9.0 %copy-start.2 = (s32[2,256]{1,0:T(2,128)S(1)}, s32[2,256]{1,0:T(2,128)}, u32[]{:S(2)}) copy-start(s32[2,256]{1,0:T(2,128)} %param.12) | copy-start | bytes 6148
  63.6 9.1 %copy-start = (s32[128,1024]{1,0:T(8,128)S(1)}, s32[128,1024]{1,0:T(8,128)}, u32[]{:S(2)}) copy-start(s32[128,1024]{1,0:T(8,128)} %neg_ref) | copy-start | bytes 1572868
  63.6 33.9 %all-to-all-start.2 = ((bf16[24,2,88,128]{3,2,1,0:T(8,128)(2,1)}), bf16[24,2,88,128]{3,2,1,0:T(8,128)(2,1)S(1)}, u32[]{:S(2)}, u32[]{:S(2)}) async-start(bf16[24,2,88,128]{3,2,1,0:T(8,128)(2,1)} %tile_sums.1), calls=%async_computation.2 | async-start | bytes 2162688 | tf_op jit(solution)/shard_map/all_to_all | solution.py:257
  99.0 36.1 %all-to-all-start.3 = ((bf16[8,2,256,128]{3,2,1,0:T(8,128)(2,1)}), bf16[8,2,256,128]{3,2,1,0:T(8,128)(2,1)S(1)}, u32[]{:S(2)}, u32[]{:S(2)}) async-start(bf16[8,2,256,128]{3,2,1,0:T(8,128)(2,1)} %broadcast_in_dim.42), calls=%async_computation.3 | async-start | bytes 2097152 | tf_op jit(solution)/shard_map/all_to_all | solution.py:257
  105.9 13.7 %copy-start.1 = (bf16[256,256]{1,0:T(8,128)(2,1)S(1)}, bf16[256,256]{1,0:T(8,128)(2,1)}, u32[]{:S(2)}) copy-start(bf16[256,256]{1,0:T(8,128)(2,1)} %param.8) | copy-start | bytes 393220
  106.0 21.3 %collective-permute-start.7 = (s16[8,128,128]{2,1,0:T(8,128)(2,1)S(1)}, s16[8,128,128]{2,1,0:T(8,128)(2,1)S(1)}, u32[]{:S(2)}, u32[]{:S(2)}) collective-permute-start(s16[8,128,128]{2,1,0:T(8,128)(2,1)S(1)} %get-tuple-element.40), channel_id=1, source_target_pairs={{0,256},{256,512},{512,0},{1,257},{257,513},{513,1},{2,258},{258,5... | collective-permute-start | bytes 786440 | tf_op jit(solution)/shard_map/ppermute | solution.py:266
  111.5 15.9 %collective-permute-start.8 = (s16[8,128,128]{2,1,0:T(8,128)(2,1)S(1)}, s16[8,128,128]{2,1,0:T(8,128)(2,1)S(1)}, u32[]{:S(2)}, u32[]{:S(2)}) collective-permute-start(s16[8,128,128]{2,1,0:T(8,128)(2,1)S(1)} %get-tuple-element.39), channel_id=1, source_target_pairs={{0,512},{256,0},{512,256},{1,513},{257,1},{513,257},{2,514},{258,2... | collective-permute-start | bytes 786440 | tf_op jit(solution)/shard_map/ppermute | solution.py:266
  113.4 10.9 %collective-permute-start.5 = (bf16[2,256,128]{2,1,0:T(8,128)(2,1)S(1)}, bf16[2,256,128]{2,1,0:T(8,128)(2,1)S(1)}, u32[]{:S(2)}, u32[]{:S(2)}) collective-permute-start(bf16[2,256,128]{2,1,0:T(8,128)(2,1)S(1)} %fusion), channel_id=1, source_target_pairs={{0,256},{256,512},{512,0},{1,257},{257,513},{513,1},{2,258},{258,5... | collective-permute-start | bytes 393224 | tf_op jit(solution)/shard_map/ppermute | solution.py:266
  116.7 10.6 %collective-permute-start.6 = (bf16[2,256,128]{2,1,0:T(8,128)(2,1)S(1)}, bf16[2,256,128]{2,1,0:T(8,128)(2,1)S(1)}, u32[]{:S(2)}, u32[]{:S(2)}) collective-permute-start(bf16[2,256,128]{2,1,0:T(8,128)(2,1)S(1)} %fusion), channel_id=1, source_target_pairs={{0,512},{256,0},{512,256},{1,513},{257,1},{513,257},{2,514},{258,2... | collective-permute-start | bytes 393224 | tf_op jit(solution)/shard_map/ppermute | solution.py:266
  138.9 8.0 %collective-permute-start.10 = (f32[8,384]{1,0:T(8,128)S(1)}, f32[8,384]{1,0:T(8,128)S(1)}, u32[]{:S(2)}, u32[]{:S(2)}) collective-permute-start(f32[8,384]{1,0:T(8,128)S(1)} %get-tuple-element.33.refs_0_), channel_id=1, source_target_pairs={{0,512},{256,0},{512,256},{1,513},{257,1},{513,257},{2,514},{258,2... | collective-permute-start | bytes 36872 | tf_op jit(solution)/shard_map/ppermute | solution.py:266
  142.6 5.9 %collective-permute-start.9 = (f32[8,384]{1,0:T(8,128)S(1)}, f32[8,384]{1,0:T(8,128)S(1)}, u32[]{:S(2)}, u32[]{:S(2)}) collective-permute-start(f32[8,384]{1,0:T(8,128)S(1)} %get-tuple-element.33.refs_0_), channel_id=1, source_target_pairs={{0,256},{256,512},{512,0},{1,257},{257,513},{513,1},{2,258},{258,5... | collective-permute-start | bytes 36872 | tf_op jit(solution)/shard_map/ppermute | solution.py:266
  166.0 6.5 %collective-permute-start.11 = (f32[8,256]{1,0:T(8,128)S(1)}, f32[8,256]{1,0:T(8,128)S(1)}, u32[]{:S(2)}, u32[]{:S(2)}) collective-permute-start(f32[8,256]{1,0:T(8,128)S(1)} %reduce_sum.28), channel_id=1, source_target_pairs={{0,1},{1,0},{2,3},{3,2},{4,5},{5,4},{6,7},{7,6},{8,9},{9,8},{10,11... | collective-permute-start | bytes 24584 | tf_op jit(solution)/shard_map/ppermute | solution.py:266
  195.5 14.5 %all-to-all-start.6 = ((f32[32,8,256]{2,1,0:T(8,128)}), f32[32,8,256]{2,1,0:T(8,128)S(1)}, u32[]{:S(2)}, u32[]{:S(2)}) async-start(f32[32,8,256]{2,1,0:T(8,128)} %broadcast_in_dim.45), calls=%async_computation.6 | async-start | bytes 524288 | tf_op jit(solution)/shard_map/all_to_all | solution.py:257

commit v11 on v10

--- a/solution.py
+++ b/solution.py
@@ -12,7 +12,7 @@
 eps = 1e-06
 T = 128
 ZL = 3
-EARLY = 8
+EARLY = 4
 FS = 88
 f32 = jnp.float32
 bf16 = jnp.bfloat16

time: 213 us -> 217 us (1.019)
  blocking collectives: 35.6 us -> 39.6 us
    ppermute x12, waiting for transfers between devices: 24.2 us -> 29.7 us  [shift(): return lax.ppermute(x, axis, [(i, (i + by) % size) for i in range(size)])]
    all_to_all x5, waiting for transfers between devices: 31.3 us -> 27.2 us  [swap(): return lax.all_to_all(x, axis, 0, 0, tiled=True)]
    all_to_all x2, blocking collectives: 35.6 us -> 39.6 us  [swap(): return lax.all_to_all(x, axis, 0, 0, tiled=True)]
  transfers between devices with their start and end apart: 17 -> 17, of which waited for: 12 -> 11; matrix products, arithmetic and copies ran while one was open for 1% -> 1% of each run, Pallas kernels for 8% -> 7%
where the time goes in v11:
time: 217 us; the launch traced here: 214 us
  starting transfers between devices  82.3 us (38%)
  waiting for transfers between devices  56.9 us (26%)
  blocking collectives  39.6 us (18%)
  Pallas kernels  28.5 us (13%)
  local copies, waits for them, and re-layouts  5.47 us (3%)
    ppermute x12, starting transfers between devices, shift(): return lax.ppermute(x, axis, [(i, (i + by) % size) for i in range(size)])  42.9 us
    all_to_all x2, blocking collectives, swap(): return lax.all_to_all(x, axis, 0, 0, tiled=True)  39.6 us
    all_to_all x5, starting transfers between devices, swap(): return lax.all_to_all(x, axis, 0, 0, tiled=True)  39.5 us
    ppermute x12, waiting for transfers between devices, shift(): return lax.ppermute(x, axis, [(i, (i + by) % size) for i in range(size)])  29.7 us
    all_to_all x5, waiting for transfers between devices, swap(): return lax.all_to_all(x, axis, 0, 0, tiled=True)  27.2 us
    pallas_call x1, Pallas kernels, count_negatives(): pl.pallas_call(functools.partial(counts_kernel, blocks), out_shape=jax.Sh...  15.3 us
  transfers between devices with their start and end apart: 17, of which 11 were waited for; matrix products, arithmetic and copies ran while one was open for 1% of the time, Pallas kernels for 7%

profile of v11, /device:TPU:1, one launch (start us, length us, event | category | flops | bytes accessed | tf_op | source)
XLA Modules:
  0.0 214.3 jit_solution(8129995605944799897)
XLA Ops:
  2.3 15.7 %all-to-all-start = ((bf16[12,88,128]{2,1,0:T(8,128)(2,1)}), bf16[12,88,128]{2,1,0:T(8,128)(2,1)S(1)}, u32[]{:S(2)}, u32[]{:S(2)}) async-start(bf16[12,88,128]{2,1,0:T(8,128)(2,1)} %cut_features.1), calls=%async_computation | async-start | bytes 540672 | tf_op jit(solution)/shard_map/all_to_all | solution.py:257
  18.9 3.3 %collective-permute-start = (bf16[512,128]{1,0:T(8,128)(2,1)S(1)}, bf16[512,128]{1,0:T(8,128)(2,1)S(1)}, u32[]{:S(2)}, u32[]{:S(2)}) collective-permute-start(bf16[512,128]{1,0:T(8,128)(2,1)S(1)} %bitcast.36), channel_id=1, source_target_pairs={{0,256},{256,512},{512,0},{1,257},{257,513},{513,1},{2,258},{258,5... | collective-permute-start | bytes 393224 | tf_op jit(solution)/shard_map/ppermute | solution.py:266
  22.3 9.0 %collective-permute-done.refs_2_ = bf16[512,128]{1,0:T(8,128)(2,1)S(1)} collective-permute-done((bf16[512,128]{1,0:T(8,128)(2,1)S(1)}, bf16[512,128]{1,0:T(8,128)(2,1)S(1)}, u32[]{:S(2)}, u32[]{:S(2)}) %collective-permute-start) | collective-permute-done | bytes 131104 | tf_op jit(solution)/shard_map/ppermute | solution.py:266
  33.1 4.1 %all-to-all-start.1 = ((bf16[4,12,88,128]{3,2,1,0:T(8,128)(2,1)}), bf16[4,12,88,128]{3,2,1,0:T(8,128)(2,1)S(1)}, u32[]{:S(2)}, u32[]{:S(2)}) async-start(bf16[4,12,88,128]{3,2,1,0:T(8,128)(2,1)} %broadcast_in_dim.19), calls=%async_computation.1 | async-start | bytes 2162688 | tf_op jit(solution)/shard_map/all_to_all | solution.py:257
  37.3 1.9 collective-permute-start.1
  39.2 4.3 %collective-permute-start.3 = (bf16[1040,128]{1,0:T(8,128)(2,1)S(1)}, bf16[1040,128]{1,0:T(8,128)(2,1)S(1)}, u32[]{:S(2)}, u32[]{:S(2)}) collective-permute-start(bf16[1040,128]{1,0:T(8,128)(2,1)S(1)} %pad_maximum_fusion.1.refs_1_), channel_id=1, source_target_pairs={{0,512},{256,0},{512,256},{1,513},{257,1},{513,257},{2,514},{258,2... | collective-permute-start | bytes 798728 | tf_op jit(solution)/shard_map/ppermute | solution.py:266
  43.5 1.9 collective-permute-start.2
  45.4 8.5 %collective-permute-done.2.refs_4_ = bf16[512,128]{1,0:T(8,128)(2,1)S(1)} collective-permute-done((bf16[512,128]{1,0:T(8,128)(2,1)S(1)}, bf16[512,128]{1,0:T(8,128)(2,1)S(1)}, u32[]{:S(2)}, u32[]{:S(2)}) %collective-permute-start.2) | collective-permute-done | bytes 131104 | tf_op jit(solution)/shard_map/ppermute | solution.py:266
  53.9 5.4 %collective-permute-start.4 = (bf16[4,12,88,128]{3,2,1,0:T(8,128)(2,1)S(1)}, bf16[4,12,88,128]{3,2,1,0:T(8,128)(2,1)S(1)}, u32[]{:S(2)}, u32[]{:S(2)}) collective-permute-start(bf16[4,12,88,128]{3,2,1,0:T(8,128)(2,1)S(1)} %all-to-all-done.1.own_ref), channel_id=1, source_target_pairs={{0,1},{1,0},{2,3},{3,2},{4,5},{5,4},{6,7},{7,6},{8,9},{9,8},{10,11... | collective-permute-start | bytes 3244040 | tf_op jit(solution)/shard_map/ppermute | solution.py:266
  59.5 2.2 %collective-permute-done.4.other_ref = bf16[4,12,88,128]{3,2,1,0:T(8,128)(2,1)S(1)} collective-permute-done((bf16[4,12,88,128]{3,2,1,0:T(8,128)(2,1)S(1)}, bf16[4,12,88,128]{3,2,1,0:T(8,128)(2,1)S(1)}, u32[]{:S(2)}, u32[]{:S(2)}) %collective-permute-start.4) | collective-permute-done | bytes 1081376 | tf_op jit(solution)/shard_map/ppermute | solution.py:266
  61.7 3.0 %tile_sums.1 = bf16[24,2,88,128]{3,2,1,0:T(8,128)(2,1)} custom-call(s32[3,4,12]{2,1,0:T(4,128)S(1)} %maximum_convert_fusion.meta_ref, s32[2]{0:T(128)S(1)} %pad_add_fusion.1.place_ref, bf16[4,12,88,128]{3,2,1,0:T(8,128)(2,1)S(1)} %all-to-all-done.1.own_ref, bf16[4,12,88,128]{3,2,1,0:T(8,128)(2,1)S(1)} %collective-permute-done.4.other_ref, ...), custom_call_target="tpu_custom_call" | custom-call | tf_op jit(solution)/shard_map/tile_sums/pallas_call | solution.py:139
  64.6 8.3 %all-to-all-start.2 = ((bf16[24,2,88,128]{3,2,1,0:T(8,128)(2,1)}), bf16[24,2,88,128]{3,2,1,0:T(8,128)(2,1)S(1)}, u32[]{:S(2)}, u32[]{:S(2)}) async-start(bf16[24,2,88,128]{3,2,1,0:T(8,128)(2,1)} %tile_sums.1), calls=%async_computation.2 | async-start | bytes 2162688 | tf_op jit(solution)/shard_map/all_to_all | solution.py:257
  73.0 15.3 %counts.1 = s16[24,128,128]{2,1,0:T(8,128)(2,1)S(1)} custom-call(s32[128,1024]{1,0:T(8,128)S(1)} %copy-done), custom_call_target="tpu_custom_call" | custom-call | flops 4294967296 | bytes 2097152 | tf_op jit(solution)/shard_map/counts/pallas_call | solution.py:67
  88.3 8.5 %all-to-all-done.2 = bf16[24,2,88,128]{3,2,1,0:T(8,128)(2,1)S(1)} async-done(((bf16[24,2,88,128]{3,2,1,0:T(8,128)(2,1)}), bf16[24,2,88,128]{3,2,1,0:T(8,128)(2,1)S(1)}, u32[]{:S(2)}, u32[]{:S(2)}) %all-to-all-start.2) | async-done | bytes 1081376 | tf_op jit(solution)/shard_map/all_to_all | solution.py:257
  98.3 7.4 %all-to-all-start.3 = ((bf16[8,2,256,128]{3,2,1,0:T(8,128)(2,1)}), bf16[8,2,256,128]{3,2,1,0:T(8,128)(2,1)S(1)}, u32[]{:S(2)}, u32[]{:S(2)}) async-start(bf16[8,2,256,128]{3,2,1,0:T(8,128)(2,1)} %broadcast_in_dim.42), calls=%async_computation.3 | async-start | bytes 2097152 | tf_op jit(solution)/shard_map/all_to_all | solution.py:257
  105.9 5.2 %collective-permute-start.7 = (s16[8,128,128]{2,1,0:T(8,128)(2,1)S(1)}, s16[8,128,128]{2,1,0:T(8,128)(2,1)S(1)}, u32[]{:S(2)}, u32[]{:S(2)}) collective-permute-start(s16[8,128,128]{2,1,0:T(8,128)(2,1)S(1)} %get-tuple-element.40), channel_id=1, source_target_pairs={{0,256},{256,512},{512,0},{1,257},{257,513},{513,1},{2,258},{258,5... | collective-permute-start | bytes 786440 | tf_op jit(solution)/shard_map/ppermute | solution.py:266
  111.1 1.9 collective-permute-start.8
  113.0 3.4 %collective-permute-start.5 = (bf16[2,256,128]{2,1,0:T(8,128)(2,1)S(1)}, bf16[2,256,128]{2,1,0:T(8,128)(2,1)S(1)}, u32[]{:S(2)}, u32[]{:S(2)}) collective-permute-start(bf16[2,256,128]{2,1,0:T(8,128)(2,1)S(1)} %fusion), channel_id=1, source_target_pairs={{0,256},{256,512},{512,0},{1,257},{257,513},{513,1},{2,258},{258,5... | collective-permute-start | bytes 393224 | tf_op jit(solution)/shard_map/ppermute | solution.py:266
  116.4 2.8 %collective-permute-start.6 = (bf16[2,256,128]{2,1,0:T(8,128)(2,1)S(1)}, bf16[2,256,128]{2,1,0:T(8,128)(2,1)S(1)}, u32[]{:S(2)}, u32[]{:S(2)}) collective-permute-start(bf16[2,256,128]{2,1,0:T(8,128)(2,1)S(1)} %fusion), channel_id=1, source_target_pairs={{0,512},{256,0},{512,256},{1,513},{257,1},{513,257},{2,514},{258,2... | collective-permute-start | bytes 393224 | tf_op jit(solution)/shard_map/ppermute | solution.py:266
  119.3 4.6 %collective-permute-done.5 = bf16[2,256,128]{2,1,0:T(8,128)(2,1)S(1)} collective-permute-done((bf16[2,256,128]{2,1,0:T(8,128)(2,1)S(1)}, bf16[2,256,128]{2,1,0:T(8,128)(2,1)S(1)}, u32[]{:S(2)}, u32[]{:S(2)}) %collective-permute-start.5) | collective-permute-done | bytes 131104 | tf_op jit(solution)/shard_map/ppermute | solution.py:266
  123.9 2.9 %collective-permute-done.6 = bf16[2,256,128]{2,1,0:T(8,128)(2,1)S(1)} collective-permute-done((bf16[2,256,128]{2,1,0:T(8,128)(2,1)S(1)}, bf16[2,256,128]{2,1,0:T(8,128)(2,1)S(1)}, u32[]{:S(2)}, u32[]{:S(2)}) %collective-permute-start.6) | collective-permute-done | bytes 131104 | tf_op jit(solution)/shard_map/ppermute | solution.py:266
  126.9 8.0 %all-to-all-done.3.a_ref = bf16[8,2,256,128]{3,2,1,0:T(8,128)(2,1)S(1)} async-done(((bf16[8,2,256,128]{3,2,1,0:T(8,128)(2,1)}), bf16[8,2,256,128]{3,2,1,0:T(8,128)(2,1)S(1)}, u32[]{:S(2)}, u32[]{:S(2)}) %all-to-all-start.3) | async-done | bytes 1048608 | tf_op jit(solution)/shard_map/all_to_all | solution.py:257
  134.9 3.8 %scores.1 = (f32[8,384]{1,0:T(8,128)S(1)}, bf16[4,2,256,384]{3,2,1,0:T(8,128)(2,1)S(1)}, bf16[4,2,256,256]{3,2,1,0:T(8,128)(2,1)S(1)}) custom-call(s32[2]{0:T(128)S(1)} %pad_add_fusion.1.place_ref, bf16[3,2,256,128]{3,2,1,0:T(8,128)(2,1)S(1)} %pad_maximum_fusion.n_ref, bf16[8,2,256,128]{3,2,1,0:T(8,128)(2,1)S(1)} %all-to-all-done.3.a_ref, ...), custom_call_target="tpu_custom_call" | custom-call | flops 2147483648 | bytes 4194304 | tf_op jit(solution)/shard_map/scores/pallas_call | solution.py:338
  138.7 4.2 %collective-permute-start.10 = (f32[8,384]{1,0:T(8,128)S(1)}, f32[8,384]{1,0:T(8,128)S(1)}, u32[]{:S(2)}, u32[]{:S(2)}) collective-permute-start(f32[8,384]{1,0:T(8,128)S(1)} %get-tuple-element.33.refs_0_), channel_id=1, source_target_pairs={{0,512},{256,0},{512,256},{1,513},{257,1},{513,257},{2,514},{258,2... | collective-permute-start | bytes 36872 | tf_op jit(solution)/shard_map/ppermute | solution.py:266
  142.9 2.9 %collective-permute-start.9 = (f32[8,384]{1,0:T(8,128)S(1)}, f32[8,384]{1,0:T(8,128)S(1)}, u32[]{:S(2)}, u32[]{:S(2)}) collective-permute-start(f32[8,384]{1,0:T(8,128)S(1)} %get-tuple-element.33.refs_0_), channel_id=1, source_target_pairs={{0,256},{256,512},{512,0},{1,257},{257,513},{513,1},{2,258},{258,5... | collective-permute-start | bytes 36872 | tf_op jit(solution)/shard_map/ppermute | solution.py:266
  146.6 1.7 collective-permute-done.9.refs_1_
  148.3 4.1 %grads.1 = (f32[8,384]{1,0:T(8,128)S(1)}, f32[256,256]{1,0:T(8,128)S(1)}) custom-call(s32[2]{0:T(128)S(1)} %pad_add_fusion.1.place_ref, bf16[3,2,256,128]{3,2,1,0:T(8,128)(2,1)S(1)} %pad_maximum_fusion.n_ref, bf16[8,2,256,128]{3,2,1,0:T(8,128)(2,1)S(1)} %all-to-all-done.3.a_ref, bf16[256,256]{1,0:T(8,128)(2,1)S(1)} %bitcast.41, ...), custom_call_target="tpu_custom_call" | custom-call | flops 2147483648 | bytes 4194304 | tf_op jit(solution)/shard_map/grads/pallas_call | solution.py:356
  152.3 14.4 %all_to_all.35 = f32[32,8,256]{2,1,0:T(8,128)S(1)} all-to-all(f32[32,8,256]{2,1,0:T(8,128)S(1)} %bitcast.39), channel_id=1, replica_groups=mesh['zl'=3,'y'=8,'x'=4,'zh'=4,'core'=2] {'y','x'}, dimensions={0} | all-to-all | bytes 524288 | tf_op jit(solution)/shard_map/all_to_all | solution.py:257
  166.8 5.7 %collective-permute-start.11 = (f32[8,256]{1,0:T(8,128)S(1)}, f32[8,256]{1,0:T(8,128)S(1)}, u32[]{:S(2)}, u32[]{:S(2)}) collective-permute-start(f32[8,256]{1,0:T(8,128)S(1)} %reduce_sum.28), channel_id=1, source_target_pairs={{0,1},{1,0},{2,3},{3,2},{4,5},{5,4},{6,7},{7,6},{8,9},{9,8},{10,11... | collective-permute-start | bytes 24584 | tf_op jit(solution)/shard_map/ppermute | solution.py:266
  173.3 25.1 %all_to_all.36 = f32[12,8,256]{2,1,0:T(8,128)S(1)} all-to-all(f32[12,8,256]{2,1,0:T(8,128)S(1)} %broadcast_in_dim.44), channel_id=1, replica_groups=mesh['zl'=3,'y'=8,'x'=4,'zh'=4,'core'=2] {'zl','zh'}, dimensions={0} | all-to-all | bytes 196608 | tf_op jit(solution)/shard_map/all_to_all | solution.py:257
  199.2 3.9 %all-to-all-start.6 = ((f32[32,8,256]{2,1,0:T(8,128)}), f32[32,8,256]{2,1,0:T(8,128)S(1)}, u32[]{:S(2)}, u32[]{:S(2)}) async-start(f32[32,8,256]{2,1,0:T(8,128)} %broadcast_in_dim.45), calls=%async_computation.6 | async-start | bytes 524288 | tf_op jit(solution)/shard_map/all_to_all | solution.py:257
  203.6 10.0 %all-to-all-done.6 = f32[32,8,256]{2,1,0:T(8,128)S(1)} async-done(((f32[32,8,256]{2,1,0:T(8,128)}), f32[32,8,256]{2,1,0:T(8,128)S(1)}, u32[]{:S(2)}, u32[]{:S(2)}) %all-to-all-start.6) | async-done | bytes 262176 | tf_op jit(solution)/shard_map/all_to_all | solution.py:257
  (52 shorter events, 9.8 us)
Async XLA Ops:
  0.6 21.7 %copy-start.4 = (s32[2,12]{1,0:T(2,128)S(1)}, s32[2,12]{1,0:T(2,128)}, u32[]{:S(2)}) copy-start(s32[2,12]{1,0:T(2,128)} %param.11) | copy-start | bytes 292
  0.6 21.7 %copy-start.3 = (s32[12]{0:T(128)S(1)}, s32[12]{0:T(128)}, u32[]{:S(2)}) copy-start(s32[12]{0:T(128)} %param.10) | copy-start | bytes 148
  2.3 29.6 %all-to-all-start = ((bf16[12,88,128]{2,1,0:T(8,128)(2,1)}), bf16[12,88,128]{2,1,0:T(8,128)(2,1)S(1)}, u32[]{:S(2)}, u32[]{:S(2)}) async-start(bf16[12,88,128]{2,1,0:T(8,128)(2,1)} %cut_features.1), calls=%async_computation | async-start | bytes 540672 | tf_op jit(solution)/shard_map/all_to_all | solution.py:257
  18.9 12.4 %collective-permute-start = (bf16[512,128]{1,0:T(8,128)(2,1)S(1)}, bf16[512,128]{1,0:T(8,128)(2,1)S(1)}, u32[]{:S(2)}, u32[]{:S(2)}) collective-permute-start(bf16[512,128]{1,0:T(8,128)(2,1)S(1)} %bitcast.36), channel_id=1, source_target_pairs={{0,256},{256,512},{512,0},{1,257},{257,513},{513,1},{2,258},{258,5... | collective-permute-start | bytes 393224 | tf_op jit(solution)/shard_map/ppermute | solution.py:266
  33.1 4.2 %slice-start = ((bf16[12,128,128]{2,1,0:T(8,128)(2,1)}), bf16[8,128,128]{2,1,0:T(8,128)(2,1)S(1)}, s32[]{:S(2)}) async-start(bf16[12,128,128]{2,1,0:T(8,128)(2,1)} %param.9), calls=%async_computation.7 | async-start | bytes 524288 | tf_op jit(solution)/shard_map/slice | solution.py:289
  33.1 20.8 %all-to-all-start.1 = ((bf16[4,12,88,128]{3,2,1,0:T(8,128)(2,1)}), bf16[4,12,88,128]{3,2,1,0:T(8,128)(2,1)S(1)}, u32[]{:S(2)}, u32[]{:S(2)}) async-start(bf16[4,12,88,128]{3,2,1,0:T(8,128)(2,1)} %broadcast_in_dim.19), calls=%async_computation.1 | async-start | bytes 2162688 | tf_op jit(solution)/shard_map/all_to_all | solution.py:257
  37.3 16.6 %collective-permute-start.1 = (bf16[1040,128]{1,0:T(8,128)(2,1)S(1)}, bf16[1040,128]{1,0:T(8,128)(2,1)S(1)}, u32[]{:S(2)}, u32[]{:S(2)}) collective-permute-start(bf16[1040,128]{1,0:T(8,128)(2,1)S(1)} %pad_maximum_fusion.1.refs_1_), channel_id=1, source_target_pairs={{0,256},{256,512},{512,0},{1,257},{257,513},{513,1},{2,258},{258,5... | collective-permute-start | bytes 798728 | tf_op jit(solution)/shard_map/ppermute | solution.py:266
  39.2 14.7 %collective-permute-start.3 = (bf16[1040,128]{1,0:T(8,128)(2,1)S(1)}, bf16[1040,128]{1,0:T(8,128)(2,1)S(1)}, u32[]{:S(2)}, u32[]{:S(2)}) collective-permute-start(bf16[1040,128]{1,0:T(8,128)(2,1)S(1)} %pad_maximum_fusion.1.refs_1_), channel_id=1, source_target_pairs={{0,512},{256,0},{512,256},{1,513},{257,1},{513,257},{2,514},{258,2... | collective-permute-start | bytes 798728 | tf_op jit(solution)/shard_map/ppermute | solution.py:266
  43.5 10.4 %collective-permute-start.2 = (bf16[512,128]{1,0:T(8,128)(2,1)S(1)}, bf16[512,128]{1,0:T(8,128)(2,1)S(1)}, u32[]{:S(2)}, u32[]{:S(2)}) collective-permute-start(bf16[512,128]{1,0:T(8,128)(2,1)S(1)} %bitcast.37), channel_id=1, source_target_pairs={{0,512},{256,0},{512,256},{1,513},{257,1},{513,257},{2,514},{258,2... | collective-permute-start | bytes 393224 | tf_op jit(solution)/shard_map/ppermute | solution.py:266
  53.9 7.7 %collective-permute-start.4 = (bf16[4,12,88,128]{3,2,1,0:T(8,128)(2,1)S(1)}, bf16[4,12,88,128]{3,2,1,0:T(8,128)(2,1)S(1)}, u32[]{:S(2)}, u32[]{:S(2)}) collective-permute-start(bf16[4,12,88,128]{3,2,1,0:T(8,128)(2,1)S(1)} %all-to-all-done.1.own_ref), channel_id=1, source_target_pairs={{0,1},{1,0},{2,3},{3,2},{4,5},{5,4},{6,7},{7,6},{8,9},{9,8},{10,11... | collective-permute-start | bytes 3244040 | tf_op jit(solution)/shard_map/ppermute | solution.py:266
  64.6 8.4 %copy-start.2 = (s32[2,256]{1,0:T(2,128)S(1)}, s32[2,256]{1,0:T(2,128)}, u32[]{:S(2)}) copy-start(s32[2,256]{1,0:T(2,128)} %param.12) | copy-start | bytes 6148
  64.6 8.4 %copy-start = (s32[128,1024]{1,0:T(8,128)S(1)}, s32[128,1024]{1,0:T(8,128)}, u32[]{:S(2)}) copy-start(s32[128,1024]{1,0:T(8,128)} %neg_ref) | copy-start | bytes 1572868
  64.6 32.2 %all-to-all-start.2 = ((bf16[24,2,88,128]{3,2,1,0:T(8,128)(2,1)}), bf16[24,2,88,128]{3,2,1,0:T(8,128)(2,1)S(1)}, u32[]{:S(2)}, u32[]{:S(2)}) async-start(bf16[24,2,88,128]{3,2,1,0:T(8,128)(2,1)} %tile_sums.1), calls=%async_computation.2 | async-start | bytes 2162688 | tf_op jit(solution)/shard_map/all_to_all | solution.py:257
  98.3 36.6 %all-to-all-start.3 = ((bf16[8,2,256,128]{3,2,1,0:T(8,128)(2,1)}), bf16[8,2,256,128]{3,2,1,0:T(8,128)(2,1)S(1)}, u32[]{:S(2)}, u32[]{:S(2)}) async-start(bf16[8,2,256,128]{3,2,1,0:T(8,128)(2,1)} %broadcast_in_dim.42), calls=%async_computation.3 | async-start | bytes 2097152 | tf_op jit(solution)/shard_map/all_to_all | solution.py:257
  105.8 13.4 %copy-start.1 = (bf16[256,256]{1,0:T(8,128)(2,1)S(1)}, bf16[256,256]{1,0:T(8,128)(2,1)}, u32[]{:S(2)}) copy-start(bf16[256,256]{1,0:T(8,128)(2,1)} %param.8) | copy-start | bytes 393220
  105.9 20.9 %collective-permute-start.7 = (s16[8,128,128]{2,1,0:T(8,128)(2,1)S(1)}, s16[8,128,128]{2,1,0:T(8,128)(2,1)S(1)}, u32[]{:S(2)}, u32[]{:S(2)}) collective-permute-start(s16[8,128,128]{2,1,0:T(8,128)(2,1)S(1)} %get-tuple-element.40), channel_id=1, source_target_pairs={{0,256},{256,512},{512,0},{1,257},{257,513},{513,1},{2,258},{258,5... | collective-permute-start | bytes 786440 | tf_op jit(solution)/shard_map/ppermute | solution.py:266
  111.1 15.8 %collective-permute-start.8 = (s16[8,128,128]{2,1,0:T(8,128)(2,1)S(1)}, s16[8,128,128]{2,1,0:T(8,128)(2,1)S(1)}, u32[]{:S(2)}, u32[]{:S(2)}) collective-permute-start(s16[8,128,128]{2,1,0:T(8,128)(2,1)S(1)} %get-tuple-element.39), channel_id=1, source_target_pairs={{0,512},{256,0},{512,256},{1,513},{257,1},{513,257},{2,514},{258,2... | collective-permute-start | bytes 786440 | tf_op jit(solution)/shard_map/ppermute | solution.py:266
  113.0 10.9 %collective-permute-start.5 = (bf16[2,256,128]{2,1,0:T(8,128)(2,1)S(1)}, bf16[2,256,128]{2,1,0:T(8,128)(2,1)S(1)}, u32[]{:S(2)}, u32[]{:S(2)}) collective-permute-start(bf16[2,256,128]{2,1,0:T(8,128)(2,1)S(1)} %fusion), channel_id=1, source_target_pairs={{0,256},{256,512},{512,0},{1,257},{257,513},{513,1},{2,258},{258,5... | collective-permute-start | bytes 393224 | tf_op jit(solution)/shard_map/ppermute | solution.py:266
  116.4 10.4 %collective-permute-start.6 = (bf16[2,256,128]{2,1,0:T(8,128)(2,1)S(1)}, bf16[2,256,128]{2,1,0:T(8,128)(2,1)S(1)}, u32[]{:S(2)}, u32[]{:S(2)}) collective-permute-start(bf16[2,256,128]{2,1,0:T(8,128)(2,1)S(1)} %fusion), channel_id=1, source_target_pairs={{0,512},{256,0},{512,256},{1,513},{257,1},{513,257},{2,514},{258,2... | collective-permute-start | bytes 393224 | tf_op jit(solution)/shard_map/ppermute | solution.py:266
  138.7 7.8 %collective-permute-start.10 = (f32[8,384]{1,0:T(8,128)S(1)}, f32[8,384]{1,0:T(8,128)S(1)}, u32[]{:S(2)}, u32[]{:S(2)}) collective-permute-start(f32[8,384]{1,0:T(8,128)S(1)} %get-tuple-element.33.refs_0_), channel_id=1, source_target_pairs={{0,512},{256,0},{512,256},{1,513},{257,1},{513,257},{2,514},{258,2... | collective-permute-start | bytes 36872 | tf_op jit(solution)/shard_map/ppermute | solution.py:266
  142.9 5.3 %collective-permute-start.9 = (f32[8,384]{1,0:T(8,128)S(1)}, f32[8,384]{1,0:T(8,128)S(1)}, u32[]{:S(2)}, u32[]{:S(2)}) collective-permute-start(f32[8,384]{1,0:T(8,128)S(1)} %get-tuple-element.33.refs_0_), channel_id=1, source_target_pairs={{0,256},{256,512},{512,0},{1,257},{257,513},{513,1},{2,258},{258,5... | collective-permute-start | bytes 36872 | tf_op jit(solution)/shard_map/ppermute | solution.py:266
  166.8 6.5 %collective-permute-start.11 = (f32[8,256]{1,0:T(8,128)S(1)}, f32[8,256]{1,0:T(8,128)S(1)}, u32[]{:S(2)}, u32[]{:S(2)}) collective-permute-start(f32[8,256]{1,0:T(8,128)S(1)} %reduce_sum.28), channel_id=1, source_target_pairs={{0,1},{1,0},{2,3},{3,2},{4,5},{5,4},{6,7},{7,6},{8,9},{9,8},{10,11... | collective-permute-start | bytes 24584 | tf_op jit(solution)/shard_map/ppermute | solution.py:266
  199.2 14.5 %all-to-all-start.6 = ((f32[32,8,256]{2,1,0:T(8,128)}), f32[32,8,256]{2,1,0:T(8,128)S(1)}, u32[]{:S(2)}, u32[]{:S(2)}) async-start(f32[32,8,256]{2,1,0:T(8,128)} %broadcast_in_dim.45), calls=%async_computation.6 | async-start | bytes 524288 | tf_op jit(solution)/shard_map/all_to_all | solution.py:257

commit v12 on v10

--- a/solution.py
+++ b/solution.py
@@ -81,7 +81,7 @@
 
 
 def tiles_kernel(cols, meta_ref, place_ref, own_ref, other_ref, *refs):
-    tile_refs, (out_ref, acc_ref) = refs[: 2 * ZL], refs[2 * ZL :]
+    *tile_refs, out_ref, acc_ref = refs
     zsize = own_ref.shape[1] // ZL
     slots = meta_ref.shape[2]
     acc_ref[...] = jnp.zeros_like(acc_ref)
@@ -100,8 +100,9 @@
                     at = lax.div(chip, zsize), behind(zl, s) * zsize + lax.rem(chip, zsize)
                     mine = lax.rem(tcol, 2) == core
                     rows = jnp.where(mine, own_ref[at], other_ref[at])
-                    start = (k - EARLY if late else k) * T
-                    tile = tile_refs[2 * s + late][start : start + T, :]
+                    split = late and s < ZL - 1
+                    start = (k - EARLY if split else k) * T
+                    tile = tile_refs[2 * s + split][start : start + T, :]
                     products.append(dot(rows, tile, NT))
                 for j in range(4):
                     k = i * 4 + j
@@ -140,7 +141,7 @@
         functools.partial(tiles_kernel, cols),
         out_shape=jax.ShapeDtypeStruct(shape, bf16),
         in_specs=[pl.BlockSpec(memory_space=pltpu.SMEM)] * 2
-        + [pl.BlockSpec(memory_space=pltpu.VMEM)] * (2 + 2 * ZL),
+        + [pl.BlockSpec(memory_space=pltpu.VMEM)] * (2 + len(tiles)),
         scratch_shapes=[pltpu.VMEM(shape, f32)],
         compiler_params=pltpu.CompilerParams(**PARAMS),
         name="tile_sums",
@@ -305,18 +306,14 @@
     next_some = shift(some, "zl", 1)
     near, next_some = lax.optimization_barrier((near, next_some))
     own = share(near, "x")
-    next_rest, last_some, last_rest = (
-        shift(rest, "zl", 1),
-        shift(some, "zl", 2),
-        shift(rest, "zl", 2),
-    )
-    own, next_rest, last_some, last_rest = lax.optimization_barrier(
-        (own, next_rest, last_some, last_rest)
-    )
-    all_tiles = [some, rest, next_some, next_rest, last_some, last_rest]
+    next_rest = shift(rest, "zl", 1)
+    last = shift(jnp.concatenate([some, rest], 0), "zl", 2)
+    own, next_rest, last = lax.optimization_barrier((own, next_rest, last))
+    all_tiles = [some, rest, next_some, next_rest, last]
     other = shift(own, "core", 1)
     late = (slots - EARLY) * T
-    metas = jnp.stack([x[late : late + 4, :slots] for x in all_tiles[1::2]]).astype(jnp.int32)
+    metas = [rest[late : late + 4], next_rest[late : late + 4], last[slots * T : slots * T + 4]]
+    metas = jnp.stack(metas)[:, :, :slots].astype(jnp.int32)
 
     part = tile_sums(metas, place, own, other, all_tiles, cols, ZL * ysize)
     part, negatives = lax.optimization_barrier((part, negatives))

time: 213 us -> 216 us (1.014)
  starting transfers between devices: 84.3 us -> 80.8 us
  waiting for transfers between devices: 55.5 us -> 58.4 us
  blocking collectives: 35.6 us -> 38.2 us
    ppermute x12 -> x11, waiting for transfers between devices: 24.2 us -> 33.3 us  [shift(): return lax.ppermute(x, axis, [(i, (i + by) % size) for i in range(size)])]
    all_to_all x5, waiting for transfers between devices: 31.3 us -> 25.1 us  [swap(): return lax.all_to_all(x, axis, 0, 0, tiled=True)]
    ppermute x12 -> x11, starting transfers between devices: 44.7 us -> 39.9 us  [shift(): return lax.ppermute(x, axis, [(i, (i + by) % size) for i in range(size)])]
    all_to_all x2, blocking collectives: 35.6 us -> 38.2 us  [swap(): return lax.all_to_all(x, axis, 0, 0, tiled=True)]
  transfers between devices with their start and end apart: 17 -> 16, of which waited for: 12 -> 10; matrix products, arithmetic and copies ran while one was open for 1% -> 1% of each run, Pallas kernels for 8% -> 7%
where the time goes in v12:
time: 216 us; the launch traced here: 214 us
  starting transfers between devices  80.8 us (37%)
  waiting for transfers between devices  58.4 us (27%)
  blocking collectives  38.2 us (18%)
  Pallas kernels  28.2 us (13%)
  local copies, waits for them, and re-layouts  6.41 us (3%)
    all_to_all x5, starting transfers between devices, swap(): return lax.all_to_all(x, axis, 0, 0, tiled=True)  41 us
    ppermute x11, starting transfers between devices, shift(): return lax.ppermute(x, axis, [(i, (i + by) % size) for i in range(size)])  39.9 us
    all_to_all x2, blocking collectives, swap(): return lax.all_to_all(x, axis, 0, 0, tiled=True)  38.2 us
    ppermute x11, waiting for transfers between devices, shift(): return lax.ppermute(x, axis, [(i, (i + by) % size) for i in range(size)])  33.3 us
    all_to_all x5, waiting for transfers between devices, swap(): return lax.all_to_all(x, axis, 0, 0, tiled=True)  25.1 us
    pallas_call x1, Pallas kernels, count_negatives(): pl.pallas_call(functools.partial(counts_kernel, blocks), out_shape=jax.Sh...  15.3 us
  transfers between devices with their start and end apart: 16, of which 10 were waited for; matrix products, arithmetic and copies ran while one was open for 1% of the time, Pallas kernels for 7%

profile of v12, /device:TPU:1, one launch (start us, length us, event | category | flops | bytes accessed | tf_op | source)
XLA Modules:
  0.0 213.7 jit_solution(4834069893120763610)
XLA Ops:
  0.6 1.6 cut_features.1
  2.3 15.7 %all-to-all-start = ((bf16[12,88,128]{2,1,0:T(8,128)(2,1)}), bf16[12,88,128]{2,1,0:T(8,128)(2,1)S(1)}, u32[]{:S(2)}, u32[]{:S(2)}) async-start(bf16[12,88,128]{2,1,0:T(8,128)(2,1)} %cut_features.1), calls=%async_computation | async-start | bytes 540672 | tf_op jit(solution)/shard_map/all_to_all | solution.py:258
  19.0 3.3 %collective-permute-start = (bf16[1024,128]{1,0:T(8,128)(2,1)S(1)}, bf16[1024,128]{1,0:T(8,128)(2,1)S(1)}, u32[]{:S(2)}, u32[]{:S(2)}) collective-permute-start(bf16[1024,128]{1,0:T(8,128)(2,1)S(1)} %bitcast.33), channel_id=1, source_target_pairs={{0,256},{256,512},{512,0},{1,257},{257,513},{513,1},{2,258},{258,5... | collective-permute-start | bytes 786440 | tf_op jit(solution)/shard_map/ppermute | solution.py:267
  22.3 12.7 %collective-permute-done.refs_2_ = bf16[1024,128]{1,0:T(8,128)(2,1)S(1)} collective-permute-done((bf16[1024,128]{1,0:T(8,128)(2,1)S(1)}, bf16[1024,128]{1,0:T(8,128)(2,1)S(1)}, u32[]{:S(2)}, u32[]{:S(2)}) %collective-permute-start) | collective-permute-done | bytes 262176 | tf_op jit(solution)/shard_map/ppermute | solution.py:267
  36.2 4.1 %all-to-all-start.1 = ((bf16[4,12,88,128]{3,2,1,0:T(8,128)(2,1)}), bf16[4,12,88,128]{3,2,1,0:T(8,128)(2,1)S(1)}, u32[]{:S(2)}, u32[]{:S(2)}) async-start(bf16[4,12,88,128]{3,2,1,0:T(8,128)(2,1)} %broadcast_in_dim.21), calls=%async_computation.1 | async-start | bytes 2162688 | tf_op jit(solution)/shard_map/all_to_all | solution.py:258
  41.4 2.7 %collective-permute-start.2 = (bf16[1552,128]{1,0:T(8,128)(2,1)S(1)}, bf16[1552,128]{1,0:T(8,128)(2,1)S(1)}, u32[]{:S(2)}, u32[]{:S(2)}) collective-permute-start(bf16[1552,128]{1,0:T(8,128)(2,1)S(1)} %pad_maximum_fusion), channel_id=1, source_target_pairs={{0,512},{256,0},{512,256},{1,513},{257,1},{513,257},{2,514},{258,2... | collective-permute-start | bytes 1191944 | tf_op jit(solution)/shard_map/ppermute | solution.py:267
  44.1 2.6 %collective-permute-start.1 = (bf16[528,128]{1,0:T(8,128)(2,1)S(1)}, bf16[528,128]{1,0:T(8,128)(2,1)S(1)}, u32[]{:S(2)}, u32[]{:S(2)}) collective-permute-start(bf16[528,128]{1,0:T(8,128)(2,1)S(1)} %pad_maximum_fusion.2.refs_1_), channel_id=1, source_target_pairs={{0,256},{256,512},{512,0},{1,257},{257,513},{513,1},{2,258},{258,5... | collective-permute-start | bytes 405512 | tf_op jit(solution)/shard_map/ppermute | solution.py:267
  46.7 8.8 %collective-permute-done.1.refs_3_ = bf16[528,128]{1,0:T(8,128)(2,1)S(1)} collective-permute-done((bf16[528,128]{1,0:T(8,128)(2,1)S(1)}, bf16[528,128]{1,0:T(8,128)(2,1)S(1)}, u32[]{:S(2)}, u32[]{:S(2)}) %collective-permute-start.1) | collective-permute-done | bytes 135200 | tf_op jit(solution)/shard_map/ppermute | solution.py:267
  55.5 4.2 %collective-permute-start.3 = (bf16[4,12,88,128]{3,2,1,0:T(8,128)(2,1)S(1)}, bf16[4,12,88,128]{3,2,1,0:T(8,128)(2,1)S(1)}, u32[]{:S(2)}, u32[]{:S(2)}) collective-permute-start(bf16[4,12,88,128]{3,2,1,0:T(8,128)(2,1)S(1)} %all-to-all-done.1.own_ref), channel_id=1, source_target_pairs={{0,1},{1,0},{2,3},{3,2},{4,5},{5,4},{6,7},{7,6},{8,9},{9,8},{10,11... | collective-permute-start | bytes 3244040 | tf_op jit(solution)/shard_map/ppermute | solution.py:267
  59.8 2.2 %collective-permute-done.3.other_ref = bf16[4,12,88,128]{3,2,1,0:T(8,128)(2,1)S(1)} collective-permute-done((bf16[4,12,88,128]{3,2,1,0:T(8,128)(2,1)S(1)}, bf16[4,12,88,128]{3,2,1,0:T(8,128)(2,1)S(1)}, u32[]{:S(2)}, u32[]{:S(2)}) %collective-permute-start.3) | collective-permute-done | bytes 1081376 | tf_op jit(solution)/shard_map/ppermute | solution.py:267
  62.0 2.8 %tile_sums.1 = bf16[24,2,88,128]{3,2,1,0:T(8,128)(2,1)} custom-call(s32[3,4,12]{2,1,0:T(4,128)S(1)} %fusion.10.meta_ref, s32[2]{0:T(128)S(1)} %pad_add_fusion.1.place_ref, bf16[4,12,88,128]{3,2,1,0:T(8,128)(2,1)S(1)} %all-to-all-done.1.own_ref, bf16[4,12,88,128]{3,2,1,0:T(8,128)(2,1)S(1)} %collective-permute-done.3.other_ref, ...), custom_call_target="tpu_custom_call" | custom-call | tf_op jit(solution)/shard_map/tile_sums/pallas_call | solution.py:140
  64.7 8.6 %all-to-all-start.2 = ((bf16[24,2,88,128]{3,2,1,0:T(8,128)(2,1)}), bf16[24,2,88,128]{3,2,1,0:T(8,128)(2,1)S(1)}, u32[]{:S(2)}, u32[]{:S(2)}) async-start(bf16[24,2,88,128]{3,2,1,0:T(8,128)(2,1)} %tile_sums.1), calls=%async_computation.2 | async-start | bytes 2162688 | tf_op jit(solution)/shard_map/all_to_all | solution.py:258
  73.4 15.3 %counts.1 = s16[24,128,128]{2,1,0:T(8,128)(2,1)S(1)} custom-call(s32[128,1024]{1,0:T(8,128)S(1)} %copy-done), custom_call_target="tpu_custom_call" | custom-call | flops 4294967296 | bytes 2097152 | tf_op jit(solution)/shard_map/counts/pallas_call | solution.py:67
  88.7 7.1 %all-to-all-done.2 = bf16[24,2,88,128]{3,2,1,0:T(8,128)(2,1)S(1)} async-done(((bf16[24,2,88,128]{3,2,1,0:T(8,128)(2,1)}), bf16[24,2,88,128]{3,2,1,0:T(8,128)(2,1)S(1)}, u32[]{:S(2)}, u32[]{:S(2)}) %all-to-all-start.2) | async-done | bytes 1081376 | tf_op jit(solution)/shard_map/all_to_all | solution.py:258
  97.3 8.6 %all-to-all-start.3 = ((bf16[8,2,256,128]{3,2,1,0:T(8,128)(2,1)}), bf16[8,2,256,128]{3,2,1,0:T(8,128)(2,1)S(1)}, u32[]{:S(2)}, u32[]{:S(2)}) async-start(bf16[8,2,256,128]{3,2,1,0:T(8,128)(2,1)} %broadcast_in_dim.42), calls=%async_computation.3 | async-start | bytes 2097152 | tf_op jit(solution)/shard_map/all_to_all | solution.py:258
  106.0 5.7 %collective-permute-start.6 = (s16[8,128,128]{2,1,0:T(8,128)(2,1)S(1)}, s16[8,128,128]{2,1,0:T(8,128)(2,1)S(1)}, u32[]{:S(2)}, u32[]{:S(2)}) collective-permute-start(s16[8,128,128]{2,1,0:T(8,128)(2,1)S(1)} %get-tuple-element.36), channel_id=1, source_target_pairs={{0,256},{256,512},{512,0},{1,257},{257,513},{513,1},{2,258},{258,5... | collective-permute-start | bytes 786440 | tf_op jit(solution)/shard_map/ppermute | solution.py:267
  111.7 1.9 collective-permute-start.7
  113.7 3.4 %collective-permute-start.4 = (bf16[2,256,128]{2,1,0:T(8,128)(2,1)S(1)}, bf16[2,256,128]{2,1,0:T(8,128)(2,1)S(1)}, u32[]{:S(2)}, u32[]{:S(2)}) collective-permute-start(bf16[2,256,128]{2,1,0:T(8,128)(2,1)S(1)} %fusion), channel_id=1, source_target_pairs={{0,256},{256,512},{512,0},{1,257},{257,513},{513,1},{2,258},{258,5... | collective-permute-start | bytes 393224 | tf_op jit(solution)/shard_map/ppermute | solution.py:267
  117.0 2.8 %collective-permute-start.5 = (bf16[2,256,128]{2,1,0:T(8,128)(2,1)S(1)}, bf16[2,256,128]{2,1,0:T(8,128)(2,1)S(1)}, u32[]{:S(2)}, u32[]{:S(2)}) collective-permute-start(bf16[2,256,128]{2,1,0:T(8,128)(2,1)S(1)} %fusion), channel_id=1, source_target_pairs={{0,512},{256,0},{512,256},{1,513},{257,1},{513,257},{2,514},{258,2... | collective-permute-start | bytes 393224 | tf_op jit(solution)/shard_map/ppermute | solution.py:267
  120.0 4.1 %collective-permute-done.4 = bf16[2,256,128]{2,1,0:T(8,128)(2,1)S(1)} collective-permute-done((bf16[2,256,128]{2,1,0:T(8,128)(2,1)S(1)}, bf16[2,256,128]{2,1,0:T(8,128)(2,1)S(1)}, u32[]{:S(2)}, u32[]{:S(2)}) %collective-permute-start.4) | collective-permute-done | bytes 131104 | tf_op jit(solution)/shard_map/ppermute | solution.py:267
  124.1 2.9 %collective-permute-done.5 = bf16[2,256,128]{2,1,0:T(8,128)(2,1)S(1)} collective-permute-done((bf16[2,256,128]{2,1,0:T(8,128)(2,1)S(1)}, bf16[2,256,128]{2,1,0:T(8,128)(2,1)S(1)}, u32[]{:S(2)}, u32[]{:S(2)}) %collective-permute-start.5) | collective-permute-done | bytes 131104 | tf_op jit(solution)/shard_map/ppermute | solution.py:267
  127.1 8.0 %all-to-all-done.3.a_ref = bf16[8,2,256,128]{3,2,1,0:T(8,128)(2,1)S(1)} async-done(((bf16[8,2,256,128]{3,2,1,0:T(8,128)(2,1)}), bf16[8,2,256,128]{3,2,1,0:T(8,128)(2,1)S(1)}, u32[]{:S(2)}, u32[]{:S(2)}) %all-to-all-start.3) | async-done | bytes 1048608 | tf_op jit(solution)/shard_map/all_to_all | solution.py:258
  135.1 3.8 %scores.1 = (f32[8,384]{1,0:T(8,128)S(1)}, bf16[4,2,256,384]{3,2,1,0:T(8,128)(2,1)S(1)}, bf16[4,2,256,256]{3,2,1,0:T(8,128)(2,1)S(1)}) custom-call(s32[2]{0:T(128)S(1)} %pad_add_fusion.1.place_ref, bf16[3,2,256,128]{3,2,1,0:T(8,128)(2,1)S(1)} %pad_maximum_fusion.1.n_ref, bf16[8,2,256,128]{3,2,1,0:T(8,128)(2,1)S(1)} %all-to-all-done.3.a_ref, ...), custom_call_target="tpu_custom_call" | custom-call | flops 2147483648 | bytes 4194304 | tf_op jit(solution)/shard_map/scores/pallas_call | solution.py:335
  138.9 5.6 %collective-permute-start.8 = (f32[8,384]{1,0:T(8,128)S(1)}, f32[8,384]{1,0:T(8,128)S(1)}, u32[]{:S(2)}, u32[]{:S(2)}) collective-permute-start(f32[8,384]{1,0:T(8,128)S(1)} %get-tuple-element.31.refs_0_), channel_id=1, source_target_pairs={{0,256},{256,512},{512,0},{1,257},{257,513},{513,1},{2,258},{258,5... | collective-permute-start | bytes 36872 | tf_op jit(solution)/shard_map/ppermute | solution.py:267
  144.5 1.9 collective-permute-start.9
  147.1 1.8 collective-permute-done.9.refs_2_
  148.9 4.1 %grads.1 = (f32[8,384]{1,0:T(8,128)S(1)}, f32[256,256]{1,0:T(8,128)S(1)}) custom-call(s32[2]{0:T(128)S(1)} %pad_add_fusion.1.place_ref, bf16[3,2,256,128]{3,2,1,0:T(8,128)(2,1)S(1)} %pad_maximum_fusion.1.n_ref, bf16[8,2,256,128]{3,2,1,0:T(8,128)(2,1)S(1)} %all-to-all-done.3.a_ref, bf16[256,256]{1,0:T(8,128)(2,1)S(1)} %bitcast.39, ...), custom_call_target="tpu_custom_call" | custom-call | flops 2147483648 | bytes 4194304 | tf_op jit(solution)/shard_map/grads/pallas_call | solution.py:353
  153.0 13.6 %all_to_all.35 = f32[32,8,256]{2,1,0:T(8,128)S(1)} all-to-all(f32[32,8,256]{2,1,0:T(8,128)S(1)} %bitcast.37), channel_id=1, replica_groups=mesh['zl'=3,'y'=8,'x'=4,'zh'=4,'core'=2] {'y','x'}, dimensions={0} | all-to-all | bytes 524288 | tf_op jit(solution)/shard_map/all_to_all | solution.py:258
  166.6 5.7 %collective-permute-start.10 = (f32[8,256]{1,0:T(8,128)S(1)}, f32[8,256]{1,0:T(8,128)S(1)}, u32[]{:S(2)}, u32[]{:S(2)}) collective-permute-start(f32[8,256]{1,0:T(8,128)S(1)} %reduce_sum.28), channel_id=1, source_target_pairs={{0,1},{1,0},{2,3},{3,2},{4,5},{5,4},{6,7},{7,6},{8,9},{9,8},{10,11... | collective-permute-start | bytes 24584 | tf_op jit(solution)/shard_map/ppermute | solution.py:267
  173.1 24.6 %all_to_all.36 = f32[12,8,256]{2,1,0:T(8,128)S(1)} all-to-all(f32[12,8,256]{2,1,0:T(8,128)S(1)} %broadcast_in_dim.44), channel_id=1, replica_groups=mesh['zl'=3,'y'=8,'x'=4,'zh'=4,'core'=2] {'zl','zh'}, dimensions={0} | all-to-all | bytes 196608 | tf_op jit(solution)/shard_map/all_to_all | solution.py:258
  198.5 3.9 %all-to-all-start.6 = ((f32[32,8,256]{2,1,0:T(8,128)}), f32[32,8,256]{2,1,0:T(8,128)S(1)}, u32[]{:S(2)}, u32[]{:S(2)}) async-start(f32[32,8,256]{2,1,0:T(8,128)} %broadcast_in_dim.45), calls=%async_computation.6 | async-start | bytes 524288 | tf_op jit(solution)/shard_map/all_to_all | solution.py:258
  202.9 10.0 %all-to-all-done.6 = f32[32,8,256]{2,1,0:T(8,128)S(1)} async-done(((f32[32,8,256]{2,1,0:T(8,128)}), f32[32,8,256]{2,1,0:T(8,128)S(1)}, u32[]{:S(2)}, u32[]{:S(2)}) %all-to-all-start.6) | async-done | bytes 262176 | tf_op jit(solution)/shard_map/all_to_all | solution.py:258
  (49 shorter events, 8.5 us)
Async XLA Ops:
  2.3 32.8 %all-to-all-start = ((bf16[12,88,128]{2,1,0:T(8,128)(2,1)}), bf16[12,88,128]{2,1,0:T(8,128)(2,1)S(1)}, u32[]{:S(2)}, u32[]{:S(2)}) async-start(bf16[12,88,128]{2,1,0:T(8,128)(2,1)} %cut_features.1), calls=%async_computation | async-start | bytes 540672 | tf_op jit(solution)/shard_map/all_to_all | solution.py:258
  19.0 16.1 %collective-permute-start = (bf16[1024,128]{1,0:T(8,128)(2,1)S(1)}, bf16[1024,128]{1,0:T(8,128)(2,1)S(1)}, u32[]{:S(2)}, u32[]{:S(2)}) collective-permute-start(bf16[1024,128]{1,0:T(8,128)(2,1)S(1)} %bitcast.33), channel_id=1, source_target_pairs={{0,256},{256,512},{512,0},{1,257},{257,513},{513,1},{2,258},{258,5... | collective-permute-start | bytes 786440 | tf_op jit(solution)/shard_map/ppermute | solution.py:267
  36.2 4.2 %copy-start.4 = (s32[12]{0:T(128)S(1)}, s32[12]{0:T(128)}, u32[]{:S(2)}) copy-start(s32[12]{0:T(128)} %param.10) | copy-start | bytes 148
  36.2 5.1 %copy-start.3 = (s32[2,12]{1,0:T(2,128)S(1)}, s32[2,12]{1,0:T(2,128)}, u32[]{:S(2)}) copy-start(s32[2,12]{1,0:T(2,128)} %param.11) | copy-start | bytes 292
  36.2 19.3 %all-to-all-start.1 = ((bf16[4,12,88,128]{3,2,1,0:T(8,128)(2,1)}), bf16[4,12,88,128]{3,2,1,0:T(8,128)(2,1)S(1)}, u32[]{:S(2)}, u32[]{:S(2)}) async-start(bf16[4,12,88,128]{3,2,1,0:T(8,128)(2,1)} %broadcast_in_dim.21), calls=%async_computation.1 | async-start | bytes 2162688 | tf_op jit(solution)/shard_map/all_to_all | solution.py:258
  41.4 14.1 %collective-permute-start.2 = (bf16[1552,128]{1,0:T(8,128)(2,1)S(1)}, bf16[1552,128]{1,0:T(8,128)(2,1)S(1)}, u32[]{:S(2)}, u32[]{:S(2)}) collective-permute-start(bf16[1552,128]{1,0:T(8,128)(2,1)S(1)} %pad_maximum_fusion), channel_id=1, source_target_pairs={{0,512},{256,0},{512,256},{1,513},{257,1},{513,257},{2,514},{258,2... | collective-permute-start | bytes 1191944 | tf_op jit(solution)/shard_map/ppermute | solution.py:267
  44.1 11.4 %collective-permute-start.1 = (bf16[528,128]{1,0:T(8,128)(2,1)S(1)}, bf16[528,128]{1,0:T(8,128)(2,1)S(1)}, u32[]{:S(2)}, u32[]{:S(2)}) collective-permute-start(bf16[528,128]{1,0:T(8,128)(2,1)S(1)} %pad_maximum_fusion.2.refs_1_), channel_id=1, source_target_pairs={{0,256},{256,512},{512,0},{1,257},{257,513},{513,1},{2,258},{258,5... | collective-permute-start | bytes 405512 | tf_op jit(solution)/shard_map/ppermute | solution.py:267
  55.5 6.5 %collective-permute-start.3 = (bf16[4,12,88,128]{3,2,1,0:T(8,128)(2,1)S(1)}, bf16[4,12,88,128]{3,2,1,0:T(8,128)(2,1)S(1)}, u32[]{:S(2)}, u32[]{:S(2)}) collective-permute-start(bf16[4,12,88,128]{3,2,1,0:T(8,128)(2,1)S(1)} %all-to-all-done.1.own_ref), channel_id=1, source_target_pairs={{0,1},{1,0},{2,3},{3,2},{4,5},{5,4},{6,7},{7,6},{8,9},{9,8},{10,11... | collective-permute-start | bytes 3244040 | tf_op jit(solution)/shard_map/ppermute | solution.py:267
  64.7 8.6 %copy-start.2 = (s32[2,256]{1,0:T(2,128)S(1)}, s32[2,256]{1,0:T(2,128)}, u32[]{:S(2)}) copy-start(s32[2,256]{1,0:T(2,128)} %param.12) | copy-start | bytes 6148
  64.7 8.6 %copy-start = (s32[128,1024]{1,0:T(8,128)S(1)}, s32[128,1024]{1,0:T(8,128)}, u32[]{:S(2)}) copy-start(s32[128,1024]{1,0:T(8,128)} %neg_ref) | copy-start | bytes 1572868
  64.7 31.0 %all-to-all-start.2 = ((bf16[24,2,88,128]{3,2,1,0:T(8,128)(2,1)}), bf16[24,2,88,128]{3,2,1,0:T(8,128)(2,1)S(1)}, u32[]{:S(2)}, u32[]{:S(2)}) async-start(bf16[24,2,88,128]{3,2,1,0:T(8,128)(2,1)} %tile_sums.1), calls=%async_computation.2 | async-start | bytes 2162688 | tf_op jit(solution)/shard_map/all_to_all | solution.py:258
  97.3 37.8 %all-to-all-start.3 = ((bf16[8,2,256,128]{3,2,1,0:T(8,128)(2,1)}), bf16[8,2,256,128]{3,2,1,0:T(8,128)(2,1)S(1)}, u32[]{:S(2)}, u32[]{:S(2)}) async-start(bf16[8,2,256,128]{3,2,1,0:T(8,128)(2,1)} %broadcast_in_dim.42), calls=%async_computation.3 | async-start | bytes 2097152 | tf_op jit(solution)/shard_map/all_to_all | solution.py:258
  105.9 14.0 %copy-start.1 = (bf16[256,256]{1,0:T(8,128)(2,1)S(1)}, bf16[256,256]{1,0:T(8,128)(2,1)}, u32[]{:S(2)}) copy-start(bf16[256,256]{1,0:T(8,128)(2,1)} %param.8) | copy-start | bytes 393220
  106.0 21.0 %collective-permute-start.6 = (s16[8,128,128]{2,1,0:T(8,128)(2,1)S(1)}, s16[8,128,128]{2,1,0:T(8,128)(2,1)S(1)}, u32[]{:S(2)}, u32[]{:S(2)}) collective-permute-start(s16[8,128,128]{2,1,0:T(8,128)(2,1)S(1)} %get-tuple-element.36), channel_id=1, source_target_pairs={{0,256},{256,512},{512,0},{1,257},{257,513},{513,1},{2,258},{258,5... | collective-permute-start | bytes 786440 | tf_op jit(solution)/shard_map/ppermute | solution.py:267
  111.7 15.3 %collective-permute-start.7 = (s16[8,128,128]{2,1,0:T(8,128)(2,1)S(1)}, s16[8,128,128]{2,1,0:T(8,128)(2,1)S(1)}, u32[]{:S(2)}, u32[]{:S(2)}) collective-permute-start(s16[8,128,128]{2,1,0:T(8,128)(2,1)S(1)} %get-tuple-element.35), channel_id=1, source_target_pairs={{0,512},{256,0},{512,256},{1,513},{257,1},{513,257},{2,514},{258,2... | collective-permute-start | bytes 786440 | tf_op jit(solution)/shard_map/ppermute | solution.py:267
  113.7 10.4 %collective-permute-start.4 = (bf16[2,256,128]{2,1,0:T(8,128)(2,1)S(1)}, bf16[2,256,128]{2,1,0:T(8,128)(2,1)S(1)}, u32[]{:S(2)}, u32[]{:S(2)}) collective-permute-start(bf16[2,256,128]{2,1,0:T(8,128)(2,1)S(1)} %fusion), channel_id=1, source_target_pairs={{0,256},{256,512},{512,0},{1,257},{257,513},{513,1},{2,258},{258,5... | collective-permute-start | bytes 393224 | tf_op jit(solution)/shard_map/ppermute | solution.py:267
  117.0 9.9 %collective-permute-start.5 = (bf16[2,256,128]{2,1,0:T(8,128)(2,1)S(1)}, bf16[2,256,128]{2,1,0:T(8,128)(2,1)S(1)}, u32[]{:S(2)}, u32[]{:S(2)}) collective-permute-start(bf16[2,256,128]{2,1,0:T(8,128)(2,1)S(1)} %fusion), channel_id=1, source_target_pairs={{0,512},{256,0},{512,256},{1,513},{257,1},{513,257},{2,514},{258,2... | collective-permute-start | bytes 393224 | tf_op jit(solution)/shard_map/ppermute | solution.py:267
  138.9 8.2 %collective-permute-start.8 = (f32[8,384]{1,0:T(8,128)S(1)}, f32[8,384]{1,0:T(8,128)S(1)}, u32[]{:S(2)}, u32[]{:S(2)}) collective-permute-start(f32[8,384]{1,0:T(8,128)S(1)} %get-tuple-element.31.refs_0_), channel_id=1, source_target_pairs={{0,256},{256,512},{512,0},{1,257},{257,513},{513,1},{2,258},{258,5... | collective-permute-start | bytes 36872 | tf_op jit(solution)/shard_map/ppermute | solution.py:267
  144.5 4.4 %collective-permute-start.9 = (f32[8,384]{1,0:T(8,128)S(1)}, f32[8,384]{1,0:T(8,128)S(1)}, u32[]{:S(2)}, u32[]{:S(2)}) collective-permute-start(f32[8,384]{1,0:T(8,128)S(1)} %get-tuple-element.31.refs_0_), channel_id=1, source_target_pairs={{0,512},{256,0},{512,256},{1,513},{257,1},{513,257},{2,514},{258,2... | collective-permute-start | bytes 36872 | tf_op jit(solution)/shard_map/ppermute | solution.py:267
  166.6 6.6 %collective-permute-start.10 = (f32[8,256]{1,0:T(8,128)S(1)}, f32[8,256]{1,0:T(8,128)S(1)}, u32[]{:S(2)}, u32[]{:S(2)}) collective-permute-start(f32[8,256]{1,0:T(8,128)S(1)} %reduce_sum.28), channel_id=1, source_target_pairs={{0,1},{1,0},{2,3},{3,2},{4,5},{5,4},{6,7},{7,6},{8,9},{9,8},{10,11... | collective-permute-start | bytes 24584 | tf_op jit(solution)/shard_map/ppermute | solution.py:267
  198.5 14.5 %all-to-all-start.6 = ((f32[32,8,256]{2,1,0:T(8,128)}), f32[32,8,256]{2,1,0:T(8,128)S(1)}, u32[]{:S(2)}, u32[]{:S(2)}) async-start(f32[32,8,256]{2,1,0:T(8,128)} %broadcast_in_dim.45), calls=%async_computation.6 | async-start | bytes 524288 | tf_op jit(solution)/shard_map/all_to_all | solution.py:258

commit v13 on v10

--- a/solution.py
+++ b/solution.py
@@ -157,6 +157,30 @@
     return z * rinv, rinv
 
 
+def sums_kernel(got_ref, keep_ref, agg_ref, sent_ref):
+    copies, _, width, _ = sent_ref.shape
+    for v in range(2):
+        shares = [
+            sum(got_ref[s * copies + y, v].astype(f32) for y in range(copies)) for s in range(ZL)
+        ]
+        agg = (jnp.concatenate(shares, 0)[:width] * keep_ref[v]).astype(bf16)
+        agg_ref[v] = agg
+        for y in range(copies):
+            sent_ref[y, v] = agg
+
+
+def own_sums(got, keep, copies):
+    return pl.pallas_call(
+        sums_kernel,
+        out_shape=(
+            jax.ShapeDtypeStruct(keep.shape, bf16),
+            jax.ShapeDtypeStruct((copies,) + keep.shape, bf16),
+        ),
+        compiler_params=pltpu.CompilerParams(**PARAMS),
+        name="own_sums",
+    )(got, keep)
+
+
 def pair_of(a_ref, p, v):
     return jnp.concatenate([a_ref[2 * p, v], a_ref[2 * p + 1, v]], 1)
 
@@ -323,11 +347,10 @@
     got = swap(part, ROW)
     counts = count_negatives(negatives, ZL * ysize)
     got, counts = lax.optimization_barrier((got, counts))
-    agg = jnp.sum(got.reshape(ZL, ysize, 2, FS, nodes).astype(f32), 1)
-    agg = agg.transpose(1, 0, 2, 3).reshape(2, ZL * FS, nodes)[:, :width]
-    agg = (agg * feature_keep.astype(f32)[:, :, None]).astype(bf16)
-    agg, counts = lax.optimization_barrier((agg, counts))
-    members = share(agg, "y")
+    keep = jnp.broadcast_to(feature_keep.astype(f32)[:, :, None], (2, width, nodes))
+    agg, sent = own_sums(got, keep, ysize)
+    agg, sent, counts = lax.optimization_barrier((agg, sent, counts))
+    members = swap(sent, "y")
     anchors = jnp.stack(around(agg, whole, "zl"))
     ahead = lambda x, s: lax.dynamic_index_in_dim(x, lax.rem(zl + s, ZL), 0, keepdims=False)
     counts = jnp.stack(around(counts.reshape(ZL, ysize, nodes, nodes), ahead, "zl"))

time: 213 us -> 213 us (level)
  no operation moved by 1% of the time
where the time goes in v13:
time: 213 us; the launch traced here: 211 us
  starting transfers between devices  84 us (39%)
  waiting for transfers between devices  54.8 us (26%)
  blocking collectives  36.9 us (17%)
  Pallas kernels  29.4 us (14%)
  local copies, waits for them, and re-layouts  4.39 us (2%)
    ppermute x12, starting transfers between devices, shift(): return lax.ppermute(x, axis, [(i, (i + by) % size) for i in range(size)])  44.3 us
    all_to_all x5, starting transfers between devices, swap(): return lax.all_to_all(x, axis, 0, 0, tiled=True)  39.7 us
    all_to_all x2, blocking collectives, swap(): return lax.all_to_all(x, axis, 0, 0, tiled=True)  36.9 us
    all_to_all x5, waiting for transfers between devices, swap(): return lax.all_to_all(x, axis, 0, 0, tiled=True)  30.6 us
    ppermute x12, waiting for transfers between devices, shift(): return lax.ppermute(x, axis, [(i, (i + by) % size) for i in range(size)])  24.2 us
    pallas_call x1, Pallas kernels, count_negatives(): pl.pallas_call(functools.partial(counts_kernel, blocks), out_shape=jax.Sh...  15.3 us
  transfers between devices with their start and end apart: 17, of which 12 were waited for; matrix products, arithmetic and copies ran while one was open for 1% of the time, Pallas kernels for 8%

profile of v13, /device:TPU:1, one launch (start us, length us, event | category | flops | bytes accessed | tf_op | source)
XLA Modules:
  0.0 210.8 jit_solution(9267264019756462398)
XLA Ops:
  2.3 15.7 %all-to-all-start = ((bf16[12,88,128]{2,1,0:T(8,128)(2,1)}), bf16[12,88,128]{2,1,0:T(8,128)(2,1)S(1)}, u32[]{:S(2)}, u32[]{:S(2)}) async-start(bf16[12,88,128]{2,1,0:T(8,128)(2,1)} %cut_features.1), calls=%async_computation | async-start | bytes 540672 | tf_op jit(solution)/shard_map/all_to_all | solution.py:281
  19.0 3.3 %collective-permute-start = (bf16[1024,128]{1,0:T(8,128)(2,1)S(1)}, bf16[1024,128]{1,0:T(8,128)(2,1)S(1)}, u32[]{:S(2)}, u32[]{:S(2)}) collective-permute-start(bf16[1024,128]{1,0:T(8,128)(2,1)S(1)} %bitcast.31), channel_id=1, source_target_pairs={{0,256},{256,512},{512,0},{1,257},{257,513},{513,1},{2,258},{258,5... | collective-permute-start | bytes 786440 | tf_op jit(solution)/shard_map/ppermute | solution.py:290
  22.3 2.8 %collective-permute-start.2 = (bf16[1024,128]{1,0:T(8,128)(2,1)S(1)}, bf16[1024,128]{1,0:T(8,128)(2,1)S(1)}, u32[]{:S(2)}, u32[]{:S(2)}) collective-permute-start(bf16[1024,128]{1,0:T(8,128)(2,1)S(1)} %bitcast.32), channel_id=1, source_target_pairs={{0,512},{256,0},{512,256},{1,513},{257,1},{513,257},{2,514},{258,2... | collective-permute-start | bytes 786440 | tf_op jit(solution)/shard_map/ppermute | solution.py:290
  25.2 9.9 %collective-permute-done.refs_2_ = bf16[1024,128]{1,0:T(8,128)(2,1)S(1)} collective-permute-done((bf16[1024,128]{1,0:T(8,128)(2,1)S(1)}, bf16[1024,128]{1,0:T(8,128)(2,1)S(1)}, u32[]{:S(2)}, u32[]{:S(2)}) %collective-permute-start) | collective-permute-done | bytes 262176 | tf_op jit(solution)/shard_map/ppermute | solution.py:290
  36.2 4.1 %all-to-all-start.1 = ((bf16[4,12,88,128]{3,2,1,0:T(8,128)(2,1)}), bf16[4,12,88,128]{3,2,1,0:T(8,128)(2,1)S(1)}, u32[]{:S(2)}, u32[]{:S(2)}) async-start(bf16[4,12,88,128]{3,2,1,0:T(8,128)(2,1)} %broadcast_in_dim.19), calls=%async_computation.1 | async-start | bytes 2162688 | tf_op jit(solution)/shard_map/all_to_all | solution.py:281
  40.4 1.9 collective-permute-start.1
  42.4 4.3 %collective-permute-start.3 = (bf16[528,128]{1,0:T(8,128)(2,1)S(1)}, bf16[528,128]{1,0:T(8,128)(2,1)S(1)}, u32[]{:S(2)}, u32[]{:S(2)}) collective-permute-start(bf16[528,128]{1,0:T(8,128)(2,1)S(1)} %pad_maximum_fusion.1.refs_1_), channel_id=1, source_target_pairs={{0,512},{256,0},{512,256},{1,513},{257,1},{513,257},{2,514},{258,2... | collective-permute-start | bytes 405512 | tf_op jit(solution)/shard_map/ppermute | solution.py:290
  48.8 4.0 %all-to-all-done.1.own_ref = bf16[4,12,88,128]{3,2,1,0:T(8,128)(2,1)S(1)} async-done(((bf16[4,12,88,128]{3,2,1,0:T(8,128)(2,1)}), bf16[4,12,88,128]{3,2,1,0:T(8,128)(2,1)S(1)}, u32[]{:S(2)}, u32[]{:S(2)}) %all-to-all-start.1) | async-done | bytes 1081376 | tf_op jit(solution)/shard_map/all_to_all | solution.py:281
  52.8 5.8 %collective-permute-start.4 = (bf16[4,12,88,128]{3,2,1,0:T(8,128)(2,1)S(1)}, bf16[4,12,88,128]{3,2,1,0:T(8,128)(2,1)S(1)}, u32[]{:S(2)}, u32[]{:S(2)}) collective-permute-start(bf16[4,12,88,128]{3,2,1,0:T(8,128)(2,1)S(1)} %all-to-all-done.1.own_ref), channel_id=1, source_target_pairs={{0,1},{1,0},{2,3},{3,2},{4,5},{5,4},{6,7},{7,6},{8,9},{9,8},{10,11... | collective-permute-start | bytes 3244040 | tf_op jit(solution)/shard_map/ppermute | solution.py:290
  58.8 2.2 %collective-permute-done.4.other_ref = bf16[4,12,88,128]{3,2,1,0:T(8,128)(2,1)S(1)} collective-permute-done((bf16[4,12,88,128]{3,2,1,0:T(8,128)(2,1)S(1)}, bf16[4,12,88,128]{3,2,1,0:T(8,128)(2,1)S(1)}, u32[]{:S(2)}, u32[]{:S(2)}) %collective-permute-start.4) | collective-permute-done | bytes 1081376 | tf_op jit(solution)/shard_map/ppermute | solution.py:290
  61.0 2.7 %tile_sums.1 = bf16[24,2,88,128]{3,2,1,0:T(8,128)(2,1)} custom-call(s32[3,4,12]{2,1,0:T(4,128)S(1)} %maximum_convert_fusion.meta_ref, s32[2]{0:T(128)S(1)} %pad_add_fusion.1.place_ref, bf16[4,12,88,128]{3,2,1,0:T(8,128)(2,1)S(1)} %all-to-all-done.1.own_ref, bf16[4,12,88,128]{3,2,1,0:T(8,128)(2,1)S(1)} %collective-permute-done.4.other_ref, ...), custom_call_target="tpu_custom_call" | custom-call | tf_op jit(solution)/shard_map/tile_sums/pallas_call | solution.py:139
  63.7 8.6 %all-to-all-start.2 = ((bf16[24,2,88,128]{3,2,1,0:T(8,128)(2,1)}), bf16[24,2,88,128]{3,2,1,0:T(8,128)(2,1)S(1)}, u32[]{:S(2)}, u32[]{:S(2)}) async-start(bf16[24,2,88,128]{3,2,1,0:T(8,128)(2,1)} %tile_sums.1), calls=%async_computation.2 | async-start | bytes 2162688 | tf_op jit(solution)/shard_map/all_to_all | solution.py:281
  72.4 15.3 %counts.1 = s16[24,128,128]{2,1,0:T(8,128)(2,1)S(1)} custom-call(s32[128,1024]{1,0:T(8,128)S(1)} %copy-done), custom_call_target="tpu_custom_call" | custom-call | flops 4294967296 | bytes 2097152 | tf_op jit(solution)/shard_map/counts/pallas_call | solution.py:67
  87.7 8.5 %all-to-all-done.2.got_ref = bf16[24,2,88,128]{3,2,1,0:T(8,128)(2,1)S(1)} async-done(((bf16[24,2,88,128]{3,2,1,0:T(8,128)(2,1)}), bf16[24,2,88,128]{3,2,1,0:T(8,128)(2,1)S(1)}, u32[]{:S(2)}, u32[]{:S(2)}) %all-to-all-start.2) | async-done | bytes 1081376 | tf_op jit(solution)/shard_map/all_to_all | solution.py:281
  97.5 7.4 %all-to-all-start.3 = ((bf16[8,2,256,128]{3,2,1,0:T(8,128)(2,1)}), bf16[8,2,256,128]{3,2,1,0:T(8,128)(2,1)S(1)}, u32[]{:S(2)}, u32[]{:S(2)}) async-start(bf16[8,2,256,128]{3,2,1,0:T(8,128)(2,1)} %get-tuple-element.35), calls=%async_computation.3 | async-start | bytes 2097152 | tf_op jit(solution)/shard_map/all_to_all | solution.py:281
  105.0 5.2 %collective-permute-start.7 = (s16[8,128,128]{2,1,0:T(8,128)(2,1)S(1)}, s16[8,128,128]{2,1,0:T(8,128)(2,1)S(1)}, u32[]{:S(2)}, u32[]{:S(2)}) collective-permute-start(s16[8,128,128]{2,1,0:T(8,128)(2,1)S(1)} %get-tuple-element.46), channel_id=1, source_target_pairs={{0,256},{256,512},{512,0},{1,257},{257,513},{513,1},{2,258},{258,5... | collective-permute-start | bytes 786440 | tf_op jit(solution)/shard_map/ppermute | solution.py:290
  110.2 1.9 collective-permute-start.8
  112.1 3.4 %collective-permute-start.5 = (bf16[2,256,128]{2,1,0:T(8,128)(2,1)S(1)}, bf16[2,256,128]{2,1,0:T(8,128)(2,1)S(1)}, u32[]{:S(2)}, u32[]{:S(2)}) collective-permute-start(bf16[2,256,128]{2,1,0:T(8,128)(2,1)S(1)} %get-tuple-element.34), channel_id=1, source_target_pairs={{0,256},{256,512},{512,0},{1,257},{257,513},{513,1},{2,258},{258,5... | collective-permute-start | bytes 393224 | tf_op jit(solution)/shard_map/ppermute | solution.py:290
  115.5 2.8 %collective-permute-start.6 = (bf16[2,256,128]{2,1,0:T(8,128)(2,1)S(1)}, bf16[2,256,128]{2,1,0:T(8,128)(2,1)S(1)}, u32[]{:S(2)}, u32[]{:S(2)}) collective-permute-start(bf16[2,256,128]{2,1,0:T(8,128)(2,1)S(1)} %get-tuple-element.34), channel_id=1, source_target_pairs={{0,512},{256,0},{512,256},{1,513},{257,1},{513,257},{2,514},{258,2... | collective-permute-start | bytes 393224 | tf_op jit(solution)/shard_map/ppermute | solution.py:290
  118.4 4.6 %collective-permute-done.5 = bf16[2,256,128]{2,1,0:T(8,128)(2,1)S(1)} collective-permute-done((bf16[2,256,128]{2,1,0:T(8,128)(2,1)S(1)}, bf16[2,256,128]{2,1,0:T(8,128)(2,1)S(1)}, u32[]{:S(2)}, u32[]{:S(2)}) %collective-permute-start.5) | collective-permute-done | bytes 131104 | tf_op jit(solution)/shard_map/ppermute | solution.py:290
  123.0 2.9 %collective-permute-done.6 = bf16[2,256,128]{2,1,0:T(8,128)(2,1)S(1)} collective-permute-done((bf16[2,256,128]{2,1,0:T(8,128)(2,1)S(1)}, bf16[2,256,128]{2,1,0:T(8,128)(2,1)S(1)}, u32[]{:S(2)}, u32[]{:S(2)}) %collective-permute-start.6) | collective-permute-done | bytes 131104 | tf_op jit(solution)/shard_map/ppermute | solution.py:290
  126.0 8.0 %all-to-all-done.3.a_ref = bf16[8,2,256,128]{3,2,1,0:T(8,128)(2,1)S(1)} async-done(((bf16[8,2,256,128]{3,2,1,0:T(8,128)(2,1)}), bf16[8,2,256,128]{3,2,1,0:T(8,128)(2,1)S(1)}, u32[]{:S(2)}, u32[]{:S(2)}) %all-to-all-start.3) | async-done | bytes 1048608 | tf_op jit(solution)/shard_map/all_to_all | solution.py:281
  134.1 3.8 %scores.1 = (f32[8,384]{1,0:T(8,128)S(1)}, bf16[4,2,256,384]{3,2,1,0:T(8,128)(2,1)S(1)}, bf16[4,2,256,256]{3,2,1,0:T(8,128)(2,1)S(1)}) custom-call(s32[2]{0:T(128)S(1)} %pad_add_fusion.1.place_ref, bf16[3,2,256,128]{3,2,1,0:T(8,128)(2,1)S(1)} %pad_maximum_fusion.n_ref, bf16[8,2,256,128]{3,2,1,0:T(8,128)(2,1)S(1)} %all-to-all-done.3.a_ref, ...), custom_call_target="tpu_custom_call" | custom-call | flops 2147483648 | bytes 4194304 | tf_op jit(solution)/shard_map/scores/pallas_call | solution.py:361
  137.8 4.2 %collective-permute-start.10 = (f32[8,384]{1,0:T(8,128)S(1)}, f32[8,384]{1,0:T(8,128)S(1)}, u32[]{:S(2)}, u32[]{:S(2)}) collective-permute-start(f32[8,384]{1,0:T(8,128)S(1)} %get-tuple-element.39.refs_0_), channel_id=1, source_target_pairs={{0,512},{256,0},{512,256},{1,513},{257,1},{513,257},{2,514},{258,2... | collective-permute-start | bytes 36872 | tf_op jit(solution)/shard_map/ppermute | solution.py:290
  142.0 2.9 %collective-permute-start.9 = (f32[8,384]{1,0:T(8,128)S(1)}, f32[8,384]{1,0:T(8,128)S(1)}, u32[]{:S(2)}, u32[]{:S(2)}) collective-permute-start(f32[8,384]{1,0:T(8,128)S(1)} %get-tuple-element.39.refs_0_), channel_id=1, source_target_pairs={{0,256},{256,512},{512,0},{1,257},{257,513},{513,1},{2,258},{258,5... | collective-permute-start | bytes 36872 | tf_op jit(solution)/shard_map/ppermute | solution.py:290
  145.7 1.7 collective-permute-done.9.refs_1_
  147.4 4.1 %grads.1 = (f32[8,384]{1,0:T(8,128)S(1)}, f32[256,256]{1,0:T(8,128)S(1)}) custom-call(s32[2]{0:T(128)S(1)} %pad_add_fusion.1.place_ref, bf16[3,2,256,128]{3,2,1,0:T(8,128)(2,1)S(1)} %pad_maximum_fusion.n_ref, bf16[8,2,256,128]{3,2,1,0:T(8,128)(2,1)S(1)} %all-to-all-done.3.a_ref, bf16[256,256]{1,0:T(8,128)(2,1)S(1)} %bitcast.37, ...), custom_call_target="tpu_custom_call" | custom-call | flops 2147483648 | bytes 4194304 | tf_op jit(solution)/shard_map/grads/pallas_call | solution.py:379
  151.5 15.0 %all_to_all.35 = f32[32,8,256]{2,1,0:T(8,128)S(1)} all-to-all(f32[32,8,256]{2,1,0:T(8,128)S(1)} %bitcast.35), channel_id=1, replica_groups=mesh['zl'=3,'y'=8,'x'=4,'zh'=4,'core'=2] {'y','x'}, dimensions={0} | all-to-all | bytes 524288 | tf_op jit(solution)/shard_map/all_to_all | solution.py:281
  166.5 5.7 %collective-permute-start.11 = (f32[8,256]{1,0:T(8,128)S(1)}, f32[8,256]{1,0:T(8,128)S(1)}, u32[]{:S(2)}, u32[]{:S(2)}) collective-permute-start(f32[8,256]{1,0:T(8,128)S(1)} %reduce_sum.18), channel_id=1, source_target_pairs={{0,1},{1,0},{2,3},{3,2},{4,5},{5,4},{6,7},{7,6},{8,9},{9,8},{10,11... | collective-permute-start | bytes 24584 | tf_op jit(solution)/shard_map/ppermute | solution.py:290
  173.0 22.0 %all_to_all.36 = f32[12,8,256]{2,1,0:T(8,128)S(1)} all-to-all(f32[12,8,256]{2,1,0:T(8,128)S(1)} %broadcast_in_dim.43), channel_id=1, replica_groups=mesh['zl'=3,'y'=8,'x'=4,'zh'=4,'core'=2] {'zl','zh'}, dimensions={0} | all-to-all | bytes 196608 | tf_op jit(solution)/shard_map/all_to_all | solution.py:281
  195.7 3.9 %all-to-all-start.6 = ((f32[32,8,256]{2,1,0:T(8,128)}), f32[32,8,256]{2,1,0:T(8,128)S(1)}, u32[]{:S(2)}, u32[]{:S(2)}) async-start(f32[32,8,256]{2,1,0:T(8,128)} %broadcast_in_dim.44), calls=%async_computation.6 | async-start | bytes 524288 | tf_op jit(solution)/shard_map/all_to_all | solution.py:281
  200.1 10.0 %all-to-all-done.6 = f32[32,8,256]{2,1,0:T(8,128)S(1)} async-done(((f32[32,8,256]{2,1,0:T(8,128)}), f32[32,8,256]{2,1,0:T(8,128)S(1)}, u32[]{:S(2)}, u32[]{:S(2)}) %all-to-all-start.6) | async-done | bytes 262176 | tf_op jit(solution)/shard_map/all_to_all | solution.py:281
  (50 shorter events, 11.2 us)
Async XLA Ops:
  0.6 24.5 %copy-start.4 = (s32[2,12]{1,0:T(2,128)S(1)}, s32[2,12]{1,0:T(2,128)}, u32[]{:S(2)}) copy-start(s32[2,12]{1,0:T(2,128)} %param.11) | copy-start | bytes 292
  2.3 32.8 %all-to-all-start = ((bf16[12,88,128]{2,1,0:T(8,128)(2,1)}), bf16[12,88,128]{2,1,0:T(8,128)(2,1)S(1)}, u32[]{:S(2)}, u32[]{:S(2)}) async-start(bf16[12,88,128]{2,1,0:T(8,128)(2,1)} %cut_features.1), calls=%async_computation | async-start | bytes 540672 | tf_op jit(solution)/shard_map/all_to_all | solution.py:281
  19.0 16.1 %collective-permute-start = (bf16[1024,128]{1,0:T(8,128)(2,1)S(1)}, bf16[1024,128]{1,0:T(8,128)(2,1)S(1)}, u32[]{:S(2)}, u32[]{:S(2)}) collective-permute-start(bf16[1024,128]{1,0:T(8,128)(2,1)S(1)} %bitcast.31), channel_id=1, source_target_pairs={{0,256},{256,512},{512,0},{1,257},{257,513},{513,1},{2,258},{258,5... | collective-permute-start | bytes 786440 | tf_op jit(solution)/shard_map/ppermute | solution.py:290
  22.3 26.5 %collective-permute-start.2 = (bf16[1024,128]{1,0:T(8,128)(2,1)S(1)}, bf16[1024,128]{1,0:T(8,128)(2,1)S(1)}, u32[]{:S(2)}, u32[]{:S(2)}) collective-permute-start(bf16[1024,128]{1,0:T(8,128)(2,1)S(1)} %bitcast.32), channel_id=1, source_target_pairs={{0,512},{256,0},{512,256},{1,513},{257,1},{513,257},{2,514},{258,2... | collective-permute-start | bytes 786440 | tf_op jit(solution)/shard_map/ppermute | solution.py:290
  36.2 4.2 %copy-start.3 = (s32[12]{0:T(128)S(1)}, s32[12]{0:T(128)}, u32[]{:S(2)}) copy-start(s32[12]{0:T(128)} %param.10) | copy-start | bytes 148
  36.2 4.2 %slice-start = ((bf16[12,128,128]{2,1,0:T(8,128)(2,1)}), bf16[4,128,128]{2,1,0:T(8,128)(2,1)S(1)}, s32[]{:S(2)}) async-start(bf16[12,128,128]{2,1,0:T(8,128)(2,1)} %param.9), calls=%async_computation.7 | async-start | bytes 262144 | tf_op jit(solution)/shard_map/slice | solution.py:313
  36.2 16.6 %all-to-all-start.1 = ((bf16[4,12,88,128]{3,2,1,0:T(8,128)(2,1)}), bf16[4,12,88,128]{3,2,1,0:T(8,128)(2,1)S(1)}, u32[]{:S(2)}, u32[]{:S(2)}) async-start(bf16[4,12,88,128]{3,2,1,0:T(8,128)(2,1)} %broadcast_in_dim.19), calls=%async_computation.1 | async-start | bytes 2162688 | tf_op jit(solution)/shard_map/all_to_all | solution.py:281
  40.4 6.7 %collective-permute-start.1 = (bf16[528,128]{1,0:T(8,128)(2,1)S(1)}, bf16[528,128]{1,0:T(8,128)(2,1)S(1)}, u32[]{:S(2)}, u32[]{:S(2)}) collective-permute-start(bf16[528,128]{1,0:T(8,128)(2,1)S(1)} %pad_maximum_fusion.1.refs_1_), channel_id=1, source_target_pairs={{0,256},{256,512},{512,0},{1,257},{257,513},{513,1},{2,258},{258,5... | collective-permute-start | bytes 405512 | tf_op jit(solution)/shard_map/ppermute | solution.py:290
  42.4 6.5 %collective-permute-start.3 = (bf16[528,128]{1,0:T(8,128)(2,1)S(1)}, bf16[528,128]{1,0:T(8,128)(2,1)S(1)}, u32[]{:S(2)}, u32[]{:S(2)}) collective-permute-start(bf16[528,128]{1,0:T(8,128)(2,1)S(1)} %pad_maximum_fusion.1.refs_1_), channel_id=1, source_target_pairs={{0,512},{256,0},{512,256},{1,513},{257,1},{513,257},{2,514},{258,2... | collective-permute-start | bytes 405512 | tf_op jit(solution)/shard_map/ppermute | solution.py:290
  52.8 8.2 %collective-permute-start.4 = (bf16[4,12,88,128]{3,2,1,0:T(8,128)(2,1)S(1)}, bf16[4,12,88,128]{3,2,1,0:T(8,128)(2,1)S(1)}, u32[]{:S(2)}, u32[]{:S(2)}) collective-permute-start(bf16[4,12,88,128]{3,2,1,0:T(8,128)(2,1)S(1)} %all-to-all-done.1.own_ref), channel_id=1, source_target_pairs={{0,1},{1,0},{2,3},{3,2},{4,5},{5,4},{6,7},{7,6},{8,9},{9,8},{10,11... | collective-permute-start | bytes 3244040 | tf_op jit(solution)/shard_map/ppermute | solution.py:290
  63.7 8.6 %copy-start.2 = (s32[2,256]{1,0:T(2,128)S(1)}, s32[2,256]{1,0:T(2,128)}, u32[]{:S(2)}) copy-start(s32[2,256]{1,0:T(2,128)} %param.12) | copy-start | bytes 6148
  63.7 8.6 %copy-start = (s32[128,1024]{1,0:T(8,128)S(1)}, s32[128,1024]{1,0:T(8,128)}, u32[]{:S(2)}) copy-start(s32[128,1024]{1,0:T(8,128)} %neg_ref) | copy-start | bytes 1572868
  63.7 32.5 %all-to-all-start.2 = ((bf16[24,2,88,128]{3,2,1,0:T(8,128)(2,1)}), bf16[24,2,88,128]{3,2,1,0:T(8,128)(2,1)S(1)}, u32[]{:S(2)}, u32[]{:S(2)}) async-start(bf16[24,2,88,128]{3,2,1,0:T(8,128)(2,1)} %tile_sums.1), calls=%async_computation.2 | async-start | bytes 2162688 | tf_op jit(solution)/shard_map/all_to_all | solution.py:281
  97.5 36.6 %all-to-all-start.3 = ((bf16[8,2,256,128]{3,2,1,0:T(8,128)(2,1)}), bf16[8,2,256,128]{3,2,1,0:T(8,128)(2,1)S(1)}, u32[]{:S(2)}, u32[]{:S(2)}) async-start(bf16[8,2,256,128]{3,2,1,0:T(8,128)(2,1)} %get-tuple-element.35), calls=%async_computation.3 | async-start | bytes 2097152 | tf_op jit(solution)/shard_map/all_to_all | solution.py:281
  104.9 13.4 %copy-start.1 = (bf16[256,256]{1,0:T(8,128)(2,1)S(1)}, bf16[256,256]{1,0:T(8,128)(2,1)}, u32[]{:S(2)}) copy-start(bf16[256,256]{1,0:T(8,128)(2,1)} %param.8) | copy-start | bytes 393220
  105.0 20.9 %collective-permute-start.7 = (s16[8,128,128]{2,1,0:T(8,128)(2,1)S(1)}, s16[8,128,128]{2,1,0:T(8,128)(2,1)S(1)}, u32[]{:S(2)}, u32[]{:S(2)}) collective-permute-start(s16[8,128,128]{2,1,0:T(8,128)(2,1)S(1)} %get-tuple-element.46), channel_id=1, source_target_pairs={{0,256},{256,512},{512,0},{1,257},{257,513},{513,1},{2,258},{258,5... | collective-permute-start | bytes 786440 | tf_op jit(solution)/shard_map/ppermute | solution.py:290
  110.2 15.8 %collective-permute-start.8 = (s16[8,128,128]{2,1,0:T(8,128)(2,1)S(1)}, s16[8,128,128]{2,1,0:T(8,128)(2,1)S(1)}, u32[]{:S(2)}, u32[]{:S(2)}) collective-permute-start(s16[8,128,128]{2,1,0:T(8,128)(2,1)S(1)} %get-tuple-element.45), channel_id=1, source_target_pairs={{0,512},{256,0},{512,256},{1,513},{257,1},{513,257},{2,514},{258,2... | collective-permute-start | bytes 786440 | tf_op jit(solution)/shard_map/ppermute | solution.py:290
  112.1 10.9 %collective-permute-start.5 = (bf16[2,256,128]{2,1,0:T(8,128)(2,1)S(1)}, bf16[2,256,128]{2,1,0:T(8,128)(2,1)S(1)}, u32[]{:S(2)}, u32[]{:S(2)}) collective-permute-start(bf16[2,256,128]{2,1,0:T(8,128)(2,1)S(1)} %get-tuple-element.34), channel_id=1, source_target_pairs={{0,256},{256,512},{512,0},{1,257},{257,513},{513,1},{2,258},{258,5... | collective-permute-start | bytes 393224 | tf_op jit(solution)/shard_map/ppermute | solution.py:290
  115.5 10.4 %collective-permute-start.6 = (bf16[2,256,128]{2,1,0:T(8,128)(2,1)S(1)}, bf16[2,256,128]{2,1,0:T(8,128)(2,1)S(1)}, u32[]{:S(2)}, u32[]{:S(2)}) collective-permute-start(bf16[2,256,128]{2,1,0:T(8,128)(2,1)S(1)} %get-tuple-element.34), channel_id=1, source_target_pairs={{0,512},{256,0},{512,256},{1,513},{257,1},{513,257},{2,514},{258,2... | collective-permute-start | bytes 393224 | tf_op jit(solution)/shard_map/ppermute | solution.py:290
  137.8 7.8 %collective-permute-start.10 = (f32[8,384]{1,0:T(8,128)S(1)}, f32[8,384]{1,0:T(8,128)S(1)}, u32[]{:S(2)}, u32[]{:S(2)}) collective-permute-start(f32[8,384]{1,0:T(8,128)S(1)} %get-tuple-element.39.refs_0_), channel_id=1, source_target_pairs={{0,512},{256,0},{512,256},{1,513},{257,1},{513,257},{2,514},{258,2... | collective-permute-start | bytes 36872 | tf_op jit(solution)/shard_map/ppermute | solution.py:290
  142.0 5.3 %collective-permute-start.9 = (f32[8,384]{1,0:T(8,128)S(1)}, f32[8,384]{1,0:T(8,128)S(1)}, u32[]{:S(2)}, u32[]{:S(2)}) collective-permute-start(f32[8,384]{1,0:T(8,128)S(1)} %get-tuple-element.39.refs_0_), channel_id=1, source_target_pairs={{0,256},{256,512},{512,0},{1,257},{257,513},{513,1},{2,258},{258,5... | collective-permute-start | bytes 36872 | tf_op jit(solution)/shard_map/ppermute | solution.py:290
  166.5 6.5 %collective-permute-start.11 = (f32[8,256]{1,0:T(8,128)S(1)}, f32[8,256]{1,0:T(8,128)S(1)}, u32[]{:S(2)}, u32[]{:S(2)}) collective-permute-start(f32[8,256]{1,0:T(8,128)S(1)} %reduce_sum.18), channel_id=1, source_target_pairs={{0,1},{1,0},{2,3},{3,2},{4,5},{5,4},{6,7},{7,6},{8,9},{9,8},{10,11... | collective-permute-start | bytes 24584 | tf_op jit(solution)/shard_map/ppermute | solution.py:290
  195.7 14.5 %all-to-all-start.6 = ((f32[32,8,256]{2,1,0:T(8,128)}), f32[32,8,256]{2,1,0:T(8,128)S(1)}, u32[]{:S(2)}, u32[]{:S(2)}) async-start(f32[32,8,256]{2,1,0:T(8,128)} %broadcast_in_dim.44), calls=%async_computation.6 | async-start | bytes 524288 | tf_op jit(solution)/shard_map/all_to_all | solution.py:281
